TPU v7x, 128 devices: a whole 4x4x4 slice. The times are simulated.
128 devices in a mesh: band: 64 (over z, y, x), mp: 2 (over core).
Axes of the slice: x: 4, y: 4, z: 4, core: 2. Of those that a mesh axis runs over, the one named last changes fastest.
Arguments:
- grid_fields: bfloat16 [131072, 100], P('band'), may hold values from -6 to 6
- w_in: bfloat16 [100, 1024], P(None, 'mp'), may hold values from -0.625 to 0.625
- enc_src: int32 [4096, 128], P('band'), may hold values from 0 to 131071, as said below
- enc_dst: int32 [4096, 128], P('band'), may hold values from 0 to 65535, as said below
- enc_weight: bfloat16 [4096, 128], P('band'), may hold values from 0.19921875 to 2
- enc_count: int32 [64], P('band'), may hold values from 32 to 64, as said below
- norm_gain: float32 [1024], replicated, may hold values from 0.1 to 1.9
- w_qkv: bfloat16 [1024, 3, 1024], P(None, None, 'mp'), may hold values from -4 to 4
- w_out_attn: bfloat16 [1024, 1024], P('mp'), may hold values from -0.1875 to 0.1875
- offsets: int32 [32], replicated, may hold values from -384 to 384, as said below
- w_decode: bfloat16 [1024, 100], P('mp'), may hold values from -0.1875 to 0.1875
- dec_src: int32 [3072, 128], P(('band', 'mp')), may hold values from 0 to 65535, as said below
- dec_dst: int32 [3072, 128], P(('band', 'mp')), may hold values from 0 to 131071, as said below
- dec_weight: bfloat16 [3072, 128], P(('band', 'mp')), may hold values from 0.19921875 to 2
Outputs:
- out_fields: bfloat16 [131072, 100], P(('band', 'mp'))
Inputs may be any that keep to these rules, and one draw needn't show every extreme that they name: `enc_src`: rows s of band b = s // 64 name grid rows from (b - 1) * 2048 to (b + 2) * 2048 - 1 that lie in the grid. `enc_dst`: row s of band b = s // 64, with t = s % 8, names mesh rows b * 1024 + t * 128 to b * 1024 + (t + 1) * 128 - 1. `enc_count`: live block slots of each band; some band has all 64. `offsets`: Distinct; they include 0, 384 and -384. `dec_src`: rows s of device d = s // 24, in band b = d // 2, name mesh rows from (b - 1) * 1024 to (b + 2) * 1024 - 1 that lie in the mesh. `dec_dst`: row s of device d = s // 24, with t = s % 8, names grid rows d * 1024 + t * 128 to d * 1024 + (t + 1) * 128 - 1.
All inputs are finite; a program needn't handle non-finite values.
Results may differ from a plain program's by a relative error of at most 0.015.
Values may be sent and summed in bfloat16 or wider, within the bound.
No kernel may reach another device: no remote copies, remote signals or barrier semaphores. Data moves between devices by JAX's collectives and lax.ppermute only.
A program may use at most 128 MiB of HBM per device.

v0:
```python
import jax
import jax.numpy as jnp
from jax import lax
from jax.sharding import PartitionSpec as P

M_DEV = 1024
QB = 512
K_OFF = 32
HEAD = 64
WIN = 384


def extended(value, sides, width):
    for axis, dim in sides:
        devices, length = (lax.axis_size(axis), value.shape[dim])
        up = [(i, (i + 1) % devices) for i in range(devices - 1)]
        down = [(j, i) for i, j in up]
        last = lax.slice_in_dim(value, length - width, length, axis=dim)
        initial = lax.slice_in_dim(value, 0, width, axis=dim)
        before = lax.ppermute(last, axis, up)
        after = lax.ppermute(initial, axis, down)
        value = jnp.concatenate([before, value, after], axis=dim)
    return value


def embed_rows(block_rows, w_in):
    return jax.nn.silu(jnp.dot(block_rows, w_in, preferred_element_type=jnp.float32)).astype(
        jnp.bfloat16
    )


def on_device(
    grid_fields,
    w_in,
    enc_src,
    enc_dst,
    enc_weight,
    enc_count,
    norm_gain,
    w_qkv,
    w_out_attn,
    offsets,
    w_decode,
    dec_src,
    dec_dst,
    dec_weight,
):
    band_rows = grid_fields.shape[0]
    quarter = w_in.shape[1]
    band_index = lax.axis_index("band")
    own_embedded = embed_rows(grid_fields, w_in)
    window = extended(own_embedded, (("band", 0),), band_rows)
    edge_len = enc_src.shape[1]
    tile_count = M_DEV // edge_len
    round_total = enc_src.shape[0] // tile_count
    live_blocks = enc_count[0]
    slot_index = jnp.arange(enc_src.shape[0], dtype=jnp.int32)
    live_weight = enc_weight * (slot_index < live_blocks)[:, None].astype(jnp.bfloat16)
    tile_base = (jnp.arange(tile_count, dtype=jnp.int32) * edge_len)[None, :, None]
    src_rounds = (enc_src - (band_index - 1) * band_rows).reshape(
        round_total, tile_count * edge_len
    )
    dst_rounds = (enc_dst - band_index * M_DEV).reshape(
        round_total, tile_count, edge_len
    ) - tile_base
    weight_rounds = live_weight.reshape(round_total, tile_count, edge_len)
    row_slots = jnp.arange(edge_len, dtype=jnp.int32)[None, :, None]
    round_count = (live_blocks + tile_count - 1) // tile_count

    def add_round(round_index, accumulated):
        sources = lax.dynamic_index_in_dim(src_rounds, round_index, 0, keepdims=False)
        targets = lax.dynamic_index_in_dim(dst_rounds, round_index, 0, keepdims=False)
        weights = lax.dynamic_index_in_dim(weight_rounds, round_index, 0, keepdims=False)
        messages = window[sources].reshape(tile_count, edge_len, quarter)
        table = jnp.where(
            targets[:, None, :] == row_slots, weights[:, None, :], jnp.zeros((), jnp.bfloat16)
        )
        return accumulated + jnp.einsum(
            "tre,ted->trd", table, messages, preferred_element_type=jnp.float32
        )

    accumulated = lax.fori_loop(
        0, round_count, add_round, jnp.zeros((tile_count, edge_len, quarter), jnp.float32)
    )
    mesh_zero = accumulated.reshape(M_DEV, quarter).astype(jnp.bfloat16)
    full_rows = lax.all_gather(mesh_zero, "mp", axis=1, tiled=True)
    full_float = full_rows.astype(jnp.float32)
    inverse = lax.rsqrt(jnp.mean(full_float * full_float, axis=1, keepdims=True) + 1e-05)
    normed = (full_float * inverse * norm_gain).astype(jnp.bfloat16)
    qkv = jnp.einsum("md,dtc->mtc", normed, w_qkv, preferred_element_type=jnp.float32).astype(
        jnp.bfloat16
    )
    queries = qkv[:, 0]
    key_value = qkv[:, 1:]
    key_value_window = extended(key_value, (("band", 0),), WIN)
    local_heads = w_qkv.shape[2] // HEAD
    mesh_total = M_DEV * lax.axis_size("band")
    outputs = []
    for block_begin in range(0, M_DEV, QB):
        local_rows = block_begin + jnp.arange(QB, dtype=jnp.int32)
        global_rows = band_index * M_DEV + local_rows[:, None] + offsets[None, :]
        inside = (global_rows >= 0) & (global_rows < mesh_total)
        head_queries = (
            queries[block_begin : block_begin + QB]
            .reshape(QB, local_heads, HEAD)
            .astype(jnp.float32)
        )
        score_list = []
        for offset_index in range(K_OFF):
            start_row = block_begin + WIN + offsets[offset_index]
            keys_here = lax.dynamic_slice_in_dim(key_value_window, start_row, QB, 0)[:, 0]
            keys_here = keys_here.reshape(QB, local_heads, HEAD).astype(jnp.float32)
            score_list.append(jnp.sum(head_queries * keys_here, axis=2))
        scores = jnp.stack(score_list, axis=2) * HEAD ** (-0.5)
        scores = jnp.where(inside[:, None, :], scores, -1e30)
        row_max = jnp.max(scores, axis=2, keepdims=True)
        expos = jnp.exp(scores - row_max)
        probs = (
            (expos / jnp.sum(expos, axis=2, keepdims=True)).astype(jnp.bfloat16).astype(jnp.float32)
        )
        attended = jnp.zeros((QB, local_heads, HEAD), jnp.float32)
        for offset_index in range(K_OFF):
            start_row = block_begin + WIN + offsets[offset_index]
            values_here = lax.dynamic_slice_in_dim(key_value_window, start_row, QB, 0)[:, 1]
            values_here = values_here.reshape(QB, local_heads, HEAD).astype(jnp.float32)
            attended = attended + probs[:, :, offset_index][:, :, None] * values_here
        outputs.append(attended.astype(jnp.bfloat16).reshape(QB, local_heads * HEAD))
    attended_rows = jnp.concatenate(outputs, axis=0)
    head_partial = jnp.dot(attended_rows, w_out_attn, preferred_element_type=jnp.float32)
    head_total = lax.psum_scatter(
        head_partial.astype(jnp.bfloat16), "mp", scatter_dimension=1, tiled=True
    ).astype(jnp.float32)
    mesh_one = (mesh_zero.astype(jnp.float32) + head_total).astype(jnp.bfloat16)
    beside_all = extended(mesh_one, (("band", 0),), M_DEV)
    partial_window = jnp.dot(beside_all, w_decode, preferred_element_type=jnp.float32)
    projected = lax.psum(partial_window.astype(jnp.bfloat16), "mp").astype(jnp.float32)
    model_index = lax.axis_index("mp")
    quarter_rows = band_rows // lax.axis_size("mp")
    channels = projected.shape[1]
    dec_tiles = quarter_rows // edge_len
    dec_rounds = dec_src.shape[0] // dec_tiles
    first_row = (band_index * lax.axis_size("mp") + model_index) * quarter_rows
    dec_sources = (dec_src - (band_index - 1) * M_DEV).reshape(-1)
    dec_base = (jnp.arange(dec_tiles, dtype=jnp.int32) * edge_len)[None, :, None]
    dec_targets = (dec_dst - first_row).reshape(dec_rounds, dec_tiles, edge_len) - dec_base
    dec_scale = dec_weight.astype(jnp.float32).reshape(dec_rounds, dec_tiles, edge_len)
    messages = projected[dec_sources].reshape(dec_rounds, dec_tiles, edge_len, channels)
    dec_slots = jnp.arange(edge_len, dtype=jnp.int32)[None, None, :, None]
    dec_table = jnp.where(dec_targets[:, :, None, :] == dec_slots, dec_scale[:, :, None, :], 0.0)
    summed = jnp.einsum(
        "qtre,qtec->trc", dec_table, messages, precision=lax.Precision.HIGHEST
    ).reshape(quarter_rows, channels)
    residual_rows = lax.dynamic_slice_in_dim(
        grid_fields, model_index * quarter_rows, quarter_rows, 0
    )
    return (residual_rows.astype(jnp.float32) + summed).astype(jnp.bfloat16)


def solution(mesh):
    return jax.shard_map(
        on_device,
        mesh=mesh,
        in_specs=(
            P("band", None),
            P(None, "mp"),
            P("band", None),
            P("band", None),
            P("band", None),
            P("band"),
            P(),
            P(None, None, "mp"),
            P("mp", None),
            P(),
            P("mp", None),
            P(("band", "mp"), None),
            P(("band", "mp"), None),
            P(("band", "mp"), None),
        ),
        out_specs=P(("band", "mp"), None),
        check_vma=False,
    )
```

profile of v0, /device:TPU:1, one launch (start us, length us, event | category | flops | bytes accessed | tf_op | source)
XLA Modules:
  0.0 611.6 jit_solution(12097166890258197808)
XLA Ops:
  6.6 3.8 multiply_convert_fusion
  11.7 5.9 collective-permute-start
  18.5 41.0 %collective-permute-done.1 = bf16[2048,512]{1,0:T(8,128)(2,1)} collective-permute-done((bf16[2048,512]{1,0:T(8,128)(2,1)}, bf16[2048,512]{1,0:T(8,128)(2,1)}, u32[]{:S(2)}, u32[]{:S(2)}) %collective-permute-start.1) | collective-permute-done | bytes 2097184 | tf_op jit(solution)/shard_map/ppermute | solution.py:21
  60.4 5.9 pad_maximum_fusion
  68.0 99.8 %while.11 = (s32[]{:T(128)}, f32[8,128,512]{2,1,0:T(8,128)}, s32[]{:T(128)}, s32[8,8,128]{2,1,0:T(8,128)S(1)}, bf16[8,8,128]{2,1,0:T(8,128)(2,1)S(1)}, /*index=5...) while((s32[]{:T(128)}, f32[8,128,512]{2,1,0:T(8,128)}, ...), condition=%wide.region_1.2_spmd.clone, body=%wide.region_0.1_spmd.clone.sunk | while | flops 135008256 | bytes 7379099 | solution.py:82
  68.0 8.7 %gather_fusion = bf16[1024,512]{1,0:T(8,128)(2,1)} fusion(bf16[6144,512]{1,0:T(8,128)(2,1)} %get-tuple-element.315, s32[1024]{0:T(1024)S(1)} %broadcast_clamp_fusion.3), kind=kCustom, calls=%fused_computation.clone.clone.1 | custom fusion | bytes 2101248 | tf_op jit(solution)/shard_map/while/body/gather | solution.py:74
  76.7 3.7 convolution_add_fusion.2
  80.5 8.7 %gather_fusion = bf16[1024,512]{1,0:T(8,128)(2,1)} fusion(bf16[6144,512]{1,0:T(8,128)(2,1)} %get-tuple-element.315, s32[1024]{0:T(1024)S(1)} %broadcast_clamp_fusion.3), kind=kCustom, calls=%fused_computation.clone.clone.1 | custom fusion | bytes 2101248 | tf_op jit(solution)/shard_map/while/body/gather | solution.py:74
  89.2 3.7 convolution_add_fusion.2
  93.0 8.7 %gather_fusion = bf16[1024,512]{1,0:T(8,128)(2,1)} fusion(bf16[6144,512]{1,0:T(8,128)(2,1)} %get-tuple-element.315, s32[1024]{0:T(1024)S(1)} %broadcast_clamp_fusion.3), kind=kCustom, calls=%fused_computation.clone.clone.1 | custom fusion | bytes 2101248 | tf_op jit(solution)/shard_map/while/body/gather | solution.py:74
  101.7 3.7 convolution_add_fusion.2
  105.5 8.7 %gather_fusion = bf16[1024,512]{1,0:T(8,128)(2,1)} fusion(bf16[6144,512]{1,0:T(8,128)(2,1)} %get-tuple-element.315, s32[1024]{0:T(1024)S(1)} %broadcast_clamp_fusion.3), kind=kCustom, calls=%fused_computation.clone.clone.1 | custom fusion | bytes 2101248 | tf_op jit(solution)/shard_map/while/body/gather | solution.py:74
  114.2 3.7 convolution_add_fusion.2
  117.9 8.7 %gather_fusion = bf16[1024,512]{1,0:T(8,128)(2,1)} fusion(bf16[6144,512]{1,0:T(8,128)(2,1)} %get-tuple-element.315, s32[1024]{0:T(1024)S(1)} %broadcast_clamp_fusion.3), kind=kCustom, calls=%fused_computation.clone.clone.1 | custom fusion | bytes 2101248 | tf_op jit(solution)/shard_map/while/body/gather | solution.py:74
  126.6 3.7 convolution_add_fusion.2
  130.4 8.7 %gather_fusion = bf16[1024,512]{1,0:T(8,128)(2,1)} fusion(bf16[6144,512]{1,0:T(8,128)(2,1)} %get-tuple-element.315, s32[1024]{0:T(1024)S(1)} %broadcast_clamp_fusion.3), kind=kCustom, calls=%fused_computation.clone.clone.1 | custom fusion | bytes 2101248 | tf_op jit(solution)/shard_map/while/body/gather | solution.py:74
  139.1 3.7 convolution_add_fusion.2
  142.9 8.7 %gather_fusion = bf16[1024,512]{1,0:T(8,128)(2,1)} fusion(bf16[6144,512]{1,0:T(8,128)(2,1)} %get-tuple-element.315, s32[1024]{0:T(1024)S(1)} %broadcast_clamp_fusion.3), kind=kCustom, calls=%fused_computation.clone.clone.1 | custom fusion | bytes 2101248 | tf_op jit(solution)/shard_map/while/body/gather | solution.py:74
  151.6 3.7 convolution_add_fusion.2
  155.4 8.7 %gather_fusion = bf16[1024,512]{1,0:T(8,128)(2,1)} fusion(bf16[6144,512]{1,0:T(8,128)(2,1)} %get-tuple-element.315, s32[1024]{0:T(1024)S(1)} %broadcast_clamp_fusion.3), kind=kCustom, calls=%fused_computation.clone.clone.1 | custom fusion | bytes 2101248 | tf_op jit(solution)/shard_map/while/body/gather | solution.py:74
  164.1 3.7 convolution_add_fusion.2
  167.8 2.7 convert_element_type.1296
  170.6 20.5 %all-gather.2.cloned.1.call-done = bf16[1024,1024]{1,0:T(8,128)(2,1)} async-done(((bf16[1024,512]{1,0:T(8,128)(2,1)}), bf16[1024,1024]{1,0:T(8,128)(2,1)}) %all-gather.2.cloned.1.call-update) | async-done | bytes 2097168 | tf_op jit(solution)/shard_map/all_gather | solution.py:86
  191.1 2.1 fusion.8
  193.2 5.7 convolution_convert_fusion.1
  201.9 3.4 collective-permute-start.2
  291.4 6.4 %convert_multiply_fusion.36 = (f32[512,1,512]{0,2,1:T(8,128)}, f32[512,1,512]{0,2,1:T(8,128)}, f32[512,1,512]{0,2,1:T(8,128)}, f32[512,1,512]{0,2,1:T(8,128)}, f...) fusion(bf16[1792,2,512]{0,2,1:T(8,128)(2,1)S(1)} %pad_maximum_f, ...), kind=kLoop, calls=%fused_computation.50 | loop fusion | flops 5242880 | bytes 15204388 | tf_op jit(solution)/shard_map/mul | solution.py:113
  301.1 9.8 %convert_multiply_fusion.32 = (f32[512,1,512]{0,2,1:T(8,128)}, f32[512,1,512]{0,2,1:T(8,128)}, f32[512,1,512]{0,2,1:T(8,128)}, f32[512,1,512]{0,2,1:T(8,128)}, f...) fusion(bf16[1792,2,512]{0,2,1:T(8,128)(2,1)} %copy-done.2, ...), kind=kLoop, calls=%fused_computation.46 | loop fusion | flops 5242880 | bytes 15204388 | tf_op jit(solution)/shard_map/mul | solution.py:113
  319.0 9.6 %convert_multiply_fusion.33 = (f32[512,1,512]{0,2,1:T(8,128)}, f32[512,1,512]{0,2,1:T(8,128)}, f32[512,1,512]{0,2,1:T(8,128)}, f32[512,1,512]{0,2,1:T(8,128)}, f...) fusion(bf16[1792,2,512]{0,2,1:T(8,128)(2,1)} %copy-done.2, ...), kind=kLoop, calls=%fused_computation.47 | loop fusion | flops 5242880 | bytes 15204388 | tf_op jit(solution)/shard_map/mul | solution.py:113
  339.4 10.0 %convert_multiply_fusion.34 = (f32[512,1,512]{0,2,1:T(8,128)}, f32[512,1,512]{0,2,1:T(8,128)}, f32[512,1,512]{0,2,1:T(8,128)}, f32[512,1,512]{0,2,1:T(8,128)}, f...) fusion(bf16[1792,2,512]{0,2,1:T(8,128)(2,1)} %copy-done.2, ...), kind=kLoop, calls=%fused_computation.48 | loop fusion | flops 5242880 | bytes 15204388 | tf_op jit(solution)/shard_map/mul | solution.py:113
  360.1 9.7 %convert_multiply_fusion.35 = (f32[512,1,512]{0,2,1:T(8,128)}, f32[512,1,512]{0,2,1:T(8,128)}, f32[512,1,512]{0,2,1:T(8,128)}, f32[512,1,512]{0,2,1:T(8,128)}, f...) fusion(bf16[1792,2,512]{0,2,1:T(8,128)(2,1)} %copy-done.2, ...), kind=kLoop, calls=%fused_computation.49 | loop fusion | flops 5242880 | bytes 15204388 | tf_op jit(solution)/shard_map/mul | solution.py:113
  379.5 1.9 reduce_sum.641
  381.4 1.9 reduce_sum.640
  383.3 1.9 reduce_sum.639
  414.5 2.4 convert_multiply_fusion.61
  418.3 9.8 %convert_multiply_fusion.52 = (f32[512,1,512]{0,2,1:T(8,128)}, f32[512,1,512]{0,2,1:T(8,128)}, f32[512,1,512]{0,2,1:T(8,128)}, f32[512,1,512]{0,2,1:T(8,128)}, f...) fusion(bf16[1792,2,512]{0,2,1:T(8,128)(2,1)} %copy-done.2, ...), kind=kLoop, calls=%fused_computation.66 | loop fusion | flops 4980736 | bytes 14680100 | tf_op jit(solution)/shard_map/mul | solution.py:113
  458.5 9.6 %convert_multiply_fusion.43 = (f32[512,1,512]{0,2,1:T(8,128)}, f32[512,1,512]{0,2,1:T(8,128)}, f32[512,1,512]{0,2,1:T(8,128)}, f32[512,1,512]{0,2,1:T(8,128)}, f...) fusion(bf16[1792,2,512]{0,2,1:T(8,128)(2,1)} %copy-done.2, ...), kind=kLoop, calls=%fused_computation.57 | loop fusion | flops 4980736 | bytes 14680100 | tf_op jit(solution)/shard_map/mul | solution.py:113
  480.4 12.0 %fusion.29 = bf16[512,512]{0,1:T(8,128)(2,1)S(1)} fusion(bf16[1792,2,512]{0,2,1:T(8,128)(2,1)S(1)} %copy-done.3, s32[]{:T(128)S(6)} %select_n.374, s32[]{:T(128)S(6)} %add.1749, s32[]{:T(128)S(6)} %select_n.373, s32[]{:T(128)S(6)} %select_n.372, s32[]{:T(128)S(6)} %select_n.371, s32[]{:T(128)S(6)} %select_n.370, s32[]{:T(128)S(6)} %select_n.369, ...), kind=kLoop, calls=%fused_computation.107 | loop fusion | flops 25165824 | bytes 17825924 | tf_op jit(solution)/shard_map/convert_element_type | solution.py:127
  492.4 12.5 %fusion.61 = bf16[512,512]{0,1:T(8,128)(2,1)S(1)} fusion(bf16[1792,2,512]{0,2,1:T(8,128)(2,1)S(1)} %copy-done.3, s32[]{:T(128)S(6)} %select_n.341, s32[]{:T(128)S(6)} %add.1749, s32[]{:T(128)S(6)} %select_n.340, s32[]{:T(128)S(6)} %select_n.339, s32[]{:T(128)S(6)} %select_n.338, s32[]{:T(128)S(6)} %select_n.337, s32[]{:T(128)S(6)} %select_n.336, ...), kind=kLoop, calls=%fused_computation.171 | loop fusion | flops 25165824 | bytes 17825924 | tf_op jit(solution)/shard_map/convert_element_type | solution.py:127
  504.9 2.6 convolution_convert_fusion.2
  507.7 15.2 %reduce-scatter.2.cloned.1.call-done = bf16[1024,512]{1,0:T(8,128)(2,1)} async-done(((bf16[1024,1024]{1,0:T(8,128)(2,1)}), bf16[1024,512]{1,0:T(8,128)(2,1)}) %reduce-scatter.2.cloned.1.call-update) | async-done | bytes 1048592 | tf_op jit(solution)/shard_map/reduce_scatter | solution.py:130
  525.7 5.0 collective-permute-start.4
  530.8 20.1 %collective-permute-done.5 = bf16[1024,512]{1,0:T(8,128)(2,1)S(1)} collective-permute-done((bf16[1024,512]{1,0:T(8,128)(2,1)S(1)}, bf16[1024,512]{1,0:T(8,128)(2,1)S(1)}, u32[]{:S(2)}, u32[]{:S(2)}) %collective-permute-start.5) | collective-permute-done | bytes 1048608 | tf_op jit(solution)/shard_map/ppermute | solution.py:21
  551.8 3.2 convolution_convert_fusion
  555.0 31.8 %all-reduce.2.cloned.1.call-done = bf16[3072,100]{0,1:T(8,128)(2,1)} async-done(((bf16[3072,100]{0,1:T(8,128)(2,1)}), bf16[3072,100]{0,1:T(8,128)(2,1)}) %all-reduce.2.cloned.1.call-update) | async-done | bytes 614416 | tf_op jit(solution)/shard_map/psum | solution.py:136
  586.8 2.3 copy.23
  589.1 12.3 %gather_fusion.1 = bf16[3072,100]{1,0:T(8,128)(2,1)} fusion(bf16[3072,100]{1,0:T(8,128)(2,1)} %copy.23, s32[3072]{0:T(1024)S(1)} %broadcast_clamp_fusion.1), kind=kCustom, calls=%fused_computation.1 | custom fusion | bytes 1241088 | tf_op jit(solution)/shard_map/gather | solution.py:147
  601.4 2.5 fusion.22
  (316 shorter events, 132.1 us)
Async XLA Ops:
  6.5 186.7 %copy-start = (bf16[1024,3,512]{2,0,1:T(8,128)(2,1)S(1)}, bf16[1024,3,512]{2,0,1:T(8,128)(2,1)}, u32[]{:S(2)}) copy-start(bf16[1024,3,512]{2,0,1:T(8,128)(2,1)} %param.23) | copy-start | bytes 9437188
  6.5 11.7 %copy-start.43 = (s32[64,128]{1,0:T(8,128)S(1)}, s32[64,128]{1,0:T(8,128)}, u32[]{:S(2)}) copy-start(s32[64,128]{1,0:T(8,128)} %param.18) | copy-start | bytes 98308
  6.5 11.8 %copy-start.45 = (bf16[64,128]{1,0:T(8,128)(2,1)S(1)}, bf16[64,128]{1,0:T(8,128)(2,1)}, u32[]{:S(2)}) copy-start(bf16[64,128]{1,0:T(8,128)(2,1)} %param.20) | copy-start | bytes 49156
  6.5 11.9 %copy-start.44 = (s32[64,128]{1,0:T(8,128)S(1)}, s32[64,128]{1,0:T(8,128)}, u32[]{:S(2)}) copy-start(s32[64,128]{1,0:T(8,128)} %param.19) | copy-start | bytes 98308
  6.5 184.6 %all-gather.2.cloned.1.call-start = ((), (), s32[]{:S(2)}) async-start(), calls=%async_computation.1 | async-start | bytes 3145728 | tf_op jit(solution)/shard_map/all_gather | solution.py:86
  10.4 49.1 %collective-permute-start.1 = (bf16[2048,512]{1,0:T(8,128)(2,1)}, bf16[2048,512]{1,0:T(8,128)(2,1)}, u32[]{:S(2)}, u32[]{:S(2)}) collective-permute-start(bf16[2048,512]{1,0:T(8,128)(2,1)} %multiply_convert_fusion), channel_id=1, source_target_pairs={{2,0},{4,2},{6,4},{8,6},{10,8},{12,10},{14,12},{16,14},{18,16},{20... | collective-permute-start | bytes 6291464 | tf_op jit(solution)/shard_map/ppermute | solution.py:21
  11.7 48.7 %collective-permute-start = (bf16[2048,512]{1,0:T(8,128)(2,1)}, bf16[2048,512]{1,0:T(8,128)(2,1)}, u32[]{:S(2)}, u32[]{:S(2)}) collective-permute-start(bf16[2048,512]{1,0:T(8,128)(2,1)} %multiply_convert_fusion), channel_id=1, source_target_pairs={{0,2},{2,4},{4,6},{6,8},{8,10},{10,12},{12,14},{14,16},{16,18},{18... | collective-permute-start | bytes 6291464 | tf_op jit(solution)/shard_map/ppermute | solution.py:20
  18.3 48.0 %copy-start.49 = (s32[8]{0:T(128)}, s32[8]{0:T(128)S(1)}, u32[]{:S(2)}) copy-start(s32[8]{0:T(128)S(1)} %iota_multiply_fusion) | copy-start | bytes 100
  167.8 25.4 %copy-start.53 = (f32[1024]{0:T(1024)S(1)}, f32[1024]{0:T(1024)}, u32[]{:S(2)}) copy-start(f32[1024]{0:T(1024)} %param.22) | copy-start | bytes 12292
  170.6 352.3 %reduce-scatter.2.cloned.1.call-start = ((), (), s32[]{:S(2)}) async-start(), calls=%async_computation.2 | async-start | bytes 3145728 | tf_op jit(solution)/shard_map/reduce_scatter | solution.py:130
  198.9 1.7 copy-start.5
  200.6 6.0 copy-start.11
  201.9 87.5 %slice-start = ((bf16[1024,3,512]{0,2,1:T(8,128)(2,1)}), bf16[1024,2,512]{0,2,1:T(8,128)(2,1)S(1)}, s32[]{:S(2)}) async-start(bf16[1024,3,512]{0,2,1:T(8,128)(2,1)} %copy-done.5), calls=%async_computation.4 | async-start | bytes 4194304 | tf_op jit(solution)/shard_map/slice | solution.py:94
  201.9 87.4 %collective-permute-start.2 = (bf16[384,2,512]{0,2,1:T(8,128)(2,1)}, bf16[384,2,512]{0,2,1:T(8,128)(2,1)S(1)}, u32[]{:S(2)}, u32[]{:S(2)}) collective-permute-start(bf16[384,2,512]{0,2,1:T(8,128)(2,1)} %get-tuple-element.143), channel_id=1, source_target_pairs={{0,2},{2,4},{4,6},{6,8},{8,10},{10,12},{12,14},{14,16},{16,18},{18... | collective-permute-start | bytes 2359304 | tf_op jit(solution)/shard_map/ppermute | solution.py:20
  205.3 84.1 %collective-permute-start.3 = (bf16[384,2,512]{0,2,1:T(8,128)(2,1)}, bf16[384,2,512]{0,2,1:T(8,128)(2,1)}, u32[]{:S(2)}, u32[]{:S(2)}) collective-permute-start(bf16[384,2,512]{0,2,1:T(8,128)(2,1)} %get-tuple-element.144), channel_id=1, source_target_pairs={{2,0},{4,2},{6,4},{8,6},{10,8},{12,10},{14,12},{16,14},{18,16},{20... | collective-permute-start | bytes 2359304 | tf_op jit(solution)/shard_map/ppermute | solution.py:21
  289.3 2.1 copy-start.6
  291.4 6.4 %copy-start.2 = (bf16[1792,2,512]{0,2,1:T(8,128)(2,1)}, bf16[1792,2,512]{0,2,1:T(8,128)(2,1)S(1)}, u32[]{:S(2)}) copy-start(bf16[1792,2,512]{0,2,1:T(8,128)(2,1)S(1)} %pad_maximum_fusion.1) | copy-start | bytes 11010052
  291.4 9.7 %copy-start.7 = (bf16[1024,3,512]{0,2,1:T(8,128)(2,1)S(1)}, bf16[1024,3,512]{0,2,1:T(8,128)(2,1)}, u32[]{:S(2)}) copy-start(bf16[1024,3,512]{0,2,1:T(8,128)(2,1)} %copy-done.5) | copy-start | bytes 9437188
  469.4 8.3 %copy-start.10 = (f32[512,1,512]{0,2,1:T(8,128)S(1)}, f32[512,1,512]{0,2,1:T(8,128)}, u32[]{:S(2)}) copy-start(f32[512,1,512]{0,2,1:T(8,128)} %get-tuple-element.132) | copy-start | bytes 3145732
  470.8 7.3 %copy-start.9 = (f32[512,1,512]{0,2,1:T(8,128)S(1)}, f32[512,1,512]{0,2,1:T(8,128)}, u32[]{:S(2)}) copy-start(f32[512,1,512]{0,2,1:T(8,128)} %get-tuple-element.133) | copy-start | bytes 3145732
  472.3 6.0 copy-start.8
  477.7 1.4 copy-start.13
  477.7 1.4 copy-start.14
  477.8 1.4 copy-start.15
  477.8 1.4 copy-start.16
  477.8 1.4 copy-start.17
  477.8 1.4 copy-start.18
  477.8 1.4 copy-start.19
  477.8 1.4 copy-start.20
  477.8 1.4 copy-start.21
  477.8 1.4 copy-start.22
  477.8 1.4 copy-start.23
  477.8 1.4 copy-start.24
  477.9 1.4 copy-start.25
  477.9 1.4 copy-start.26
  478.3 2.1 copy-start.3
  492.4 12.5 %copy-start.51 = (bf16[512,1024]{1,0:T(8,128)(2,1)S(1)}, bf16[512,1024]{1,0:T(8,128)(2,1)}, u32[]{:S(2)}) copy-start(bf16[512,1024]{1,0:T(8,128)(2,1)} %param.24) | copy-start | bytes 3145732
  507.6 15.3 %copy-start.4 = (f32[8,128,512]{2,1,0:T(8,128)S(1)}, f32[8,128,512]{2,1,0:T(8,128)}, u32[]{:S(2)}) copy-start(f32[8,128,512]{2,1,0:T(8,128)} %get-tuple-element.48) | copy-start | bytes 6291460
  507.6 23.2 %copy-start.46 = (s32[24,128]{1,0:T(8,128)S(1)}, s32[24,128]{1,0:T(8,128)}, u32[]{:S(2)}) copy-start(s32[24,128]{1,0:T(8,128)} %param.28) | copy-start | bytes 36868
  507.6 23.2 %copy-start.50 = (s32[8]{0:T(128)S(1)}, s32[8]{0:T(128)}, u32[]{:S(2)}) copy-start(s32[8]{0:T(128)} %copy-done.49) | copy-start | bytes 100
  507.6 23.2 %copy-start.48 = (bf16[24,128]{1,0:T(8,128)(2,1)S(1)}, bf16[24,128]{1,0:T(8,128)(2,1)}, u32[]{:S(2)}) copy-start(bf16[24,128]{1,0:T(8,128)(2,1)} %param.29) | copy-start | bytes 18436
  507.6 23.3 %copy-start.47 = (s32[24,128]{1,0:T(8,128)S(1)}, s32[24,128]{1,0:T(8,128)}, u32[]{:S(2)}) copy-start(s32[24,128]{1,0:T(8,128)} %param.27) | copy-start | bytes 36868
  507.6 44.2 %copy-start.52 = (bf16[512,100]{0,1:T(8,128)(2,1)S(1)}, bf16[512,100]{0,1:T(8,128)(2,1)}, u32[]{:S(2)}) copy-start(bf16[512,100]{0,1:T(8,128)(2,1)} %param.26) | copy-start | bytes 307204
  507.6 79.2 %all-reduce.2.cloned.1.call-start = ((), (), s32[]{:S(2)}) async-start(), calls=%async_computation.3 | async-start | bytes 1277952 | tf_op jit(solution)/shard_map/psum | solution.py:136
  524.4 26.5 %collective-permute-start.5 = (bf16[1024,512]{1,0:T(8,128)(2,1)S(1)}, bf16[1024,512]{1,0:T(8,128)(2,1)S(1)}, u32[]{:S(2)}, u32[]{:S(2)}) collective-permute-start(bf16[1024,512]{1,0:T(8,128)(2,1)S(1)} %add_convert_fusion), channel_id=1, source_target_pairs={{2,0},{4,2},{6,4},{8,6},{10,8},{12,10},{14,12},{16,14},{18,16},{20... | collective-permute-start | bytes 3145736 | tf_op jit(solution)/shard_map/ppermute | solution.py:21
  525.7 26.1 %collective-permute-start.4 = (bf16[1024,512]{1,0:T(8,128)(2,1)S(1)}, bf16[1024,512]{1,0:T(8,128)(2,1)}, u32[]{:S(2)}, u32[]{:S(2)}) collective-permute-start(bf16[1024,512]{1,0:T(8,128)(2,1)S(1)} %add_convert_fusion), channel_id=1, source_target_pairs={{0,2},{2,4},{4,6},{6,8},{8,10},{10,12},{12,14},{14,16},{16,18},{18... | collective-permute-start | bytes 3145736 | tf_op jit(solution)/shard_map/ppermute | solution.py:20
  589.1 15.8 %copy-start.1 = (bf16[1024,3,512]{2,0,1:T(8,128)(2,1)S(1)}, bf16[1024,3,512]{2,0,1:T(8,128)(2,1)}, u32[]{:S(2)}) copy-start(bf16[1024,3,512]{2,0,1:T(8,128)(2,1)} %param.23) | copy-start | bytes 9437188
  601.4 2.7 copy-start.12
  (16 other events, 21.3 us)
Sparse Core Ops, SparseCore 0:
  170.7 20.3 all-gather.1
  507.7 15.0 reduce-scatter.1
  555.1 31.6 all-reduce.1
where the time goes:
time: 623 us; the launch traced here: 612 us
  other arithmetic  200 us (32%)
  waiting for transfers between devices  130 us (21%)
  local copies, waits for them, and re-layouts  119 us (19%)
  between operations  96.5 us (15%)
  matrix products  47.6 us (8%)
  starting transfers between devices  18.2 us (3%)
    reduce_sum x64, other arithmetic, on_device(): score_list.append(jnp.sum(head_queries * keys_here, axis=2))  88.7 us
    gather x8, local copies, waits for them, and re-layouts, add_round(): messages = window[sources].reshape(tile_count, edge_len, quarter)  69.6 us
    mul x8, other arithmetic, on_device(): score_list.append(jnp.sum(head_queries * keys_here, axis=2))  67.2 us
    ppermute x3, waiting for transfers between devices, extended(): after = lax.ppermute(initial, axis, down)  61.1 us
    psum x1, waiting for transfers between devices, on_device(): lax.psum(partial_window.astype(jnp.bfloat16), 'mp').astype(jnp.float32)  31.8 us
    dot_general x8, matrix products, add_round(): jnp.einsum('tre,ted->trd', table, messages, preferred_element_type=jnp.fl...  29.9 us
    unnamed x172, local copies, waits for them, and re-layouts  28.3 us
    convert_element_type x2, other arithmetic, on_device(): attended.astype(jnp.bfloat16).reshape(QB, local_heads * HEAD)  24.5 us
  transfers between devices with their start and end apart: 9, of which 7 were waited for; matrix products, arithmetic and copies ran while one was open for 0% of the time, Pallas kernels for 0%

commit v1 on v0

v1 whole, which is shorter than its diff:
```python
import math
import jax
import jax.numpy as jnp
from jax import lax
from jax.experimental import pallas as pl
from jax.experimental.pallas import tpu as pltpu
from jax.sharding import PartitionSpec as P

D = 1024
C = 100
LANES = 128
TILE = 128
ROWS = 512
WIN = 384
K_OFF = 32
HALF = 512
G_BAND = 2048
EDGE_ROUNDS = 8
TILES = 4
STEP = 256
SPAN = TILE + 2 * WIN
WINDOW = ROWS + 2 * WIN
GQ = 1024
DEC_ROUNDS = 3
DEC_TILES = 8
MASKED = -1e30
SCALE = 64 ** (-0.5) * math.log2(math.e)
F32 = jnp.float32
BF16 = jnp.bfloat16
VMEM_BYTES = 56 * 1024 * 1024


def vmem():
    return pl.BlockSpec(memory_space=pltpu.VMEM)


def smem():
    return pl.BlockSpec(memory_space=pltpu.SMEM)


def call(body, operands, smem_count, outs, scratch, flops, touched, name):
    specs = [smem()] * smem_count + [vmem()] * (len(operands) - smem_count)
    return pl.pallas_call(
        body,
        out_shape=outs,
        in_specs=specs,
        out_specs=jax.tree.map(lambda _: vmem(), outs),
        scratch_shapes=scratch,
        compiler_params=pltpu.CompilerParams(vmem_limit_bytes=VMEM_BYTES),
        cost_estimate=pl.CostEstimate(flops=flops, bytes_accessed=touched, transcendentals=0),
        name=name,
    )(*operands)


def matmul(a, b):
    return jnp.dot(a, b, preferred_element_type=F32)


def encode_body(
    info, src, before, own, after, win_own, win_peer, dst, weight, gain,
    mesh_zero, normed,
    rows, first, second, w_in, weights, total,
):
    core, live, grid_base, mesh_base = info[0], info[1], info[2], info[3]
    rows[...] = jnp.zeros_like(rows)
    for place, part in enumerate((before, own, after)):
        rows[place * G_BAND : (place + 1) * G_BAND, :C] = part[...].astype(F32)

    @pl.when(core == 0)
    def _():
        w_in[:, :HALF] = win_own[...]
        w_in[:, HALF:] = win_peer[...]

    @pl.when(core != 0)
    def _():
        w_in[:, :HALF] = win_peer[...]
        w_in[:, HALF:] = win_own[...]

    slots = lax.broadcasted_iota(jnp.int32, weights.shape, 0)
    weights[...] = jnp.where(slots < live, weight[...].astype(F32), 0.0)
    total[...] = jnp.zeros_like(total)
    row_slots = lax.broadcasted_iota(jnp.int32, (TILE, LANES), 0)
    steps = EDGE_ROUNDS * TILE // STEP
    rounds = STEP // TILE

    def slot_of(step, part):
        tile, chunk = step // steps, step % steps
        return (chunk * rounds + part) * 2 * TILES + core * TILES + tile

    def gather(step, buffer):
        for part in range(rounds):
            slot = slot_of(step, part)
            for edge in range(TILE):
                index = src[slot, edge] - grid_base
                buffer[pl.ds(part * TILE + edge, 1), :] = rows[pl.ds(index, 1), :]

    def add(step, buffer):
        tile = step // steps
        half = matmul(buffer[...].astype(BF16), w_in[...])
        embedded = (half + half * jnp.tanh(half)).astype(BF16)
        tables = []
        for part in range(rounds):
            slot = slot_of(step, part)
            target = dst[pl.ds(slot, 1), :] - (mesh_base + tile * TILE)
            tables.append(jnp.where(row_slots == target, weights[pl.ds(slot, 1), :], 0.0))
        table = jnp.concatenate(tables, axis=1).astype(BF16)
        place = pl.ds(pl.multiple_of(tile * TILE, TILE), TILE)
        total[place, :] += matmul(table, embedded)

    gather(0, first)

    def pair(index, carry):
        gather(2 * index + 1, second)
        add(2 * index, first)
        gather(jnp.minimum(2 * index + 2, TILES * steps - 1), first)
        add(2 * index + 1, second)
        return carry

    lax.fori_loop(0, TILES * steps // 2, pair, 0)

    def finish(tile, carry):
        place = pl.ds(pl.multiple_of(tile * TILE, TILE), TILE)
        rounded = total[place, :].astype(BF16)
        mesh_zero[place, :] = rounded
        values = rounded.astype(F32)
        inverse = lax.rsqrt(jnp.mean(values * values, axis=1, keepdims=True) + 1e-05)
        normed[place, :] = (values * inverse * gain[...]).astype(BF16)
        return carry

    lax.fori_loop(0, TILES, finish, 0)


def project_body(offsets, normed, w_own, w_peer, queries, keys, values_t, bias):
    rows = normed[...]
    for half, weight in enumerate((w_own, w_peer)):
        place = slice(half * HALF, (half + 1) * HALF)
        queries[:, place] = matmul(rows, weight[:, :HALF]).astype(BF16)
        keys[:, place] = matmul(rows, weight[:, HALF : 2 * HALF]).astype(BF16)
        values = matmul(rows, weight[:, 2 * HALF : 3 * HALF])
        values_t[place, :] = values.T.astype(BF16)
    for chunk in range(SPAN // TILE):
        row = lax.broadcasted_iota(jnp.int32, (TILE, LANES), 0) + (chunk * TILE - WIN)
        away = row - lax.broadcasted_iota(jnp.int32, (TILE, LANES), 1)
        hit = away == offsets[0]
        for k in range(1, K_OFF):
            hit = hit | (away == offsets[k])
        bias[chunk * TILE : (chunk + 1) * TILE, :] = jnp.where(hit, 0.0, MASKED)


def attend_body(
    info, before, after, queries, keys_own, values_own, bias, w_own, w_peer, mesh_zero,
    out_own, out_peer, dec_own, dec_peer,
    projected,
    keys, values_t, masks, attended, w_decode,
):
    core, first_device, last_device = info[0], info[4], info[5]

    @pl.when(core == 0)
    def _():
        w_decode[:HALF, :] = dec_own[...]
        w_decode[HALF:, :] = dec_peer[...]

    @pl.when(core != 0)
    def _():
        w_decode[:HALF, :] = dec_peer[...]
        w_decode[HALF:, :] = dec_own[...]

    keys[WIN : WIN + ROWS, :] = keys_own[...]
    values_t[:, WIN : WIN + ROWS] = values_own[...]
    for begin, part in ((0, before), (WIN + ROWS, after)):
        rows = part[...]
        for half, weight in enumerate((w_own, w_peer)):
            place = slice(half * HALF, (half + 1) * HALF)
            keys[begin : begin + WIN, place] = matmul(rows, weight[:, HALF : 2 * HALF]).astype(BF16)
            values = matmul(rows, weight[:, 2 * HALF : 3 * HALF])
            values_t[place, begin : begin + WIN] = values.T.astype(BF16)
    low = jnp.where(first_device == 1, MASKED, 0.0)
    high = jnp.where(last_device == 1, MASKED, 0.0)
    for block in range(TILES):
        for chunk in range(SPAN // TILE):
            place = slice(chunk * TILE, (chunk + 1) * TILE)
            mask = bias[place, :]
            if block + chunk < WIN // TILE:
                mask = mask + low
            if block + chunk >= (WIN + ROWS) // TILE:
                mask = mask + high
            masks[block, place, :] = mask
    lane = lax.broadcasted_iota(jnp.int32, (TILE, LANES), 1)

    def head_pair(pair, carry):
        place = pl.ds(pl.multiple_of(pair * LANES, LANES), LANES)
        for block in range(TILES):
            own = slice(block * TILE, (block + 1) * TILE)
            seen = slice(block * TILE, block * TILE + SPAN)
            query = queries[own, place].astype(F32)
            stacked = jnp.concatenate(
                [jnp.where(lane < 64, query, 0.0), jnp.where(lane < 64, 0.0, query)], axis=0
            ).astype(BF16)
            score = lax.dot_general(
                keys[seen, place], stacked, (((1,), (1,)), ((), ())), preferred_element_type=F32
            )
            mask = masks[block]
            score = score * SCALE + jnp.concatenate([mask, mask], axis=1)
            top = jnp.max(score, axis=0, keepdims=True)
            expos = jnp.exp2(score - top)
            inverse = 1.0 / jnp.sum(expos, axis=0, keepdims=True)
            result = matmul(values_t[place, seen], expos.astype(BF16)) * inverse
            both = jnp.concatenate([result[:64, :TILE], result[64:, TILE:]], axis=0)
            attended[place, own] = both.astype(BF16)
        return carry

    lax.fori_loop(0, D // LANES, head_pair, 0)
    term_own = matmul(attended[:HALF, :].T, out_own[...]).astype(BF16).astype(F32)
    term_peer = matmul(attended[HALF:, :].T, out_peer[...]).astype(BF16).astype(F32)
    mesh_one = (mesh_zero[...].astype(F32) + (term_own + term_peer)).astype(BF16)
    projected[...] = matmul(mesh_one, w_decode[...]).astype(BF16)


def decode_body(
    info, src, own, peer, before_same, before_other, after_same, after_other, dst, weight, grid,
    out, rows, messages,
):
    core, mesh_base, row_base = info[0], info[6], info[7]
    other = 1 - core
    for place, part in (
        (core, before_same), (other, before_other), (2 + core, own), (2 + other, peer),
        (4 + core, after_same), (4 + other, after_other),
    ):
        rows[pl.ds(pl.multiple_of(place * ROWS, ROWS), ROWS), :] = part[...].astype(F32)
    row_slots = lax.broadcasted_iota(jnp.int32, (TILE, LANES), 0)

    def tile_sum(tile, carry):
        tables = []
        for part in range(DEC_ROUNDS):
            slot = part * DEC_TILES + tile
            for edge in range(TILE):
                index = src[slot, edge] - mesh_base
                messages[pl.ds(part * TILE + edge, 1), :] = rows[pl.ds(index, 1), :]
            target = dst[pl.ds(slot, 1), :] - (row_base + tile * TILE)
            tables.append(jnp.where(row_slots == target, weight[pl.ds(slot, 1), :], 0.0))
        table = jnp.concatenate(tables, axis=1).astype(BF16)
        summed = matmul(table, messages[...].astype(BF16))
        place = pl.ds(pl.multiple_of(tile * TILE, TILE), TILE)
        fields = grid[pl.ds(pl.multiple_of(core * GQ + tile * TILE, TILE), TILE), :]
        out[place, :] = (fields.astype(F32) + summed[:, :C]).astype(BF16)
        return carry

    lax.fori_loop(0, DEC_TILES, tile_sum, 0)


def shifted(value, step):
    bands = lax.axis_size("band")
    pairs = [(i, i + step) for i in range(bands) if 0 <= i + step < bands]
    return lax.ppermute(value, "band", pairs)


def swapped(value):
    return lax.ppermute(value, "mp", [(0, 1), (1, 0)])


def ring_shifted(value, step):
    devices = lax.axis_size("band") * 2
    pairs = [(i, i + step) for i in range(devices) if 0 <= i + step < devices]
    return lax.ppermute(value, ("band", "mp"), pairs)


def band_other(value, step):
    bands = lax.axis_size("band")
    pairs = [
        (2 * i + j, 2 * (i + step) + 1 - j)
        for i in range(bands) for j in range(2) if 0 <= i + step < bands
    ]
    return lax.ppermute(value, ("band", "mp"), pairs)


def on_device(
    grid_fields, w_in, enc_src, enc_dst, enc_weight, enc_count, norm_gain, w_qkv, w_out_attn,
    offsets, w_decode, dec_src, dec_dst, dec_weight,
):
    band = lax.axis_index("band")
    core = lax.axis_index("mp")
    bands = lax.axis_size("band")
    device = 2 * band + core
    info = jnp.stack([
        core,
        enc_count[0],
        (band - 1) * G_BAND,
        device * ROWS,
        (device == 0).astype(jnp.int32),
        (device == 2 * bands - 1).astype(jnp.int32),
        (band - 1) * 2 * ROWS,
        device * GQ,
    ]).astype(jnp.int32)
    grid_before = shifted(grid_fields, 1)
    grid_after = shifted(grid_fields, -1)
    win_own = jnp.pad(w_in * 0.5, ((0, LANES - C), (0, 0)))
    win_peer = swapped(win_own)
    dec_own = jnp.pad(w_decode, ((0, 0), (0, LANES - C)))
    dec_peer = swapped(dec_own)
    qkv_own = w_qkv.reshape(D, 3 * HALF)
    qkv_peer = swapped(qkv_own)
    out_peer = swapped(w_out_attn)
    mesh_zero, normed = call(
        encode_body,
        (info, enc_src, grid_before, grid_fields, grid_after, win_own, win_peer, enc_dst,
         enc_weight, norm_gain.reshape(1, D)),
        2,
        [jax.ShapeDtypeStruct((ROWS, D), BF16)] * 2,
        [
            pltpu.VMEM((3 * G_BAND, LANES), F32),
            pltpu.VMEM((STEP, LANES), F32),
            pltpu.VMEM((STEP, LANES), F32),
            pltpu.VMEM((LANES, D), BF16),
            pltpu.VMEM(enc_weight.shape, F32),
            pltpu.VMEM((ROWS, D), F32),
        ],
        8 * 10 ** 9, 4 * 10 ** 6, "encode",
    )
    halo_before = ring_shifted(normed[ROWS - WIN :], 1)
    halo_after = ring_shifted(normed[:WIN], -1)
    queries, keys, values_t, bias = call(
        project_body,
        (offsets, normed, qkv_own, qkv_peer),
        1,
        [
            jax.ShapeDtypeStruct((ROWS, D), BF16),
            jax.ShapeDtypeStruct((ROWS, D), BF16),
            jax.ShapeDtypeStruct((D, ROWS), BF16),
            jax.ShapeDtypeStruct((SPAN, TILE), F32),
        ],
        [],
        3 * 10 ** 9, 10 ** 7, "project",
    )
    projected = call(
        attend_body,
        (info, halo_before, halo_after, queries, keys, values_t, bias, qkv_own, qkv_peer,
         mesh_zero, w_out_attn, out_peer, dec_own, dec_peer),
        1,
        jax.ShapeDtypeStruct((ROWS, LANES), BF16),
        [
            pltpu.VMEM((WINDOW, D), BF16),
            pltpu.VMEM((D, WINDOW), BF16),
            pltpu.VMEM((TILES, SPAN, TILE), F32),
            pltpu.VMEM((D, ROWS), BF16),
            pltpu.VMEM((D, LANES), BF16),
        ],
        20 * 10 ** 9, 2 * 10 ** 7, "attend",
    )
    peer = swapped(projected)
    before_same = shifted(projected, 1)
    after_same = shifted(projected, -1)
    before_other = band_other(projected, 1)
    after_other = band_other(projected, -1)
    return call(
        decode_body,
        (info, dec_src, projected, peer, before_same, before_other, after_same, after_other,
         dec_dst, dec_weight.astype(F32), grid_fields),
        2,
        jax.ShapeDtypeStruct((GQ, C), BF16),
        [
            pltpu.VMEM((6 * ROWS, LANES), F32),
            pltpu.VMEM((DEC_ROUNDS * TILE, LANES), F32),
        ],
        10 ** 9, 3 * 10 ** 6, "decode",
    )


def solution(mesh):
    return jax.shard_map(
        on_device,
        mesh=mesh,
        in_specs=(
            P("band", None),
            P(None, "mp"),
            P("band", None),
            P("band", None),
            P("band", None),
            P("band"),
            P(),
            P(None, None, "mp"),
            P("mp", None),
            P(),
            P("mp", None),
            P(("band", "mp"), None),
            P(("band", "mp"), None),
            P(("band", "mp"), None),
        ),
        out_specs=P(("band", "mp"), None),
        check_vma=False,
    )
```

time: 623 us -> 132 us (0.21)
  the two profiles are of different devices: /device:TPU:1 before, /device:TPU:97 now
where the time goes in v1:
time: 132 us; the launch traced here: 130 us
  Pallas kernels  61.2 us (46%)
  starting transfers between devices  37.3 us (28%)
  waiting for transfers between devices  16.3 us (12%)
  local copies, waits for them, and re-layouts  14.1 us (11%)
    pallas_call x4, Pallas kernels, call(): pl.pallas_call(body, out_shape=outs, in_specs=specs, out_specs=jax.tree.m...  61.2 us
    ppermute x4, starting transfers between devices, shifted(): return lax.ppermute(value, 'band', pairs)  19.8 us
    ppermute x4, waiting for transfers between devices, shifted(): return lax.ppermute(value, 'band', pairs)  14.9 us
    ppermute x5, starting transfers between devices, swapped(): return lax.ppermute(value, 'mp', [(0, 1), (1, 0)])  7.53 us
    unnamed x35, local copies, waits for them, and re-layouts  7.09 us
    ppermute x2, starting transfers between devices, band_other(): return lax.ppermute(value, ('band', 'mp'), pairs)  5 us
    ppermute x2, starting transfers between devices, ring_shifted(): return lax.ppermute(value, ('band', 'mp'), pairs)  4.94 us
    reshape x1, local copies, waits for them, and re-layouts, on_device(): qkv_own = w_qkv.reshape(D, 3 * HALF)  2.98 us
  transfers between devices with their start and end apart: 13, of which 4 were waited for; matrix products, arithmetic and copies ran while one was open for 3% of the time, Pallas kernels for 17%

profile of v1, /device:TPU:97, one launch (start us, length us, event | category | flops | bytes accessed | tf_op | source)
XLA Modules:
  0.0 130.5 jit_solution(3164847128493139871)
XLA Ops:
  0.0 3.2 %copy.25 = bf16[1024,3,512]{0,2,1:T(8,128)(2,1)S(1)} copy(bf16[1024,3,512]{2,0,1:T(8,128)(2,1)} %param.21) | data formatting | bytes 6291456 | tf_op args[7]
  3.2 0.0 copy-start.3
  3.2 3.0 %copy.27.w_own = bf16[1024,1536]{1,0:T(8,128)(2,1)} copy(bf16[1024,1536]{0,1:T(8,128)(2,1)S(1)} %bitcast.9) | data formatting | bytes 6291456 | tf_op jit(solution)/shard_map/reshape | solution.py:300
  6.2 0.7 collective-permute-start.5
  6.9 1.3 copy.22.own.grid
  8.2 3.1 %collective-permute-start = (bf16[2048,100]{1,0:T(8,128)(2,1)S(1)}, bf16[2048,100]{1,0:T(8,128)(2,1)S(1)}, u32[]{:S(2)}, u32[]{:S(2)}) collective-permute-start(bf16[2048,100]{1,0:T(8,128)(2,1)S(1)} %copy.22.own.grid), channel_id=1, source_target_pairs={{0,2},{2,4},{4,6},{6,8},{8,10},{10,12},{12,14},{14,16},{16,18},{18... | collective-permute-start | bytes 1228808 | tf_op jit(solution)/shard_map/ppermute | solution.py:254
  11.3 6.4 %collective-permute-start.1 = (bf16[2048,100]{1,0:T(8,128)(2,1)S(1)}, bf16[2048,100]{1,0:T(8,128)(2,1)S(1)}, u32[]{:S(2)}, u32[]{:S(2)}) collective-permute-start(bf16[2048,100]{1,0:T(8,128)(2,1)S(1)} %copy.22.own.grid), channel_id=1, source_target_pairs={{2,0},{4,2},{6,4},{8,6},{10,8},{12,10},{14,12},{16,14},{18,16},{20... | collective-permute-start | bytes 1228808 | tf_op jit(solution)/shard_map/ppermute | solution.py:254
  17.7 0.0 copy-done.3
  17.7 0.0 copy-start.1
  17.7 0.6 collective-permute-start.2
  18.4 0.1 collective-permute-start.6
  19.1 0.7 stack.39.info
  19.8 0.0 collective-permute-done.2.win_peer
  19.8 8.0 %collective-permute-done.before = bf16[2048,100]{1,0:T(8,128)(2,1)S(1)} collective-permute-done((bf16[2048,100]{1,0:T(8,128)(2,1)S(1)}, bf16[2048,100]{1,0:T(8,128)(2,1)S(1)}, u32[]{:S(2)}, u32[]{:S(2)}) %collective-permute-start) | collective-permute-done | bytes 409632 | tf_op jit(solution)/shard_map/ppermute | solution.py:254
  27.8 0.9 collective-permute-done.1.after
  28.7 0.8 copy-done.8
  29.5 12.6 %encode.1 = (bf16[512,1024]{1,0:T(8,128)(2,1)}, bf16[512,1024]{1,0:T(8,128)(2,1)}) custom-call(s32[8]{0:T(128)} %stack.39.info, s32[64,128]{1,0:T(8,128)} %src.2, bf16[2048,100]{1,0:T(8,128)(2,1)} %copy-done.7, bf16[2048,100]{1,0:T(8,128)(2,1)} %copy-done, bf16[2048,100]{1,0:T(8,128)(2,1)} %copy-done.8, bf16[128,512]{1,0:T(8,128)(2,1)} %copy-done.1, ...), custom_call_target="tpu_custom_call" | custom-call | flops 8000000000 | bytes 4000000 | tf_op jit(solution)/shard_map/encode/pallas_call | solution.py:43
  42.1 1.5 %fusion = (bf16[384,1024]{1,0:T(8,128)(2,1)S(1)}, bf16[384,1024]{1,0:T(8,128)(2,1)S(1)}) fusion(bf16[512,1024]{1,0:T(8,128)(2,1)} %get-tuple-element.11.normed), kind=kLoop, calls=%fused_computation.1 | loop fusion | bytes 3145728 | tf_op jit(solution)/shard_map/slice | solution.py:320
  43.7 1.9 %collective-permute-start.3 = (bf16[384,1024]{1,0:T(8,128)(2,1)S(1)}, bf16[384,1024]{1,0:T(8,128)(2,1)}, u32[]{:S(2)}, u32[]{:S(2)}) collective-permute-start(bf16[384,1024]{1,0:T(8,128)(2,1)S(1)} %get-tuple-element.18), channel_id=1, source_target_pairs={{0,1},{1,2},{2,3},{3,4},{4,5},{5,6},{6,7},{7,8},{8,9},{9,10},{10,1... | collective-permute-start | bytes 2359304 | tf_op jit(solution)/shard_map/ppermute | solution.py:264
  45.6 3.0 %collective-permute-start.4 = (bf16[384,1024]{1,0:T(8,128)(2,1)S(1)}, bf16[384,1024]{1,0:T(8,128)(2,1)}, u32[]{:S(2)}, u32[]{:S(2)}) collective-permute-start(bf16[384,1024]{1,0:T(8,128)(2,1)S(1)} %get-tuple-element.17), channel_id=1, source_target_pairs={{1,0},{2,1},{3,2},{4,3},{5,4},{6,5},{7,6},{8,7},{9,8},{10,9},{11,1... | collective-permute-start | bytes 2359304 | tf_op jit(solution)/shard_map/ppermute | solution.py:264
  48.6 0.1 copy.28
  48.8 0.0 copy-start.2
  48.8 6.0 %collective-permute-start.7 = (bf16[512,128]{1,0:T(8,128)(2,1)S(1)}, bf16[512,128]{1,0:T(8,128)(2,1)S(1)}, u32[]{:S(2)}, u32[]{:S(2)}) collective-permute-start(bf16[512,128]{1,0:T(8,128)(2,1)S(1)} %pad.9.dec_own), channel_id=1, source_target_pairs={{0,1},{1,0},{2,3},{3,2},{4,5},{5,4},{6,7},{7,6},{8,9},{9,8},{10,11... | collective-permute-start | bytes 393224 | tf_op jit(solution)/shard_map/ppermute | solution.py:258
  54.9 0.0 collective-permute-done.5.w_peer
  54.9 9.3 %project.1 = (bf16[512,1024]{1,0:T(8,128)(2,1)}, bf16[512,1024]{1,0:T(8,128)(2,1)}, bf16[1024,512]{1,0:T(8,128)(2,1)}, f32[896,128]{1,0:T(8,128)}) custom-call(s32[32]{0:T(128)} %offsets.1, bf16[512,1024]{1,0:T(8,128)(2,1)} %get-tuple-element.11.normed, bf16[1024,1536]{1,0:T(8,128)(2,1)} %copy.27.w_own, bf16[1024,1536]{1,0:T(8,128)(2,1)} %collective-permute-done.5.w_peer), custom_call_target="tpu_custom_call" | custom-call | flops 3000000000 | bytes 10000000 | tf_op jit(solution)/shard_map/project/pallas_call | solution.py:43
  64.1 0.0 collective-permute-done.7.dec_peer
  64.1 0.0 collective-permute-done.6.out_peer
  64.2 0.0 collective-permute-done.3.before
  64.2 0.0 collective-permute-done.4.after
  64.2 0.6 copy-done.11
  64.8 0.4 copy-done.6
  65.2 32.3 %attend.1.own = bf16[512,128]{1,0:T(8,128)(2,1)} custom-call(s32[8]{0:T(128)} %stack.39.info, bf16[384,1024]{1,0:T(8,128)(2,1)} %collective-permute-done.3.before, bf16[384,1024]{1,0:T(8,128)(2,1)} %collective-permute-done.4.after, bf16[512,1024]{1,0:T(8,128)(2,1)} %get-tuple-element.12.queries, bf16[512,1024]{1,0:T(8,128)(2,1)} %get-tuple-element.13.keys_own, ...), custom_call_target="tpu_custom_call" | custom-call | flops 20000000000 | bytes 20000000 | tf_op jit(solution)/shard_map/attend/pallas_call | solution.py:43
  97.5 1.9 %collective-permute-start.10 = (bf16[512,128]{1,0:T(8,128)(2,1)}, bf16[512,128]{1,0:T(8,128)(2,1)S(1)}, u32[]{:S(2)}, u32[]{:S(2)}) collective-permute-start(bf16[512,128]{1,0:T(8,128)(2,1)} %attend.1.own), channel_id=1, source_target_pairs={{0,3},{1,2},{2,5},{3,4},{4,7},{5,6},{6,9},{7,8},{8,11},{9,10},{10,... | collective-permute-start | bytes 393224 | tf_op jit(solution)/shard_map/ppermute | solution.py:273
  99.4 7.5 %collective-permute-start.11 = (bf16[512,128]{1,0:T(8,128)(2,1)}, bf16[512,128]{1,0:T(8,128)(2,1)S(1)}, u32[]{:S(2)}, u32[]{:S(2)}) collective-permute-start(bf16[512,128]{1,0:T(8,128)(2,1)} %attend.1.own), channel_id=1, source_target_pairs={{2,0},{4,2},{6,4},{8,6},{10,8},{12,10},{14,12},{16,14},{18,16},{20... | collective-permute-start | bytes 393224 | tf_op jit(solution)/shard_map/ppermute | solution.py:254
  106.9 3.1 %collective-permute-start.12 = (bf16[512,128]{1,0:T(8,128)(2,1)}, bf16[512,128]{1,0:T(8,128)(2,1)S(1)}, u32[]{:S(2)}, u32[]{:S(2)}) collective-permute-start(bf16[512,128]{1,0:T(8,128)(2,1)} %attend.1.own), channel_id=1, source_target_pairs={{2,1},{3,0},{4,3},{5,2},{6,5},{7,4},{8,7},{9,6},{10,9},{11,8},{12,... | collective-permute-start | bytes 393224 | tf_op jit(solution)/shard_map/ppermute | solution.py:273
  110.0 0.1 collective-permute-start.8
  110.1 2.8 %collective-permute-start.9 = (bf16[512,128]{1,0:T(8,128)(2,1)}, bf16[512,128]{1,0:T(8,128)(2,1)S(1)}, u32[]{:S(2)}, u32[]{:S(2)}) collective-permute-start(bf16[512,128]{1,0:T(8,128)(2,1)} %attend.1.own), channel_id=1, source_target_pairs={{0,2},{2,4},{4,6},{6,8},{8,10},{10,12},{12,14},{14,16},{16,18},{18... | collective-permute-start | bytes 393224 | tf_op jit(solution)/shard_map/ppermute | solution.py:254
  112.9 0.0 copy-done.5
  112.9 0.6 convert_element_type.6.weight
  113.5 0.0 collective-permute-done.10.before_other
  113.5 0.0 collective-permute-done.11.after_same
  113.6 1.4 %collective-permute-done.12.after_other = bf16[512,128]{1,0:T(8,128)(2,1)S(1)} collective-permute-done((bf16[512,128]{1,0:T(8,128)(2,1)}, bf16[512,128]{1,0:T(8,128)(2,1)S(1)}, u32[]{:S(2)}, u32[]{:S(2)}) %collective-permute-start.12) | collective-permute-done | bytes 131104 | tf_op jit(solution)/shard_map/ppermute | solution.py:273
  115.0 0.0 collective-permute-done.8.peer
  115.0 6.0 %collective-permute-done.9.before_same = bf16[512,128]{1,0:T(8,128)(2,1)S(1)} collective-permute-done((bf16[512,128]{1,0:T(8,128)(2,1)}, bf16[512,128]{1,0:T(8,128)(2,1)S(1)}, u32[]{:S(2)}, u32[]{:S(2)}) %collective-permute-start.9) | collective-permute-done | bytes 131104 | tf_op jit(solution)/shard_map/ppermute | solution.py:254
  121.0 0.0 copy-done.13
  121.0 0.6 copy-done.15
  121.6 7.0 %decode.1 = bf16[1024,100]{1,0:T(8,128)(2,1)} custom-call(s32[8]{0:T(128)} %stack.39.info, s32[24,128]{1,0:T(8,128)} %src.3, bf16[512,128]{1,0:T(8,128)(2,1)} %attend.1.own, bf16[512,128]{1,0:T(8,128)(2,1)} %copy-done.14, bf16[512,128]{1,0:T(8,128)(2,1)} %copy-done.15, bf16[512,128]{1,0:T(8,128)(2,1)} %copy-done.10, bf16[512,128]{1,0:T(8,128)(2,1)} %copy-done.12, ...), custom_call_target="tpu_custom_call" | custom-call | flops 1000000000 | bytes 3000000 | tf_op jit(solution)/shard_map/decode/pallas_call | solution.py:43
  128.6 1.8 %copy.31 = bf16[1024,100]{0,1:T(8,128)(2,1)} copy(bf16[1024,100]{1,0:T(8,128)(2,1)} %decode.1) | data formatting | bytes 409600 | tf_op jit(solution)/shard_map/decode/pallas_call | solution.py:43
  (25 shorter events, 0.1 us)
Async XLA Ops:
  3.2 14.5 %copy-start.3 = (bf16[100,512]{1,0:T(8,128)(2,1)S(1)}, bf16[100,512]{1,0:T(8,128)(2,1)}, u32[]{:S(2)}) copy-start(bf16[100,512]{1,0:T(8,128)(2,1)} %param.15) | copy-start | bytes 307204
  6.2 48.7 %collective-permute-start.5 = (bf16[1024,1536]{1,0:T(8,128)(2,1)}, bf16[1024,1536]{1,0:T(8,128)(2,1)}, u32[]{:S(2)}, u32[]{:S(2)}) collective-permute-start(bf16[1024,1536]{1,0:T(8,128)(2,1)} %copy.27.w_own), channel_id=1, source_target_pairs={{0,1},{1,0},{2,3},{3,2},{4,5},{5,4},{6,7},{7,6},{8,9},{9,8},{10,11... | collective-permute-start | bytes 9437192 | tf_op jit(solution)/shard_map/ppermute | solution.py:258
  8.2 20.5 %copy-start = (bf16[2048,100]{1,0:T(8,128)(2,1)}, bf16[2048,100]{1,0:T(8,128)(2,1)S(1)}, u32[]{:S(2)}) copy-start(bf16[2048,100]{1,0:T(8,128)(2,1)S(1)} %copy.22.own.grid) | copy-start | bytes 1228804
  8.2 19.7 %collective-permute-start = (bf16[2048,100]{1,0:T(8,128)(2,1)S(1)}, bf16[2048,100]{1,0:T(8,128)(2,1)S(1)}, u32[]{:S(2)}, u32[]{:S(2)}) collective-permute-start(bf16[2048,100]{1,0:T(8,128)(2,1)S(1)} %copy.22.own.grid), channel_id=1, source_target_pairs={{0,2},{2,4},{4,6},{6,8},{8,10},{10,12},{12,14},{14,16},{16,18},{18... | collective-permute-start | bytes 1228808 | tf_op jit(solution)/shard_map/ppermute | solution.py:254
  11.3 17.4 %collective-permute-start.1 = (bf16[2048,100]{1,0:T(8,128)(2,1)S(1)}, bf16[2048,100]{1,0:T(8,128)(2,1)S(1)}, u32[]{:S(2)}, u32[]{:S(2)}) collective-permute-start(bf16[2048,100]{1,0:T(8,128)(2,1)S(1)} %copy.22.own.grid), channel_id=1, source_target_pairs={{2,0},{4,2},{6,4},{8,6},{10,8},{12,10},{14,12},{16,14},{18,16},{20... | collective-permute-start | bytes 1228808 | tf_op jit(solution)/shard_map/ppermute | solution.py:254
  17.7 11.0 %copy-start.1 = (bf16[128,512]{1,0:T(8,128)(2,1)}, bf16[128,512]{1,0:T(8,128)(2,1)S(1)}, u32[]{:S(2)}) copy-start(bf16[128,512]{1,0:T(8,128)(2,1)S(1)} %pad.8.win_own) | copy-start | bytes 393220
  17.7 2.1 %collective-permute-start.2 = (bf16[128,512]{1,0:T(8,128)(2,1)S(1)}, bf16[128,512]{1,0:T(8,128)(2,1)S(1)}, u32[]{:S(2)}, u32[]{:S(2)}) collective-permute-start(bf16[128,512]{1,0:T(8,128)(2,1)S(1)} %pad.8.win_own), channel_id=1, source_target_pairs={{0,1},{1,0},{2,3},{3,2},{4,5},{5,4},{6,7},{7,6},{8,9},{9,8},{10,11... | collective-permute-start | bytes 393224 | tf_op jit(solution)/shard_map/ppermute | solution.py:258
  18.4 45.8 %collective-permute-start.6 = (bf16[512,1024]{1,0:T(8,128)(2,1)}, bf16[512,1024]{1,0:T(8,128)(2,1)S(1)}, u32[]{:S(2)}, u32[]{:S(2)}) collective-permute-start(bf16[512,1024]{1,0:T(8,128)(2,1)} %out_own.1), channel_id=1, source_target_pairs={{0,1},{1,0},{2,3},{3,2},{4,5},{5,4},{6,7},{7,6},{8,9},{9,8},{10,11... | collective-permute-start | bytes 3145736 | tf_op jit(solution)/shard_map/ppermute | solution.py:258
  19.8 8.9 %copy-start.9 = (bf16[128,512]{1,0:T(8,128)(2,1)}, bf16[128,512]{1,0:T(8,128)(2,1)S(1)}, u32[]{:S(2)}) copy-start(bf16[128,512]{1,0:T(8,128)(2,1)S(1)} %collective-permute-done.2.win_peer) | copy-start | bytes 393220
  27.8 0.9 copy-start.7
  28.7 0.8 copy-start.8
  42.1 6.5 %copy-start.4 = (bf16[512,100]{0,1:T(8,128)(2,1)S(1)}, bf16[512,100]{0,1:T(8,128)(2,1)}, u32[]{:S(2)}) copy-start(bf16[512,100]{0,1:T(8,128)(2,1)} %param.24) | copy-start | bytes 307204
  43.7 20.5 %collective-permute-start.3 = (bf16[384,1024]{1,0:T(8,128)(2,1)S(1)}, bf16[384,1024]{1,0:T(8,128)(2,1)}, u32[]{:S(2)}, u32[]{:S(2)}) collective-permute-start(bf16[384,1024]{1,0:T(8,128)(2,1)S(1)} %get-tuple-element.18), channel_id=1, source_target_pairs={{0,1},{1,2},{2,3},{3,4},{4,5},{5,6},{6,7},{7,8},{8,9},{9,10},{10,1... | collective-permute-start | bytes 2359304 | tf_op jit(solution)/shard_map/ppermute | solution.py:264
  45.6 18.6 %collective-permute-start.4 = (bf16[384,1024]{1,0:T(8,128)(2,1)S(1)}, bf16[384,1024]{1,0:T(8,128)(2,1)}, u32[]{:S(2)}, u32[]{:S(2)}) collective-permute-start(bf16[384,1024]{1,0:T(8,128)(2,1)S(1)} %get-tuple-element.17), channel_id=1, source_target_pairs={{1,0},{2,1},{3,2},{4,3},{5,4},{6,5},{7,6},{8,7},{9,8},{10,9},{11,1... | collective-permute-start | bytes 2359304 | tf_op jit(solution)/shard_map/ppermute | solution.py:264
  48.8 15.3 %copy-start.2 = (bf16[512,128]{1,0:T(8,128)(2,1)}, bf16[512,128]{1,0:T(8,128)(2,1)S(1)}, u32[]{:S(2)}) copy-start(bf16[512,128]{1,0:T(8,128)(2,1)S(1)} %pad.9.dec_own) | copy-start | bytes 393220
  48.8 15.3 %collective-permute-start.7 = (bf16[512,128]{1,0:T(8,128)(2,1)S(1)}, bf16[512,128]{1,0:T(8,128)(2,1)S(1)}, u32[]{:S(2)}, u32[]{:S(2)}) collective-permute-start(bf16[512,128]{1,0:T(8,128)(2,1)S(1)} %pad.9.dec_own), channel_id=1, source_target_pairs={{0,1},{1,0},{2,3},{3,2},{4,5},{5,4},{6,7},{7,6},{8,9},{9,8},{10,11... | collective-permute-start | bytes 393224 | tf_op jit(solution)/shard_map/ppermute | solution.py:258
  64.1 0.7 copy-start.11
  64.1 1.0 copy-start.6
  65.2 47.8 %copy-start.5 = (bf16[24,128]{1,0:T(8,128)(2,1)S(1)}, bf16[24,128]{1,0:T(8,128)(2,1)}, u32[]{:S(2)}) copy-start(bf16[24,128]{1,0:T(8,128)(2,1)} %param.27) | copy-start | bytes 18436
  97.5 16.1 %collective-permute-start.10 = (bf16[512,128]{1,0:T(8,128)(2,1)}, bf16[512,128]{1,0:T(8,128)(2,1)S(1)}, u32[]{:S(2)}, u32[]{:S(2)}) collective-permute-start(bf16[512,128]{1,0:T(8,128)(2,1)} %attend.1.own), channel_id=1, source_target_pairs={{0,3},{1,2},{2,5},{3,4},{4,7},{5,6},{6,9},{7,8},{8,11},{9,10},{10,... | collective-permute-start | bytes 393224 | tf_op jit(solution)/shard_map/ppermute | solution.py:273
  99.4 14.2 %collective-permute-start.11 = (bf16[512,128]{1,0:T(8,128)(2,1)}, bf16[512,128]{1,0:T(8,128)(2,1)S(1)}, u32[]{:S(2)}, u32[]{:S(2)}) collective-permute-start(bf16[512,128]{1,0:T(8,128)(2,1)} %attend.1.own), channel_id=1, source_target_pairs={{2,0},{4,2},{6,4},{8,6},{10,8},{12,10},{14,12},{16,14},{18,16},{20... | collective-permute-start | bytes 393224 | tf_op jit(solution)/shard_map/ppermute | solution.py:254
  106.9 8.1 %collective-permute-start.12 = (bf16[512,128]{1,0:T(8,128)(2,1)}, bf16[512,128]{1,0:T(8,128)(2,1)S(1)}, u32[]{:S(2)}, u32[]{:S(2)}) collective-permute-start(bf16[512,128]{1,0:T(8,128)(2,1)} %attend.1.own), channel_id=1, source_target_pairs={{2,1},{3,0},{4,3},{5,2},{6,5},{7,4},{8,7},{9,6},{10,9},{11,8},{12,... | collective-permute-start | bytes 393224 | tf_op jit(solution)/shard_map/ppermute | solution.py:273
  110.0 5.0 %collective-permute-start.8 = (bf16[512,128]{1,0:T(8,128)(2,1)}, bf16[512,128]{1,0:T(8,128)(2,1)S(1)}, u32[]{:S(2)}, u32[]{:S(2)}) collective-permute-start(bf16[512,128]{1,0:T(8,128)(2,1)} %attend.1.own), channel_id=1, source_target_pairs={{0,1},{1,0},{2,3},{3,2},{4,5},{5,4},{6,7},{7,6},{8,9},{9,8},{10,11... | collective-permute-start | bytes 393224 | tf_op jit(solution)/shard_map/ppermute | solution.py:258
  110.1 10.9 %collective-permute-start.9 = (bf16[512,128]{1,0:T(8,128)(2,1)}, bf16[512,128]{1,0:T(8,128)(2,1)S(1)}, u32[]{:S(2)}, u32[]{:S(2)}) collective-permute-start(bf16[512,128]{1,0:T(8,128)(2,1)} %attend.1.own), channel_id=1, source_target_pairs={{0,2},{2,4},{4,6},{6,8},{8,10},{10,12},{12,14},{14,16},{16,18},{18... | collective-permute-start | bytes 393224 | tf_op jit(solution)/shard_map/ppermute | solution.py:254
  113.5 7.4 %copy-start.10 = (bf16[512,128]{1,0:T(8,128)(2,1)}, bf16[512,128]{1,0:T(8,128)(2,1)S(1)}, u32[]{:S(2)}) copy-start(bf16[512,128]{1,0:T(8,128)(2,1)S(1)} %collective-permute-done.10.before_other) | copy-start | bytes 393220
  113.5 7.4 %copy-start.12 = (bf16[512,128]{1,0:T(8,128)(2,1)}, bf16[512,128]{1,0:T(8,128)(2,1)S(1)}, u32[]{:S(2)}) copy-start(bf16[512,128]{1,0:T(8,128)(2,1)S(1)} %collective-permute-done.11.after_same) | copy-start | bytes 393220
  115.0 6.0 %copy-start.13 = (bf16[512,128]{1,0:T(8,128)(2,1)}, bf16[512,128]{1,0:T(8,128)(2,1)S(1)}, u32[]{:S(2)}) copy-start(bf16[512,128]{1,0:T(8,128)(2,1)S(1)} %collective-permute-done.12.after_other) | copy-start | bytes 393220
  115.0 6.0 %copy-start.14 = (bf16[512,128]{1,0:T(8,128)(2,1)}, bf16[512,128]{1,0:T(8,128)(2,1)S(1)}, u32[]{:S(2)}) copy-start(bf16[512,128]{1,0:T(8,128)(2,1)S(1)} %collective-permute-done.8.peer) | copy-start | bytes 393220
  121.0 0.6 copy-start.15

commit v2 on v1

v2 whole, which is shorter than its diff:
```python
import math
import jax
import jax.numpy as jnp
from jax import lax
from jax.experimental import pallas as pl
from jax.experimental.pallas import tpu as pltpu
from jax.sharding import PartitionSpec as P

D = 1024
C = 100
LANES = 128
TILE = 128
ROWS = 512
WIN = 384
K_OFF = 32
HALF = 512
G_BAND = 2048
EDGE_ROUNDS = 8
TILES = 4
STEP = 256
SPAN = TILE + 2 * WIN
GQ = 1024
DEC_ROUNDS = 3
DEC_TILES = 8
MASKED = -1e30
SCALE = 64 ** (-0.5) * math.log2(math.e)
F32 = jnp.float32
BF16 = jnp.bfloat16
VMEM_BYTES = 20 * 1024 * 1024


def vmem():
    return pl.BlockSpec(memory_space=pltpu.VMEM)


def smem():
    return pl.BlockSpec(memory_space=pltpu.SMEM)


def call(body, operands, smem_count, outs, scratch, flops, touched, name):
    specs = [smem()] * smem_count + [vmem()] * (len(operands) - smem_count)
    return pl.pallas_call(
        body,
        out_shape=outs,
        in_specs=specs,
        out_specs=jax.tree.map(lambda _: vmem(), outs),
        scratch_shapes=scratch,
        compiler_params=pltpu.CompilerParams(vmem_limit_bytes=VMEM_BYTES),
        cost_estimate=pl.CostEstimate(flops=flops, bytes_accessed=touched, transcendentals=0),
        name=name,
    )(*operands)


def matmul(a, b):
    return jnp.dot(a, b, preferred_element_type=F32)


def matmul_t(a, b):
    return lax.dot_general(a, b, (((1,), (1,)), ((), ())), preferred_element_type=F32)


def to_rows(part, wide, rows, begin):
    wide[:C, :] = part[...].astype(F32)
    for block in range(G_BAND // LANES):
        columns = slice(block * LANES, (block + 1) * LANES)
        rows[begin + block * LANES : begin + (block + 1) * LANES, :] = wide[:, columns].T


def prepare_body(offsets, grid, rows, mask, wide):
    wide[...] = jnp.zeros_like(wide)
    to_rows(grid, wide, rows, 0)
    for chunk in range(SPAN // TILE):
        row = lax.broadcasted_iota(jnp.int32, (TILE, LANES), 0) + (chunk * TILE - WIN)
        away = row - lax.broadcasted_iota(jnp.int32, (TILE, LANES), 1)
        hit = away == offsets[0]
        for k in range(1, K_OFF):
            hit = hit | (away == offsets[k])
        mask[chunk * TILE : (chunk + 1) * TILE, :] = jnp.where(hit, 0.0, MASKED).astype(BF16)


def encode_body(
    info, src, sent, swapped_rows, own_rows, win_own, win_peer, dst, weight, gain,
    mesh_zero, normed, to_peer, to_band,
    rows, wide, first, second, w_wide, w_in, weights, total,
):
    core, live, grid_base, mesh_base = info[0], info[1], info[2], info[3]
    wide[...] = jnp.zeros_like(wide)
    rows[G_BAND : 2 * G_BAND, :] = own_rows[...]
    w_wide[...] = jnp.zeros_like(w_wide)

    @pl.when(core == 0)
    def _():
        to_rows(sent, wide, rows, 0)
        to_rows(swapped_rows, wide, rows, 2 * G_BAND)
        w_wide[:C, :HALF] = win_own[...].astype(F32) * 0.5
        w_wide[:C, HALF:] = win_peer[...].astype(F32) * 0.5

    @pl.when(core != 0)
    def _():
        to_rows(swapped_rows, wide, rows, 0)
        to_rows(sent, wide, rows, 2 * G_BAND)
        w_wide[:C, :HALF] = win_peer[...].astype(F32) * 0.5
        w_wide[:C, HALF:] = win_own[...].astype(F32) * 0.5

    w_in[...] = w_wide[...].astype(BF16)
    slots = lax.broadcasted_iota(jnp.int32, weights.shape, 0)
    weights[...] = jnp.where(slots < live, weight[...].astype(F32), 0.0)
    total[...] = jnp.zeros_like(total)
    row_slots = lax.broadcasted_iota(jnp.int32, (TILE, LANES), 0)
    steps = EDGE_ROUNDS * TILE // STEP
    rounds = STEP // TILE

    def slot_of(step, part):
        tile, chunk = step // steps, step % steps
        return (chunk * rounds + part) * 2 * TILES + core * TILES + tile

    def gather(step, buffer):
        for part in range(rounds):
            slot = slot_of(step, part)
            for edge in range(TILE):
                index = src[slot, edge] - grid_base
                buffer[pl.ds(part * TILE + edge, 1), :] = rows[pl.ds(index, 1), :]

    def add(step, buffer):
        tile = step // steps
        half = matmul(buffer[...].astype(BF16), w_in[...])
        embedded = (half + half * jnp.tanh(half)).astype(BF16)
        tables = []
        for part in range(rounds):
            slot = slot_of(step, part)
            target = dst[pl.ds(slot, 1), :] - (mesh_base + tile * TILE)
            tables.append(jnp.where(row_slots == target, weights[pl.ds(slot, 1), :], 0.0))
        table = jnp.concatenate(tables, axis=1).astype(BF16)
        place = pl.ds(pl.multiple_of(tile * TILE, TILE), TILE)
        total[place, :] += matmul(table, embedded)

    gather(0, first)

    def pair(index, carry):
        gather(2 * index + 1, second)
        add(2 * index, first)
        gather(jnp.minimum(2 * index + 2, TILES * steps - 1), first)
        add(2 * index + 1, second)
        return carry

    lax.fori_loop(0, TILES * steps // 2, pair, 0)

    def finish(tile, carry):
        place = pl.ds(pl.multiple_of(tile * TILE, TILE), TILE)
        rounded = total[place, :].astype(BF16)
        mesh_zero[place, :] = rounded
        values = rounded.astype(F32)
        inverse = lax.rsqrt(jnp.mean(values * values, axis=1, keepdims=True) + 1e-05)
        normed[place, :] = (values * inverse * gain[...]).astype(BF16)
        return carry

    lax.fori_loop(0, TILES, finish, 0)

    @pl.when(core == 0)
    def _():
        to_peer[...] = normed[ROWS - WIN :, :]
        to_band[...] = normed[:WIN, :]

    @pl.when(core != 0)
    def _():
        to_peer[...] = normed[:WIN, :]
        to_band[...] = normed[ROWS - WIN :, :]


def identity_pair():
    row = lax.broadcasted_iota(jnp.int32, (TILE, LANES), 0)
    lane = lax.broadcasted_iota(jnp.int32, (TILE, LANES), 1)
    eye = jnp.where(row == lane, 1.0, 0.0).astype(BF16)
    return jnp.concatenate([eye, eye], axis=0), lane


def lanes_of(pair):
    return pl.ds(pl.multiple_of(pair * LANES, LANES), LANES)


def rows_of(block):
    return slice(block * TILE, (block + 1) * TILE)


def score_block(query, lane, eyes, keys, mask, scores):
    query = query.astype(F32)
    stacked = jnp.concatenate(
        [jnp.where(lane < 64, query, 0.0), jnp.where(lane < 64, 0.0, query)], axis=0
    ).astype(BF16)
    scores[...] = matmul_t(
        jnp.concatenate([keys, mask], axis=1), jnp.concatenate([stacked, eyes], axis=1)
    )


def column_top(scores):
    top = scores[:TILE, :]
    for begin in range(TILE, scores.shape[0], TILE):
        top = jnp.maximum(top, scores[begin : begin + TILE, :])
    return jnp.max(top, axis=0, keepdims=True)


def weigh(scores, top, values):
    expos = jnp.exp2((scores[...] - top).astype(BF16))
    ones = jnp.ones((16, scores.shape[0]), BF16)
    result = matmul(jnp.concatenate([values, ones], axis=0), expos)
    both = jnp.concatenate([result[:64, :TILE], result[64:TILE, TILE:]], axis=0)
    return both, result[TILE : TILE + 1, :]


def pipeline(score, finish, first, second):
    buffers = (first, second)
    score(0, 0, first)

    def head_pair(pair, carry):
        for block in range(TILES):
            if block + 1 < TILES:
                score(pair, block + 1, buffers[(block + 1) % 2])
            else:
                score(jnp.minimum(pair + 1, D // LANES - 1), 0, first)
            finish(pair, block, buffers[block % 2])
        return carry

    lax.fori_loop(0, D // LANES, head_pair, 0)


def project_body(
    normed, halo, w_own, w_peer, mask,
    queries, halo_keys, halo_values, sums, stats,
    keys, values_t, first, second,
):
    rows = normed[...]
    beside = halo[...]
    for half, weight in enumerate((w_own, w_peer)):
        place = slice(half * HALF, (half + 1) * HALF)
        queries[:, place] = (matmul(rows, weight[0]) * SCALE).astype(BF16)
        keys[:, place] = matmul(rows, weight[1]).astype(BF16)
        values_t[place, :] = matmul(rows, weight[2]).T.astype(BF16)
        halo_keys[:, place] = matmul(beside, weight[1]).astype(BF16)
        halo_values[place, :] = matmul(beside, weight[2]).T.astype(BF16)
    eyes, lane = identity_pair()

    def score(pair, block, scores):
        begin = WIN - block * TILE
        score_block(
            queries[rows_of(block), lanes_of(pair)], lane, eyes, keys[:, lanes_of(pair)],
            mask[begin : begin + ROWS, :], scores,
        )

    def finish(pair, block, scores):
        top = column_top(scores)
        both, total = weigh(scores, top, values_t[lanes_of(pair), :])
        sums[lanes_of(pair), rows_of(block)] = both
        columns = slice(2 * block * TILE, 2 * (block + 1) * TILE)
        stats[pair, 0:1, columns] = top
        stats[pair, 1:2, columns] = total

    pipeline(score, finish, first, second)


def attend_body(
    info, halo, peer_keys, peer_values, queries, sums, stats, mask, w_own, w_peer,
    mesh_zero, out_own, out_peer, dec_own, dec_peer,
    projected,
    keys, values_t, masks, attended, dec_wide, first, second,
):
    core, first_device, last_device = info[0], info[4], info[5]
    dec_wide[...] = jnp.zeros_like(dec_wide)

    @pl.when(core == 0)
    def _():
        dec_wide[:C, :HALF] = dec_own[...].astype(F32)
        dec_wide[:C, HALF:] = dec_peer[...].astype(F32)
        keys[WIN:, :] = peer_keys[...]
        values_t[:, WIN:] = peer_values[...]

    @pl.when(core != 0)
    def _():
        dec_wide[:C, :HALF] = dec_peer[...].astype(F32)
        dec_wide[:C, HALF:] = dec_own[...].astype(F32)
        keys[:WIN, :] = peer_keys[...]
        values_t[:, :WIN] = peer_values[...]

    begin = pl.ds(pl.multiple_of(core * WIN, WIN), WIN)
    beside = halo[...]
    for half, weight in enumerate((w_own, w_peer)):
        place = slice(half * HALF, (half + 1) * HALF)
        keys[begin, place] = matmul(beside, weight[1]).astype(BF16)
        values_t[place, begin] = matmul(beside, weight[2]).T.astype(BF16)
    low = jnp.where(first_device == 1, MASKED, 0.0)
    high = jnp.where(last_device == 1, MASKED, 0.0)
    for block in range(TILES):
        below, above = WIN - block * TILE, SPAN - block * TILE
        if below > 0:
            masks[block, :below, :] = (mask[:below, :].astype(F32) + low).astype(BF16)
        if above < SPAN:
            masks[block, below:, :] = (mask[above:, :].astype(F32) + high).astype(BF16)
    eyes, lane = identity_pair()

    def score(pair, block, scores):
        seen = slice(block * TILE, block * TILE + WIN)
        score_block(
            queries[rows_of(block), lanes_of(pair)], lane, eyes, keys[seen, lanes_of(pair)],
            masks[block], scores,
        )

    def finish(pair, block, scores):
        seen = slice(block * TILE, block * TILE + WIN)
        columns = slice(2 * block * TILE, 2 * (block + 1) * TILE)
        old, sum_old = stats[pair, 0:1, columns], stats[pair, 1:2, columns]
        top = jnp.maximum(old, column_top(scores))
        both, total = weigh(scores, top, values_t[lanes_of(pair), seen])
        shrink = jnp.exp2(old - top)
        inverse = 1.0 / (sum_old * shrink + total)
        shrink = shrink * inverse
        before = sums[lanes_of(pair), rows_of(block)]
        result = jnp.concatenate([
            before[:64] * shrink[:, :TILE] + both[:64] * inverse[:, :TILE],
            before[64:] * shrink[:, TILE:] + both[64:] * inverse[:, TILE:],
        ], axis=0)
        attended[lanes_of(pair), rows_of(block)] = result.astype(BF16)

    pipeline(score, finish, first, second)
    term_own = matmul(attended[:HALF, :].T, out_own[...]).astype(BF16).astype(F32)
    term_peer = matmul(attended[HALF:, :].T, out_peer[...]).astype(BF16).astype(F32)
    mesh_one = (mesh_zero[...].astype(F32) + (term_own + term_peer)).astype(BF16)
    projected[...] = matmul_t(mesh_one, dec_wide[...].astype(BF16)).astype(BF16)


def decode_body(
    info, src, own, sent, swapped_rows, dst, weight, grid, out, rows, messages, weights
):
    core, mesh_base, row_base = info[0], info[6], info[7]
    other = 1 - core

    def put(place, part):
        rows[pl.ds(pl.multiple_of(place * ROWS, ROWS), ROWS), :] = part.astype(F32)

    put(2 + core, own[0])
    put(2 + other, own[1])
    put(4 * core + core, sent[0])
    put(4 * core + other, sent[1])
    put(4 * other + other, swapped_rows[0])
    put(4 * other + core, swapped_rows[1])
    weights[...] = weight[...].astype(F32)
    row_slots = lax.broadcasted_iota(jnp.int32, (TILE, LANES), 0)

    def tile_sum(tile, carry):
        tables = []
        for part in range(DEC_ROUNDS):
            slot = part * DEC_TILES + tile
            for edge in range(TILE):
                index = src[slot, edge] - mesh_base
                messages[pl.ds(part * TILE + edge, 1), :] = rows[pl.ds(index, 1), :]
            target = dst[pl.ds(slot, 1), :] - (row_base + tile * TILE)
            tables.append(jnp.where(row_slots == target, weights[pl.ds(slot, 1), :], 0.0))
        table = jnp.concatenate(tables, axis=1).astype(BF16)
        summed = matmul(table, messages[...].astype(BF16)).T
        place = pl.ds(pl.multiple_of(tile * TILE, TILE), TILE)
        fields = grid[:, pl.ds(pl.multiple_of(core * GQ + tile * TILE, TILE), TILE)]
        out[:, place] = (fields.astype(F32) + summed[:C, :]).astype(BF16)
        return carry

    lax.fori_loop(0, DEC_TILES, tile_sum, 0)


def swapped(value):
    return lax.ppermute(value, "mp", [(0, 1), (1, 0)])


def up_and_down(value):
    bands = lax.axis_size("band")
    pairs = [(2 * i, 2 * i + 2) for i in range(bands - 1)]
    pairs += [(2 * i + 3, 2 * i + 1) for i in range(bands - 1)]
    return lax.ppermute(value, ("band", "mp"), pairs)


def over_the_edge(value):
    bands = lax.axis_size("band")
    pairs = [(2 * i + 1, 2 * i + 2) for i in range(bands - 1)]
    pairs += [(j, i) for i, j in pairs]
    return lax.ppermute(value, ("band", "mp"), pairs)


def on_device(
    grid_fields, w_in, enc_src, enc_dst, enc_weight, enc_count, norm_gain, w_qkv, w_out_attn,
    offsets, w_decode, dec_src, dec_dst, dec_weight,
):
    band = lax.axis_index("band")
    core = lax.axis_index("mp")
    bands = lax.axis_size("band")
    device = 2 * band + core
    grid = grid_fields.T
    grid_sent = up_and_down(grid)
    grid_swapped = swapped(grid_sent)
    info = jnp.stack([
        core,
        enc_count[0],
        (band - 1) * G_BAND,
        device * ROWS,
        (device == 0).astype(jnp.int32),
        (device == 2 * bands - 1).astype(jnp.int32),
        (band - 1) * 2 * ROWS,
        device * GQ,
    ]).astype(jnp.int32)
    win_peer = swapped(w_in)
    dec_own = w_decode.T
    dec_peer = swapped(dec_own)
    qkv_own = w_qkv.transpose(1, 0, 2)
    qkv_peer = swapped(qkv_own)
    out_peer = swapped(w_out_attn)
    own_rows, mask = call(
        prepare_body,
        (offsets, grid),
        1,
        [
            jax.ShapeDtypeStruct((G_BAND, LANES), F32),
            jax.ShapeDtypeStruct((SPAN, TILE), BF16),
        ],
        [pltpu.VMEM((LANES, G_BAND), F32)],
        10 ** 7, 2 * 10 ** 6, "prepare",
    )
    mesh_zero, normed, to_peer, to_band = call(
        encode_body,
        (info, enc_src, grid_sent, grid_swapped, own_rows, w_in, win_peer, enc_dst,
         enc_weight, norm_gain.reshape(1, D)),
        2,
        [jax.ShapeDtypeStruct((ROWS, D), BF16)] * 2 + [jax.ShapeDtypeStruct((WIN, D), BF16)] * 2,
        [
            pltpu.VMEM((3 * G_BAND, LANES), F32),
            pltpu.VMEM((LANES, G_BAND), F32),
            pltpu.VMEM((STEP, LANES), F32),
            pltpu.VMEM((STEP, LANES), F32),
            pltpu.VMEM((LANES, D), F32),
            pltpu.VMEM((LANES, D), BF16),
            pltpu.VMEM(enc_weight.shape, F32),
            pltpu.VMEM((ROWS, D), F32),
        ],
        8 * 10 ** 9, 4 * 10 ** 6, "encode",
    )
    halo_peer = swapped(to_peer)
    halo_band = over_the_edge(to_band)
    queries, peer_keys, peer_values, sums, stats = call(
        project_body,
        (normed, halo_peer, qkv_own, qkv_peer, mask),
        0,
        [
            jax.ShapeDtypeStruct((ROWS, D), BF16),
            jax.ShapeDtypeStruct((WIN, D), BF16),
            jax.ShapeDtypeStruct((D, WIN), BF16),
            jax.ShapeDtypeStruct((D, ROWS), F32),
            jax.ShapeDtypeStruct((D // LANES, 8, 2 * ROWS), F32),
        ],
        [
            pltpu.VMEM((ROWS, D), BF16),
            pltpu.VMEM((D, ROWS), BF16),
            pltpu.VMEM((ROWS, 2 * TILE), F32),
            pltpu.VMEM((ROWS, 2 * TILE), F32),
        ],
        10 ** 10, 10 ** 7, "project",
    )
    projected = call(
        attend_body,
        (info, halo_band, peer_keys, peer_values, queries, sums, stats, mask, qkv_own,
         qkv_peer, mesh_zero, w_out_attn, out_peer, dec_own, dec_peer),
        1,
        jax.ShapeDtypeStruct((ROWS, LANES), BF16),
        [
            pltpu.VMEM((2 * WIN, D), BF16),
            pltpu.VMEM((D, 2 * WIN), BF16),
            pltpu.VMEM((TILES, WIN, TILE), BF16),
            pltpu.VMEM((D, ROWS), BF16),
            pltpu.VMEM((LANES, D), F32),
            pltpu.VMEM((WIN, 2 * TILE), F32),
            pltpu.VMEM((WIN, 2 * TILE), F32),
        ],
        10 ** 10, 2 * 10 ** 7, "attend",
    )
    own_pair = jnp.stack([projected, swapped(projected)])
    pair_sent = up_and_down(own_pair)
    pair_swapped = swapped(pair_sent)
    return call(
        decode_body,
        (info, dec_src, own_pair, pair_sent, pair_swapped, dec_dst, dec_weight, grid),
        2,
        jax.ShapeDtypeStruct((C, GQ), BF16),
        [
            pltpu.VMEM((6 * ROWS, LANES), F32),
            pltpu.VMEM((DEC_ROUNDS * TILE, LANES), F32),
            pltpu.VMEM(dec_weight.shape, F32),
        ],
        10 ** 9, 3 * 10 ** 6, "decode",
    ).T


def solution(mesh):
    return jax.shard_map(
        on_device,
        mesh=mesh,
        in_specs=(
            P("band", None),
            P(None, "mp"),
            P("band", None),
            P("band", None),
            P("band", None),
            P("band"),
            P(),
            P(None, None, "mp"),
            P("mp", None),
            P(),
            P("mp", None),
            P(("band", "mp"), None),
            P(("band", "mp"), None),
            P(("band", "mp"), None),
        ),
        out_specs=P(("band", "mp"), None),
        check_vma=False,
    )
```

time: 132 us -> 89.5 us (0.68)
  Pallas kernels: 61.2 us -> 45.1 us
  starting transfers between devices: 37.3 us -> 26.8 us
  local copies, waits for them, and re-layouts: 14.1 us -> 5.6 us
  waiting for transfers between devices: 16.3 us -> 10.8 us
    ppermute x8 -> x3, starting transfers between devices: 29.8 us -> 13.1 us  [the longest x2 11 us: up_and_down(): return lax.ppermute(value, ('band', 'mp'), pairs)]
    pallas_call x4 -> x5, Pallas kernels: 61.2 us -> 45.1 us  [call(): pl.pallas_call(body, out_shape=outs, in_specs=specs, out_specs=jax.tree.m...]
    ppermute x8 -> x3, waiting for transfers between devices: 16.3 us -> 8.66 us  [the longest x2 8.66 us: up_and_down(): return lax.ppermute(value, ('band', 'mp'), pairs)]
    ppermute x5 -> x8, starting transfers between devices: 7.53 us -> 13.7 us  [swapped(): return lax.ppermute(value, 'mp', [(0, 1), (1, 0)])]
    reshape x1 -> x0, local copies, waits for them, and re-layouts: 2.98 us -> none  [on_device(): qkv_own = w_qkv.reshape(D, 3 * HALF)]
    ppermute x5 -> x8, waiting for transfers between devices: 0.01 us -> 2.16 us  [swapped(): return lax.ppermute(value, 'mp', [(0, 1), (1, 0)])]
    pallas_call x1 -> x0, local copies, waits for them, and re-layouts: 1.8 us -> none  [call(): pl.pallas_call(body, out_shape=outs, in_specs=specs, out_specs=jax.tree.m...]
    unnamed x35 -> x28, local copies, waits for them, and re-layouts: 7.09 us -> 5.51 us
  transfers between devices with their start and end apart: 13 -> 11, of which waited for: 4 -> 4; matrix products, arithmetic and copies ran while one was open for 3% -> 0% of each run, Pallas kernels for 17% -> 31%
where the time goes in v2:
time: 89.5 us; the launch traced here: 89.1 us
  Pallas kernels  45.1 us (50%)
  starting transfers between devices  26.8 us (30%)
  waiting for transfers between devices  10.8 us (12%)
  local copies, waits for them, and re-layouts  5.6 us (6%)
    pallas_call x5, Pallas kernels, call(): pl.pallas_call(body, out_shape=outs, in_specs=specs, out_specs=jax.tree.m...  45.1 us
    ppermute x8, starting transfers between devices, swapped(): return lax.ppermute(value, 'mp', [(0, 1), (1, 0)])  13.7 us
    ppermute x2, starting transfers between devices, up_and_down(): return lax.ppermute(value, ('band', 'mp'), pairs)  11 us
    ppermute x2, waiting for transfers between devices, up_and_down(): return lax.ppermute(value, ('band', 'mp'), pairs)  8.66 us
    unnamed x28, local copies, waits for them, and re-layouts  5.51 us
    ppermute x8, waiting for transfers between devices, swapped(): return lax.ppermute(value, 'mp', [(0, 1), (1, 0)])  2.16 us
    ppermute x1, starting transfers between devices, over_the_edge(): return lax.ppermute(value, ('band', 'mp'), pairs)  2.09 us
  transfers between devices with their start and end apart: 11, of which 4 were waited for; matrix products, arithmetic and copies ran while one was open for 0% of the time, Pallas kernels for 31%

profile of v2, /device:TPU:97, one launch (start us, length us, event | category | flops | bytes accessed | tf_op | source)
XLA Modules:
  0.0 89.1 jit_solution(17763517627969978049)
XLA Ops:
  0.0 0.7 collective-permute-start.5
  0.7 6.7 %collective-permute-start = (bf16[100,2048]{1,0:T(8,128)(2,1)}, bf16[100,2048]{1,0:T(8,128)(2,1)}, u32[]{:S(2)}, u32[]{:S(2)}) collective-permute-start(bf16[100,2048]{1,0:T(8,128)(2,1)} %bitcast.14), channel_id=1, source_target_pairs={{0,2},{2,4},{4,6},{6,8},{8,10},{10,12},{12,14},{14,16},{16,18},{18... | collective-permute-start | bytes 1228808 | tf_op jit(solution)/shard_map/ppermute | solution.py:374
  7.4 5.4 %collective-permute-done.sent = bf16[100,2048]{1,0:T(8,128)(2,1)} collective-permute-done((bf16[100,2048]{1,0:T(8,128)(2,1)}, bf16[100,2048]{1,0:T(8,128)(2,1)}, u32[]{:S(2)}, u32[]{:S(2)}) %collective-permute-start) | collective-permute-done | bytes 409632 | tf_op jit(solution)/shard_map/ppermute | solution.py:374
  12.7 2.5 %collective-permute-start.1 = (bf16[100,2048]{1,0:T(8,128)(2,1)}, bf16[100,2048]{1,0:T(8,128)(2,1)}, u32[]{:S(2)}, u32[]{:S(2)}) collective-permute-start(bf16[100,2048]{1,0:T(8,128)(2,1)} %collective-permute-done.sent), channel_id=1, source_target_pairs={{0,1},{1,0},{2,3},{3,2},{4,5},{5,4},{6,7},{7,6},{8,9},{9,8},{10,11... | collective-permute-start | bytes 1228808 | tf_op jit(solution)/shard_map/ppermute | solution.py:367
  15.2 0.0 collective-permute-start.2
  15.9 0.1 stack.48.info
  16.0 0.0 copy-start
  16.0 1.0 %copy-done = bf16[2048,100]{0,1:T(8,128)(2,1)S(1)} copy-done((bf16[2048,100]{0,1:T(8,128)(2,1)S(1)}, bf16[2048,100]{0,1:T(8,128)(2,1)}, u32[]{:S(2)}) %copy-start) | copy-done | bytes 409624
  17.0 0.7 copy-done.2
  17.6 2.6 %prepare.1 = (f32[2048,128]{1,0:T(8,128)S(1)}, bf16[896,128]{1,0:T(8,128)(2,1)S(1)}) custom-call(s32[32]{0:T(128)S(1)} %copy-done.2, bf16[100,2048]{1,0:T(8,128)(2,1)S(1)} %bitcast.15), custom_call_target="tpu_custom_call" | custom-call | flops 10000000 | bytes 2000000 | tf_op jit(solution)/shard_map/prepare/pallas_call | solution.py:42
  20.2 0.0 collective-permute-done.2.win_peer
  20.2 0.0 collective-permute-done.1.swapped_rows
  20.2 0.0 copy-start.5
  20.2 0.9 copy-done.5
  21.1 0.8 copy-done.7
  21.9 0.8 copy-done.8
  22.7 0.7 copy-done.9
  23.4 0.7 copy-done.13
  24.1 11.8 %encode.1 = (bf16[512,1024]{1,0:T(8,128)(2,1)S(1)}, bf16[512,1024]{1,0:T(8,128)(2,1)S(1)}, bf16[384,1024]{1,0:T(8,128)(2,1)S(1)}, bf16[384,1024]{1,0:T(8,128)(2,1)S(1)}) custom-call(s32[8]{0:T(128)S(1)} %stack.48.info, s32[64,128]{1,0:T(8,128)S(1)} %copy-done.7, bf16[100,2048]{1,0:T(8,128)(2,1)} %collective-permute-done.sent, ...), custom_call_target="tpu_custom_call" | custom-call | flops 8000000000 | bytes 4000000 | tf_op jit(solution)/shard_map/encode/pallas_call | solution.py:42
  35.9 0.6 collective-permute-start.4
  36.5 0.0 copy-done.4
  36.5 0.1 collective-permute-start.6
  36.6 0.0 copy-done.6
  36.6 0.4 collective-permute-start.7
  37.0 2.1 %collective-permute-start.3 = (bf16[384,1024]{1,0:T(8,128)(2,1)S(1)}, bf16[384,1024]{1,0:T(8,128)(2,1)S(1)}, u32[]{:S(2)}, u32[]{:S(2)}) collective-permute-start(bf16[384,1024]{1,0:T(8,128)(2,1)S(1)} %get-tuple-element.17), channel_id=1, source_target_pairs={{1,2},{3,4},{5,6},{7,8},{9,10},{11,12},{13,14},{15,16},{17,18},{19... | collective-permute-start | bytes 2359304 | tf_op jit(solution)/shard_map/ppermute | solution.py:381
  39.1 0.0 collective-permute-done.4.halo
  39.1 0.0 collective-permute-done.5.w_peer
  39.1 0.0 copy-done.3
  39.1 12.9 %project.1 = (bf16[512,1024]{1,0:T(8,128)(2,1)S(1)}, bf16[384,1024]{1,0:T(8,128)(2,1)S(1)}, bf16[1024,384]{1,0:T(8,128)(2,1)S(1)}, f32[1024,512]{1,0:T(8,128)S(1)}, f32[8,8,1024]{2,1,0:T(8,128)S(1)}) custom-call(bf16[512,1024]{1,0:T(8,128)(2,1)S(1)} %get-tuple-element.18.normed, bf16[384,1024]{1,0:T(8,128)(2,1)S(1)} %collective-permute-done.4.halo, ...), custom_call_target="tpu_custom_call" | custom-call | flops 10000000000 | bytes 10000000 | tf_op jit(solution)/shard_map/project/pallas_call | solution.py:42
  52.0 0.0 collective-permute-done.7.dec_peer
  52.0 0.0 collective-permute-done.6.out_peer
  52.0 0.0 collective-permute-done.3.halo
  52.1 0.0 copy-start.1
  52.1 0.0 copy-start.10
  52.1 0.0 copy-start.11
  52.1 0.0 copy-start.12
  52.1 11.0 %attend.1 = bf16[512,128]{1,0:T(8,128)(2,1)S(1)} custom-call(s32[8]{0:T(128)S(1)} %stack.48.info, bf16[384,1024]{1,0:T(8,128)(2,1)S(1)} %collective-permute-done.3.halo, bf16[384,1024]{1,0:T(8,128)(2,1)S(1)} %get-tuple-element.21.peer_keys, bf16[1024,384]{1,0:T(8,128)(2,1)S(1)} %get-tuple-element.22.peer_values, ...), custom_call_target="tpu_custom_call" | custom-call | flops 10000000000 | bytes 20000000 | tf_op jit(solution)/shard_map/attend/pallas_call | solution.py:42
  63.1 4.2 %collective-permute-start.8 = (bf16[512,128]{1,0:T(8,128)(2,1)S(1)}, bf16[512,128]{1,0:T(8,128)(2,1)S(1)}, u32[]{:S(2)}, u32[]{:S(2)}) collective-permute-start(bf16[512,128]{1,0:T(8,128)(2,1)S(1)} %attend.1), channel_id=1, source_target_pairs={{0,1},{1,0},{2,3},{3,2},{4,5},{5,4},{6,7},{7,6},{8,9},{9,8},{10,11... | collective-permute-start | bytes 393224 | tf_op jit(solution)/shard_map/ppermute | solution.py:367
  67.3 1.0 %collective-permute-done.8 = bf16[512,128]{1,0:T(8,128)(2,1)S(1)} collective-permute-done((bf16[512,128]{1,0:T(8,128)(2,1)S(1)}, bf16[512,128]{1,0:T(8,128)(2,1)S(1)}, u32[]{:S(2)}, u32[]{:S(2)}) %collective-permute-start.8) | collective-permute-done | bytes 131104 | tf_op jit(solution)/shard_map/ppermute | solution.py:367
  68.3 4.3 %collective-permute-start.9 = (bf16[2,512,128]{2,1,0:T(8,128)(2,1)S(1)}, bf16[2,512,128]{2,1,0:T(8,128)(2,1)S(1)}, u32[]{:S(2)}, u32[]{:S(2)}) collective-permute-start(bf16[2,512,128]{2,1,0:T(8,128)(2,1)S(1)} %pad_maximum_fusion.own), channel_id=1, source_target_pairs={{0,2},{2,4},{4,6},{6,8},{8,10},{10,12},{12,14},{14,16},{16,18},{18... | collective-permute-start | bytes 786440 | tf_op jit(solution)/shard_map/ppermute | solution.py:374
  72.6 3.3 %collective-permute-done.9.sent = bf16[2,512,128]{2,1,0:T(8,128)(2,1)S(1)} collective-permute-done((bf16[2,512,128]{2,1,0:T(8,128)(2,1)S(1)}, bf16[2,512,128]{2,1,0:T(8,128)(2,1)S(1)}, u32[]{:S(2)}, u32[]{:S(2)}) %collective-permute-start.9) | collective-permute-done | bytes 262176 | tf_op jit(solution)/shard_map/ppermute | solution.py:374
  75.9 5.2 %collective-permute-start.10 = (bf16[2,512,128]{2,1,0:T(8,128)(2,1)S(1)}, bf16[2,512,128]{2,1,0:T(8,128)(2,1)S(1)}, u32[]{:S(2)}, u32[]{:S(2)}) collective-permute-start(bf16[2,512,128]{2,1,0:T(8,128)(2,1)S(1)} %collective-permute-done.9.sent), channel_id=1, source_target_pairs={{0,1},{1,0},{2,3},{3,2},{4,5},{5,4},{6,7},{7,6},{8,9},{9,8},{10,11... | collective-permute-start | bytes 786440 | tf_op jit(solution)/shard_map/ppermute | solution.py:367
  81.2 1.2 %collective-permute-done.10.swapped_rows = bf16[2,512,128]{2,1,0:T(8,128)(2,1)S(1)} collective-permute-done((bf16[2,512,128]{2,1,0:T(8,128)(2,1)S(1)}, bf16[2,512,128]{2,1,0:T(8,128)(2,1)S(1)}, u32[]{:S(2)}, u32[]{:S(2)}) %collective-permute-start.10) | collective-permute-done | bytes 262176 | tf_op jit(solution)/shard_map/ppermute | solution.py:367
  82.3 0.0 copy-done.1
  82.3 0.0 copy-done.10
  82.3 0.0 copy-done.11
  82.3 0.0 copy-done.12
  82.3 6.7 %decode.1 = bf16[100,1024]{1,0:T(8,128)(2,1)} custom-call(s32[8]{0:T(128)S(1)} %stack.48.info, s32[24,128]{1,0:T(8,128)S(1)} %copy-done.10, bf16[2,512,128]{2,1,0:T(8,128)(2,1)S(1)} %pad_maximum_fusion.own, bf16[2,512,128]{2,1,0:T(8,128)(2,1)S(1)} %collective-permute-done.9.sent, bf16[2,512,128]{2,1,0:T(8,128)(2,1)S(1)} %collective-permute-done.10.swapped_rows, ...), custom_call_target="tpu_custom_call" | custom-call | flops 1000000000 | bytes 3000000 | tf_op jit(solution)/shard_map/decode/pallas_call | solution.py:42
  (9 shorter events, 0.0 us)
Async XLA Ops:
  0.0 39.1 %collective-permute-start.5 = (bf16[3,1024,512]{2,1,0:T(8,128)(2,1)}, bf16[3,1024,512]{2,1,0:T(8,128)(2,1)S(1)}, u32[]{:S(2)}, u32[]{:S(2)}) collective-permute-start(bf16[3,1024,512]{2,1,0:T(8,128)(2,1)} %bitcast.18), channel_id=1, source_target_pairs={{0,1},{1,0},{2,3},{3,2},{4,5},{5,4},{6,7},{7,6},{8,9},{9,8},{10,11... | collective-permute-start | bytes 9437192 | tf_op jit(solution)/shard_map/ppermute | solution.py:367
  0.7 12.0 %collective-permute-start = (bf16[100,2048]{1,0:T(8,128)(2,1)}, bf16[100,2048]{1,0:T(8,128)(2,1)}, u32[]{:S(2)}, u32[]{:S(2)}) collective-permute-start(bf16[100,2048]{1,0:T(8,128)(2,1)} %bitcast.14), channel_id=1, source_target_pairs={{0,2},{2,4},{4,6},{6,8},{8,10},{10,12},{12,14},{14,16},{16,18},{18... | collective-permute-start | bytes 1228808 | tf_op jit(solution)/shard_map/ppermute | solution.py:374
  12.7 7.5 %collective-permute-start.1 = (bf16[100,2048]{1,0:T(8,128)(2,1)}, bf16[100,2048]{1,0:T(8,128)(2,1)}, u32[]{:S(2)}, u32[]{:S(2)}) collective-permute-start(bf16[100,2048]{1,0:T(8,128)(2,1)} %collective-permute-done.sent), channel_id=1, source_target_pairs={{0,1},{1,0},{2,3},{3,2},{4,5},{5,4},{6,7},{7,6},{8,9},{9,8},{10,11... | collective-permute-start | bytes 1228808 | tf_op jit(solution)/shard_map/ppermute | solution.py:367
  15.2 5.0 %collective-permute-start.2 = (bf16[100,512]{1,0:T(8,128)(2,1)}, bf16[100,512]{1,0:T(8,128)(2,1)S(1)}, u32[]{:S(2)}, u32[]{:S(2)}) collective-permute-start(bf16[100,512]{1,0:T(8,128)(2,1)} %win_own.1), channel_id=1, source_target_pairs={{0,1},{1,0},{2,3},{3,2},{4,5},{5,4},{6,7},{7,6},{8,9},{9,8},{10,11... | collective-permute-start | bytes 307208 | tf_op jit(solution)/shard_map/ppermute | solution.py:367
  16.0 1.0 %copy-start = (bf16[2048,100]{0,1:T(8,128)(2,1)S(1)}, bf16[2048,100]{0,1:T(8,128)(2,1)}, u32[]{:S(2)}) copy-start(bf16[2048,100]{0,1:T(8,128)(2,1)} %param.14) | copy-start | bytes 1228804
  17.0 0.7 copy-start.2
  20.2 0.9 %copy-start.5 = (bf16[100,512]{1,0:T(8,128)(2,1)S(1)}, bf16[100,512]{1,0:T(8,128)(2,1)}, u32[]{:S(2)}) copy-start(bf16[100,512]{1,0:T(8,128)(2,1)} %win_own.1) | copy-start | bytes 307204
  21.1 0.8 copy-start.7
  21.9 0.8 copy-start.8
  22.7 0.7 copy-start.9
  23.4 0.7 copy-start.13
  24.1 12.4 %copy-start.4 = (bf16[512,1024]{1,0:T(8,128)(2,1)S(1)}, bf16[512,1024]{1,0:T(8,128)(2,1)}, u32[]{:S(2)}) copy-start(bf16[512,1024]{1,0:T(8,128)(2,1)} %out_own.1) | copy-start | bytes 3145732
  24.1 12.5 %copy-start.6 = (bf16[512,100]{0,1:T(8,128)(2,1)S(1)}, bf16[512,100]{0,1:T(8,128)(2,1)}, u32[]{:S(2)}) copy-start(bf16[512,100]{0,1:T(8,128)(2,1)} %param.24) | copy-start | bytes 307204
  24.1 15.0 %copy-start.3 = (bf16[1024,3,512]{2,0,1:T(8,128)(2,1)S(1)}, bf16[1024,3,512]{2,0,1:T(8,128)(2,1)}, u32[]{:S(2)}) copy-start(bf16[1024,3,512]{2,0,1:T(8,128)(2,1)} %param.21) | copy-start | bytes 9437188
  35.9 3.2 %collective-permute-start.4 = (bf16[384,1024]{1,0:T(8,128)(2,1)S(1)}, bf16[384,1024]{1,0:T(8,128)(2,1)S(1)}, u32[]{:S(2)}, u32[]{:S(2)}) collective-permute-start(bf16[384,1024]{1,0:T(8,128)(2,1)S(1)} %get-tuple-element.19), channel_id=1, source_target_pairs={{0,1},{1,0},{2,3},{3,2},{4,5},{5,4},{6,7},{7,6},{8,9},{9,8},{10,11... | collective-permute-start | bytes 2359304 | tf_op jit(solution)/shard_map/ppermute | solution.py:367
  36.5 15.6 %collective-permute-start.6 = (bf16[512,1024]{1,0:T(8,128)(2,1)S(1)}, bf16[512,1024]{1,0:T(8,128)(2,1)S(1)}, u32[]{:S(2)}, u32[]{:S(2)}) collective-permute-start(bf16[512,1024]{1,0:T(8,128)(2,1)S(1)} %copy-done.4), channel_id=1, source_target_pairs={{0,1},{1,0},{2,3},{3,2},{4,5},{5,4},{6,7},{7,6},{8,9},{9,8},{10,11... | collective-permute-start | bytes 3145736 | tf_op jit(solution)/shard_map/ppermute | solution.py:367
  36.6 15.5 %collective-permute-start.7 = (bf16[100,512]{1,0:T(8,128)(2,1)S(1)}, bf16[100,512]{1,0:T(8,128)(2,1)S(1)}, u32[]{:S(2)}, u32[]{:S(2)}) collective-permute-start(bf16[100,512]{1,0:T(8,128)(2,1)S(1)} %bitcast.21), channel_id=1, source_target_pairs={{0,1},{1,0},{2,3},{3,2},{4,5},{5,4},{6,7},{7,6},{8,9},{9,8},{10,11... | collective-permute-start | bytes 307208 | tf_op jit(solution)/shard_map/ppermute | solution.py:367
  37.0 15.1 %collective-permute-start.3 = (bf16[384,1024]{1,0:T(8,128)(2,1)S(1)}, bf16[384,1024]{1,0:T(8,128)(2,1)S(1)}, u32[]{:S(2)}, u32[]{:S(2)}) collective-permute-start(bf16[384,1024]{1,0:T(8,128)(2,1)S(1)} %get-tuple-element.17), channel_id=1, source_target_pairs={{1,2},{3,4},{5,6},{7,8},{9,10},{11,12},{13,14},{15,16},{17,18},{19... | collective-permute-start | bytes 2359304 | tf_op jit(solution)/shard_map/ppermute | solution.py:381
  52.1 30.3 %copy-start.1 = (bf16[2048,100]{0,1:T(8,128)(2,1)S(1)}, bf16[2048,100]{0,1:T(8,128)(2,1)}, u32[]{:S(2)}) copy-start(bf16[2048,100]{0,1:T(8,128)(2,1)} %param.14) | copy-start | bytes 1228804
  52.1 30.3 %copy-start.10 = (s32[24,128]{1,0:T(8,128)S(1)}, s32[24,128]{1,0:T(8,128)}, u32[]{:S(2)}) copy-start(s32[24,128]{1,0:T(8,128)} %src.3) | copy-start | bytes 36868
  52.1 30.3 %copy-start.11 = (s32[24,128]{1,0:T(8,128)S(1)}, s32[24,128]{1,0:T(8,128)}, u32[]{:S(2)}) copy-start(s32[24,128]{1,0:T(8,128)} %dst.3) | copy-start | bytes 36868
  52.1 30.2 %copy-start.12 = (bf16[24,128]{1,0:T(8,128)(2,1)S(1)}, bf16[24,128]{1,0:T(8,128)(2,1)}, u32[]{:S(2)}) copy-start(bf16[24,128]{1,0:T(8,128)(2,1)} %weight.3) | copy-start | bytes 18436
  63.1 5.2 %collective-permute-start.8 = (bf16[512,128]{1,0:T(8,128)(2,1)S(1)}, bf16[512,128]{1,0:T(8,128)(2,1)S(1)}, u32[]{:S(2)}, u32[]{:S(2)}) collective-permute-start(bf16[512,128]{1,0:T(8,128)(2,1)S(1)} %attend.1), channel_id=1, source_target_pairs={{0,1},{1,0},{2,3},{3,2},{4,5},{5,4},{6,7},{7,6},{8,9},{9,8},{10,11... | collective-permute-start | bytes 393224 | tf_op jit(solution)/shard_map/ppermute | solution.py:367
  68.3 7.6 %collective-permute-start.9 = (bf16[2,512,128]{2,1,0:T(8,128)(2,1)S(1)}, bf16[2,512,128]{2,1,0:T(8,128)(2,1)S(1)}, u32[]{:S(2)}, u32[]{:S(2)}) collective-permute-start(bf16[2,512,128]{2,1,0:T(8,128)(2,1)S(1)} %pad_maximum_fusion.own), channel_id=1, source_target_pairs={{0,2},{2,4},{4,6},{6,8},{8,10},{10,12},{12,14},{14,16},{16,18},{18... | collective-permute-start | bytes 786440 | tf_op jit(solution)/shard_map/ppermute | solution.py:374
  75.9 6.4 %collective-permute-start.10 = (bf16[2,512,128]{2,1,0:T(8,128)(2,1)S(1)}, bf16[2,512,128]{2,1,0:T(8,128)(2,1)S(1)}, u32[]{:S(2)}, u32[]{:S(2)}) collective-permute-start(bf16[2,512,128]{2,1,0:T(8,128)(2,1)S(1)} %collective-permute-done.9.sent), channel_id=1, source_target_pairs={{0,1},{1,0},{2,3},{3,2},{4,5},{5,4},{6,7},{7,6},{8,9},{9,8},{10,11... | collective-permute-start | bytes 786440 | tf_op jit(solution)/shard_map/ppermute | solution.py:367

commit v3 on v2

--- a/solution.py
+++ b/solution.py
@@ -17,7 +17,7 @@
 G_BAND = 2048
 EDGE_ROUNDS = 8
 TILES = 4
-STEP = 256
+STEP = 512
 SPAN = TILE + 2 * WIN
 GQ = 1024
 DEC_ROUNDS = 3
@@ -37,7 +37,7 @@
     return pl.BlockSpec(memory_space=pltpu.SMEM)
 
 
-def call(body, operands, smem_count, outs, scratch, flops, touched, name):
+def call(body, operands, smem_count, outs, scratch, flops, touched, name, aliases={}):
     specs = [smem()] * smem_count + [vmem()] * (len(operands) - smem_count)
     return pl.pallas_call(
         body,
@@ -47,6 +47,7 @@
         scratch_shapes=scratch,
         compiler_params=pltpu.CompilerParams(vmem_limit_bytes=VMEM_BYTES),
         cost_estimate=pl.CostEstimate(flops=flops, bytes_accessed=touched, transcendentals=0),
+        input_output_aliases=aliases,
         name=name,
     )(*operands)
 
@@ -63,12 +64,18 @@
     wide[:C, :] = part[...].astype(F32)
     for block in range(G_BAND // LANES):
         columns = slice(block * LANES, (block + 1) * LANES)
-        rows[begin + block * LANES : begin + (block + 1) * LANES, :] = wide[:, columns].T
-
-
-def prepare_body(offsets, grid, rows, mask, wide):
+        place = pl.multiple_of(begin + block * LANES, LANES)
+        rows[pl.ds(place, LANES), :] = wide[:, columns].T
+
+
+def prepare_body(
+    info, offsets, grid, src, dst, weight, gain, win_own, win_peer,
+    own_rows, mask, sources, targets, weights, gains, w_in,
+    wide, w_wide,
+):
+    core, live, mesh_base = info[0], info[1], info[3]
     wide[...] = jnp.zeros_like(wide)
-    to_rows(grid, wide, rows, 0)
+    to_rows(grid, wide, own_rows, 0)
     for chunk in range(SPAN // TILE):
         row = lax.broadcasted_iota(jnp.int32, (TILE, LANES), 0) + (chunk * TILE - WIN)
         away = row - lax.broadcasted_iota(jnp.int32, (TILE, LANES), 1)
@@ -76,35 +83,40 @@
         for k in range(1, K_OFF):
             hit = hit | (away == offsets[k])
         mask[chunk * TILE : (chunk + 1) * TILE, :] = jnp.where(hit, 0.0, MASKED).astype(BF16)
-
-
-def encode_body(
-    info, src, sent, swapped_rows, own_rows, win_own, win_peer, dst, weight, gain,
-    mesh_zero, normed, to_peer, to_band,
-    rows, wide, first, second, w_wide, w_in, weights, total,
-):
-    core, live, grid_base, mesh_base = info[0], info[1], info[2], info[3]
+    slots = lax.broadcasted_iota(jnp.int32, weights.shape, 0)
+    weights[...] = jnp.where(slots < live, weight[...].astype(F32), 0.0)
+    targets[...] = dst[...] - mesh_base
+    sources[...] = src[...] - info[2]
+    gains[...] = gain[...]
+    w_wide[...] = jnp.zeros_like(w_wide)
+
+    @pl.when(core == 0)
+    def _():
+        w_wide[:C, :HALF] = win_own[...].astype(F32) * 0.5
+        w_wide[:C, HALF:] = win_peer[...].astype(F32) * 0.5
+
+    @pl.when(core != 0)
+    def _():
+        w_wide[:C, :HALF] = win_peer[...].astype(F32) * 0.5
+        w_wide[:C, HALF:] = win_own[...].astype(F32) * 0.5
+
+    w_in[...] = w_wide[...].astype(BF16)
+
+
+def unpack_body(info, own_rows, sent, rows, wide):
     wide[...] = jnp.zeros_like(wide)
     rows[G_BAND : 2 * G_BAND, :] = own_rows[...]
-    w_wide[...] = jnp.zeros_like(w_wide)
-
-    @pl.when(core == 0)
-    def _():
-        to_rows(sent, wide, rows, 0)
-        to_rows(swapped_rows, wide, rows, 2 * G_BAND)
-        w_wide[:C, :HALF] = win_own[...].astype(F32) * 0.5
-        w_wide[:C, HALF:] = win_peer[...].astype(F32) * 0.5
-
-    @pl.when(core != 0)
-    def _():
-        to_rows(swapped_rows, wide, rows, 0)
-        to_rows(sent, wide, rows, 2 * G_BAND)
-        w_wide[:C, :HALF] = win_peer[...].astype(F32) * 0.5
-        w_wide[:C, HALF:] = win_own[...].astype(F32) * 0.5
-
-    w_in[...] = w_wide[...].astype(BF16)
-    slots = lax.broadcasted_iota(jnp.int32, weights.shape, 0)
-    weights[...] = jnp.where(slots < live, weight[...].astype(F32), 0.0)
+    to_rows(sent, wide, rows, info[0] * 2 * G_BAND)
+
+
+def encode_body(
+    info, src, grid_rows, swapped_rows, w_in, targets, weights, gain,
+    rows, mesh_zero, normed, to_peer, to_band,
+    wide, first, second, total,
+):
+    core = info[0]
+    wide[...] = jnp.zeros_like(wide)
+    to_rows(swapped_rows, wide, rows, (1 - core) * 2 * G_BAND)
     total[...] = jnp.zeros_like(total)
     row_slots = lax.broadcasted_iota(jnp.int32, (TILE, LANES), 0)
     steps = EDGE_ROUNDS * TILE // STEP
@@ -118,7 +130,7 @@
         for part in range(rounds):
             slot = slot_of(step, part)
             for edge in range(TILE):
-                index = src[slot, edge] - grid_base
+                index = src[slot, edge]
                 buffer[pl.ds(part * TILE + edge, 1), :] = rows[pl.ds(index, 1), :]
 
     def add(step, buffer):
@@ -128,7 +140,7 @@
         tables = []
         for part in range(rounds):
             slot = slot_of(step, part)
-            target = dst[pl.ds(slot, 1), :] - (mesh_base + tile * TILE)
+            target = targets[pl.ds(slot, 1), :] - tile * TILE
             tables.append(jnp.where(row_slots == target, weights[pl.ds(slot, 1), :], 0.0))
         table = jnp.concatenate(tables, axis=1).astype(BF16)
         place = pl.ds(pl.multiple_of(tile * TILE, TILE), TILE)
@@ -391,7 +403,6 @@
     device = 2 * band + core
     grid = grid_fields.T
     grid_sent = up_and_down(grid)
-    grid_swapped = swapped(grid_sent)
     info = jnp.stack([
         core,
         enc_count[0],
@@ -408,34 +419,48 @@
     qkv_own = w_qkv.transpose(1, 0, 2)
     qkv_peer = swapped(qkv_own)
     out_peer = swapped(w_out_attn)
-    own_rows, mask = call(
+    edges = jax.ShapeDtypeStruct(enc_src.shape, jnp.int32)
+    own_rows, mask, sources, targets, weights, gain, w_in_all = call(
         prepare_body,
-        (offsets, grid),
-        1,
+        (info, offsets, grid, enc_src, enc_dst, enc_weight, norm_gain.reshape(1, D), w_in,
+         win_peer),
+        2,
         [
             jax.ShapeDtypeStruct((G_BAND, LANES), F32),
             jax.ShapeDtypeStruct((SPAN, TILE), BF16),
+            edges,
+            edges,
+            jax.ShapeDtypeStruct(enc_weight.shape, F32),
+            jax.ShapeDtypeStruct((1, D), F32),
+            jax.ShapeDtypeStruct((LANES, D), BF16),
         ],
+        [pltpu.VMEM((LANES, G_BAND), F32), pltpu.VMEM((LANES, D), F32)],
+        8 * 10 ** 9, 2 * 10 ** 6, "prepare",
+    )
+    grid_sent, own_rows = lax.optimization_barrier((grid_sent, own_rows))
+    grid_swapped = swapped(grid_sent)
+    grid_rows = call(
+        unpack_body,
+        (info, own_rows, grid_sent),
+        1,
+        jax.ShapeDtypeStruct((3 * G_BAND, LANES), F32),
         [pltpu.VMEM((LANES, G_BAND), F32)],
-        10 ** 7, 2 * 10 ** 6, "prepare",
-    )
-    mesh_zero, normed, to_peer, to_band = call(
+        2 * 10 ** 9, 2 * 10 ** 6, "unpack",
+    )
+    _, mesh_zero, normed, to_peer, to_band = call(
         encode_body,
-        (info, enc_src, grid_sent, grid_swapped, own_rows, w_in, win_peer, enc_dst,
-         enc_weight, norm_gain.reshape(1, D)),
+        (info, sources, grid_rows, grid_swapped, w_in_all, targets, weights, gain),
         2,
-        [jax.ShapeDtypeStruct((ROWS, D), BF16)] * 2 + [jax.ShapeDtypeStruct((WIN, D), BF16)] * 2,
+        [jax.ShapeDtypeStruct((3 * G_BAND, LANES), F32)]
+        + [jax.ShapeDtypeStruct((ROWS, D), BF16)] * 2
+        + [jax.ShapeDtypeStruct((WIN, D), BF16)] * 2,
         [
-            pltpu.VMEM((3 * G_BAND, LANES), F32),
             pltpu.VMEM((LANES, G_BAND), F32),
             pltpu.VMEM((STEP, LANES), F32),
             pltpu.VMEM((STEP, LANES), F32),
-            pltpu.VMEM((LANES, D), F32),
-            pltpu.VMEM((LANES, D), BF16),
-            pltpu.VMEM(enc_weight.shape, F32),
             pltpu.VMEM((ROWS, D), F32),
         ],
-        8 * 10 ** 9, 4 * 10 ** 6, "encode",
+        8 * 10 ** 9, 4 * 10 ** 6, "encode", {2: 0},
     )
     halo_peer = swapped(to_peer)
     halo_band = over_the_edge(to_band)

time: 89.5 us -> 80.6 us (0.901)
  waiting for transfers between devices: 10.8 us -> 6.18 us
  starting transfers between devices: 26.8 us -> 23.5 us
  Pallas kernels: 45.1 us -> 44 us
    ppermute x2, waiting for transfers between devices: 8.66 us -> 3.3 us  [up_and_down(): return lax.ppermute(value, ('band', 'mp'), pairs)]
    ppermute x8, starting transfers between devices: 13.7 us -> 10.2 us  [swapped(): return lax.ppermute(value, 'mp', [(0, 1), (1, 0)])]
    pallas_call x5 -> x6, Pallas kernels: 45.1 us -> 44 us  [call(): pl.pallas_call(body, out_shape=outs, in_specs=specs, out_specs=jax.tree.m...]
  transfers between devices with their start and end apart: 11 -> 11, of which waited for: 4 -> 4; matrix products, arithmetic and copies ran while one was open for 0% -> 0% of each run, Pallas kernels for 31% -> 33%
where the time goes in v3:
time: 80.6 us; the launch traced here: 80.1 us
  Pallas kernels  44 us (55%)
  starting transfers between devices  23.5 us (29%)
  waiting for transfers between devices  6.18 us (8%)
  local copies, waits for them, and re-layouts  5.59 us (7%)
  between operations  0.84 us (1%)
    pallas_call x6, Pallas kernels, call(): pl.pallas_call(body, out_shape=outs, in_specs=specs, out_specs=jax.tree.m...  44 us
    ppermute x2, starting transfers between devices, up_and_down(): return lax.ppermute(value, ('band', 'mp'), pairs)  11.2 us
    ppermute x8, starting transfers between devices, swapped(): return lax.ppermute(value, 'mp', [(0, 1), (1, 0)])  10.2 us
    unnamed x28, local copies, waits for them, and re-layouts  5.51 us
    ppermute x2, waiting for transfers between devices, up_and_down(): return lax.ppermute(value, ('band', 'mp'), pairs)  3.3 us
    ppermute x8, waiting for transfers between devices, swapped(): return lax.ppermute(value, 'mp', [(0, 1), (1, 0)])  2.88 us
    ppermute x1, starting transfers between devices, over_the_edge(): return lax.ppermute(value, ('band', 'mp'), pairs)  2.09 us
  transfers between devices with their start and end apart: 11, of which 4 were waited for; matrix products, arithmetic and copies ran while one was open for 0% of the time, Pallas kernels for 33%

profile of v3, /device:TPU:97, one launch (start us, length us, event | category | flops | bytes accessed | tf_op | source)
XLA Modules:
  0.0 80.1 jit_solution(10624274829064059434)
XLA Ops:
  0.0 0.7 collective-permute-start.5
  0.7 0.0 collective-permute-start
  0.7 6.7 %collective-permute-start.1 = (bf16[100,2048]{1,0:T(8,128)(2,1)}, bf16[100,2048]{1,0:T(8,128)(2,1)}, u32[]{:S(2)}, u32[]{:S(2)}) collective-permute-start(bf16[100,2048]{1,0:T(8,128)(2,1)} %bitcast.18), channel_id=1, source_target_pairs={{0,2},{2,4},{4,6},{6,8},{8,10},{10,12},{12,14},{14,16},{16,18},{18... | collective-permute-start | bytes 1228808 | tf_op jit(solution)/shard_map/ppermute | solution.py:386
  8.0 0.1 stack.48.info
  8.1 0.0 collective-permute-done.win_peer
  8.1 0.0 copy-start.2
  8.1 1.0 %copy-done.2 = bf16[2048,100]{0,1:T(8,128)(2,1)S(1)} copy-done((bf16[2048,100]{0,1:T(8,128)(2,1)S(1)}, bf16[2048,100]{0,1:T(8,128)(2,1)}, u32[]{:S(2)}) %copy-start.2) | copy-done | bytes 409624
  9.1 0.9 %copy-done.4 = bf16[100,512]{1,0:T(8,128)(2,1)S(1)} copy-done((bf16[100,512]{1,0:T(8,128)(2,1)S(1)}, bf16[100,512]{1,0:T(8,128)(2,1)}, u32[]{:S(2)}) %copy-start.4) | copy-done | bytes 102424
  10.0 0.8 copy-done.6
  10.8 0.8 copy-done.7
  11.5 0.7 copy-done.8
  12.2 0.7 copy-done.12
  12.9 0.7 copy-done.13
  13.6 2.7 %prepare.1 = (f32[2048,128]{1,0:T(8,128)S(1)}, bf16[896,128]{1,0:T(8,128)(2,1)S(1)}, s32[64,128]{1,0:T(8,128)S(1)}, s32[64,128]{1,0:T(8,128)S(1)}, f32[64,128]{1...) custom-call(s32[8]{0:T(128)S(1)} %stack.48.info, s32[32]{0:T(128)S(1)} %copy-done.13, ...), custom_call_target="tpu_custom_call" | custom-call | flops 8000000000 | bytes 2000000 | tf_op jit(solution)/shard_map/prepare/pallas_call | solution.py:42
  16.3 0.0 collective-permute-done.1.sent
  16.3 0.1 collective-permute-start.2
  16.4 1.2 %unpack.1.grid_rows = f32[6144,128]{1,0:T(8,128)S(1)} custom-call(s32[8]{0:T(128)S(1)} %stack.48.info, f32[2048,128]{1,0:T(8,128)S(1)} %get-tuple-element.25.own_rows, bf16[100,2048]{1,0:T(8,128)(2,1)} %collective-permute-done.1.sent), custom_call_target="tpu_custom_call" | custom-call | flops 2000000000 | bytes 2000000 | tf_op jit(solution)/shard_map/unpack/pallas_call | solution.py:42
  17.6 0.7 collective-permute-done.2.swapped_rows
  18.3 9.3 %encode.1 = (f32[6144,128]{1,0:T(8,128)S(1)}, bf16[512,1024]{1,0:T(8,128)(2,1)S(1)}, bf16[512,1024]{1,0:T(8,128)(2,1)S(1)}, bf16[384,1024]{1,0:T(8,128)(2,1)S(1)}, bf16[384,1024]{1,0:T(8,128)(2,1)S(1)}) custom-call(s32[8]{0:T(128)S(1)} %stack.48.info, s32[64,128]{1,0:T(8,128)S(1)} %get-tuple-element.23.src, ...), custom_call_target="tpu_custom_call", output_to_operand_aliasing={{0}: (2, {})} | custom-call | flops 8000000000 | bytes 4000000 | tf_op jit(solution)/shard_map/encode/pallas_call | solution.py:42
  27.7 0.2 collective-permute-start.4
  27.9 0.0 copy-done.1
  27.9 0.3 collective-permute-start.6
  28.3 0.0 copy-done.5
  28.3 0.2 collective-permute-start.7
  28.5 2.1 %collective-permute-start.3 = (bf16[384,1024]{1,0:T(8,128)(2,1)S(1)}, bf16[384,1024]{1,0:T(8,128)(2,1)S(1)}, u32[]{:S(2)}, u32[]{:S(2)}) collective-permute-start(bf16[384,1024]{1,0:T(8,128)(2,1)S(1)} %get-tuple-element.31), channel_id=1, source_target_pairs={{1,2},{3,4},{5,6},{7,8},{9,10},{11,12},{13,14},{15,16},{17,18},{19... | collective-permute-start | bytes 2359304 | tf_op jit(solution)/shard_map/ppermute | solution.py:393
  30.6 0.0 collective-permute-done.4.halo
  30.6 0.0 collective-permute-done.5.w_peer
  30.6 0.0 copy-done
  30.6 12.9 %project.1 = (bf16[512,1024]{1,0:T(8,128)(2,1)S(1)}, bf16[384,1024]{1,0:T(8,128)(2,1)S(1)}, bf16[1024,384]{1,0:T(8,128)(2,1)S(1)}, f32[1024,512]{1,0:T(8,128)S(1)}, f32[8,8,1024]{2,1,0:T(8,128)S(1)}) custom-call(bf16[512,1024]{1,0:T(8,128)(2,1)S(1)} %get-tuple-element.32.normed, bf16[384,1024]{1,0:T(8,128)(2,1)S(1)} %collective-permute-done.4.halo, ...), custom_call_target="tpu_custom_call" | custom-call | flops 10000000000 | bytes 10000000 | tf_op jit(solution)/shard_map/project/pallas_call | solution.py:42
  43.5 0.0 collective-permute-done.7.dec_peer
  43.5 0.0 collective-permute-done.6.out_peer
  43.6 0.0 collective-permute-done.3.halo
  43.6 0.0 copy-start.3
  43.6 0.0 copy-start.9
  43.6 0.0 copy-start.10
  43.6 0.0 copy-start.11
  43.6 11.0 %attend.1 = bf16[512,128]{1,0:T(8,128)(2,1)S(1)} custom-call(s32[8]{0:T(128)S(1)} %stack.48.info, bf16[384,1024]{1,0:T(8,128)(2,1)S(1)} %collective-permute-done.3.halo, bf16[384,1024]{1,0:T(8,128)(2,1)S(1)} %get-tuple-element.35.peer_keys, bf16[1024,384]{1,0:T(8,128)(2,1)S(1)} %get-tuple-element.36.peer_values, ...), custom_call_target="tpu_custom_call" | custom-call | flops 10000000000 | bytes 20000000 | tf_op jit(solution)/shard_map/attend/pallas_call | solution.py:42
  54.6 3.7 %collective-permute-start.8 = (bf16[512,128]{1,0:T(8,128)(2,1)S(1)}, bf16[512,128]{1,0:T(8,128)(2,1)S(1)}, u32[]{:S(2)}, u32[]{:S(2)}) collective-permute-start(bf16[512,128]{1,0:T(8,128)(2,1)S(1)} %attend.1), channel_id=1, source_target_pairs={{0,1},{1,0},{2,3},{3,2},{4,5},{5,4},{6,7},{7,6},{8,9},{9,8},{10,11... | collective-permute-start | bytes 393224 | tf_op jit(solution)/shard_map/ppermute | solution.py:379
  58.3 1.0 %collective-permute-done.8 = bf16[512,128]{1,0:T(8,128)(2,1)S(1)} collective-permute-done((bf16[512,128]{1,0:T(8,128)(2,1)S(1)}, bf16[512,128]{1,0:T(8,128)(2,1)S(1)}, u32[]{:S(2)}, u32[]{:S(2)}) %collective-permute-start.8) | collective-permute-done | bytes 131104 | tf_op jit(solution)/shard_map/ppermute | solution.py:379
  59.3 4.6 %collective-permute-start.9 = (bf16[2,512,128]{2,1,0:T(8,128)(2,1)S(1)}, bf16[2,512,128]{2,1,0:T(8,128)(2,1)S(1)}, u32[]{:S(2)}, u32[]{:S(2)}) collective-permute-start(bf16[2,512,128]{2,1,0:T(8,128)(2,1)S(1)} %pad_maximum_fusion.own), channel_id=1, source_target_pairs={{0,2},{2,4},{4,6},{6,8},{8,10},{10,12},{12,14},{14,16},{16,18},{18... | collective-permute-start | bytes 786440 | tf_op jit(solution)/shard_map/ppermute | solution.py:386
  63.9 3.3 %collective-permute-done.9.sent = bf16[2,512,128]{2,1,0:T(8,128)(2,1)S(1)} collective-permute-done((bf16[2,512,128]{2,1,0:T(8,128)(2,1)S(1)}, bf16[2,512,128]{2,1,0:T(8,128)(2,1)S(1)}, u32[]{:S(2)}, u32[]{:S(2)}) %collective-permute-start.9) | collective-permute-done | bytes 262176 | tf_op jit(solution)/shard_map/ppermute | solution.py:386
  67.2 5.0 %collective-permute-start.10 = (bf16[2,512,128]{2,1,0:T(8,128)(2,1)S(1)}, bf16[2,512,128]{2,1,0:T(8,128)(2,1)S(1)}, u32[]{:S(2)}, u32[]{:S(2)}) collective-permute-start(bf16[2,512,128]{2,1,0:T(8,128)(2,1)S(1)} %collective-permute-done.9.sent), channel_id=1, source_target_pairs={{0,1},{1,0},{2,3},{3,2},{4,5},{5,4},{6,7},{7,6},{8,9},{9,8},{10,11... | collective-permute-start | bytes 786440 | tf_op jit(solution)/shard_map/ppermute | solution.py:379
  72.2 1.2 %collective-permute-done.10.swapped_rows = bf16[2,512,128]{2,1,0:T(8,128)(2,1)S(1)} collective-permute-done((bf16[2,512,128]{2,1,0:T(8,128)(2,1)S(1)}, bf16[2,512,128]{2,1,0:T(8,128)(2,1)S(1)}, u32[]{:S(2)}, u32[]{:S(2)}) %collective-permute-start.10) | collective-permute-done | bytes 262176 | tf_op jit(solution)/shard_map/ppermute | solution.py:379
  73.3 0.0 copy-done.3
  73.3 0.0 copy-done.9
  73.3 0.0 copy-done.10
  73.4 0.0 copy-done.11
  73.4 6.7 %decode.1 = bf16[100,1024]{1,0:T(8,128)(2,1)} custom-call(s32[8]{0:T(128)S(1)} %stack.48.info, s32[24,128]{1,0:T(8,128)S(1)} %copy-done.9, bf16[2,512,128]{2,1,0:T(8,128)(2,1)S(1)} %pad_maximum_fusion.own, bf16[2,512,128]{2,1,0:T(8,128)(2,1)S(1)} %collective-permute-done.9.sent, bf16[2,512,128]{2,1,0:T(8,128)(2,1)S(1)} %collective-permute-done.10.swapped_rows, ...), custom_call_target="tpu_custom_call" | custom-call | flops 1000000000 | bytes 3000000 | tf_op jit(solution)/shard_map/decode/pallas_call | solution.py:42
  (10 shorter events, 0.0 us)
Async XLA Ops:
  0.0 30.6 %collective-permute-start.5 = (bf16[3,1024,512]{2,1,0:T(8,128)(2,1)}, bf16[3,1024,512]{2,1,0:T(8,128)(2,1)S(1)}, u32[]{:S(2)}, u32[]{:S(2)}) collective-permute-start(bf16[3,1024,512]{2,1,0:T(8,128)(2,1)} %bitcast.15), channel_id=1, source_target_pairs={{0,1},{1,0},{2,3},{3,2},{4,5},{5,4},{6,7},{7,6},{8,9},{9,8},{10,11... | collective-permute-start | bytes 9437192 | tf_op jit(solution)/shard_map/ppermute | solution.py:379
  0.7 7.4 %collective-permute-start = (bf16[100,512]{1,0:T(8,128)(2,1)}, bf16[100,512]{1,0:T(8,128)(2,1)S(1)}, u32[]{:S(2)}, u32[]{:S(2)}) collective-permute-start(bf16[100,512]{1,0:T(8,128)(2,1)} %win_own.1), channel_id=1, source_target_pairs={{0,1},{1,0},{2,3},{3,2},{4,5},{5,4},{6,7},{7,6},{8,9},{9,8},{10,11... | collective-permute-start | bytes 307208 | tf_op jit(solution)/shard_map/ppermute | solution.py:379
  0.7 15.6 %collective-permute-start.1 = (bf16[100,2048]{1,0:T(8,128)(2,1)}, bf16[100,2048]{1,0:T(8,128)(2,1)}, u32[]{:S(2)}, u32[]{:S(2)}) collective-permute-start(bf16[100,2048]{1,0:T(8,128)(2,1)} %bitcast.18), channel_id=1, source_target_pairs={{0,2},{2,4},{4,6},{6,8},{8,10},{10,12},{12,14},{14,16},{16,18},{18... | collective-permute-start | bytes 1228808 | tf_op jit(solution)/shard_map/ppermute | solution.py:386
  8.1 1.0 %copy-start.2 = (bf16[2048,100]{0,1:T(8,128)(2,1)S(1)}, bf16[2048,100]{0,1:T(8,128)(2,1)}, u32[]{:S(2)}) copy-start(bf16[2048,100]{0,1:T(8,128)(2,1)} %param.14) | copy-start | bytes 1228804
  9.1 0.9 %copy-start.4 = (bf16[100,512]{1,0:T(8,128)(2,1)S(1)}, bf16[100,512]{1,0:T(8,128)(2,1)}, u32[]{:S(2)}) copy-start(bf16[100,512]{1,0:T(8,128)(2,1)} %win_own.1) | copy-start | bytes 307204
  10.0 0.8 copy-start.6
  10.8 0.8 copy-start.7
  11.5 0.7 copy-start.8
  12.2 0.7 copy-start.12
  12.9 0.7 copy-start.13
  16.3 2.1 %collective-permute-start.2 = (bf16[100,2048]{1,0:T(8,128)(2,1)}, bf16[100,2048]{1,0:T(8,128)(2,1)S(1)}, u32[]{:S(2)}, u32[]{:S(2)}) collective-permute-start(bf16[100,2048]{1,0:T(8,128)(2,1)} %collective-permute-done.1.sent), channel_id=1, source_target_pairs={{0,1},{1,0},{2,3},{3,2},{4,5},{5,4},{6,7},{7,6},{8,9},{9,8},{10,11... | collective-permute-start | bytes 1228808 | tf_op jit(solution)/shard_map/ppermute | solution.py:379
  18.3 9.6 %copy-start.1 = (bf16[512,1024]{1,0:T(8,128)(2,1)S(1)}, bf16[512,1024]{1,0:T(8,128)(2,1)}, u32[]{:S(2)}) copy-start(bf16[512,1024]{1,0:T(8,128)(2,1)} %out_own.1) | copy-start | bytes 3145732
  18.3 10.0 %copy-start.5 = (bf16[512,100]{0,1:T(8,128)(2,1)S(1)}, bf16[512,100]{0,1:T(8,128)(2,1)}, u32[]{:S(2)}) copy-start(bf16[512,100]{0,1:T(8,128)(2,1)} %param.24) | copy-start | bytes 307204
  18.3 12.2 %copy-start = (bf16[1024,3,512]{2,0,1:T(8,128)(2,1)S(1)}, bf16[1024,3,512]{2,0,1:T(8,128)(2,1)}, u32[]{:S(2)}) copy-start(bf16[1024,3,512]{2,0,1:T(8,128)(2,1)} %param.21) | copy-start | bytes 9437188
  27.7 2.9 %collective-permute-start.4 = (bf16[384,1024]{1,0:T(8,128)(2,1)S(1)}, bf16[384,1024]{1,0:T(8,128)(2,1)S(1)}, u32[]{:S(2)}, u32[]{:S(2)}) collective-permute-start(bf16[384,1024]{1,0:T(8,128)(2,1)S(1)} %get-tuple-element.33), channel_id=1, source_target_pairs={{0,1},{1,0},{2,3},{3,2},{4,5},{5,4},{6,7},{7,6},{8,9},{9,8},{10,11... | collective-permute-start | bytes 2359304 | tf_op jit(solution)/shard_map/ppermute | solution.py:379
  27.9 15.6 %collective-permute-start.6 = (bf16[512,1024]{1,0:T(8,128)(2,1)S(1)}, bf16[512,1024]{1,0:T(8,128)(2,1)S(1)}, u32[]{:S(2)}, u32[]{:S(2)}) collective-permute-start(bf16[512,1024]{1,0:T(8,128)(2,1)S(1)} %copy-done.1), channel_id=1, source_target_pairs={{0,1},{1,0},{2,3},{3,2},{4,5},{5,4},{6,7},{7,6},{8,9},{9,8},{10,11... | collective-permute-start | bytes 3145736 | tf_op jit(solution)/shard_map/ppermute | solution.py:379
  28.3 15.2 %collective-permute-start.7 = (bf16[100,512]{1,0:T(8,128)(2,1)S(1)}, bf16[100,512]{1,0:T(8,128)(2,1)S(1)}, u32[]{:S(2)}, u32[]{:S(2)}) collective-permute-start(bf16[100,512]{1,0:T(8,128)(2,1)S(1)} %bitcast.21), channel_id=1, source_target_pairs={{0,1},{1,0},{2,3},{3,2},{4,5},{5,4},{6,7},{7,6},{8,9},{9,8},{10,11... | collective-permute-start | bytes 307208 | tf_op jit(solution)/shard_map/ppermute | solution.py:379
  28.5 15.1 %collective-permute-start.3 = (bf16[384,1024]{1,0:T(8,128)(2,1)S(1)}, bf16[384,1024]{1,0:T(8,128)(2,1)S(1)}, u32[]{:S(2)}, u32[]{:S(2)}) collective-permute-start(bf16[384,1024]{1,0:T(8,128)(2,1)S(1)} %get-tuple-element.31), channel_id=1, source_target_pairs={{1,2},{3,4},{5,6},{7,8},{9,10},{11,12},{13,14},{15,16},{17,18},{19... | collective-permute-start | bytes 2359304 | tf_op jit(solution)/shard_map/ppermute | solution.py:393
  43.6 29.8 %copy-start.3 = (bf16[2048,100]{0,1:T(8,128)(2,1)S(1)}, bf16[2048,100]{0,1:T(8,128)(2,1)}, u32[]{:S(2)}) copy-start(bf16[2048,100]{0,1:T(8,128)(2,1)} %param.14) | copy-start | bytes 1228804
  43.6 29.8 %copy-start.9 = (s32[24,128]{1,0:T(8,128)S(1)}, s32[24,128]{1,0:T(8,128)}, u32[]{:S(2)}) copy-start(s32[24,128]{1,0:T(8,128)} %src.3) | copy-start | bytes 36868
  43.6 29.8 %copy-start.10 = (s32[24,128]{1,0:T(8,128)S(1)}, s32[24,128]{1,0:T(8,128)}, u32[]{:S(2)}) copy-start(s32[24,128]{1,0:T(8,128)} %dst.3) | copy-start | bytes 36868
  43.6 29.8 %copy-start.11 = (bf16[24,128]{1,0:T(8,128)(2,1)S(1)}, bf16[24,128]{1,0:T(8,128)(2,1)}, u32[]{:S(2)}) copy-start(bf16[24,128]{1,0:T(8,128)(2,1)} %weight.3) | copy-start | bytes 18436
  54.6 4.7 %collective-permute-start.8 = (bf16[512,128]{1,0:T(8,128)(2,1)S(1)}, bf16[512,128]{1,0:T(8,128)(2,1)S(1)}, u32[]{:S(2)}, u32[]{:S(2)}) collective-permute-start(bf16[512,128]{1,0:T(8,128)(2,1)S(1)} %attend.1), channel_id=1, source_target_pairs={{0,1},{1,0},{2,3},{3,2},{4,5},{5,4},{6,7},{7,6},{8,9},{9,8},{10,11... | collective-permute-start | bytes 393224 | tf_op jit(solution)/shard_map/ppermute | solution.py:379
  59.3 7.9 %collective-permute-start.9 = (bf16[2,512,128]{2,1,0:T(8,128)(2,1)S(1)}, bf16[2,512,128]{2,1,0:T(8,128)(2,1)S(1)}, u32[]{:S(2)}, u32[]{:S(2)}) collective-permute-start(bf16[2,512,128]{2,1,0:T(8,128)(2,1)S(1)} %pad_maximum_fusion.own), channel_id=1, source_target_pairs={{0,2},{2,4},{4,6},{6,8},{8,10},{10,12},{12,14},{14,16},{16,18},{18... | collective-permute-start | bytes 786440 | tf_op jit(solution)/shard_map/ppermute | solution.py:386
  67.2 6.1 %collective-permute-start.10 = (bf16[2,512,128]{2,1,0:T(8,128)(2,1)S(1)}, bf16[2,512,128]{2,1,0:T(8,128)(2,1)S(1)}, u32[]{:S(2)}, u32[]{:S(2)}) collective-permute-start(bf16[2,512,128]{2,1,0:T(8,128)(2,1)S(1)} %collective-permute-done.9.sent), channel_id=1, source_target_pairs={{0,1},{1,0},{2,3},{3,2},{4,5},{5,4},{6,7},{7,6},{8,9},{9,8},{10,11... | collective-permute-start | bytes 786440 | tf_op jit(solution)/shard_map/ppermute | solution.py:379

commit v4 on v3

--- a/solution.py
+++ b/solution.py
@@ -111,7 +111,7 @@
 
 def encode_body(
     info, src, grid_rows, swapped_rows, w_in, targets, weights, gain,
-    rows, mesh_zero, normed, to_peer, to_band,
+    rows, mesh_zero, normed, to_band,
     wide, first, second, total,
 ):
     core = info[0]
@@ -170,12 +170,10 @@
 
     @pl.when(core == 0)
     def _():
-        to_peer[...] = normed[ROWS - WIN :, :]
         to_band[...] = normed[:WIN, :]
 
     @pl.when(core != 0)
     def _():
-        to_peer[...] = normed[:WIN, :]
         to_band[...] = normed[ROWS - WIN :, :]
 
 
@@ -236,19 +234,33 @@
 
 
 def project_body(
-    normed, halo, w_own, w_peer, mask,
-    queries, halo_keys, halo_values, sums, stats,
-    keys, values_t, first, second,
+    info, normed, w_own, w_peer, queries, keys, values_t, keys_sent, values_sent
 ):
     rows = normed[...]
-    beside = halo[...]
     for half, weight in enumerate((w_own, w_peer)):
         place = slice(half * HALF, (half + 1) * HALF)
-        queries[:, place] = (matmul(rows, weight[0]) * SCALE).astype(BF16)
         keys[:, place] = matmul(rows, weight[1]).astype(BF16)
         values_t[place, :] = matmul(rows, weight[2]).T.astype(BF16)
-        halo_keys[:, place] = matmul(beside, weight[1]).astype(BF16)
-        halo_values[place, :] = matmul(beside, weight[2]).T.astype(BF16)
+        queries[:, place] = (matmul(rows, weight[0]) * SCALE).astype(BF16)
+
+    @pl.when(info[0] == 0)
+    def _():
+        for half in range(2):
+            place = slice(half * HALF, (half + 1) * HALF)
+            other = slice((1 - half) * HALF, (2 - half) * HALF)
+            keys_sent[:, other] = keys[ROWS - WIN :, place]
+            values_sent[other, :] = values_t[place, ROWS - WIN :]
+
+    @pl.when(info[0] != 0)
+    def _():
+        for half in range(2):
+            place = slice(half * HALF, (half + 1) * HALF)
+            other = slice((1 - half) * HALF, (2 - half) * HALF)
+            keys_sent[:, other] = keys[:WIN, place]
+            values_sent[other, :] = values_t[place, :WIN]
+
+
+def own_body(queries, keys, values_t, mask, sums, stats, first, second):
     eyes, lane = identity_pair()
 
     def score(pair, block, scores):
@@ -338,41 +350,49 @@
     projected[...] = matmul_t(mesh_one, dec_wide[...].astype(BF16)).astype(BF16)
 
 
-def decode_body(
-    info, src, own, sent, swapped_rows, dst, weight, grid, out, rows, messages, weights
-):
+def put_half(rows, place, part):
+    rows[pl.ds(pl.multiple_of(place * ROWS, ROWS), ROWS), :] = part.astype(F32)
+
+
+def tables_body(info, own, src, dst, weight, rows, sources, tables, weights):
     core, mesh_base, row_base = info[0], info[6], info[7]
-    other = 1 - core
-
-    def put(place, part):
-        rows[pl.ds(pl.multiple_of(place * ROWS, ROWS), ROWS), :] = part.astype(F32)
-
-    put(2 + core, own[0])
-    put(2 + other, own[1])
-    put(4 * core + core, sent[0])
-    put(4 * core + other, sent[1])
-    put(4 * other + other, swapped_rows[0])
-    put(4 * other + core, swapped_rows[1])
+    put_half(rows, 2 + core, own[0])
+    put_half(rows, 3 - core, own[1])
+    sources[...] = src[...] - mesh_base
     weights[...] = weight[...].astype(F32)
     row_slots = lax.broadcasted_iota(jnp.int32, (TILE, LANES), 0)
-
-    def tile_sum(tile, carry):
-        tables = []
+    for tile in range(DEC_TILES):
         for part in range(DEC_ROUNDS):
-            slot = part * DEC_TILES + tile
+            slot = slice(part * DEC_TILES + tile, part * DEC_TILES + tile + 1)
+            target = dst[slot, :] - (row_base + tile * TILE)
+            tables[rows_of(tile), rows_of(part)] = jnp.where(
+                row_slots == target, weights[slot, :], 0.0
+            ).astype(BF16)
+
+
+def decode_body(info, src, rows_in, sent, swapped_rows, tables, grid, rows, out, messages):
+    core = info[0]
+    other = 1 - core
+    put_half(rows, 4 * core + core, sent[0])
+    put_half(rows, 4 * core + other, sent[1])
+    put_half(rows, 4 * other + other, swapped_rows[0])
+    put_half(rows, 4 * other + core, swapped_rows[1])
+
+    def gather(tile, carry):
+        begin = pl.multiple_of(tile * DEC_ROUNDS * TILE, TILE)
+        for part in range(DEC_ROUNDS):
             for edge in range(TILE):
-                index = src[slot, edge] - mesh_base
-                messages[pl.ds(part * TILE + edge, 1), :] = rows[pl.ds(index, 1), :]
-            target = dst[pl.ds(slot, 1), :] - (row_base + tile * TILE)
-            tables.append(jnp.where(row_slots == target, weights[pl.ds(slot, 1), :], 0.0))
-        table = jnp.concatenate(tables, axis=1).astype(BF16)
-        summed = matmul(table, messages[...].astype(BF16)).T
-        place = pl.ds(pl.multiple_of(tile * TILE, TILE), TILE)
+                index = src[part * DEC_TILES + tile, edge]
+                messages[pl.ds(begin + part * TILE + edge, 1), :] = rows[pl.ds(index, 1), :]
+        return carry
+
+    lax.fori_loop(0, DEC_TILES, gather, 0)
+    span = DEC_ROUNDS * TILE
+    for tile in range(DEC_TILES):
+        message = messages[tile * span : (tile + 1) * span, :].astype(BF16)
+        summed = matmul(tables[rows_of(tile), :], message).T
         fields = grid[:, pl.ds(pl.multiple_of(core * GQ + tile * TILE, TILE), TILE)]
-        out[:, place] = (fields.astype(F32) + summed[:C, :]).astype(BF16)
-        return carry
-
-    lax.fori_loop(0, DEC_TILES, tile_sum, 0)
+        out[:, rows_of(tile)] = (fields.astype(F32) + summed[:C, :]).astype(BF16)
 
 
 def swapped(value):
@@ -447,13 +467,13 @@
         [pltpu.VMEM((LANES, G_BAND), F32)],
         2 * 10 ** 9, 2 * 10 ** 6, "unpack",
     )
-    _, mesh_zero, normed, to_peer, to_band = call(
+    _, mesh_zero, normed, to_band = call(
         encode_body,
         (info, sources, grid_rows, grid_swapped, w_in_all, targets, weights, gain),
         2,
         [jax.ShapeDtypeStruct((3 * G_BAND, LANES), F32)]
         + [jax.ShapeDtypeStruct((ROWS, D), BF16)] * 2
-        + [jax.ShapeDtypeStruct((WIN, D), BF16)] * 2,
+        + [jax.ShapeDtypeStruct((WIN, D), BF16)],
         [
             pltpu.VMEM((LANES, G_BAND), F32),
             pltpu.VMEM((STEP, LANES), F32),
@@ -462,26 +482,32 @@
         ],
         8 * 10 ** 9, 4 * 10 ** 6, "encode", {2: 0},
     )
-    halo_peer = swapped(to_peer)
     halo_band = over_the_edge(to_band)
-    queries, peer_keys, peer_values, sums, stats = call(
+    queries, keys, values_t, keys_sent, values_sent = call(
         project_body,
-        (normed, halo_peer, qkv_own, qkv_peer, mask),
-        0,
+        (info, normed, qkv_own, qkv_peer),
+        1,
         [
             jax.ShapeDtypeStruct((ROWS, D), BF16),
+            jax.ShapeDtypeStruct((ROWS, D), BF16),
+            jax.ShapeDtypeStruct((D, ROWS), BF16),
             jax.ShapeDtypeStruct((WIN, D), BF16),
             jax.ShapeDtypeStruct((D, WIN), BF16),
+        ],
+        [],
+        6 * 10 ** 9, 10 ** 7, "project",
+    )
+    peer_keys, peer_values = swapped(keys_sent), swapped(values_sent)
+    sums, stats = call(
+        own_body,
+        (queries, keys, values_t, mask),
+        0,
+        [
             jax.ShapeDtypeStruct((D, ROWS), F32),
             jax.ShapeDtypeStruct((D // LANES, 8, 2 * ROWS), F32),
         ],
-        [
-            pltpu.VMEM((ROWS, D), BF16),
-            pltpu.VMEM((D, ROWS), BF16),
-            pltpu.VMEM((ROWS, 2 * TILE), F32),
-            pltpu.VMEM((ROWS, 2 * TILE), F32),
-        ],
-        10 ** 10, 10 ** 7, "project",
+        [pltpu.VMEM((ROWS, 2 * TILE), F32), pltpu.VMEM((ROWS, 2 * TILE), F32)],
+        8 * 10 ** 9, 10 ** 7, "own",
     )
     projected = call(
         attend_body,
@@ -502,19 +528,32 @@
     )
     own_pair = jnp.stack([projected, swapped(projected)])
     pair_sent = up_and_down(own_pair)
+    mesh_rows, dec_sources, dec_tables = call(
+        tables_body,
+        (info, own_pair, dec_src, dec_dst, dec_weight),
+        1,
+        [
+            jax.ShapeDtypeStruct((6 * ROWS, LANES), F32),
+            jax.ShapeDtypeStruct(dec_src.shape, jnp.int32),
+            jax.ShapeDtypeStruct((GQ, DEC_ROUNDS * TILE), BF16),
+        ],
+        [pltpu.VMEM(dec_weight.shape, F32)],
+        3 * 10 ** 9, 2 * 10 ** 6, "tables",
+    )
+    pair_sent, mesh_rows = lax.optimization_barrier((pair_sent, mesh_rows))
     pair_swapped = swapped(pair_sent)
-    return call(
+    _, out = call(
         decode_body,
-        (info, dec_src, own_pair, pair_sent, pair_swapped, dec_dst, dec_weight, grid),
+        (info, dec_sources, mesh_rows, pair_sent, pair_swapped, dec_tables, grid),
         2,
-        jax.ShapeDtypeStruct((C, GQ), BF16),
-        [
-            pltpu.VMEM((6 * ROWS, LANES), F32),
-            pltpu.VMEM((DEC_ROUNDS * TILE, LANES), F32),
-            pltpu.VMEM(dec_weight.shape, F32),
-        ],
-        10 ** 9, 3 * 10 ** 6, "decode",
-    ).T
+        [
+            jax.ShapeDtypeStruct((6 * ROWS, LANES), F32),
+            jax.ShapeDtypeStruct((C, GQ), BF16),
+        ],
+        [pltpu.VMEM((DEC_TILES * DEC_ROUNDS * TILE, LANES), F32)],
+        10 ** 9, 3 * 10 ** 6, "decode", {2: 0},
+    )
+    return out.T
 
 
 def solution(mesh):

time: 80.6 us -> 77.2 us (0.958)
  Pallas kernels: 44 us -> 41.6 us
  waiting for transfers between devices: 6.18 us -> 5.16 us
    pallas_call x6 -> x8, Pallas kernels: 44 us -> 41.6 us  [call(): pl.pallas_call(body, out_shape=outs, in_specs=specs, out_specs=jax.tree.m...]
    ppermute x8 -> x9, waiting for transfers between devices: 2.88 us -> 2.64 us  [swapped(): return lax.ppermute(value, 'mp', [(0, 1), (1, 0)])]
    ppermute x8 -> x9, starting transfers between devices: 10.2 us -> 10.3 us  [swapped(): return lax.ppermute(value, 'mp', [(0, 1), (1, 0)])]
  transfers between devices with their start and end apart: 11 -> 12, of which waited for: 4 -> 4; matrix products, arithmetic and copies ran while one was open for 0% -> 0% of each run, Pallas kernels for 33% -> 34%
where the time goes in v4:
time: 77.2 us; the launch traced here: 76.7 us
  Pallas kernels  41.6 us (54%)
  starting transfers between devices  23.4 us (30%)
  local copies, waits for them, and re-layouts  5.6 us (7%)
  waiting for transfers between devices  5.16 us (7%)
  between operations  0.9 us (1%)
    pallas_call x8, Pallas kernels, call(): pl.pallas_call(body, out_shape=outs, in_specs=specs, out_specs=jax.tree.m...  41.6 us
    ppermute x2, starting transfers between devices, up_and_down(): return lax.ppermute(value, ('band', 'mp'), pairs)  11.2 us
    ppermute x9, starting transfers between devices, swapped(): return lax.ppermute(value, 'mp', [(0, 1), (1, 0)])  10.3 us
    unnamed x28, local copies, waits for them, and re-layouts  5.51 us
    ppermute x9, waiting for transfers between devices, swapped(): return lax.ppermute(value, 'mp', [(0, 1), (1, 0)])  2.64 us
    ppermute x2, waiting for transfers between devices, up_and_down(): return lax.ppermute(value, ('band', 'mp'), pairs)  2.51 us
    ppermute x1, starting transfers between devices, over_the_edge(): return lax.ppermute(value, ('band', 'mp'), pairs)  1.92 us
  transfers between devices with their start and end apart: 12, of which 4 were waited for; matrix products, arithmetic and copies ran while one was open for 0% of the time, Pallas kernels for 34%

profile of v4, /device:TPU:97, one launch (start us, length us, event | category | flops | bytes accessed | tf_op | source)
XLA Modules:
  0.0 76.7 jit_solution(2482402132495022376)
XLA Ops:
  0.0 0.7 collective-permute-start.4
  0.7 0.0 collective-permute-start
  0.7 6.7 %collective-permute-start.1 = (bf16[100,2048]{1,0:T(8,128)(2,1)}, bf16[100,2048]{1,0:T(8,128)(2,1)}, u32[]{:S(2)}, u32[]{:S(2)}) collective-permute-start(bf16[100,2048]{1,0:T(8,128)(2,1)} %bitcast.18), channel_id=1, source_target_pairs={{0,2},{2,4},{4,6},{6,8},{8,10},{10,12},{12,14},{14,16},{16,18},{18... | collective-permute-start | bytes 1228808 | tf_op jit(solution)/shard_map/ppermute | solution.py:406
  8.0 0.1 stack.48.info
  8.1 0.0 collective-permute-done.win_peer
  8.1 0.0 copy-start.2
  8.1 1.0 %copy-done.2 = bf16[2048,100]{0,1:T(8,128)(2,1)S(1)} copy-done((bf16[2048,100]{0,1:T(8,128)(2,1)S(1)}, bf16[2048,100]{0,1:T(8,128)(2,1)}, u32[]{:S(2)}) %copy-start.2) | copy-done | bytes 409624
  9.1 0.9 %copy-done.4 = bf16[100,512]{1,0:T(8,128)(2,1)S(1)} copy-done((bf16[100,512]{1,0:T(8,128)(2,1)S(1)}, bf16[100,512]{1,0:T(8,128)(2,1)}, u32[]{:S(2)}) %copy-start.4) | copy-done | bytes 102424
  10.0 0.8 copy-done.6
  10.8 0.8 copy-done.7
  11.5 0.7 copy-done.8
  12.2 0.7 copy-done.12
  12.9 0.7 copy-done.13
  13.6 2.7 %prepare.1 = (f32[2048,128]{1,0:T(8,128)S(1)}, bf16[896,128]{1,0:T(8,128)(2,1)S(1)}, s32[64,128]{1,0:T(8,128)S(1)}, s32[64,128]{1,0:T(8,128)S(1)}, f32[64,128]{1...) custom-call(s32[8]{0:T(128)S(1)} %stack.48.info, s32[32]{0:T(128)S(1)} %copy-done.13, ...), custom_call_target="tpu_custom_call" | custom-call | flops 8000000000 | bytes 2000000 | tf_op jit(solution)/shard_map/prepare/pallas_call | solution.py:42
  16.3 0.0 collective-permute-done.1.sent
  16.3 0.1 collective-permute-start.2
  16.4 0.5 collective-permute-start.7
  16.9 1.2 %unpack.1.grid_rows = f32[6144,128]{1,0:T(8,128)S(1)} custom-call(s32[8]{0:T(128)S(1)} %stack.48.info, f32[2048,128]{1,0:T(8,128)S(1)} %get-tuple-element.32.own_rows, bf16[100,2048]{1,0:T(8,128)(2,1)} %collective-permute-done.1.sent), custom_call_target="tpu_custom_call" | custom-call | flops 2000000000 | bytes 2000000 | tf_op jit(solution)/shard_map/unpack/pallas_call | solution.py:42
  18.1 0.2 collective-permute-done.2.swapped_rows
  18.3 9.3 %encode.1 = (f32[6144,128]{1,0:T(8,128)S(1)}, bf16[512,1024]{1,0:T(8,128)(2,1)S(1)}, bf16[512,1024]{1,0:T(8,128)(2,1)S(1)}, bf16[384,1024]{1,0:T(8,128)(2,1)S(1)}) custom-call(s32[8]{0:T(128)S(1)} %stack.48.info, s32[64,128]{1,0:T(8,128)S(1)} %get-tuple-element.30.src, f32[6144,128]{1,0:T(8,128)S(1)} %unpack.1.grid_rows, ...), custom_call_target="tpu_custom_call", output_to_operand_aliasing={{0}: (2, {})} | custom-call | flops 8000000000 | bytes 4000000 | tf_op jit(solution)/shard_map/encode/pallas_call | solution.py:42
  27.7 1.9 %collective-permute-start.3 = (bf16[384,1024]{1,0:T(8,128)(2,1)S(1)}, bf16[384,1024]{1,0:T(8,128)(2,1)S(1)}, u32[]{:S(2)}, u32[]{:S(2)}) collective-permute-start(bf16[384,1024]{1,0:T(8,128)(2,1)S(1)} %get-tuple-element.38), channel_id=1, source_target_pairs={{1,2},{3,4},{5,6},{7,8},{9,10},{11,12},{13,14},{15,16},{17,18},{19... | collective-permute-start | bytes 2359304 | tf_op jit(solution)/shard_map/ppermute | solution.py:413
  29.6 0.0 collective-permute-done.4.w_peer
  29.6 0.0 copy-start.5
  29.6 4.1 %project.1 = (bf16[512,1024]{1,0:T(8,128)(2,1)S(1)}, bf16[512,1024]{1,0:T(8,128)(2,1)S(1)}, bf16[1024,512]{1,0:T(8,128)(2,1)S(1)}, bf16[384,1024]{1,0:T(8,128)(2,1)S(1)}, bf16[1024,384]{1,0:T(8,128)(2,1)S(1)}) custom-call(s32[8]{0:T(128)S(1)} %stack.48.info, bf16[512,1024]{1,0:T(8,128)(2,1)S(1)} %get-tuple-element.39.normed, ...), custom_call_target="tpu_custom_call" | custom-call | flops 6000000000 | bytes 10000000 | tf_op jit(solution)/shard_map/project/pallas_call | solution.py:42
  33.8 3.4 %collective-permute-start.5 = (bf16[384,1024]{1,0:T(8,128)(2,1)S(1)}, bf16[384,1024]{1,0:T(8,128)(2,1)S(1)}, u32[]{:S(2)}, u32[]{:S(2)}) collective-permute-start(bf16[384,1024]{1,0:T(8,128)(2,1)S(1)} %get-tuple-element.40), channel_id=1, source_target_pairs={{0,1},{1,0},{2,3},{3,2},{4,5},{5,4},{6,7},{7,6},{8,9},{9,8},{10,11... | collective-permute-start | bytes 2359304 | tf_op jit(solution)/shard_map/ppermute | solution.py:399
  37.2 0.1 collective-permute-start.6
  37.3 0.4 collective-permute-start.8
  37.7 7.9 %own.1 = (f32[1024,512]{1,0:T(8,128)S(1)}, f32[8,8,1024]{2,1,0:T(8,128)S(1)}) custom-call(bf16[512,1024]{1,0:T(8,128)(2,1)S(1)} %get-tuple-element.42.queries, bf16[512,1024]{1,0:T(8,128)(2,1)S(1)} %get-tuple-element.43.keys, bf16[1024,512]{1,0:T(8,128)(2,1)S(1)} %get-tuple-element.44.values_t, bf16[896,128]{1,0:T(8,128)(2,1)S(1)} %get-tuple-element.45.mask), custom_call_target="tpu_custom_call" | custom-call | flops 8000000000 | bytes 10000000 | tf_op jit(solution)/shard_map/own/pallas_call | solution.py:42
  45.6 0.0 collective-permute-done.8.dec_peer
  45.6 0.0 collective-permute-done.7.out_peer
  45.6 0.0 collective-permute-done.3.halo
  45.7 0.0 collective-permute-done.5.peer_keys
  45.7 0.0 collective-permute-done.6.peer_values
  45.7 0.0 copy-start.9
  45.7 0.0 copy-start.10
  45.7 0.0 copy-start.11
  45.7 11.2 %attend.1 = bf16[512,128]{1,0:T(8,128)(2,1)S(1)} custom-call(s32[8]{0:T(128)S(1)} %stack.48.info, bf16[384,1024]{1,0:T(8,128)(2,1)S(1)} %collective-permute-done.3.halo, bf16[384,1024]{1,0:T(8,128)(2,1)S(1)} %collective-permute-done.5.peer_keys, bf16[1024,384]{1,0:T(8,128)(2,1)S(1)} %collective-permute-done.6.peer_values, ...), custom_call_target="tpu_custom_call" | custom-call | flops 10000000000 | bytes 20000000 | tf_op jit(solution)/shard_map/attend/pallas_call | solution.py:42
  56.9 0.2 collective-permute-start.9
  57.1 1.2 %collective-permute-done.9 = bf16[512,128]{1,0:T(8,128)(2,1)S(1)} collective-permute-done((bf16[512,128]{1,0:T(8,128)(2,1)S(1)}, bf16[512,128]{1,0:T(8,128)(2,1)S(1)}, u32[]{:S(2)}, u32[]{:S(2)}) %collective-permute-start.9) | collective-permute-done | bytes 131104 | tf_op jit(solution)/shard_map/ppermute | solution.py:399
  58.4 0.0 copy-start.3
  58.4 4.6 %collective-permute-start.10 = (bf16[2,512,128]{2,1,0:T(8,128)(2,1)S(1)}, bf16[2,512,128]{2,1,0:T(8,128)(2,1)S(1)}, u32[]{:S(2)}, u32[]{:S(2)}) collective-permute-start(bf16[2,512,128]{2,1,0:T(8,128)(2,1)S(1)} %pad_maximum_fusion.own), channel_id=1, source_target_pairs={{0,2},{2,4},{4,6},{6,8},{8,10},{10,12},{12,14},{14,16},{16,18},{18... | collective-permute-start | bytes 786440 | tf_op jit(solution)/shard_map/ppermute | solution.py:406
  63.0 0.0 copy-done.9
  63.0 0.0 copy-done.10
  63.0 0.8 tables.1
  63.8 2.5 %collective-permute-done.10.sent = bf16[2,512,128]{2,1,0:T(8,128)(2,1)S(1)} collective-permute-done((bf16[2,512,128]{2,1,0:T(8,128)(2,1)S(1)}, bf16[2,512,128]{2,1,0:T(8,128)(2,1)S(1)}, u32[]{:S(2)}, u32[]{:S(2)}) %collective-permute-start.10) | collective-permute-done | bytes 262176 | tf_op jit(solution)/shard_map/ppermute | solution.py:406
  66.3 4.9 %collective-permute-start.11 = (bf16[2,512,128]{2,1,0:T(8,128)(2,1)S(1)}, bf16[2,512,128]{2,1,0:T(8,128)(2,1)S(1)}, u32[]{:S(2)}, u32[]{:S(2)}) collective-permute-start(bf16[2,512,128]{2,1,0:T(8,128)(2,1)S(1)} %collective-permute-done.10.sent), channel_id=1, source_target_pairs={{0,1},{1,0},{2,3},{3,2},{4,5},{5,4},{6,7},{7,6},{8,9},{9,8},{10,11... | collective-permute-start | bytes 786440 | tf_op jit(solution)/shard_map/ppermute | solution.py:399
  71.2 1.2 %collective-permute-done.11.swapped_rows = bf16[2,512,128]{2,1,0:T(8,128)(2,1)S(1)} collective-permute-done((bf16[2,512,128]{2,1,0:T(8,128)(2,1)S(1)}, bf16[2,512,128]{2,1,0:T(8,128)(2,1)S(1)}, u32[]{:S(2)}, u32[]{:S(2)}) %collective-permute-start.11) | collective-permute-done | bytes 262176 | tf_op jit(solution)/shard_map/ppermute | solution.py:399
  72.3 4.4 %decode.1 = (f32[3072,128]{1,0:T(8,128)S(1)}, bf16[100,1024]{1,0:T(8,128)(2,1)}) custom-call(s32[8]{0:T(128)S(1)} %stack.48.info, s32[24,128]{1,0:T(8,128)S(1)} %get-tuple-element.49.src, f32[3072,128]{1,0:T(8,128)S(1)} %get-tuple-element.51.rows_in, bf16[2,512,128]{2,1,0:T(8,128)(2,1)S(1)} %collective-permute-done.10.sent, ...), custom_call_target="tpu_custom_call", output_to_operand_aliasing={{0}: (2, {})} | custom-call | flops 1000000000 | bytes 3000000 | tf_op jit(solution)/shard_map/decode/pallas_call | solution.py:42
  (14 shorter events, 0.0 us)
Async XLA Ops:
  0.0 29.6 %collective-permute-start.4 = (bf16[3,1024,512]{2,1,0:T(8,128)(2,1)}, bf16[3,1024,512]{2,1,0:T(8,128)(2,1)S(1)}, u32[]{:S(2)}, u32[]{:S(2)}) collective-permute-start(bf16[3,1024,512]{2,1,0:T(8,128)(2,1)} %bitcast.15), channel_id=1, source_target_pairs={{0,1},{1,0},{2,3},{3,2},{4,5},{5,4},{6,7},{7,6},{8,9},{9,8},{10,11... | collective-permute-start | bytes 9437192 | tf_op jit(solution)/shard_map/ppermute | solution.py:399
  0.7 7.4 %collective-permute-start = (bf16[100,512]{1,0:T(8,128)(2,1)}, bf16[100,512]{1,0:T(8,128)(2,1)S(1)}, u32[]{:S(2)}, u32[]{:S(2)}) collective-permute-start(bf16[100,512]{1,0:T(8,128)(2,1)} %win_own.1), channel_id=1, source_target_pairs={{0,1},{1,0},{2,3},{3,2},{4,5},{5,4},{6,7},{7,6},{8,9},{9,8},{10,11... | collective-permute-start | bytes 307208 | tf_op jit(solution)/shard_map/ppermute | solution.py:399
  0.7 15.6 %collective-permute-start.1 = (bf16[100,2048]{1,0:T(8,128)(2,1)}, bf16[100,2048]{1,0:T(8,128)(2,1)}, u32[]{:S(2)}, u32[]{:S(2)}) collective-permute-start(bf16[100,2048]{1,0:T(8,128)(2,1)} %bitcast.18), channel_id=1, source_target_pairs={{0,2},{2,4},{4,6},{6,8},{8,10},{10,12},{12,14},{14,16},{16,18},{18... | collective-permute-start | bytes 1228808 | tf_op jit(solution)/shard_map/ppermute | solution.py:406
  8.1 1.0 %copy-start.2 = (bf16[2048,100]{0,1:T(8,128)(2,1)S(1)}, bf16[2048,100]{0,1:T(8,128)(2,1)}, u32[]{:S(2)}) copy-start(bf16[2048,100]{0,1:T(8,128)(2,1)} %param.14) | copy-start | bytes 1228804
  9.1 0.9 %copy-start.4 = (bf16[100,512]{1,0:T(8,128)(2,1)S(1)}, bf16[100,512]{1,0:T(8,128)(2,1)}, u32[]{:S(2)}) copy-start(bf16[100,512]{1,0:T(8,128)(2,1)} %win_own.1) | copy-start | bytes 307204
  10.0 0.8 copy-start.6
  10.8 0.8 copy-start.7
  11.5 0.7 copy-start.8
  12.2 0.7 copy-start.12
  12.9 0.7 copy-start.13
  13.6 2.8 %copy-start.1 = (bf16[512,1024]{1,0:T(8,128)(2,1)S(1)}, bf16[512,1024]{1,0:T(8,128)(2,1)}, u32[]{:S(2)}) copy-start(bf16[512,1024]{1,0:T(8,128)(2,1)} %out_own.1) | copy-start | bytes 3145732
  16.3 2.1 %collective-permute-start.2 = (bf16[100,2048]{1,0:T(8,128)(2,1)}, bf16[100,2048]{1,0:T(8,128)(2,1)S(1)}, u32[]{:S(2)}, u32[]{:S(2)}) collective-permute-start(bf16[100,2048]{1,0:T(8,128)(2,1)} %collective-permute-done.1.sent), channel_id=1, source_target_pairs={{0,1},{1,0},{2,3},{3,2},{4,5},{5,4},{6,7},{7,6},{8,9},{9,8},{10,11... | collective-permute-start | bytes 1228808 | tf_op jit(solution)/shard_map/ppermute | solution.py:399
  16.4 29.3 %collective-permute-start.7 = (bf16[512,1024]{1,0:T(8,128)(2,1)S(1)}, bf16[512,1024]{1,0:T(8,128)(2,1)S(1)}, u32[]{:S(2)}, u32[]{:S(2)}) collective-permute-start(bf16[512,1024]{1,0:T(8,128)(2,1)S(1)} %copy-done.1), channel_id=1, source_target_pairs={{0,1},{1,0},{2,3},{3,2},{4,5},{5,4},{6,7},{7,6},{8,9},{9,8},{10,11... | collective-permute-start | bytes 3145736 | tf_op jit(solution)/shard_map/ppermute | solution.py:399
  18.3 11.3 %copy-start = (bf16[1024,3,512]{2,0,1:T(8,128)(2,1)S(1)}, bf16[1024,3,512]{2,0,1:T(8,128)(2,1)}, u32[]{:S(2)}) copy-start(bf16[1024,3,512]{2,0,1:T(8,128)(2,1)} %param.21) | copy-start | bytes 9437188
  27.7 18.0 %collective-permute-start.3 = (bf16[384,1024]{1,0:T(8,128)(2,1)S(1)}, bf16[384,1024]{1,0:T(8,128)(2,1)S(1)}, u32[]{:S(2)}, u32[]{:S(2)}) collective-permute-start(bf16[384,1024]{1,0:T(8,128)(2,1)S(1)} %get-tuple-element.38), channel_id=1, source_target_pairs={{1,2},{3,4},{5,6},{7,8},{9,10},{11,12},{13,14},{15,16},{17,18},{19... | collective-permute-start | bytes 2359304 | tf_op jit(solution)/shard_map/ppermute | solution.py:413
  29.6 7.7 %copy-start.5 = (bf16[512,100]{0,1:T(8,128)(2,1)S(1)}, bf16[512,100]{0,1:T(8,128)(2,1)}, u32[]{:S(2)}) copy-start(bf16[512,100]{0,1:T(8,128)(2,1)} %param.24) | copy-start | bytes 307204
  33.8 11.9 %collective-permute-start.5 = (bf16[384,1024]{1,0:T(8,128)(2,1)S(1)}, bf16[384,1024]{1,0:T(8,128)(2,1)S(1)}, u32[]{:S(2)}, u32[]{:S(2)}) collective-permute-start(bf16[384,1024]{1,0:T(8,128)(2,1)S(1)} %get-tuple-element.40), channel_id=1, source_target_pairs={{0,1},{1,0},{2,3},{3,2},{4,5},{5,4},{6,7},{7,6},{8,9},{9,8},{10,11... | collective-permute-start | bytes 2359304 | tf_op jit(solution)/shard_map/ppermute | solution.py:399
  37.2 8.5 %collective-permute-start.6 = (bf16[1024,384]{1,0:T(8,128)(2,1)S(1)}, bf16[1024,384]{1,0:T(8,128)(2,1)S(1)}, u32[]{:S(2)}, u32[]{:S(2)}) collective-permute-start(bf16[1024,384]{1,0:T(8,128)(2,1)S(1)} %get-tuple-element.41), channel_id=1, source_target_pairs={{0,1},{1,0},{2,3},{3,2},{4,5},{5,4},{6,7},{7,6},{8,9},{9,8},{10,11... | collective-permute-start | bytes 2359304 | tf_op jit(solution)/shard_map/ppermute | solution.py:399
  37.3 8.4 %collective-permute-start.8 = (bf16[100,512]{1,0:T(8,128)(2,1)S(1)}, bf16[100,512]{1,0:T(8,128)(2,1)S(1)}, u32[]{:S(2)}, u32[]{:S(2)}) collective-permute-start(bf16[100,512]{1,0:T(8,128)(2,1)S(1)} %bitcast.21), channel_id=1, source_target_pairs={{0,1},{1,0},{2,3},{3,2},{4,5},{5,4},{6,7},{7,6},{8,9},{9,8},{10,11... | collective-permute-start | bytes 307208 | tf_op jit(solution)/shard_map/ppermute | solution.py:399
  45.7 17.3 %copy-start.9 = (s32[24,128]{1,0:T(8,128)S(1)}, s32[24,128]{1,0:T(8,128)}, u32[]{:S(2)}) copy-start(s32[24,128]{1,0:T(8,128)} %src.3) | copy-start | bytes 36868
  45.7 17.3 %copy-start.10 = (s32[24,128]{1,0:T(8,128)S(1)}, s32[24,128]{1,0:T(8,128)}, u32[]{:S(2)}) copy-start(s32[24,128]{1,0:T(8,128)} %dst.3) | copy-start | bytes 36868
  45.7 17.3 %copy-start.11 = (bf16[24,128]{1,0:T(8,128)(2,1)S(1)}, bf16[24,128]{1,0:T(8,128)(2,1)}, u32[]{:S(2)}) copy-start(bf16[24,128]{1,0:T(8,128)(2,1)} %weight.3) | copy-start | bytes 18436
  56.9 1.4 %collective-permute-start.9 = (bf16[512,128]{1,0:T(8,128)(2,1)S(1)}, bf16[512,128]{1,0:T(8,128)(2,1)S(1)}, u32[]{:S(2)}, u32[]{:S(2)}) collective-permute-start(bf16[512,128]{1,0:T(8,128)(2,1)S(1)} %attend.1), channel_id=1, source_target_pairs={{0,1},{1,0},{2,3},{3,2},{4,5},{5,4},{6,7},{7,6},{8,9},{9,8},{10,11... | collective-permute-start | bytes 393224 | tf_op jit(solution)/shard_map/ppermute | solution.py:399
  58.4 13.9 %copy-start.3 = (bf16[2048,100]{0,1:T(8,128)(2,1)S(1)}, bf16[2048,100]{0,1:T(8,128)(2,1)}, u32[]{:S(2)}) copy-start(bf16[2048,100]{0,1:T(8,128)(2,1)} %param.14) | copy-start | bytes 1228804
  58.4 7.9 %collective-permute-start.10 = (bf16[2,512,128]{2,1,0:T(8,128)(2,1)S(1)}, bf16[2,512,128]{2,1,0:T(8,128)(2,1)S(1)}, u32[]{:S(2)}, u32[]{:S(2)}) collective-permute-start(bf16[2,512,128]{2,1,0:T(8,128)(2,1)S(1)} %pad_maximum_fusion.own), channel_id=1, source_target_pairs={{0,2},{2,4},{4,6},{6,8},{8,10},{10,12},{12,14},{14,16},{16,18},{18... | collective-permute-start | bytes 786440 | tf_op jit(solution)/shard_map/ppermute | solution.py:406
  66.3 6.1 %collective-permute-start.11 = (bf16[2,512,128]{2,1,0:T(8,128)(2,1)S(1)}, bf16[2,512,128]{2,1,0:T(8,128)(2,1)S(1)}, u32[]{:S(2)}, u32[]{:S(2)}) collective-permute-start(bf16[2,512,128]{2,1,0:T(8,128)(2,1)S(1)} %collective-permute-done.10.sent), channel_id=1, source_target_pairs={{0,1},{1,0},{2,3},{3,2},{4,5},{5,4},{6,7},{7,6},{8,9},{9,8},{10,11... | collective-permute-start | bytes 786440 | tf_op jit(solution)/shard_map/ppermute | solution.py:399

commit v5 on v4

--- a/solution.py
+++ b/solution.py
@@ -22,6 +22,7 @@
 GQ = 1024
 DEC_ROUNDS = 3
 DEC_TILES = 8
+GROUP = 2
 MASKED = -1e30
 SCALE = 64 ** (-0.5) * math.log2(math.e)
 F32 = jnp.float32
@@ -210,7 +211,7 @@
 
 
 def weigh(scores, top, values):
-    expos = jnp.exp2((scores[...] - top).astype(BF16))
+    expos = jnp.exp2(scores[...] - top).astype(BF16)
     ones = jnp.ones((16, scores.shape[0]), BF16)
     result = matmul(jnp.concatenate([values, ones], axis=0), expos)
     both = jnp.concatenate([result[:64, :TILE], result[64:TILE, TILE:]], axis=0)
@@ -219,18 +220,28 @@
 
 def pipeline(score, finish, first, second):
     buffers = (first, second)
-    score(0, 0, first)
-
-    def head_pair(pair, carry):
+    groups = D // LANES // GROUP
+
+    def part_of(buffer, member):
+        return buffer.at[:, member * 2 * TILE : (member + 1) * 2 * TILE]
+
+    for member in range(GROUP):
+        score(member, 0, part_of(first, member))
+
+    def head_group(group, carry):
         for block in range(TILES):
-            if block + 1 < TILES:
-                score(pair, block + 1, buffers[(block + 1) % 2])
-            else:
-                score(jnp.minimum(pair + 1, D // LANES - 1), 0, first)
-            finish(pair, block, buffers[block % 2])
+            here, ahead = buffers[block % 2], buffers[(block + 1) % 2]
+            for member in range(GROUP):
+                if block + 1 < TILES:
+                    pair = group * GROUP + member
+                else:
+                    pair = jnp.minimum(group + 1, groups - 1) * GROUP + member
+                score(pair, (block + 1) % TILES, part_of(ahead, member))
+            for member in range(GROUP):
+                finish(group * GROUP + member, block, part_of(here, member))
         return carry
 
-    lax.fori_loop(0, D // LANES, head_pair, 0)
+    lax.fori_loop(0, groups, head_group, 0)
 
 
 def project_body(
@@ -347,17 +358,16 @@
     term_own = matmul(attended[:HALF, :].T, out_own[...]).astype(BF16).astype(F32)
     term_peer = matmul(attended[HALF:, :].T, out_peer[...]).astype(BF16).astype(F32)
     mesh_one = (mesh_zero[...].astype(F32) + (term_own + term_peer)).astype(BF16)
-    projected[...] = matmul_t(mesh_one, dec_wide[...].astype(BF16)).astype(BF16)
-
-
-def put_half(rows, place, part):
-    rows[pl.ds(pl.multiple_of(place * ROWS, ROWS), ROWS), :] = part.astype(F32)
-
-
-def tables_body(info, own, src, dst, weight, rows, sources, tables, weights):
+    projected[...] = matmul_t(dec_wide[...].astype(BF16), mesh_one)[:C, :].astype(BF16)
+
+
+def half_term(part, spread, place):
+    rows = pl.ds(pl.multiple_of(place * ROWS, ROWS), ROWS)
+    return matmul(part, spread[rows, :])
+
+
+def spread_body(info, own, src, dst, weight, grid, spread, base, sources, tables, weights):
     core, mesh_base, row_base = info[0], info[6], info[7]
-    put_half(rows, 2 + core, own[0])
-    put_half(rows, 3 - core, own[1])
     sources[...] = src[...] - mesh_base
     weights[...] = weight[...].astype(F32)
     row_slots = lax.broadcasted_iota(jnp.int32, (TILE, LANES), 0)
@@ -368,31 +378,41 @@
             tables[rows_of(tile), rows_of(part)] = jnp.where(
                 row_slots == target, weights[slot, :], 0.0
             ).astype(BF16)
-
-
-def decode_body(info, src, rows_in, sent, swapped_rows, tables, grid, rows, out, messages):
+    mesh_slots = lax.broadcasted_iota(jnp.int32, (ROWS, LANES), 0)
+
+    def half(place, carry):
+        begin = pl.multiple_of(place * ROWS, ROWS)
+        for tile in range(DEC_TILES):
+            picks = []
+            for part in range(DEC_ROUNDS):
+                slot = slice(part * DEC_TILES + tile, part * DEC_TILES + tile + 1)
+                hit = mesh_slots == sources[slot, :] - begin
+                picks.append(jnp.where(hit, 1.0, 0.0).astype(BF16))
+            spread[pl.ds(begin, ROWS), rows_of(tile)] = matmul_t(
+                jnp.concatenate(picks, axis=1), tables[rows_of(tile), :]
+            ).astype(BF16)
+        return carry
+
+    lax.fori_loop(0, 6, half, 0)
+    fields = grid[:, pl.ds(pl.multiple_of(core * GQ, GQ), GQ)].astype(F32)
+    terms = half_term(own[0], spread, 2 + core) + half_term(own[1], spread, 3 - core)
+    base[...] = fields + terms
+
+
+def sent_body(info, sent, spread, base, total):
     core = info[0]
-    other = 1 - core
-    put_half(rows, 4 * core + core, sent[0])
-    put_half(rows, 4 * core + other, sent[1])
-    put_half(rows, 4 * other + other, swapped_rows[0])
-    put_half(rows, 4 * other + core, swapped_rows[1])
-
-    def gather(tile, carry):
-        begin = pl.multiple_of(tile * DEC_ROUNDS * TILE, TILE)
-        for part in range(DEC_ROUNDS):
-            for edge in range(TILE):
-                index = src[part * DEC_TILES + tile, edge]
-                messages[pl.ds(begin + part * TILE + edge, 1), :] = rows[pl.ds(index, 1), :]
-        return carry
-
-    lax.fori_loop(0, DEC_TILES, gather, 0)
-    span = DEC_ROUNDS * TILE
-    for tile in range(DEC_TILES):
-        message = messages[tile * span : (tile + 1) * span, :].astype(BF16)
-        summed = matmul(tables[rows_of(tile), :], message).T
-        fields = grid[:, pl.ds(pl.multiple_of(core * GQ + tile * TILE, TILE), TILE)]
-        out[:, rows_of(tile)] = (fields.astype(F32) + summed[:C, :]).astype(BF16)
+    total[...] = (
+        base[...]
+        + half_term(sent[0], spread, 5 * core)
+        + half_term(sent[1], spread, 3 * core + 1)
+    )
+
+
+def decode_body(info, swapped_rows, spread, total, out):
+    other = 1 - info[0]
+    terms = half_term(swapped_rows[0], spread, 5 * other)
+    terms = terms + half_term(swapped_rows[1], spread, 3 * other + 1)
+    out[...] = (total[...] + terms).astype(BF16)
 
 
 def swapped(value):
@@ -506,7 +526,7 @@
             jax.ShapeDtypeStruct((D, ROWS), F32),
             jax.ShapeDtypeStruct((D // LANES, 8, 2 * ROWS), F32),
         ],
-        [pltpu.VMEM((ROWS, 2 * TILE), F32), pltpu.VMEM((ROWS, 2 * TILE), F32)],
+        [pltpu.VMEM((ROWS, 2 * GROUP * TILE), F32)] * 2,
         8 * 10 ** 9, 10 ** 7, "own",
     )
     projected = call(
@@ -514,46 +534,46 @@
         (info, halo_band, peer_keys, peer_values, queries, sums, stats, mask, qkv_own,
          qkv_peer, mesh_zero, w_out_attn, out_peer, dec_own, dec_peer),
         1,
-        jax.ShapeDtypeStruct((ROWS, LANES), BF16),
+        jax.ShapeDtypeStruct((C, ROWS), BF16),
         [
             pltpu.VMEM((2 * WIN, D), BF16),
             pltpu.VMEM((D, 2 * WIN), BF16),
             pltpu.VMEM((TILES, WIN, TILE), BF16),
             pltpu.VMEM((D, ROWS), BF16),
             pltpu.VMEM((LANES, D), F32),
-            pltpu.VMEM((WIN, 2 * TILE), F32),
-            pltpu.VMEM((WIN, 2 * TILE), F32),
+            pltpu.VMEM((WIN, 2 * GROUP * TILE), F32),
+            pltpu.VMEM((WIN, 2 * GROUP * TILE), F32),
         ],
         10 ** 10, 2 * 10 ** 7, "attend",
     )
     own_pair = jnp.stack([projected, swapped(projected)])
     pair_sent = up_and_down(own_pair)
-    mesh_rows, dec_sources, dec_tables = call(
-        tables_body,
-        (info, own_pair, dec_src, dec_dst, dec_weight),
+    spread, base = call(
+        spread_body,
+        (info, own_pair, dec_src, dec_dst, dec_weight, grid),
         1,
         [
-            jax.ShapeDtypeStruct((6 * ROWS, LANES), F32),
-            jax.ShapeDtypeStruct(dec_src.shape, jnp.int32),
-            jax.ShapeDtypeStruct((GQ, DEC_ROUNDS * TILE), BF16),
+            jax.ShapeDtypeStruct((6 * ROWS, GQ), BF16),
+            jax.ShapeDtypeStruct((C, GQ), F32),
         ],
-        [pltpu.VMEM(dec_weight.shape, F32)],
-        3 * 10 ** 9, 2 * 10 ** 6, "tables",
-    )
-    pair_sent, mesh_rows = lax.optimization_barrier((pair_sent, mesh_rows))
+        [
+            pltpu.VMEM(dec_src.shape, jnp.int32),
+            pltpu.VMEM((GQ, DEC_ROUNDS * TILE), BF16),
+            pltpu.VMEM(dec_weight.shape, F32),
+        ],
+        8 * 10 ** 9, 2 * 10 ** 6, "spread",
+    )
+    pair_sent, base = lax.optimization_barrier((pair_sent, base))
     pair_swapped = swapped(pair_sent)
-    _, out = call(
-        decode_body,
-        (info, dec_sources, mesh_rows, pair_sent, pair_swapped, dec_tables, grid),
-        2,
-        [
-            jax.ShapeDtypeStruct((6 * ROWS, LANES), F32),
-            jax.ShapeDtypeStruct((C, GQ), BF16),
-        ],
-        [pltpu.VMEM((DEC_TILES * DEC_ROUNDS * TILE, LANES), F32)],
-        10 ** 9, 3 * 10 ** 6, "decode", {2: 0},
-    )
-    return out.T
+    sums_out = jax.ShapeDtypeStruct((C, GQ), F32)
+    total = call(
+        sent_body, (info, pair_sent, spread, base), 1, sums_out, [],
+        10 ** 9, 3 * 10 ** 6, "sent",
+    )
+    return call(
+        decode_body, (info, pair_swapped, spread, total), 1,
+        jax.ShapeDtypeStruct((C, GQ), BF16), [], 10 ** 9, 3 * 10 ** 6, "decode",
+    ).T
 
 
 def solution(mesh):

time: 77.2 us -> 72.2 us (0.935)
  waiting for transfers between devices: 5.16 us -> 1.64 us
  starting transfers between devices: 23.4 us -> 20.4 us
  Pallas kernels: 41.6 us -> 43.1 us
    ppermute x9, starting transfers between devices: 10.3 us -> 6.73 us  [swapped(): return lax.ppermute(value, 'mp', [(0, 1), (1, 0)])]
    ppermute x2, waiting for transfers between devices: 2.51 us -> 0.01 us  [up_and_down(): return lax.ppermute(value, ('band', 'mp'), pairs)]
    pallas_call x8 -> x9, Pallas kernels: 41.6 us -> 43.1 us  [call(): pl.pallas_call(body, out_shape=outs, in_specs=specs, out_specs=jax.tree.m...]
    ppermute x9, waiting for transfers between devices: 2.64 us -> 1.64 us  [swapped(): return lax.ppermute(value, 'mp', [(0, 1), (1, 0)])]
  transfers between devices with their start and end apart: 12 -> 12, of which waited for: 4 -> 3; matrix products, arithmetic and copies ran while one was open for 0% -> 0% of each run, Pallas kernels for 34% -> 44%
where the time goes in v5:
time: 72.2 us; the launch traced here: 71.8 us
  Pallas kernels  43.1 us (60%)
  starting transfers between devices  20.4 us (28%)
  local copies, waits for them, and re-layouts  5.6 us (8%)
  waiting for transfers between devices  1.64 us (2%)
  between operations  0.94 us (1%)
    pallas_call x9, Pallas kernels, call(): pl.pallas_call(body, out_shape=outs, in_specs=specs, out_specs=jax.tree.m...  43.1 us
    ppermute x2, starting transfers between devices, up_and_down(): return lax.ppermute(value, ('band', 'mp'), pairs)  11.8 us
    ppermute x9, starting transfers between devices, swapped(): return lax.ppermute(value, 'mp', [(0, 1), (1, 0)])  6.73 us
    unnamed x28, local copies, waits for them, and re-layouts  5.51 us
    ppermute x1, starting transfers between devices, over_the_edge(): return lax.ppermute(value, ('band', 'mp'), pairs)  1.92 us
    ppermute x9, waiting for transfers between devices, swapped(): return lax.ppermute(value, 'mp', [(0, 1), (1, 0)])  1.64 us
  transfers between devices with their start and end apart: 12, of which 3 were waited for; matrix products, arithmetic and copies ran while one was open for 0% of the time, Pallas kernels for 44%

profile of v5, /device:TPU:97, one launch (start us, length us, event | category | flops | bytes accessed | tf_op | source)
XLA Modules:
  0.0 71.8 jit_solution(17746757216525718122)
XLA Ops:
  0.0 0.7 collective-permute-start.4
  0.7 0.0 collective-permute-start
  0.7 6.7 %collective-permute-start.1 = (bf16[100,2048]{1,0:T(8,128)(2,1)}, bf16[100,2048]{1,0:T(8,128)(2,1)}, u32[]{:S(2)}, u32[]{:S(2)}) collective-permute-start(bf16[100,2048]{1,0:T(8,128)(2,1)} %bitcast.18), channel_id=1, source_target_pairs={{0,2},{2,4},{4,6},{6,8},{8,10},{10,12},{12,14},{14,16},{16,18},{18... | collective-permute-start | bytes 1228808 | tf_op jit(solution)/shard_map/ppermute | solution.py:426
  8.0 0.1 stack.48.info
  8.1 0.0 collective-permute-done.win_peer
  8.1 0.0 copy-start.2
  8.1 1.0 %copy-done.2 = bf16[2048,100]{0,1:T(8,128)(2,1)S(1)} copy-done((bf16[2048,100]{0,1:T(8,128)(2,1)S(1)}, bf16[2048,100]{0,1:T(8,128)(2,1)}, u32[]{:S(2)}) %copy-start.2) | copy-done | bytes 409624
  9.1 0.9 %copy-done.4 = bf16[100,512]{1,0:T(8,128)(2,1)S(1)} copy-done((bf16[100,512]{1,0:T(8,128)(2,1)S(1)}, bf16[100,512]{1,0:T(8,128)(2,1)}, u32[]{:S(2)}) %copy-start.4) | copy-done | bytes 102424
  10.0 0.8 %copy-done.6 = s32[64,128]{1,0:T(8,128)S(1)} copy-done((s32[64,128]{1,0:T(8,128)S(1)}, s32[64,128]{1,0:T(8,128)}, u32[]{:S(2)}) %copy-start.6) | copy-done | bytes 32792
  10.8 0.8 %copy-done.7 = s32[64,128]{1,0:T(8,128)S(1)} copy-done((s32[64,128]{1,0:T(8,128)S(1)}, s32[64,128]{1,0:T(8,128)}, u32[]{:S(2)}) %copy-start.7) | copy-done | bytes 32792
  11.5 0.7 copy-done.8
  12.2 0.7 copy-done.12
  12.9 0.7 copy-done.13
  13.6 2.7 %prepare.1 = (f32[2048,128]{1,0:T(8,128)S(1)}, bf16[896,128]{1,0:T(8,128)(2,1)S(1)}, s32[64,128]{1,0:T(8,128)S(1)}, s32[64,128]{1,0:T(8,128)S(1)}, f32[64,128]{1...) custom-call(s32[8]{0:T(128)S(1)} %stack.48.info, s32[32]{0:T(128)S(1)} %copy-done.13, ...), custom_call_target="tpu_custom_call" | custom-call | flops 8000000000 | bytes 2000000 | tf_op jit(solution)/shard_map/prepare/pallas_call | solution.py:43
  16.3 0.0 collective-permute-done.1.sent
  16.3 0.1 collective-permute-start.2
  16.4 0.0 copy-done.1
  16.4 0.5 collective-permute-start.7
  16.9 1.2 %unpack.1.grid_rows = f32[6144,128]{1,0:T(8,128)S(1)} custom-call(s32[8]{0:T(128)S(1)} %stack.48.info, f32[2048,128]{1,0:T(8,128)S(1)} %get-tuple-element.30.own_rows, bf16[100,2048]{1,0:T(8,128)(2,1)} %collective-permute-done.1.sent), custom_call_target="tpu_custom_call" | custom-call | flops 2000000000 | bytes 2000000 | tf_op jit(solution)/shard_map/unpack/pallas_call | solution.py:43
  18.1 0.2 collective-permute-done.2.swapped_rows
  18.3 9.3 %encode.1 = (f32[6144,128]{1,0:T(8,128)S(1)}, bf16[512,1024]{1,0:T(8,128)(2,1)S(1)}, bf16[512,1024]{1,0:T(8,128)(2,1)S(1)}, bf16[384,1024]{1,0:T(8,128)(2,1)S(1)}) custom-call(s32[8]{0:T(128)S(1)} %stack.48.info, s32[64,128]{1,0:T(8,128)S(1)} %get-tuple-element.28.src, f32[6144,128]{1,0:T(8,128)S(1)} %unpack.1.grid_rows, ...), custom_call_target="tpu_custom_call", output_to_operand_aliasing={{0}: (2, {})} | custom-call | flops 8000000000 | bytes 4000000 | tf_op jit(solution)/shard_map/encode/pallas_call | solution.py:43
  27.7 1.9 %collective-permute-start.3 = (bf16[384,1024]{1,0:T(8,128)(2,1)S(1)}, bf16[384,1024]{1,0:T(8,128)(2,1)S(1)}, u32[]{:S(2)}, u32[]{:S(2)}) collective-permute-start(bf16[384,1024]{1,0:T(8,128)(2,1)S(1)} %get-tuple-element.36), channel_id=1, source_target_pairs={{1,2},{3,4},{5,6},{7,8},{9,10},{11,12},{13,14},{15,16},{17,18},{19... | collective-permute-start | bytes 2359304 | tf_op jit(solution)/shard_map/ppermute | solution.py:433
  29.6 0.0 collective-permute-done.4.w_peer
  29.6 0.0 copy-start.5
  29.6 4.1 %project.1 = (bf16[512,1024]{1,0:T(8,128)(2,1)S(1)}, bf16[512,1024]{1,0:T(8,128)(2,1)S(1)}, bf16[1024,512]{1,0:T(8,128)(2,1)S(1)}, bf16[384,1024]{1,0:T(8,128)(2,1)S(1)}, bf16[1024,384]{1,0:T(8,128)(2,1)S(1)}) custom-call(s32[8]{0:T(128)S(1)} %stack.48.info, bf16[512,1024]{1,0:T(8,128)(2,1)S(1)} %get-tuple-element.37.normed, ...), custom_call_target="tpu_custom_call" | custom-call | flops 6000000000 | bytes 10000000 | tf_op jit(solution)/shard_map/project/pallas_call | solution.py:43
  33.8 3.5 %collective-permute-start.5 = (bf16[384,1024]{1,0:T(8,128)(2,1)S(1)}, bf16[384,1024]{1,0:T(8,128)(2,1)S(1)}, u32[]{:S(2)}, u32[]{:S(2)}) collective-permute-start(bf16[384,1024]{1,0:T(8,128)(2,1)S(1)} %get-tuple-element.38), channel_id=1, source_target_pairs={{0,1},{1,0},{2,3},{3,2},{4,5},{5,4},{6,7},{7,6},{8,9},{9,8},{10,11... | collective-permute-start | bytes 2359304 | tf_op jit(solution)/shard_map/ppermute | solution.py:419
  37.2 0.1 collective-permute-start.6
  37.3 0.4 collective-permute-start.8
  37.7 6.2 %own.1 = (f32[1024,512]{1,0:T(8,128)S(1)}, f32[8,8,1024]{2,1,0:T(8,128)S(1)}) custom-call(bf16[512,1024]{1,0:T(8,128)(2,1)S(1)} %get-tuple-element.40.queries, bf16[512,1024]{1,0:T(8,128)(2,1)S(1)} %get-tuple-element.41.keys, bf16[1024,512]{1,0:T(8,128)(2,1)S(1)} %get-tuple-element.42.values_t, bf16[896,128]{1,0:T(8,128)(2,1)S(1)} %get-tuple-element.43.mask), custom_call_target="tpu_custom_call" | custom-call | flops 8000000000 | bytes 10000000 | tf_op jit(solution)/shard_map/own/pallas_call | solution.py:43
  44.0 0.0 collective-permute-done.8.dec_peer
  44.0 0.0 collective-permute-done.7.out_peer
  44.0 0.0 collective-permute-done.3.halo
  44.0 0.0 collective-permute-done.5.peer_keys
  44.0 0.0 collective-permute-done.6.peer_values
  44.0 0.0 copy-start.3
  44.0 0.0 copy-start.9
  44.0 0.0 copy-start.10
  44.1 0.0 copy-start.11
  44.1 9.8 %attend.1 = bf16[100,512]{1,0:T(8,128)(2,1)S(1)} custom-call(s32[8]{0:T(128)S(1)} %stack.48.info, bf16[384,1024]{1,0:T(8,128)(2,1)S(1)} %collective-permute-done.3.halo, bf16[384,1024]{1,0:T(8,128)(2,1)S(1)} %collective-permute-done.5.peer_keys, bf16[1024,384]{1,0:T(8,128)(2,1)S(1)} %collective-permute-done.6.peer_values, ...), custom_call_target="tpu_custom_call" | custom-call | flops 10000000000 | bytes 20000000 | tf_op jit(solution)/shard_map/attend/pallas_call | solution.py:43
  53.9 1.4 %collective-permute-start.9 = (bf16[100,512]{1,0:T(8,128)(2,1)S(1)}, bf16[100,512]{1,0:T(8,128)(2,1)S(1)}, u32[]{:S(2)}, u32[]{:S(2)}) collective-permute-start(bf16[100,512]{1,0:T(8,128)(2,1)S(1)} %attend.1), channel_id=1, source_target_pairs={{0,1},{1,0},{2,3},{3,2},{4,5},{5,4},{6,7},{7,6},{8,9},{9,8},{10,11... | collective-permute-start | bytes 307208 | tf_op jit(solution)/shard_map/ppermute | solution.py:419
  55.3 1.0 %collective-permute-done.9 = bf16[100,512]{1,0:T(8,128)(2,1)S(1)} collective-permute-done((bf16[100,512]{1,0:T(8,128)(2,1)S(1)}, bf16[100,512]{1,0:T(8,128)(2,1)S(1)}, u32[]{:S(2)}, u32[]{:S(2)}) %collective-permute-start.9) | collective-permute-done | bytes 102432 | tf_op jit(solution)/shard_map/ppermute | solution.py:419
  56.3 5.1 %collective-permute-start.10 = (bf16[2,100,512]{2,1,0:T(8,128)(2,1)S(1)}, bf16[2,100,512]{2,1,0:T(8,128)(2,1)S(1)}, u32[]{:S(2)}, u32[]{:S(2)}) collective-permute-start(bf16[2,100,512]{2,1,0:T(8,128)(2,1)S(1)} %pad_maximum_fusion.own), channel_id=1, source_target_pairs={{0,2},{2,4},{4,6},{6,8},{8,10},{10,12},{12,14},{14,16},{16,18},{18... | collective-permute-start | bytes 614408 | tf_op jit(solution)/shard_map/ppermute | solution.py:426
  61.4 7.1 %spread.1 = (bf16[3072,1024]{1,0:T(8,128)(2,1)S(1)}, f32[100,1024]{1,0:T(8,128)S(1)}) custom-call(s32[8]{0:T(128)S(1)} %stack.48.info, bf16[2,100,512]{2,1,0:T(8,128)(2,1)S(1)} %pad_maximum_fusion.own, s32[24,128]{1,0:T(8,128)S(1)} %copy-done.9, s32[24,128]{1,0:T(8,128)S(1)} %copy-done.10, bf16[24,128]{1,0:T(8,128)(2,1)S(1)} %copy-done.11, ...), custom_call_target="tpu_custom_call" | custom-call | flops 8000000000 | bytes 2000000 | tf_op jit(solution)/shard_map/spread/pallas_call | solution.py:43
  68.5 0.0 collective-permute-done.10.sent
  68.5 0.1 collective-permute-start.11
  68.6 1.0 %sent.1.total = f32[100,1024]{1,0:T(8,128)S(1)} custom-call(s32[8]{0:T(128)S(1)} %stack.48.info, bf16[2,100,512]{2,1,0:T(8,128)(2,1)S(1)} %collective-permute-done.10.sent, bf16[3072,1024]{1,0:T(8,128)(2,1)S(1)} %get-tuple-element.49.spread, f32[100,1024]{1,0:T(8,128)S(1)} %get-tuple-element.50.base), custom_call_target="tpu_custom_call" | custom-call | flops 1000000000 | bytes 3000000 | tf_op jit(solution)/shard_map/sent/pallas_call | solution.py:43
  69.6 0.4 collective-permute-done.11.swapped_rows
  70.1 1.7 %decode.1 = bf16[100,1024]{1,0:T(8,128)(2,1)} custom-call(s32[8]{0:T(128)S(1)} %stack.48.info, bf16[2,100,512]{2,1,0:T(8,128)(2,1)S(1)} %collective-permute-done.11.swapped_rows, bf16[3072,1024]{1,0:T(8,128)(2,1)S(1)} %get-tuple-element.49.spread, f32[100,1024]{1,0:T(8,128)S(1)} %sent.1.total), custom_call_target="tpu_custom_call" | custom-call | flops 1000000000 | bytes 3000000 | tf_op jit(solution)/shard_map/decode/pallas_call | solution.py:43
  (15 shorter events, 0.0 us)
Async XLA Ops:
  0.0 29.6 %collective-permute-start.4 = (bf16[3,1024,512]{2,1,0:T(8,128)(2,1)}, bf16[3,1024,512]{2,1,0:T(8,128)(2,1)S(1)}, u32[]{:S(2)}, u32[]{:S(2)}) collective-permute-start(bf16[3,1024,512]{2,1,0:T(8,128)(2,1)} %bitcast.15), channel_id=1, source_target_pairs={{0,1},{1,0},{2,3},{3,2},{4,5},{5,4},{6,7},{7,6},{8,9},{9,8},{10,11... | collective-permute-start | bytes 9437192 | tf_op jit(solution)/shard_map/ppermute | solution.py:419
  0.7 7.4 %collective-permute-start = (bf16[100,512]{1,0:T(8,128)(2,1)}, bf16[100,512]{1,0:T(8,128)(2,1)S(1)}, u32[]{:S(2)}, u32[]{:S(2)}) collective-permute-start(bf16[100,512]{1,0:T(8,128)(2,1)} %win_own.1), channel_id=1, source_target_pairs={{0,1},{1,0},{2,3},{3,2},{4,5},{5,4},{6,7},{7,6},{8,9},{9,8},{10,11... | collective-permute-start | bytes 307208 | tf_op jit(solution)/shard_map/ppermute | solution.py:419
  0.7 15.6 %collective-permute-start.1 = (bf16[100,2048]{1,0:T(8,128)(2,1)}, bf16[100,2048]{1,0:T(8,128)(2,1)}, u32[]{:S(2)}, u32[]{:S(2)}) collective-permute-start(bf16[100,2048]{1,0:T(8,128)(2,1)} %bitcast.18), channel_id=1, source_target_pairs={{0,2},{2,4},{4,6},{6,8},{8,10},{10,12},{12,14},{14,16},{16,18},{18... | collective-permute-start | bytes 1228808 | tf_op jit(solution)/shard_map/ppermute | solution.py:426
  8.1 1.0 %copy-start.2 = (bf16[2048,100]{0,1:T(8,128)(2,1)S(1)}, bf16[2048,100]{0,1:T(8,128)(2,1)}, u32[]{:S(2)}) copy-start(bf16[2048,100]{0,1:T(8,128)(2,1)} %param.14) | copy-start | bytes 1228804
  9.1 0.9 %copy-start.4 = (bf16[100,512]{1,0:T(8,128)(2,1)S(1)}, bf16[100,512]{1,0:T(8,128)(2,1)}, u32[]{:S(2)}) copy-start(bf16[100,512]{1,0:T(8,128)(2,1)} %win_own.1) | copy-start | bytes 307204
  10.0 0.8 %copy-start.6 = (s32[64,128]{1,0:T(8,128)S(1)}, s32[64,128]{1,0:T(8,128)}, u32[]{:S(2)}) copy-start(s32[64,128]{1,0:T(8,128)} %src.2) | copy-start | bytes 98308
  10.8 0.8 %copy-start.7 = (s32[64,128]{1,0:T(8,128)S(1)}, s32[64,128]{1,0:T(8,128)}, u32[]{:S(2)}) copy-start(s32[64,128]{1,0:T(8,128)} %dst.2) | copy-start | bytes 98308
  11.5 0.7 copy-start.8
  12.2 0.7 copy-start.12
  12.9 0.7 copy-start.13
  13.6 2.8 %copy-start.1 = (bf16[512,1024]{1,0:T(8,128)(2,1)S(1)}, bf16[512,1024]{1,0:T(8,128)(2,1)}, u32[]{:S(2)}) copy-start(bf16[512,1024]{1,0:T(8,128)(2,1)} %out_own.1) | copy-start | bytes 3145732
  16.3 2.1 %collective-permute-start.2 = (bf16[100,2048]{1,0:T(8,128)(2,1)}, bf16[100,2048]{1,0:T(8,128)(2,1)S(1)}, u32[]{:S(2)}, u32[]{:S(2)}) collective-permute-start(bf16[100,2048]{1,0:T(8,128)(2,1)} %collective-permute-done.1.sent), channel_id=1, source_target_pairs={{0,1},{1,0},{2,3},{3,2},{4,5},{5,4},{6,7},{7,6},{8,9},{9,8},{10,11... | collective-permute-start | bytes 1228808 | tf_op jit(solution)/shard_map/ppermute | solution.py:419
  16.4 27.6 %collective-permute-start.7 = (bf16[512,1024]{1,0:T(8,128)(2,1)S(1)}, bf16[512,1024]{1,0:T(8,128)(2,1)S(1)}, u32[]{:S(2)}, u32[]{:S(2)}) collective-permute-start(bf16[512,1024]{1,0:T(8,128)(2,1)S(1)} %copy-done.1), channel_id=1, source_target_pairs={{0,1},{1,0},{2,3},{3,2},{4,5},{5,4},{6,7},{7,6},{8,9},{9,8},{10,11... | collective-permute-start | bytes 3145736 | tf_op jit(solution)/shard_map/ppermute | solution.py:419
  18.3 11.3 %copy-start = (bf16[1024,3,512]{2,0,1:T(8,128)(2,1)S(1)}, bf16[1024,3,512]{2,0,1:T(8,128)(2,1)}, u32[]{:S(2)}) copy-start(bf16[1024,3,512]{2,0,1:T(8,128)(2,1)} %param.21) | copy-start | bytes 9437188
  27.7 16.3 %collective-permute-start.3 = (bf16[384,1024]{1,0:T(8,128)(2,1)S(1)}, bf16[384,1024]{1,0:T(8,128)(2,1)S(1)}, u32[]{:S(2)}, u32[]{:S(2)}) collective-permute-start(bf16[384,1024]{1,0:T(8,128)(2,1)S(1)} %get-tuple-element.36), channel_id=1, source_target_pairs={{1,2},{3,4},{5,6},{7,8},{9,10},{11,12},{13,14},{15,16},{17,18},{19... | collective-permute-start | bytes 2359304 | tf_op jit(solution)/shard_map/ppermute | solution.py:433
  29.6 7.7 %copy-start.5 = (bf16[512,100]{0,1:T(8,128)(2,1)S(1)}, bf16[512,100]{0,1:T(8,128)(2,1)}, u32[]{:S(2)}) copy-start(bf16[512,100]{0,1:T(8,128)(2,1)} %param.24) | copy-start | bytes 307204
  33.8 10.2 %collective-permute-start.5 = (bf16[384,1024]{1,0:T(8,128)(2,1)S(1)}, bf16[384,1024]{1,0:T(8,128)(2,1)S(1)}, u32[]{:S(2)}, u32[]{:S(2)}) collective-permute-start(bf16[384,1024]{1,0:T(8,128)(2,1)S(1)} %get-tuple-element.38), channel_id=1, source_target_pairs={{0,1},{1,0},{2,3},{3,2},{4,5},{5,4},{6,7},{7,6},{8,9},{9,8},{10,11... | collective-permute-start | bytes 2359304 | tf_op jit(solution)/shard_map/ppermute | solution.py:419
  37.2 6.8 %collective-permute-start.6 = (bf16[1024,384]{1,0:T(8,128)(2,1)S(1)}, bf16[1024,384]{1,0:T(8,128)(2,1)S(1)}, u32[]{:S(2)}, u32[]{:S(2)}) collective-permute-start(bf16[1024,384]{1,0:T(8,128)(2,1)S(1)} %get-tuple-element.39), channel_id=1, source_target_pairs={{0,1},{1,0},{2,3},{3,2},{4,5},{5,4},{6,7},{7,6},{8,9},{9,8},{10,11... | collective-permute-start | bytes 2359304 | tf_op jit(solution)/shard_map/ppermute | solution.py:419
  37.3 6.7 %collective-permute-start.8 = (bf16[100,512]{1,0:T(8,128)(2,1)S(1)}, bf16[100,512]{1,0:T(8,128)(2,1)S(1)}, u32[]{:S(2)}, u32[]{:S(2)}) collective-permute-start(bf16[100,512]{1,0:T(8,128)(2,1)S(1)} %bitcast.21), channel_id=1, source_target_pairs={{0,1},{1,0},{2,3},{3,2},{4,5},{5,4},{6,7},{7,6},{8,9},{9,8},{10,11... | collective-permute-start | bytes 307208 | tf_op jit(solution)/shard_map/ppermute | solution.py:419
  44.0 17.4 %copy-start.3 = (bf16[2048,100]{0,1:T(8,128)(2,1)S(1)}, bf16[2048,100]{0,1:T(8,128)(2,1)}, u32[]{:S(2)}) copy-start(bf16[2048,100]{0,1:T(8,128)(2,1)} %param.14) | copy-start | bytes 1228804
  44.0 17.4 %copy-start.9 = (s32[24,128]{1,0:T(8,128)S(1)}, s32[24,128]{1,0:T(8,128)}, u32[]{:S(2)}) copy-start(s32[24,128]{1,0:T(8,128)} %src.3) | copy-start | bytes 36868
  44.0 17.4 %copy-start.10 = (s32[24,128]{1,0:T(8,128)S(1)}, s32[24,128]{1,0:T(8,128)}, u32[]{:S(2)}) copy-start(s32[24,128]{1,0:T(8,128)} %dst.3) | copy-start | bytes 36868
  44.1 17.4 %copy-start.11 = (bf16[24,128]{1,0:T(8,128)(2,1)S(1)}, bf16[24,128]{1,0:T(8,128)(2,1)}, u32[]{:S(2)}) copy-start(bf16[24,128]{1,0:T(8,128)(2,1)} %weight.3) | copy-start | bytes 18436
  53.9 2.4 %collective-permute-start.9 = (bf16[100,512]{1,0:T(8,128)(2,1)S(1)}, bf16[100,512]{1,0:T(8,128)(2,1)S(1)}, u32[]{:S(2)}, u32[]{:S(2)}) collective-permute-start(bf16[100,512]{1,0:T(8,128)(2,1)S(1)} %attend.1), channel_id=1, source_target_pairs={{0,1},{1,0},{2,3},{3,2},{4,5},{5,4},{6,7},{7,6},{8,9},{9,8},{10,11... | collective-permute-start | bytes 307208 | tf_op jit(solution)/shard_map/ppermute | solution.py:419
  56.3 12.2 %collective-permute-start.10 = (bf16[2,100,512]{2,1,0:T(8,128)(2,1)S(1)}, bf16[2,100,512]{2,1,0:T(8,128)(2,1)S(1)}, u32[]{:S(2)}, u32[]{:S(2)}) collective-permute-start(bf16[2,100,512]{2,1,0:T(8,128)(2,1)S(1)} %pad_maximum_fusion.own), channel_id=1, source_target_pairs={{0,2},{2,4},{4,6},{6,8},{8,10},{10,12},{12,14},{14,16},{16,18},{18... | collective-permute-start | bytes 614408 | tf_op jit(solution)/shard_map/ppermute | solution.py:426
  68.5 1.5 %collective-permute-start.11 = (bf16[2,100,512]{2,1,0:T(8,128)(2,1)S(1)}, bf16[2,100,512]{2,1,0:T(8,128)(2,1)S(1)}, u32[]{:S(2)}, u32[]{:S(2)}) collective-permute-start(bf16[2,100,512]{2,1,0:T(8,128)(2,1)S(1)} %collective-permute-done.10.sent), channel_id=1, source_target_pairs={{0,1},{1,0},{2,3},{3,2},{4,5},{5,4},{6,7},{7,6},{8,9},{9,8},{10,11... | collective-permute-start | bytes 614408 | tf_op jit(solution)/shard_map/ppermute | solution.py:419

commit v6 on v5

--- a/solution.py
+++ b/solution.py
@@ -69,14 +69,38 @@
         rows[pl.ds(place, LANES), :] = wide[:, columns].T
 
 
+def by_core(core, wide, own, peer):
+    @pl.when(core == 0)
+    def _():
+        wide[:C, :HALF] = own[...].astype(F32)
+        wide[:C, HALF:] = peer[...].astype(F32)
+
+    @pl.when(core != 0)
+    def _():
+        wide[:C, :HALF] = peer[...].astype(F32)
+        wide[:C, HALF:] = own[...].astype(F32)
+
+
+def turn_body(grid, own_rows, wide):
+    wide[...] = jnp.zeros_like(wide)
+    to_rows(grid, wide, own_rows, 0)
+
+
 def prepare_body(
-    info, offsets, grid, src, dst, weight, gain, win_own, win_peer,
-    own_rows, mask, sources, targets, weights, gains, w_in,
-    wide, w_wide,
+    info, offsets, own_rows, src, dst, weight, gain, win_own, win_peer, dec_own, dec_peer, w_out,
+    mask, sources, targets, weights, gains, w_in, w_decode, fold,
+    w_wide,
 ):
     core, live, mesh_base = info[0], info[1], info[3]
-    wide[...] = jnp.zeros_like(wide)
-    to_rows(grid, wide, own_rows, 0)
+    w_wide[...] = jnp.zeros_like(w_wide)
+    by_core(core, w_wide, win_own, win_peer)
+    w_in[...] = (w_wide[...] * 0.5).astype(BF16)
+    by_core(core, w_wide, dec_own, dec_peer)
+    w_decode[...] = w_wide[...].astype(BF16)
+    folded = matmul_t(w_decode[...], w_out[...])
+    upper = folded.astype(BF16)
+    fold[:LANES, :] = upper
+    fold[LANES:, :] = (folded - upper.astype(F32)).astype(BF16)
     for chunk in range(SPAN // TILE):
         row = lax.broadcasted_iota(jnp.int32, (TILE, LANES), 0) + (chunk * TILE - WIN)
         away = row - lax.broadcasted_iota(jnp.int32, (TILE, LANES), 1)
@@ -89,19 +113,6 @@
     targets[...] = dst[...] - mesh_base
     sources[...] = src[...] - info[2]
     gains[...] = gain[...]
-    w_wide[...] = jnp.zeros_like(w_wide)
-
-    @pl.when(core == 0)
-    def _():
-        w_wide[:C, :HALF] = win_own[...].astype(F32) * 0.5
-        w_wide[:C, HALF:] = win_peer[...].astype(F32) * 0.5
-
-    @pl.when(core != 0)
-    def _():
-        w_wide[:C, :HALF] = win_peer[...].astype(F32) * 0.5
-        w_wide[:C, HALF:] = win_own[...].astype(F32) * 0.5
-
-    w_in[...] = w_wide[...].astype(BF16)
 
 
 def unpack_body(info, own_rows, sent, rows, wide):
@@ -110,22 +121,20 @@
     to_rows(sent, wide, rows, info[0] * 2 * G_BAND)
 
 
-def encode_body(
-    info, src, grid_rows, swapped_rows, w_in, targets, weights, gain,
-    rows, mesh_zero, normed, to_band,
-    wide, first, second, total,
+def encode_tiles(
+    core, order, src, w_in, targets, weights, gain, rows, mesh_zero, normed, first, second, total
 ):
-    core = info[0]
-    wide[...] = jnp.zeros_like(wide)
-    to_rows(swapped_rows, wide, rows, (1 - core) * 2 * G_BAND)
-    total[...] = jnp.zeros_like(total)
     row_slots = lax.broadcasted_iota(jnp.int32, (TILE, LANES), 0)
     steps = EDGE_ROUNDS * TILE // STEP
     rounds = STEP // TILE
+    count = len(order) * steps
+
+    def tile_of(step):
+        place = order[0] + step // steps
+        return jnp.where(core == 0, place, TILES - 1 - place)
 
     def slot_of(step, part):
-        tile, chunk = step // steps, step % steps
-        return (chunk * rounds + part) * 2 * TILES + core * TILES + tile
+        return (step % steps * rounds + part) * 2 * TILES + core * TILES + tile_of(step)
 
     def gather(step, buffer):
         for part in range(rounds):
@@ -135,7 +144,7 @@
                 buffer[pl.ds(part * TILE + edge, 1), :] = rows[pl.ds(index, 1), :]
 
     def add(step, buffer):
-        tile = step // steps
+        tile = tile_of(step)
         half = matmul(buffer[...].astype(BF16), w_in[...])
         embedded = (half + half * jnp.tanh(half)).astype(BF16)
         tables = []
@@ -147,19 +156,23 @@
         place = pl.ds(pl.multiple_of(tile * TILE, TILE), TILE)
         total[place, :] += matmul(table, embedded)
 
+    for step in range(0, count, steps):
+        place = pl.ds(pl.multiple_of(tile_of(step) * TILE, TILE), TILE)
+        total[place, :] = jnp.zeros((TILE, D), F32)
     gather(0, first)
 
     def pair(index, carry):
         gather(2 * index + 1, second)
         add(2 * index, first)
-        gather(jnp.minimum(2 * index + 2, TILES * steps - 1), first)
+        if count > 2:
+            gather(jnp.minimum(2 * index + 2, count - 1), first)
         add(2 * index + 1, second)
         return carry
 
-    lax.fori_loop(0, TILES * steps // 2, pair, 0)
-
-    def finish(tile, carry):
-        place = pl.ds(pl.multiple_of(tile * TILE, TILE), TILE)
+    lax.fori_loop(0, count // 2, pair, 0)
+
+    def finish(step, carry):
+        place = pl.ds(pl.multiple_of(tile_of(step * steps) * TILE, TILE), TILE)
         rounded = total[place, :].astype(BF16)
         mesh_zero[place, :] = rounded
         values = rounded.astype(F32)
@@ -167,15 +180,33 @@
         normed[place, :] = (values * inverse * gain[...]).astype(BF16)
         return carry
 
-    lax.fori_loop(0, TILES, finish, 0)
-
-    @pl.when(core == 0)
-    def _():
-        to_band[...] = normed[:WIN, :]
-
-    @pl.when(core != 0)
-    def _():
-        to_band[...] = normed[ROWS - WIN :, :]
+    lax.fori_loop(0, len(order), finish, 0)
+
+
+def encode_body(
+    info, src, grid_rows, swapped_rows, w_in, targets, weights, gain,
+    rows, mesh_zero, normed, to_band,
+    wide, first, second, total,
+):
+    core = info[0]
+    wide[...] = jnp.zeros_like(wide)
+    to_rows(swapped_rows, wide, rows, (1 - core) * 2 * G_BAND)
+    encode_tiles(
+        core, range(TILES - 1), src, w_in, targets, weights, gain, rows, mesh_zero, normed,
+        first, second, total,
+    )
+    to_band[...] = normed[pl.ds(pl.multiple_of(core * TILE, TILE), WIN), :]
+
+
+def last_body(
+    info, src, rows, w_in, targets, weights, gain, zero_in, normed_in,
+    mesh_zero, normed,
+    first, second, total,
+):
+    encode_tiles(
+        info[0], range(TILES - 1, TILES), src, w_in, targets, weights, gain, rows, mesh_zero,
+        normed, first, second, total,
+    )
 
 
 def identity_pair():
@@ -245,9 +276,11 @@
 
 
 def project_body(
-    info, normed, w_own, w_peer, queries, keys, values_t, keys_sent, values_sent
+    info, normed, w_own, w_peer, mesh_zero, w_decode,
+    queries, keys, values_t, keys_sent, values_sent, straight,
 ):
     rows = normed[...]
+    straight[...] = matmul_t(w_decode[...], mesh_zero[...])
     for half, weight in enumerate((w_own, w_peer)):
         place = slice(half * HALF, (half + 1) * HALF)
         keys[:, place] = matmul(rows, weight[1]).astype(BF16)
@@ -294,24 +327,19 @@
 
 def attend_body(
     info, halo, peer_keys, peer_values, queries, sums, stats, mask, w_own, w_peer,
-    mesh_zero, out_own, out_peer, dec_own, dec_peer,
+    straight, fold_own, fold_peer,
     projected,
-    keys, values_t, masks, attended, dec_wide, first, second,
+    keys, values_t, masks, attended, first, second,
 ):
     core, first_device, last_device = info[0], info[4], info[5]
-    dec_wide[...] = jnp.zeros_like(dec_wide)
 
     @pl.when(core == 0)
     def _():
-        dec_wide[:C, :HALF] = dec_own[...].astype(F32)
-        dec_wide[:C, HALF:] = dec_peer[...].astype(F32)
         keys[WIN:, :] = peer_keys[...]
         values_t[:, WIN:] = peer_values[...]
 
     @pl.when(core != 0)
     def _():
-        dec_wide[:C, :HALF] = dec_peer[...].astype(F32)
-        dec_wide[:C, HALF:] = dec_own[...].astype(F32)
         keys[:WIN, :] = peer_keys[...]
         values_t[:, :WIN] = peer_values[...]
 
@@ -355,10 +383,8 @@
         attended[lanes_of(pair), rows_of(block)] = result.astype(BF16)
 
     pipeline(score, finish, first, second)
-    term_own = matmul(attended[:HALF, :].T, out_own[...]).astype(BF16).astype(F32)
-    term_peer = matmul(attended[HALF:, :].T, out_peer[...]).astype(BF16).astype(F32)
-    mesh_one = (mesh_zero[...].astype(F32) + (term_own + term_peer)).astype(BF16)
-    projected[...] = matmul_t(dec_wide[...].astype(BF16), mesh_one)[:C, :].astype(BF16)
+    both = matmul(fold_own[...], attended[:HALF, :]) + matmul(fold_peer[...], attended[HALF:, :])
+    projected[...] = (straight[...] + both[:LANES, :] + both[LANES:, :])[:C, :].astype(BF16)
 
 
 def half_term(part, spread, place):
@@ -458,26 +484,31 @@
     dec_peer = swapped(dec_own)
     qkv_own = w_qkv.transpose(1, 0, 2)
     qkv_peer = swapped(qkv_own)
-    out_peer = swapped(w_out_attn)
     edges = jax.ShapeDtypeStruct(enc_src.shape, jnp.int32)
-    own_rows, mask, sources, targets, weights, gain, w_in_all = call(
+    own_rows = call(
+        turn_body, (grid,), 0, jax.ShapeDtypeStruct((G_BAND, LANES), F32),
+        [pltpu.VMEM((LANES, G_BAND), F32)], 5 * 10 ** 9, 2 * 10 ** 6, "turn",
+    )
+    mask, sources, targets, weights, gain, w_in_all, dec_all, fold_own = call(
         prepare_body,
-        (info, offsets, grid, enc_src, enc_dst, enc_weight, norm_gain.reshape(1, D), w_in,
-         win_peer),
+        (info, offsets, own_rows, enc_src, enc_dst, enc_weight, norm_gain.reshape(1, D), w_in,
+         win_peer, dec_own, dec_peer, w_out_attn),
         2,
         [
-            jax.ShapeDtypeStruct((G_BAND, LANES), F32),
             jax.ShapeDtypeStruct((SPAN, TILE), BF16),
             edges,
             edges,
             jax.ShapeDtypeStruct(enc_weight.shape, F32),
             jax.ShapeDtypeStruct((1, D), F32),
             jax.ShapeDtypeStruct((LANES, D), BF16),
+            jax.ShapeDtypeStruct((LANES, D), BF16),
+            jax.ShapeDtypeStruct((2 * LANES, HALF), BF16),
         ],
-        [pltpu.VMEM((LANES, G_BAND), F32), pltpu.VMEM((LANES, D), F32)],
+        [pltpu.VMEM((LANES, D), F32)],
         8 * 10 ** 9, 2 * 10 ** 6, "prepare",
     )
-    grid_sent, own_rows = lax.optimization_barrier((grid_sent, own_rows))
+    fold_peer = swapped(fold_own)
+    grid_sent, own_rows, w_in_all = lax.optimization_barrier((grid_sent, own_rows, w_in_all))
     grid_swapped = swapped(grid_sent)
     grid_rows = call(
         unpack_body,
@@ -487,25 +518,33 @@
         [pltpu.VMEM((LANES, G_BAND), F32)],
         2 * 10 ** 9, 2 * 10 ** 6, "unpack",
     )
-    _, mesh_zero, normed, to_band = call(
+    band_rows = jax.ShapeDtypeStruct((ROWS, D), BF16)
+    step_buffers = [pltpu.VMEM((STEP, LANES), F32)] * 2 + [pltpu.VMEM((ROWS, D), F32)]
+    grid_rows, mesh_zero, normed, to_band = call(
         encode_body,
         (info, sources, grid_rows, grid_swapped, w_in_all, targets, weights, gain),
         2,
-        [jax.ShapeDtypeStruct((3 * G_BAND, LANES), F32)]
-        + [jax.ShapeDtypeStruct((ROWS, D), BF16)] * 2
-        + [jax.ShapeDtypeStruct((WIN, D), BF16)],
         [
-            pltpu.VMEM((LANES, G_BAND), F32),
-            pltpu.VMEM((STEP, LANES), F32),
-            pltpu.VMEM((STEP, LANES), F32),
-            pltpu.VMEM((ROWS, D), F32),
+            jax.ShapeDtypeStruct((3 * G_BAND, LANES), F32),
+            band_rows,
+            band_rows,
+            jax.ShapeDtypeStruct((WIN, D), BF16),
         ],
-        8 * 10 ** 9, 4 * 10 ** 6, "encode", {2: 0},
+        [pltpu.VMEM((LANES, G_BAND), F32)] + step_buffers,
+        7 * 10 ** 9, 4 * 10 ** 6, "encode", {2: 0},
     )
     halo_band = over_the_edge(to_band)
-    queries, keys, values_t, keys_sent, values_sent = call(
+    mesh_zero, normed = call(
+        last_body,
+        (info, sources, grid_rows, w_in_all, targets, weights, gain, mesh_zero, normed),
+        2,
+        [band_rows, band_rows],
+        step_buffers,
+        3 * 10 ** 9, 4 * 10 ** 6, "last", {7: 0, 8: 1},
+    )
+    queries, keys, values_t, keys_sent, values_sent, straight = call(
         project_body,
-        (info, normed, qkv_own, qkv_peer),
+        (info, normed, qkv_own, qkv_peer, mesh_zero, dec_all),
         1,
         [
             jax.ShapeDtypeStruct((ROWS, D), BF16),
@@ -513,6 +552,7 @@
             jax.ShapeDtypeStruct((D, ROWS), BF16),
             jax.ShapeDtypeStruct((WIN, D), BF16),
             jax.ShapeDtypeStruct((D, WIN), BF16),
+            jax.ShapeDtypeStruct((LANES, ROWS), F32),
         ],
         [],
         6 * 10 ** 9, 10 ** 7, "project",
@@ -532,7 +572,7 @@
     projected = call(
         attend_body,
         (info, halo_band, peer_keys, peer_values, queries, sums, stats, mask, qkv_own,
-         qkv_peer, mesh_zero, w_out_attn, out_peer, dec_own, dec_peer),
+         qkv_peer, straight, fold_own, fold_peer),
         1,
         jax.ShapeDtypeStruct((C, ROWS), BF16),
         [
@@ -540,7 +580,6 @@
             pltpu.VMEM((D, 2 * WIN), BF16),
             pltpu.VMEM((TILES, WIN, TILE), BF16),
             pltpu.VMEM((D, ROWS), BF16),
-            pltpu.VMEM((LANES, D), F32),
             pltpu.VMEM((WIN, 2 * GROUP * TILE), F32),
             pltpu.VMEM((WIN, 2 * GROUP * TILE), F32),
         ],

time: 72.2 us -> 71.7 us (level)
  starting transfers between devices: 20.4 us -> 18.8 us
  Pallas kernels: 43.1 us -> 44.1 us
    ppermute x9, starting transfers between devices: 6.73 us -> 4.55 us  [swapped(): return lax.ppermute(value, 'mp', [(0, 1), (1, 0)])]
    pallas_call x9 -> x11, Pallas kernels: 43.1 us -> 44.1 us  [call(): pl.pallas_call(body, out_shape=outs, in_specs=specs, out_specs=jax.tree.m...]
    unnamed x28 -> x32, local copies, waits for them, and re-layouts: 5.51 us -> 5.13 us
  transfers between devices with their start and end apart: 12 -> 12, of which waited for: 3 -> 3; matrix products, arithmetic and copies ran while one was open for 0% -> 0% of each run, Pallas kernels for 44% -> 48%
where the time goes in v6:
time: 71.7 us; the launch traced here: 71.4 us
  Pallas kernels  44.1 us (62%)
  starting transfers between devices  18.8 us (26%)
  local copies, waits for them, and re-layouts  5.22 us (7%)
  waiting for transfers between devices  2.22 us (3%)
  between operations  1.02 us (1%)
    pallas_call x11, Pallas kernels, call(): pl.pallas_call(body, out_shape=outs, in_specs=specs, out_specs=jax.tree.m...  44.1 us
    ppermute x2, starting transfers between devices, up_and_down(): return lax.ppermute(value, ('band', 'mp'), pairs)  12.3 us
    unnamed x32, local copies, waits for them, and re-layouts  5.13 us
    ppermute x9, starting transfers between devices, swapped(): return lax.ppermute(value, 'mp', [(0, 1), (1, 0)])  4.55 us
    ppermute x9, waiting for transfers between devices, swapped(): return lax.ppermute(value, 'mp', [(0, 1), (1, 0)])  2.21 us
    ppermute x1, starting transfers between devices, over_the_edge(): return lax.ppermute(value, ('band', 'mp'), pairs)  1.92 us
  transfers between devices with their start and end apart: 12, of which 3 were waited for; matrix products, arithmetic and copies ran while one was open for 0% of the time, Pallas kernels for 48%

profile of v6, /device:TPU:97, one launch (start us, length us, event | category | flops | bytes accessed | tf_op | source)
XLA Modules:
  0.0 71.4 jit_solution(6951262270378396212)
XLA Ops:
  0.0 0.7 collective-permute-start.5
  0.7 0.0 collective-permute-start
  0.7 0.5 collective-permute-start.1
  1.2 6.7 %collective-permute-start.2 = (bf16[100,2048]{1,0:T(8,128)(2,1)}, bf16[100,2048]{1,0:T(8,128)(2,1)}, u32[]{:S(2)}, u32[]{:S(2)}) collective-permute-start(bf16[100,2048]{1,0:T(8,128)(2,1)} %bitcast.18), channel_id=1, source_target_pairs={{0,2},{2,4},{4,6},{6,8},{8,10},{10,12},{12,14},{14,16},{16,18},{18... | collective-permute-start | bytes 1228808 | tf_op jit(solution)/shard_map/ppermute | solution.py:452
  7.9 0.0 copy-start.2
  7.9 1.0 %copy-done.2 = bf16[2048,100]{0,1:T(8,128)(2,1)S(1)} copy-done((bf16[2048,100]{0,1:T(8,128)(2,1)S(1)}, bf16[2048,100]{0,1:T(8,128)(2,1)}, u32[]{:S(2)}) %copy-start.2) | copy-done | bytes 409624
  8.9 0.2 turn.1.own_rows
  9.1 1.0 %copy-done.14 = f32[2048,128]{1,0:T(8,128)} copy-done((f32[2048,128]{1,0:T(8,128)}, f32[2048,128]{1,0:T(8,128)S(1)}, u32[]{:S(2)}) %copy-start.14) | copy-done | bytes 1048600
  10.8 0.1 stack.48.info
  10.8 0.0 collective-permute-done.win_peer
  10.8 0.0 collective-permute-done.1.dec_peer
  10.9 0.0 copy-start.1
  10.9 1.2 %copy-done.1 = bf16[512,1024]{1,0:T(8,128)(2,1)S(1)} copy-done((bf16[512,1024]{1,0:T(8,128)(2,1)S(1)}, bf16[512,1024]{1,0:T(8,128)(2,1)}, u32[]{:S(2)}) %copy-start.1) | copy-done | bytes 1048600
  12.1 0.7 copy-done.13
  12.8 1.2 %copy-done.15 = f32[2048,128]{1,0:T(8,128)S(1)} copy-done((f32[2048,128]{1,0:T(8,128)S(1)}, f32[2048,128]{1,0:T(8,128)}, u32[]{:S(2)}) %copy-start.15) | copy-done | bytes 1048600
  14.0 3.4 %prepare.1 = (bf16[896,128]{1,0:T(8,128)(2,1)S(1)}, s32[64,128]{1,0:T(8,128)S(1)}, s32[64,128]{1,0:T(8,128)S(1)}, f32[64,128]{1,0:T(8,128)S(1)}, f32[1,1024]{1,0...) custom-call(s32[8]{0:T(128)S(1)} %stack.48.info, ...), custom_call_target="tpu_custom_call" | custom-call | flops 8000000000 | bytes 2000000 | tf_op jit(solution)/shard_map/prepare/pallas_call | solution.py:43
  17.4 0.0 collective-permute-done.2.sent
  17.4 0.1 collective-permute-start.3
  17.5 1.2 %unpack.1.grid_rows = f32[6144,128]{1,0:T(8,128)S(1)} custom-call(s32[8]{0:T(128)S(1)} %stack.48.info, f32[2048,128]{1,0:T(8,128)S(1)} %copy-done.15, bf16[100,2048]{1,0:T(8,128)(2,1)} %collective-permute-done.2.sent), custom_call_target="tpu_custom_call" | custom-call | flops 2000000000 | bytes 2000000 | tf_op jit(solution)/shard_map/unpack/pallas_call | solution.py:43
  18.7 0.7 %collective-permute-done.3.swapped_rows = bf16[100,2048]{1,0:T(8,128)(2,1)S(1)} collective-permute-done((bf16[100,2048]{1,0:T(8,128)(2,1)}, bf16[100,2048]{1,0:T(8,128)(2,1)S(1)}, u32[]{:S(2)}, u32[]{:S(2)}) %collective-permute-start.3) | collective-permute-done | bytes 409632 | tf_op jit(solution)/shard_map/ppermute | solution.py:445
  19.5 7.5 %encode.1 = (f32[6144,128]{1,0:T(8,128)S(1)}, bf16[512,1024]{1,0:T(8,128)(2,1)S(1)}, bf16[512,1024]{1,0:T(8,128)(2,1)S(1)}, bf16[384,1024]{1,0:T(8,128)(2,1)S(1)}) custom-call(s32[8]{0:T(128)S(1)} %stack.48.info, s32[64,128]{1,0:T(8,128)S(1)} %get-tuple-element.34.src, f32[6144,128]{1,0:T(8,128)S(1)} %unpack.1.grid_rows, ...), custom_call_target="tpu_custom_call", output_to_operand_aliasing={{0}: (2, {})} | custom-call | flops 7000000000 | bytes 4000000 | tf_op jit(solution)/shard_map/encode/pallas_call | solution.py:43
  26.9 1.9 %collective-permute-start.4 = (bf16[384,1024]{1,0:T(8,128)(2,1)S(1)}, bf16[384,1024]{1,0:T(8,128)(2,1)S(1)}, u32[]{:S(2)}, u32[]{:S(2)}) collective-permute-start(bf16[384,1024]{1,0:T(8,128)(2,1)S(1)} %get-tuple-element.42), channel_id=1, source_target_pairs={{1,2},{3,4},{5,6},{7,8},{9,10},{11,12},{13,14},{15,16},{17,18},{19... | collective-permute-start | bytes 2359304 | tf_op jit(solution)/shard_map/ppermute | solution.py:459
  28.9 0.0 copy-start
  28.9 3.0 %last.1 = (bf16[512,1024]{1,0:T(8,128)(2,1)S(1)}, bf16[512,1024]{1,0:T(8,128)(2,1)S(1)}) custom-call(s32[8]{0:T(128)S(1)} %stack.48.info, s32[64,128]{1,0:T(8,128)S(1)} %get-tuple-element.34.src, f32[6144,128]{1,0:T(8,128)S(1)} %get-tuple-element.43.rows, ...), custom_call_target="tpu_custom_call", output_to_operand_aliasing={{0}: (7, {}), {1}: (8, {})} | custom-call | flops 3000000000 | bytes 4000000 | tf_op jit(solution)/shard_map/last/pallas_call | solution.py:43
  31.9 0.0 collective-permute-done.5.w_peer
  31.9 4.4 %project.1 = (bf16[512,1024]{1,0:T(8,128)(2,1)S(1)}, bf16[512,1024]{1,0:T(8,128)(2,1)S(1)}, bf16[1024,512]{1,0:T(8,128)(2,1)S(1)}, bf16[384,1024]{1,0:T(8,128)(2...) custom-call(s32[8]{0:T(128)S(1)} %stack.48.info, bf16[512,1024]{1,0:T(8,128)(2,1)S(1)} %get-tuple-element.46.normed, ...), custom_call_target="tpu_custom_call" | custom-call | flops 6000000000 | bytes 10000000 | tf_op jit(solution)/shard_map/project/pallas_call | solution.py:43
  36.3 2.3 %collective-permute-start.6 = (bf16[384,1024]{1,0:T(8,128)(2,1)S(1)}, bf16[384,1024]{1,0:T(8,128)(2,1)S(1)}, u32[]{:S(2)}, u32[]{:S(2)}) collective-permute-start(bf16[384,1024]{1,0:T(8,128)(2,1)S(1)} %get-tuple-element.49), channel_id=1, source_target_pairs={{0,1},{1,0},{2,3},{3,2},{4,5},{5,4},{6,7},{7,6},{8,9},{9,8},{10,11... | collective-permute-start | bytes 2359304 | tf_op jit(solution)/shard_map/ppermute | solution.py:445
  38.7 0.3 collective-permute-start.7
  38.9 0.2 collective-permute-start.8
  39.2 6.3 %own.1 = (f32[1024,512]{1,0:T(8,128)S(1)}, f32[8,8,1024]{2,1,0:T(8,128)S(1)}) custom-call(bf16[512,1024]{1,0:T(8,128)(2,1)S(1)} %get-tuple-element.51.queries, bf16[512,1024]{1,0:T(8,128)(2,1)S(1)} %get-tuple-element.52.keys, bf16[1024,512]{1,0:T(8,128)(2,1)S(1)} %get-tuple-element.53.values_t, bf16[896,128]{1,0:T(8,128)(2,1)S(1)} %get-tuple-element.54.mask), custom_call_target="tpu_custom_call" | custom-call | flops 8000000000 | bytes 10000000 | tf_op jit(solution)/shard_map/own/pallas_call | solution.py:43
  45.5 0.0 collective-permute-done.8.fold_peer
  45.5 0.0 collective-permute-done.4.halo
  45.5 0.0 collective-permute-done.6.peer_keys
  45.6 0.0 collective-permute-done.7.peer_values
  45.6 0.0 copy-start.3
  45.6 0.0 copy-start.9
  45.6 0.0 copy-start.10
  45.6 0.0 copy-start.11
  45.6 8.4 %attend.1 = bf16[100,512]{1,0:T(8,128)(2,1)S(1)} custom-call(s32[8]{0:T(128)S(1)} %stack.48.info, bf16[384,1024]{1,0:T(8,128)(2,1)S(1)} %collective-permute-done.4.halo, bf16[384,1024]{1,0:T(8,128)(2,1)S(1)} %collective-permute-done.6.peer_keys, bf16[1024,384]{1,0:T(8,128)(2,1)S(1)} %collective-permute-done.7.peer_values, ...), custom_call_target="tpu_custom_call" | custom-call | flops 10000000000 | bytes 20000000 | tf_op jit(solution)/shard_map/attend/pallas_call | solution.py:43
  54.0 0.4 collective-permute-start.9
  54.3 1.0 %collective-permute-done.9 = bf16[100,512]{1,0:T(8,128)(2,1)S(1)} collective-permute-done((bf16[100,512]{1,0:T(8,128)(2,1)S(1)}, bf16[100,512]{1,0:T(8,128)(2,1)S(1)}, u32[]{:S(2)}, u32[]{:S(2)}) %collective-permute-start.9) | collective-permute-done | bytes 102432 | tf_op jit(solution)/shard_map/ppermute | solution.py:445
  55.4 5.6 %collective-permute-start.10 = (bf16[2,100,512]{2,1,0:T(8,128)(2,1)S(1)}, bf16[2,100,512]{2,1,0:T(8,128)(2,1)S(1)}, u32[]{:S(2)}, u32[]{:S(2)}) collective-permute-start(bf16[2,100,512]{2,1,0:T(8,128)(2,1)S(1)} %pad_maximum_fusion.own), channel_id=1, source_target_pairs={{0,2},{2,4},{4,6},{6,8},{8,10},{10,12},{12,14},{14,16},{16,18},{18... | collective-permute-start | bytes 614408 | tf_op jit(solution)/shard_map/ppermute | solution.py:452
  61.1 7.1 %spread.1 = (bf16[3072,1024]{1,0:T(8,128)(2,1)S(1)}, f32[100,1024]{1,0:T(8,128)S(1)}) custom-call(s32[8]{0:T(128)S(1)} %stack.48.info, bf16[2,100,512]{2,1,0:T(8,128)(2,1)S(1)} %pad_maximum_fusion.own, s32[24,128]{1,0:T(8,128)S(1)} %copy-done.9, s32[24,128]{1,0:T(8,128)S(1)} %copy-done.10, bf16[24,128]{1,0:T(8,128)(2,1)S(1)} %copy-done.11, ...), custom_call_target="tpu_custom_call" | custom-call | flops 8000000000 | bytes 2000000 | tf_op jit(solution)/shard_map/spread/pallas_call | solution.py:43
  68.2 0.0 collective-permute-done.10.sent
  68.2 0.1 collective-permute-start.11
  68.3 1.0 %sent.1.total = f32[100,1024]{1,0:T(8,128)S(1)} custom-call(s32[8]{0:T(128)S(1)} %stack.48.info, bf16[2,100,512]{2,1,0:T(8,128)(2,1)S(1)} %collective-permute-done.10.sent, bf16[3072,1024]{1,0:T(8,128)(2,1)S(1)} %get-tuple-element.61.spread, f32[100,1024]{1,0:T(8,128)S(1)} %get-tuple-element.62.base), custom_call_target="tpu_custom_call" | custom-call | flops 1000000000 | bytes 3000000 | tf_op jit(solution)/shard_map/sent/pallas_call | solution.py:43
  69.3 0.4 collective-permute-done.11.swapped_rows
  69.7 1.7 %decode.1 = bf16[100,1024]{1,0:T(8,128)(2,1)} custom-call(s32[8]{0:T(128)S(1)} %stack.48.info, bf16[2,100,512]{2,1,0:T(8,128)(2,1)S(1)} %collective-permute-done.11.swapped_rows, bf16[3072,1024]{1,0:T(8,128)(2,1)S(1)} %get-tuple-element.61.spread, f32[100,1024]{1,0:T(8,128)S(1)} %sent.1.total), custom_call_target="tpu_custom_call" | custom-call | flops 1000000000 | bytes 3000000 | tf_op jit(solution)/shard_map/decode/pallas_call | solution.py:43
  (21 shorter events, 0.1 us)
Async XLA Ops:
  0.0 31.9 %collective-permute-start.5 = (bf16[3,1024,512]{2,1,0:T(8,128)(2,1)}, bf16[3,1024,512]{2,1,0:T(8,128)(2,1)S(1)}, u32[]{:S(2)}, u32[]{:S(2)}) collective-permute-start(bf16[3,1024,512]{2,1,0:T(8,128)(2,1)} %bitcast.15), channel_id=1, source_target_pairs={{0,1},{1,0},{2,3},{3,2},{4,5},{5,4},{6,7},{7,6},{8,9},{9,8},{10,11... | collective-permute-start | bytes 9437192 | tf_op jit(solution)/shard_map/ppermute | solution.py:445
  0.7 10.2 %collective-permute-start = (bf16[100,512]{1,0:T(8,128)(2,1)}, bf16[100,512]{1,0:T(8,128)(2,1)S(1)}, u32[]{:S(2)}, u32[]{:S(2)}) collective-permute-start(bf16[100,512]{1,0:T(8,128)(2,1)} %win_own.1), channel_id=1, source_target_pairs={{0,1},{1,0},{2,3},{3,2},{4,5},{5,4},{6,7},{7,6},{8,9},{9,8},{10,11... | collective-permute-start | bytes 307208 | tf_op jit(solution)/shard_map/ppermute | solution.py:445
  0.7 10.2 %collective-permute-start.1 = (bf16[100,512]{1,0:T(8,128)(2,1)}, bf16[100,512]{1,0:T(8,128)(2,1)}, u32[]{:S(2)}, u32[]{:S(2)}) collective-permute-start(bf16[100,512]{1,0:T(8,128)(2,1)} %bitcast.21), channel_id=1, source_target_pairs={{0,1},{1,0},{2,3},{3,2},{4,5},{5,4},{6,7},{7,6},{8,9},{9,8},{10,11... | collective-permute-start | bytes 307208 | tf_op jit(solution)/shard_map/ppermute | solution.py:445
  1.2 16.2 %collective-permute-start.2 = (bf16[100,2048]{1,0:T(8,128)(2,1)}, bf16[100,2048]{1,0:T(8,128)(2,1)}, u32[]{:S(2)}, u32[]{:S(2)}) collective-permute-start(bf16[100,2048]{1,0:T(8,128)(2,1)} %bitcast.18), channel_id=1, source_target_pairs={{0,2},{2,4},{4,6},{6,8},{8,10},{10,12},{12,14},{14,16},{16,18},{18... | collective-permute-start | bytes 1228808 | tf_op jit(solution)/shard_map/ppermute | solution.py:452
  7.9 1.0 %copy-start.2 = (bf16[2048,100]{0,1:T(8,128)(2,1)S(1)}, bf16[2048,100]{0,1:T(8,128)(2,1)}, u32[]{:S(2)}) copy-start(bf16[2048,100]{0,1:T(8,128)(2,1)} %param.14) | copy-start | bytes 1228804
  8.9 2.0 %copy-start.4 = (bf16[100,512]{1,0:T(8,128)(2,1)S(1)}, bf16[100,512]{1,0:T(8,128)(2,1)}, u32[]{:S(2)}) copy-start(bf16[100,512]{1,0:T(8,128)(2,1)} %win_own.1) | copy-start | bytes 307204
  8.9 2.0 %copy-start.5 = (bf16[512,100]{0,1:T(8,128)(2,1)S(1)}, bf16[512,100]{0,1:T(8,128)(2,1)}, u32[]{:S(2)}) copy-start(bf16[512,100]{0,1:T(8,128)(2,1)} %param.24) | copy-start | bytes 307204
  8.9 2.0 %copy-start.6 = (s32[64,128]{1,0:T(8,128)S(1)}, s32[64,128]{1,0:T(8,128)}, u32[]{:S(2)}) copy-start(s32[64,128]{1,0:T(8,128)} %src.2) | copy-start | bytes 98308
  8.9 2.0 %copy-start.7 = (s32[64,128]{1,0:T(8,128)S(1)}, s32[64,128]{1,0:T(8,128)}, u32[]{:S(2)}) copy-start(s32[64,128]{1,0:T(8,128)} %dst.2) | copy-start | bytes 98308
  8.9 2.0 %copy-start.8 = (bf16[64,128]{1,0:T(8,128)(2,1)S(1)}, bf16[64,128]{1,0:T(8,128)(2,1)}, u32[]{:S(2)}) copy-start(bf16[64,128]{1,0:T(8,128)(2,1)} %weight.2) | copy-start | bytes 49156
  8.9 2.0 %copy-start.12 = (f32[1024]{0:T(1024)S(1)}, f32[1024]{0:T(1024)}, u32[]{:S(2)}) copy-start(f32[1024]{0:T(1024)} %param.20) | copy-start | bytes 12292
  9.1 1.0 %copy-start.14 = (f32[2048,128]{1,0:T(8,128)}, f32[2048,128]{1,0:T(8,128)S(1)}, u32[]{:S(2)}) copy-start(f32[2048,128]{1,0:T(8,128)S(1)} %turn.1.own_rows) | copy-start | bytes 3145732
  10.9 1.2 %copy-start.1 = (bf16[512,1024]{1,0:T(8,128)(2,1)S(1)}, bf16[512,1024]{1,0:T(8,128)(2,1)}, u32[]{:S(2)}) copy-start(bf16[512,1024]{1,0:T(8,128)(2,1)} %w_out.1) | copy-start | bytes 3145732
  12.1 0.7 copy-start.13
  12.8 1.2 %copy-start.15 = (f32[2048,128]{1,0:T(8,128)S(1)}, f32[2048,128]{1,0:T(8,128)}, u32[]{:S(2)}) copy-start(f32[2048,128]{1,0:T(8,128)} %copy-done.14) | copy-start | bytes 3145732
  17.4 2.1 %collective-permute-start.3 = (bf16[100,2048]{1,0:T(8,128)(2,1)}, bf16[100,2048]{1,0:T(8,128)(2,1)S(1)}, u32[]{:S(2)}, u32[]{:S(2)}) collective-permute-start(bf16[100,2048]{1,0:T(8,128)(2,1)} %collective-permute-done.2.sent), channel_id=1, source_target_pairs={{0,1},{1,0},{2,3},{3,2},{4,5},{5,4},{6,7},{7,6},{8,9},{9,8},{10,11... | collective-permute-start | bytes 1228808 | tf_op jit(solution)/shard_map/ppermute | solution.py:445
  26.9 18.6 %collective-permute-start.4 = (bf16[384,1024]{1,0:T(8,128)(2,1)S(1)}, bf16[384,1024]{1,0:T(8,128)(2,1)S(1)}, u32[]{:S(2)}, u32[]{:S(2)}) collective-permute-start(bf16[384,1024]{1,0:T(8,128)(2,1)S(1)} %get-tuple-element.42), channel_id=1, source_target_pairs={{1,2},{3,4},{5,6},{7,8},{9,10},{11,12},{13,14},{15,16},{17,18},{19... | collective-permute-start | bytes 2359304 | tf_op jit(solution)/shard_map/ppermute | solution.py:459
  28.9 3.0 %copy-start = (bf16[1024,3,512]{2,0,1:T(8,128)(2,1)S(1)}, bf16[1024,3,512]{2,0,1:T(8,128)(2,1)}, u32[]{:S(2)}) copy-start(bf16[1024,3,512]{2,0,1:T(8,128)(2,1)} %param.21) | copy-start | bytes 9437188
  36.3 9.2 %collective-permute-start.6 = (bf16[384,1024]{1,0:T(8,128)(2,1)S(1)}, bf16[384,1024]{1,0:T(8,128)(2,1)S(1)}, u32[]{:S(2)}, u32[]{:S(2)}) collective-permute-start(bf16[384,1024]{1,0:T(8,128)(2,1)S(1)} %get-tuple-element.49), channel_id=1, source_target_pairs={{0,1},{1,0},{2,3},{3,2},{4,5},{5,4},{6,7},{7,6},{8,9},{9,8},{10,11... | collective-permute-start | bytes 2359304 | tf_op jit(solution)/shard_map/ppermute | solution.py:445
  38.7 6.9 %collective-permute-start.7 = (bf16[1024,384]{1,0:T(8,128)(2,1)S(1)}, bf16[1024,384]{1,0:T(8,128)(2,1)S(1)}, u32[]{:S(2)}, u32[]{:S(2)}) collective-permute-start(bf16[1024,384]{1,0:T(8,128)(2,1)S(1)} %get-tuple-element.50), channel_id=1, source_target_pairs={{0,1},{1,0},{2,3},{3,2},{4,5},{5,4},{6,7},{7,6},{8,9},{9,8},{10,11... | collective-permute-start | bytes 2359304 | tf_op jit(solution)/shard_map/ppermute | solution.py:445
  38.9 6.6 %collective-permute-start.8 = (bf16[256,512]{1,0:T(8,128)(2,1)S(1)}, bf16[256,512]{1,0:T(8,128)(2,1)S(1)}, u32[]{:S(2)}, u32[]{:S(2)}) collective-permute-start(bf16[256,512]{1,0:T(8,128)(2,1)S(1)} %get-tuple-element.58.fold_own), channel_id=1, source_target_pairs={{0,1},{1,0},{2,3},{3,2},{4,5},{5,4},{6,7},{7,6},{8,9},{9,8},{10,11... | collective-permute-start | bytes 786440 | tf_op jit(solution)/shard_map/ppermute | solution.py:445
  45.6 15.5 %copy-start.3 = (bf16[2048,100]{0,1:T(8,128)(2,1)S(1)}, bf16[2048,100]{0,1:T(8,128)(2,1)}, u32[]{:S(2)}) copy-start(bf16[2048,100]{0,1:T(8,128)(2,1)} %param.14) | copy-start | bytes 1228804
  45.6 15.5 %copy-start.9 = (s32[24,128]{1,0:T(8,128)S(1)}, s32[24,128]{1,0:T(8,128)}, u32[]{:S(2)}) copy-start(s32[24,128]{1,0:T(8,128)} %src.3) | copy-start | bytes 36868
  45.6 15.5 %copy-start.10 = (s32[24,128]{1,0:T(8,128)S(1)}, s32[24,128]{1,0:T(8,128)}, u32[]{:S(2)}) copy-start(s32[24,128]{1,0:T(8,128)} %dst.3) | copy-start | bytes 36868
  45.6 15.5 %copy-start.11 = (bf16[24,128]{1,0:T(8,128)(2,1)S(1)}, bf16[24,128]{1,0:T(8,128)(2,1)}, u32[]{:S(2)}) copy-start(bf16[24,128]{1,0:T(8,128)(2,1)} %weight.3) | copy-start | bytes 18436
  54.0 1.4 %collective-permute-start.9 = (bf16[100,512]{1,0:T(8,128)(2,1)S(1)}, bf16[100,512]{1,0:T(8,128)(2,1)S(1)}, u32[]{:S(2)}, u32[]{:S(2)}) collective-permute-start(bf16[100,512]{1,0:T(8,128)(2,1)S(1)} %attend.1), channel_id=1, source_target_pairs={{0,1},{1,0},{2,3},{3,2},{4,5},{5,4},{6,7},{7,6},{8,9},{9,8},{10,11... | collective-permute-start | bytes 307208 | tf_op jit(solution)/shard_map/ppermute | solution.py:445
  55.4 12.8 %collective-permute-start.10 = (bf16[2,100,512]{2,1,0:T(8,128)(2,1)S(1)}, bf16[2,100,512]{2,1,0:T(8,128)(2,1)S(1)}, u32[]{:S(2)}, u32[]{:S(2)}) collective-permute-start(bf16[2,100,512]{2,1,0:T(8,128)(2,1)S(1)} %pad_maximum_fusion.own), channel_id=1, source_target_pairs={{0,2},{2,4},{4,6},{6,8},{8,10},{10,12},{12,14},{14,16},{16,18},{18... | collective-permute-start | bytes 614408 | tf_op jit(solution)/shard_map/ppermute | solution.py:452
  68.2 1.5 %collective-permute-start.11 = (bf16[2,100,512]{2,1,0:T(8,128)(2,1)S(1)}, bf16[2,100,512]{2,1,0:T(8,128)(2,1)S(1)}, u32[]{:S(2)}, u32[]{:S(2)}) collective-permute-start(bf16[2,100,512]{2,1,0:T(8,128)(2,1)S(1)} %collective-permute-done.10.sent), channel_id=1, source_target_pairs={{0,1},{1,0},{2,3},{3,2},{4,5},{5,4},{6,7},{7,6},{8,9},{9,8},{10,11... | collective-permute-start | bytes 614408 | tf_op jit(solution)/shard_map/ppermute | solution.py:445

commit v7 on v6

--- a/solution.py
+++ b/solution.py
@@ -23,11 +23,12 @@
 DEC_ROUNDS = 3
 DEC_TILES = 8
 GROUP = 2
+EARLY = 3
 MASKED = -1e30
 SCALE = 64 ** (-0.5) * math.log2(math.e)
 F32 = jnp.float32
 BF16 = jnp.bfloat16
-VMEM_BYTES = 20 * 1024 * 1024
+MIB = 1024 * 1024
 
 
 def vmem():
@@ -38,7 +39,7 @@
     return pl.BlockSpec(memory_space=pltpu.SMEM)
 
 
-def call(body, operands, smem_count, outs, scratch, flops, touched, name, aliases={}):
+def call(body, operands, smem_count, outs, scratch, flops, room, name, aliases={}):
     specs = [smem()] * smem_count + [vmem()] * (len(operands) - smem_count)
     return pl.pallas_call(
         body,
@@ -46,8 +47,8 @@
         in_specs=specs,
         out_specs=jax.tree.map(lambda _: vmem(), outs),
         scratch_shapes=scratch,
-        compiler_params=pltpu.CompilerParams(vmem_limit_bytes=VMEM_BYTES),
-        cost_estimate=pl.CostEstimate(flops=flops, bytes_accessed=touched, transcendentals=0),
+        compiler_params=pltpu.CompilerParams(vmem_limit_bytes=room * MIB),
+        cost_estimate=pl.CostEstimate(flops=flops, bytes_accessed=2 * 10 ** 6, transcendentals=0),
         input_output_aliases=aliases,
         name=name,
     )(*operands)
@@ -81,26 +82,7 @@
         wide[:C, HALF:] = own[...].astype(F32)
 
 
-def turn_body(grid, own_rows, wide):
-    wide[...] = jnp.zeros_like(wide)
-    to_rows(grid, wide, own_rows, 0)
-
-
-def prepare_body(
-    info, offsets, own_rows, src, dst, weight, gain, win_own, win_peer, dec_own, dec_peer, w_out,
-    mask, sources, targets, weights, gains, w_in, w_decode, fold,
-    w_wide,
-):
-    core, live, mesh_base = info[0], info[1], info[3]
-    w_wide[...] = jnp.zeros_like(w_wide)
-    by_core(core, w_wide, win_own, win_peer)
-    w_in[...] = (w_wide[...] * 0.5).astype(BF16)
-    by_core(core, w_wide, dec_own, dec_peer)
-    w_decode[...] = w_wide[...].astype(BF16)
-    folded = matmul_t(w_decode[...], w_out[...])
-    upper = folded.astype(BF16)
-    fold[:LANES, :] = upper
-    fold[LANES:, :] = (folded - upper.astype(F32)).astype(BF16)
+def mask_body(offsets, mask):
     for chunk in range(SPAN // TILE):
         row = lax.broadcasted_iota(jnp.int32, (TILE, LANES), 0) + (chunk * TILE - WIN)
         away = row - lax.broadcasted_iota(jnp.int32, (TILE, LANES), 1)
@@ -108,6 +90,19 @@
         for k in range(1, K_OFF):
             hit = hit | (away == offsets[k])
         mask[chunk * TILE : (chunk + 1) * TILE, :] = jnp.where(hit, 0.0, MASKED).astype(BF16)
+
+
+def prepare_body(
+    info, mask, src, dst, weight, gain, win_own, win_peer, dec_own, dec_peer,
+    sources, targets, weights, gains, w_in, w_decode,
+    w_wide,
+):
+    core, live, mesh_base = info[0], info[1], info[3]
+    w_wide[...] = jnp.zeros_like(w_wide)
+    by_core(core, w_wide, win_own, win_peer)
+    w_in[...] = (w_wide[...] * 0.5).astype(BF16)
+    by_core(core, w_wide, dec_own, dec_peer)
+    w_decode[...] = w_wide[...].astype(BF16)
     slots = lax.broadcasted_iota(jnp.int32, weights.shape, 0)
     weights[...] = jnp.where(slots < live, weight[...].astype(F32), 0.0)
     targets[...] = dst[...] - mesh_base
@@ -115,9 +110,13 @@
     gains[...] = gain[...]
 
 
-def unpack_body(info, own_rows, sent, rows, wide):
+def unpack_body(info, grid, sent, w_out, w_decode, rows, fold, wide):
+    folded = matmul_t(w_decode[...], w_out[...])
+    upper = folded.astype(BF16)
+    fold[:LANES, :] = upper
+    fold[LANES:, :] = (folded - upper.astype(F32)).astype(BF16)
     wide[...] = jnp.zeros_like(wide)
-    rows[G_BAND : 2 * G_BAND, :] = own_rows[...]
+    to_rows(grid, wide, rows, G_BAND)
     to_rows(sent, wide, rows, info[0] * 2 * G_BAND)
 
 
@@ -392,8 +391,8 @@
     return matmul(part, spread[rows, :])
 
 
-def spread_body(info, own, src, dst, weight, grid, spread, base, sources, tables, weights):
-    core, mesh_base, row_base = info[0], info[6], info[7]
+def spread_halves(info, src, dst, weight, spread, sources, tables, weights, places):
+    mesh_base, row_base = info[6], info[7]
     sources[...] = src[...] - mesh_base
     weights[...] = weight[...].astype(F32)
     row_slots = lax.broadcasted_iota(jnp.int32, (TILE, LANES), 0)
@@ -419,7 +418,18 @@
             ).astype(BF16)
         return carry
 
-    lax.fori_loop(0, 6, half, 0)
+    lax.fori_loop(places[0], places[-1] + 1, half, 0)
+
+
+def early_body(info, w_in, src, dst, weight, spread, sources, tables, weights):
+    spread_halves(info, src, dst, weight, spread, sources, tables, weights, range(EARLY))
+
+
+def spread_body(
+    info, spread_in, own, src, dst, weight, grid, spread, base, sources, tables, weights
+):
+    core = info[0]
+    spread_halves(info, src, dst, weight, spread, sources, tables, weights, range(EARLY, 6))
     fields = grid[:, pl.ds(pl.multiple_of(core * GQ, GQ), GQ)].astype(F32)
     terms = half_term(own[0], spread, 2 + core) + half_term(own[1], spread, 3 - core)
     base[...] = fields + terms
@@ -485,39 +495,50 @@
     qkv_own = w_qkv.transpose(1, 0, 2)
     qkv_peer = swapped(qkv_own)
     edges = jax.ShapeDtypeStruct(enc_src.shape, jnp.int32)
-    own_rows = call(
-        turn_body, (grid,), 0, jax.ShapeDtypeStruct((G_BAND, LANES), F32),
-        [pltpu.VMEM((LANES, G_BAND), F32)], 5 * 10 ** 9, 2 * 10 ** 6, "turn",
-    )
-    mask, sources, targets, weights, gain, w_in_all, dec_all, fold_own = call(
+    mask = call(
+        mask_body, (offsets,), 1, jax.ShapeDtypeStruct((SPAN, TILE), BF16), [],
+        5 * 10 ** 9, 4, "mask",
+    )
+    sources, targets, weights, gain, w_in_all, dec_all = call(
         prepare_body,
-        (info, offsets, own_rows, enc_src, enc_dst, enc_weight, norm_gain.reshape(1, D), w_in,
-         win_peer, dec_own, dec_peer, w_out_attn),
-        2,
+        (info, mask, enc_src, enc_dst, enc_weight, norm_gain.reshape(1, D), w_in, win_peer,
+         dec_own, dec_peer),
+        1,
         [
-            jax.ShapeDtypeStruct((SPAN, TILE), BF16),
             edges,
             edges,
             jax.ShapeDtypeStruct(enc_weight.shape, F32),
             jax.ShapeDtypeStruct((1, D), F32),
             jax.ShapeDtypeStruct((LANES, D), BF16),
             jax.ShapeDtypeStruct((LANES, D), BF16),
+        ],
+        [pltpu.VMEM((LANES, D), F32)],
+        5 * 10 ** 9, 6, "prepare",
+    )
+    spread_out = jax.ShapeDtypeStruct((6 * ROWS, GQ), BF16)
+    spread_scratch = [
+        pltpu.VMEM(dec_src.shape, jnp.int32),
+        pltpu.VMEM((GQ, DEC_ROUNDS * TILE), BF16),
+        pltpu.VMEM(dec_weight.shape, F32),
+    ]
+    spread = call(
+        early_body, (info, w_in_all, dec_src, dec_dst, dec_weight), 1, spread_out,
+        spread_scratch, 5 * 10 ** 9, 10, "early",
+    )
+    grid_sent, w_in_all, spread = lax.optimization_barrier((grid_sent, w_in_all, spread))
+    grid_swapped = swapped(grid_sent)
+    grid_rows, fold_own = call(
+        unpack_body,
+        (info, grid, grid_sent, w_out_attn, dec_all),
+        1,
+        [
+            jax.ShapeDtypeStruct((3 * G_BAND, LANES), F32),
             jax.ShapeDtypeStruct((2 * LANES, HALF), BF16),
         ],
-        [pltpu.VMEM((LANES, D), F32)],
-        8 * 10 ** 9, 2 * 10 ** 6, "prepare",
+        [pltpu.VMEM((LANES, G_BAND), F32)],
+        2 * 10 ** 9, 6, "unpack",
     )
     fold_peer = swapped(fold_own)
-    grid_sent, own_rows, w_in_all = lax.optimization_barrier((grid_sent, own_rows, w_in_all))
-    grid_swapped = swapped(grid_sent)
-    grid_rows = call(
-        unpack_body,
-        (info, own_rows, grid_sent),
-        1,
-        jax.ShapeDtypeStruct((3 * G_BAND, LANES), F32),
-        [pltpu.VMEM((LANES, G_BAND), F32)],
-        2 * 10 ** 9, 2 * 10 ** 6, "unpack",
-    )
     band_rows = jax.ShapeDtypeStruct((ROWS, D), BF16)
     step_buffers = [pltpu.VMEM((STEP, LANES), F32)] * 2 + [pltpu.VMEM((ROWS, D), F32)]
     grid_rows, mesh_zero, normed, to_band = call(
@@ -531,7 +552,7 @@
             jax.ShapeDtypeStruct((WIN, D), BF16),
         ],
         [pltpu.VMEM((LANES, G_BAND), F32)] + step_buffers,
-        7 * 10 ** 9, 4 * 10 ** 6, "encode", {2: 0},
+        7 * 10 ** 9, 14, "encode", {2: 0},
     )
     halo_band = over_the_edge(to_band)
     mesh_zero, normed = call(
@@ -540,7 +561,7 @@
         2,
         [band_rows, band_rows],
         step_buffers,
-        3 * 10 ** 9, 4 * 10 ** 6, "last", {7: 0, 8: 1},
+        3 * 10 ** 9, 14, "last", {7: 0, 8: 1},
     )
     queries, keys, values_t, keys_sent, values_sent, straight = call(
         project_body,
@@ -555,7 +576,7 @@
             jax.ShapeDtypeStruct((LANES, ROWS), F32),
         ],
         [],
-        6 * 10 ** 9, 10 ** 7, "project",
+        6 * 10 ** 9, 10, "project",
     )
     peer_keys, peer_values = swapped(keys_sent), swapped(values_sent)
     sums, stats = call(
@@ -567,7 +588,7 @@
             jax.ShapeDtypeStruct((D // LANES, 8, 2 * ROWS), F32),
         ],
         [pltpu.VMEM((ROWS, 2 * GROUP * TILE), F32)] * 2,
-        8 * 10 ** 9, 10 ** 7, "own",
+        8 * 10 ** 9, 12, "own",
     )
     projected = call(
         attend_body,
@@ -583,35 +604,27 @@
             pltpu.VMEM((WIN, 2 * GROUP * TILE), F32),
             pltpu.VMEM((WIN, 2 * GROUP * TILE), F32),
         ],
-        10 ** 10, 2 * 10 ** 7, "attend",
+        10 ** 10, 16, "attend",
     )
     own_pair = jnp.stack([projected, swapped(projected)])
     pair_sent = up_and_down(own_pair)
     spread, base = call(
         spread_body,
-        (info, own_pair, dec_src, dec_dst, dec_weight, grid),
+        (info, spread, own_pair, dec_src, dec_dst, dec_weight, grid),
         1,
-        [
-            jax.ShapeDtypeStruct((6 * ROWS, GQ), BF16),
-            jax.ShapeDtypeStruct((C, GQ), F32),
-        ],
-        [
-            pltpu.VMEM(dec_src.shape, jnp.int32),
-            pltpu.VMEM((GQ, DEC_ROUNDS * TILE), BF16),
-            pltpu.VMEM(dec_weight.shape, F32),
-        ],
-        8 * 10 ** 9, 2 * 10 ** 6, "spread",
+        [spread_out, jax.ShapeDtypeStruct((C, GQ), F32)],
+        spread_scratch, 8 * 10 ** 9, 10, "spread", {1: 0},
     )
     pair_sent, base = lax.optimization_barrier((pair_sent, base))
     pair_swapped = swapped(pair_sent)
     sums_out = jax.ShapeDtypeStruct((C, GQ), F32)
     total = call(
         sent_body, (info, pair_sent, spread, base), 1, sums_out, [],
-        10 ** 9, 3 * 10 ** 6, "sent",
+        10 ** 9, 6, "sent",
     )
     return call(
         decode_body, (info, pair_swapped, spread, total), 1,
-        jax.ShapeDtypeStruct((C, GQ), BF16), [], 10 ** 9, 3 * 10 ** 6, "decode",
+        jax.ShapeDtypeStruct((C, GQ), BF16), [], 10 ** 9, 6, "decode",
     ).T
 
 

time: 71.7 us -> 70.7 us (0.986)
  local copies, waits for them, and re-layouts: 5.22 us -> 2.4 us
  starting transfers between devices: 18.8 us -> 20.3 us
  Pallas kernels: 44.1 us -> 44.9 us
    unnamed x32, local copies, waits for them, and re-layouts: 5.13 us -> 2.32 us
    ppermute x2, starting transfers between devices: 12.3 us -> 13.1 us  [up_and_down(): return lax.ppermute(value, ('band', 'mp'), pairs)]
    pallas_call x11 -> x12, Pallas kernels: 44.1 us -> 44.9 us  [call(): pl.pallas_call(body, out_shape=outs, in_specs=specs, out_specs=jax.tree.m...]
  transfers between devices with their start and end apart: 12 -> 12, of which waited for: 3 -> 3; matrix products, arithmetic and copies ran while one was open for 0% -> 0% of each run, Pallas kernels for 48% -> 50%
where the time goes in v7:
time: 70.7 us; the launch traced here: 70.4 us
  Pallas kernels  44.9 us (64%)
  starting transfers between devices  20.3 us (29%)
  local copies, waits for them, and re-layouts  2.4 us (3%)
  waiting for transfers between devices  1.73 us (2%)
  between operations  1.03 us (1%)
    pallas_call x12, Pallas kernels, call(): pl.pallas_call(body, out_shape=outs, in_specs=specs, out_specs=jax.tree.m...  44.9 us
    ppermute x2, starting transfers between devices, up_and_down(): return lax.ppermute(value, ('band', 'mp'), pairs)  13.1 us
    ppermute x9, starting transfers between devices, swapped(): return lax.ppermute(value, 'mp', [(0, 1), (1, 0)])  5.11 us
    unnamed x32, local copies, waits for them, and re-layouts  2.32 us
    ppermute x1, starting transfers between devices, over_the_edge(): return lax.ppermute(value, ('band', 'mp'), pairs)  2.1 us
    ppermute x9, waiting for transfers between devices, swapped(): return lax.ppermute(value, 'mp', [(0, 1), (1, 0)])  1.72 us
  transfers between devices with their start and end apart: 12, of which 3 were waited for; matrix products, arithmetic and copies ran while one was open for 0% of the time, Pallas kernels for 50%

profile of v7, /device:TPU:97, one launch (start us, length us, event | category | flops | bytes accessed | tf_op | source)
XLA Modules:
  0.0 70.4 jit_solution(15577615683920877409)
XLA Ops:
  0.0 0.7 collective-permute-start.5
  0.7 0.0 collective-permute-start
  0.7 0.5 collective-permute-start.1
  1.2 0.0 copy-start.7
  1.2 0.0 copy-start.11
  1.2 6.8 %collective-permute-start.2 = (bf16[100,2048]{1,0:T(8,128)(2,1)}, bf16[100,2048]{1,0:T(8,128)(2,1)}, u32[]{:S(2)}, u32[]{:S(2)}) collective-permute-start(bf16[100,2048]{1,0:T(8,128)(2,1)} %bitcast.18), channel_id=1, source_target_pairs={{0,2},{2,4},{4,6},{6,8},{8,10},{10,12},{12,14},{14,16},{16,18},{18... | collective-permute-start | bytes 1228808 | tf_op jit(solution)/shard_map/ppermute | solution.py:462
  8.0 0.0 copy-start.12
  8.0 0.6 copy-done.12
  8.7 2.4 %mask.1 = bf16[896,128]{1,0:T(8,128)(2,1)S(1)} custom-call(s32[32]{0:T(128)S(1)} %copy-done.12), custom_call_target="tpu_custom_call" | custom-call | flops 5000000000 | bytes 2000000 | tf_op jit(solution)/shard_map/mask/pallas_call | solution.py:44
  11.1 0.7 copy-done.13
  12.4 0.1 stack.48.info
  12.5 0.0 collective-permute-done.win_peer
  12.5 0.0 collective-permute-done.1.dec_peer
  12.6 0.9 %copy-done.14 = bf16[896,128]{1,0:T(8,128)(2,1)S(1)} copy-done((bf16[896,128]{1,0:T(8,128)(2,1)S(1)}, bf16[896,128]{1,0:T(8,128)(2,1)}, u32[]{:S(2)}) %copy-start.14) | copy-done | bytes 229400
  13.5 1.1 %prepare.1 = (s32[64,128]{1,0:T(8,128)S(1)}, s32[64,128]{1,0:T(8,128)S(1)}, f32[64,128]{1,0:T(8,128)S(1)}, f32[1,1024]{1,0:T(1,128)S(1)}, bf16[128,1024]{1,0:T(8,128)(2,1)S(1)}, /*index=5*/bf16[128,1024]{1,0:T(8,128)(2,1)S(1)}) custom-call(s32[8]{0:T(128)S(1)} %stack.48.info, bf16[896,128]{1,0:T(8,128)(2,1)S(1)} %copy-done.14, s32[64,128]{1,0:T(8,128)S(1)} %copy-done.5, ...), custom_call_target="tpu_custom_call" | custom-call | flops 5000000000 | bytes 2000000 | tf_op jit(solution)/shard_map/prepare/pallas_call | solution.py:44
  14.6 0.0 copy-done.8
  14.6 0.0 copy-done.9
  14.7 0.0 copy-start.1
  14.7 0.0 copy-start.2
  14.7 3.7 %early.1.spread_in = bf16[3072,1024]{1,0:T(8,128)(2,1)S(1)} custom-call(s32[8]{0:T(128)S(1)} %stack.48.info, bf16[128,1024]{1,0:T(8,128)(2,1)S(1)} %get-tuple-element.39.w_in, s32[24,128]{1,0:T(8,128)S(1)} %copy-done.8, s32[24,128]{1,0:T(8,128)S(1)} %copy-done.9, bf16[24,128]{1,0:T(8,128)(2,1)S(1)} %copy-done.10), custom_call_target="tpu_custom_call" | custom-call | flops 5000000000 | bytes 2000000 | tf_op jit(solution)/shard_map/early/pallas_call | solution.py:44
  18.4 0.0 collective-permute-done.2.sent
  18.4 0.1 collective-permute-start.3
  18.5 1.5 %unpack.1 = (f32[6144,128]{1,0:T(8,128)S(1)}, bf16[256,512]{1,0:T(8,128)(2,1)S(1)}) custom-call(s32[8]{0:T(128)S(1)} %stack.48.info, bf16[100,2048]{1,0:T(8,128)(2,1)S(1)} %bitcast.19, bf16[100,2048]{1,0:T(8,128)(2,1)} %collective-permute-done.2.sent, bf16[512,1024]{1,0:T(8,128)(2,1)S(1)} %copy-done.1, bf16[128,1024]{1,0:T(8,128)(2,1)S(1)} %get-tuple-element.37.w_decode), custom_call_target="tpu_custom_call" | custom-call | flops 2000000000 | bytes 2000000 | tf_op jit(solution)/shard_map/unpack/pallas_call | solution.py:44
  20.1 0.4 collective-permute-done.3.swapped_rows
  20.4 7.5 %encode.1 = (f32[6144,128]{1,0:T(8,128)S(1)}, bf16[512,1024]{1,0:T(8,128)(2,1)S(1)}, bf16[512,1024]{1,0:T(8,128)(2,1)S(1)}, bf16[384,1024]{1,0:T(8,128)(2,1)S(1)}) custom-call(s32[8]{0:T(128)S(1)} %stack.48.info, s32[64,128]{1,0:T(8,128)S(1)} %get-tuple-element.34.src, f32[6144,128]{1,0:T(8,128)S(1)} %get-tuple-element.38.grid_rows, ...), custom_call_target="tpu_custom_call", output_to_operand_aliasing={{0}: (2, {})} | custom-call | flops 7000000000 | bytes 2000000 | tf_op jit(solution)/shard_map/encode/pallas_call | solution.py:44
  27.9 2.1 %collective-permute-start.4 = (bf16[384,1024]{1,0:T(8,128)(2,1)S(1)}, bf16[384,1024]{1,0:T(8,128)(2,1)S(1)}, u32[]{:S(2)}, u32[]{:S(2)}) collective-permute-start(bf16[384,1024]{1,0:T(8,128)(2,1)S(1)} %get-tuple-element.43), channel_id=1, source_target_pairs={{1,2},{3,4},{5,6},{7,8},{9,10},{11,12},{13,14},{15,16},{17,18},{19... | collective-permute-start | bytes 2359304 | tf_op jit(solution)/shard_map/ppermute | solution.py:469
  30.0 0.0 copy-start
  30.0 3.0 %last.1 = (bf16[512,1024]{1,0:T(8,128)(2,1)S(1)}, bf16[512,1024]{1,0:T(8,128)(2,1)S(1)}) custom-call(s32[8]{0:T(128)S(1)} %stack.48.info, s32[64,128]{1,0:T(8,128)S(1)} %get-tuple-element.34.src, f32[6144,128]{1,0:T(8,128)S(1)} %get-tuple-element.44.rows, ...), custom_call_target="tpu_custom_call", output_to_operand_aliasing={{0}: (7, {}), {1}: (8, {})} | custom-call | flops 3000000000 | bytes 2000000 | tf_op jit(solution)/shard_map/last/pallas_call | solution.py:44
  33.0 0.0 collective-permute-done.5.w_peer
  33.1 4.4 %project.1 = (bf16[512,1024]{1,0:T(8,128)(2,1)S(1)}, bf16[512,1024]{1,0:T(8,128)(2,1)S(1)}, bf16[1024,512]{1,0:T(8,128)(2,1)S(1)}, bf16[384,1024]{1,0:T(8,128)(2...) custom-call(s32[8]{0:T(128)S(1)} %stack.48.info, bf16[512,1024]{1,0:T(8,128)(2,1)S(1)} %get-tuple-element.47.normed, ...), custom_call_target="tpu_custom_call" | custom-call | flops 6000000000 | bytes 2000000 | tf_op jit(solution)/shard_map/project/pallas_call | solution.py:44
  37.5 1.5 %collective-permute-start.6 = (bf16[384,1024]{1,0:T(8,128)(2,1)S(1)}, bf16[384,1024]{1,0:T(8,128)(2,1)S(1)}, u32[]{:S(2)}, u32[]{:S(2)}) collective-permute-start(bf16[384,1024]{1,0:T(8,128)(2,1)S(1)} %get-tuple-element.49), channel_id=1, source_target_pairs={{0,1},{1,0},{2,3},{3,2},{4,5},{5,4},{6,7},{7,6},{8,9},{9,8},{10,11... | collective-permute-start | bytes 2359304 | tf_op jit(solution)/shard_map/ppermute | solution.py:455
  39.0 0.1 collective-permute-start.7
  39.1 0.4 collective-permute-start.8
  39.5 6.2 %own.1 = (f32[1024,512]{1,0:T(8,128)S(1)}, f32[8,8,1024]{2,1,0:T(8,128)S(1)}) custom-call(bf16[512,1024]{1,0:T(8,128)(2,1)S(1)} %get-tuple-element.51.queries, bf16[512,1024]{1,0:T(8,128)(2,1)S(1)} %get-tuple-element.52.keys, bf16[1024,512]{1,0:T(8,128)(2,1)S(1)} %get-tuple-element.53.values_t, bf16[896,128]{1,0:T(8,128)(2,1)S(1)} %copy-done.15), custom_call_target="tpu_custom_call" | custom-call | flops 8000000000 | bytes 2000000 | tf_op jit(solution)/shard_map/own/pallas_call | solution.py:44
  45.7 0.0 collective-permute-done.8.fold_peer
  45.8 0.0 collective-permute-done.4.halo
  45.8 0.0 collective-permute-done.6.peer_keys
  45.8 0.0 collective-permute-done.7.peer_values
  45.8 8.3 %attend.1 = bf16[100,512]{1,0:T(8,128)(2,1)S(1)} custom-call(s32[8]{0:T(128)S(1)} %stack.48.info, bf16[384,1024]{1,0:T(8,128)(2,1)S(1)} %collective-permute-done.4.halo, bf16[384,1024]{1,0:T(8,128)(2,1)S(1)} %collective-permute-done.6.peer_keys, bf16[1024,384]{1,0:T(8,128)(2,1)S(1)} %collective-permute-done.7.peer_values, ...), custom_call_target="tpu_custom_call" | custom-call | flops 10000000000 | bytes 2000000 | tf_op jit(solution)/shard_map/attend/pallas_call | solution.py:44
  54.1 0.2 collective-permute-start.9
  54.3 1.2 %collective-permute-done.9 = bf16[100,512]{1,0:T(8,128)(2,1)S(1)} collective-permute-done((bf16[100,512]{1,0:T(8,128)(2,1)S(1)}, bf16[100,512]{1,0:T(8,128)(2,1)S(1)}, u32[]{:S(2)}, u32[]{:S(2)}) %collective-permute-start.9) | collective-permute-done | bytes 102432 | tf_op jit(solution)/shard_map/ppermute | solution.py:455
  55.5 6.3 %collective-permute-start.10 = (bf16[2,100,512]{2,1,0:T(8,128)(2,1)S(1)}, bf16[2,100,512]{2,1,0:T(8,128)(2,1)S(1)}, u32[]{:S(2)}, u32[]{:S(2)}) collective-permute-start(bf16[2,100,512]{2,1,0:T(8,128)(2,1)S(1)} %pad_maximum_fusion.own), channel_id=1, source_target_pairs={{0,2},{2,4},{4,6},{6,8},{8,10},{10,12},{12,14},{14,16},{16,18},{18... | collective-permute-start | bytes 614408 | tf_op jit(solution)/shard_map/ppermute | solution.py:462
  61.8 4.1 %spread.1 = (bf16[3072,1024]{1,0:T(8,128)(2,1)S(1)}, f32[100,1024]{1,0:T(8,128)S(1)}) custom-call(s32[8]{0:T(128)S(1)} %stack.48.info, bf16[3072,1024]{1,0:T(8,128)(2,1)S(1)} %early.1.spread_in, bf16[2,100,512]{2,1,0:T(8,128)(2,1)S(1)} %pad_maximum_fusion.own, s32[24,128]{1,0:T(8,128)S(1)} %copy-done.8, ...), custom_call_target="tpu_custom_call", output_to_operand_aliasing={{0}: (1, {})} | custom-call | flops 8000000000 | bytes 2000000 | tf_op jit(solution)/shard_map/spread/pallas_call | solution.py:44
  66.0 0.0 collective-permute-done.10.sent
  66.0 1.7 %collective-permute-start.11 = (bf16[2,100,512]{2,1,0:T(8,128)(2,1)S(1)}, bf16[2,100,512]{2,1,0:T(8,128)(2,1)S(1)}, u32[]{:S(2)}, u32[]{:S(2)}) collective-permute-start(bf16[2,100,512]{2,1,0:T(8,128)(2,1)S(1)} %collective-permute-done.10.sent), channel_id=1, source_target_pairs={{0,1},{1,0},{2,3},{3,2},{4,5},{5,4},{6,7},{7,6},{8,9},{9,8},{10,11... | collective-permute-start | bytes 614408 | tf_op jit(solution)/shard_map/ppermute | solution.py:455
  67.6 1.0 %sent.1.total = f32[100,1024]{1,0:T(8,128)S(1)} custom-call(s32[8]{0:T(128)S(1)} %stack.48.info, bf16[2,100,512]{2,1,0:T(8,128)(2,1)S(1)} %collective-permute-done.10.sent, bf16[3072,1024]{1,0:T(8,128)(2,1)S(1)} %get-tuple-element.61.spread, f32[100,1024]{1,0:T(8,128)S(1)} %get-tuple-element.62.base), custom_call_target="tpu_custom_call" | custom-call | flops 1000000000 | bytes 2000000 | tf_op jit(solution)/shard_map/sent/pallas_call | solution.py:44
  68.6 0.1 collective-permute-done.11.swapped_rows
  68.7 1.7 %decode.1 = bf16[100,1024]{1,0:T(8,128)(2,1)} custom-call(s32[8]{0:T(128)S(1)} %stack.48.info, bf16[2,100,512]{2,1,0:T(8,128)(2,1)S(1)} %collective-permute-done.11.swapped_rows, bf16[3072,1024]{1,0:T(8,128)(2,1)S(1)} %get-tuple-element.61.spread, f32[100,1024]{1,0:T(8,128)S(1)} %sent.1.total), custom_call_target="tpu_custom_call" | custom-call | flops 1000000000 | bytes 2000000 | tf_op jit(solution)/shard_map/decode/pallas_call | solution.py:44
  (22 shorter events, 0.1 us)
Async XLA Ops:
  0.0 33.1 %collective-permute-start.5 = (bf16[3,1024,512]{2,1,0:T(8,128)(2,1)}, bf16[3,1024,512]{2,1,0:T(8,128)(2,1)S(1)}, u32[]{:S(2)}, u32[]{:S(2)}) collective-permute-start(bf16[3,1024,512]{2,1,0:T(8,128)(2,1)} %bitcast.15), channel_id=1, source_target_pairs={{0,1},{1,0},{2,3},{3,2},{4,5},{5,4},{6,7},{7,6},{8,9},{9,8},{10,11... | collective-permute-start | bytes 9437192 | tf_op jit(solution)/shard_map/ppermute | solution.py:455
  0.7 11.8 %collective-permute-start = (bf16[100,512]{1,0:T(8,128)(2,1)}, bf16[100,512]{1,0:T(8,128)(2,1)S(1)}, u32[]{:S(2)}, u32[]{:S(2)}) collective-permute-start(bf16[100,512]{1,0:T(8,128)(2,1)} %win_own.1), channel_id=1, source_target_pairs={{0,1},{1,0},{2,3},{3,2},{4,5},{5,4},{6,7},{7,6},{8,9},{9,8},{10,11... | collective-permute-start | bytes 307208 | tf_op jit(solution)/shard_map/ppermute | solution.py:455
  0.7 11.8 %collective-permute-start.1 = (bf16[100,512]{1,0:T(8,128)(2,1)}, bf16[100,512]{1,0:T(8,128)(2,1)}, u32[]{:S(2)}, u32[]{:S(2)}) collective-permute-start(bf16[100,512]{1,0:T(8,128)(2,1)} %bitcast.21), channel_id=1, source_target_pairs={{0,1},{1,0},{2,3},{3,2},{4,5},{5,4},{6,7},{7,6},{8,9},{9,8},{10,11... | collective-permute-start | bytes 307208 | tf_op jit(solution)/shard_map/ppermute | solution.py:455
  1.2 11.3 %copy-start.3 = (bf16[100,512]{1,0:T(8,128)(2,1)S(1)}, bf16[100,512]{1,0:T(8,128)(2,1)}, u32[]{:S(2)}) copy-start(bf16[100,512]{1,0:T(8,128)(2,1)} %win_own.1) | copy-start | bytes 307204
  1.2 11.3 %copy-start.4 = (bf16[512,100]{0,1:T(8,128)(2,1)S(1)}, bf16[512,100]{0,1:T(8,128)(2,1)}, u32[]{:S(2)}) copy-start(bf16[512,100]{0,1:T(8,128)(2,1)} %param.24) | copy-start | bytes 307204
  1.2 11.4 %copy-start.5 = (s32[64,128]{1,0:T(8,128)S(1)}, s32[64,128]{1,0:T(8,128)}, u32[]{:S(2)}) copy-start(s32[64,128]{1,0:T(8,128)} %src.3) | copy-start | bytes 98308
  1.2 11.4 %copy-start.6 = (s32[64,128]{1,0:T(8,128)S(1)}, s32[64,128]{1,0:T(8,128)}, u32[]{:S(2)}) copy-start(s32[64,128]{1,0:T(8,128)} %dst.3) | copy-start | bytes 98308
  1.2 11.4 %copy-start.7 = (bf16[64,128]{1,0:T(8,128)(2,1)S(1)}, bf16[64,128]{1,0:T(8,128)(2,1)}, u32[]{:S(2)}) copy-start(bf16[64,128]{1,0:T(8,128)(2,1)} %weight.3) | copy-start | bytes 49156
  1.2 11.4 %copy-start.11 = (f32[1024]{0:T(1024)S(1)}, f32[1024]{0:T(1024)}, u32[]{:S(2)}) copy-start(f32[1024]{0:T(1024)} %param.20) | copy-start | bytes 12292
  1.2 17.2 %collective-permute-start.2 = (bf16[100,2048]{1,0:T(8,128)(2,1)}, bf16[100,2048]{1,0:T(8,128)(2,1)}, u32[]{:S(2)}, u32[]{:S(2)}) collective-permute-start(bf16[100,2048]{1,0:T(8,128)(2,1)} %bitcast.18), channel_id=1, source_target_pairs={{0,2},{2,4},{4,6},{6,8},{8,10},{10,12},{12,14},{14,16},{16,18},{18... | collective-permute-start | bytes 1228808 | tf_op jit(solution)/shard_map/ppermute | solution.py:462
  8.0 0.7 copy-start.12
  11.1 0.7 copy-start.13
  12.6 0.9 %copy-start.14 = (bf16[896,128]{1,0:T(8,128)(2,1)S(1)}, bf16[896,128]{1,0:T(8,128)(2,1)}, u32[]{:S(2)}) copy-start(bf16[896,128]{1,0:T(8,128)(2,1)} %copy-done.13) | copy-start | bytes 688132
  13.5 1.1 %copy-start.8 = (s32[24,128]{1,0:T(8,128)S(1)}, s32[24,128]{1,0:T(8,128)}, u32[]{:S(2)}) copy-start(s32[24,128]{1,0:T(8,128)} %src.5) | copy-start | bytes 36868
  13.5 1.1 %copy-start.9 = (s32[24,128]{1,0:T(8,128)S(1)}, s32[24,128]{1,0:T(8,128)}, u32[]{:S(2)}) copy-start(s32[24,128]{1,0:T(8,128)} %dst.5) | copy-start | bytes 36868
  13.5 1.1 %copy-start.10 = (bf16[24,128]{1,0:T(8,128)(2,1)S(1)}, bf16[24,128]{1,0:T(8,128)(2,1)}, u32[]{:S(2)}) copy-start(bf16[24,128]{1,0:T(8,128)(2,1)} %weight.5) | copy-start | bytes 18436
  14.7 3.8 %copy-start.1 = (bf16[512,1024]{1,0:T(8,128)(2,1)S(1)}, bf16[512,1024]{1,0:T(8,128)(2,1)}, u32[]{:S(2)}) copy-start(bf16[512,1024]{1,0:T(8,128)(2,1)} %w_out.1) | copy-start | bytes 3145732
  14.7 3.8 %copy-start.2 = (bf16[2048,100]{0,1:T(8,128)(2,1)S(1)}, bf16[2048,100]{0,1:T(8,128)(2,1)}, u32[]{:S(2)}) copy-start(bf16[2048,100]{0,1:T(8,128)(2,1)} %param.14) | copy-start | bytes 1228804
  18.4 2.1 %collective-permute-start.3 = (bf16[100,2048]{1,0:T(8,128)(2,1)}, bf16[100,2048]{1,0:T(8,128)(2,1)S(1)}, u32[]{:S(2)}, u32[]{:S(2)}) collective-permute-start(bf16[100,2048]{1,0:T(8,128)(2,1)} %collective-permute-done.2.sent), channel_id=1, source_target_pairs={{0,1},{1,0},{2,3},{3,2},{4,5},{5,4},{6,7},{7,6},{8,9},{9,8},{10,11... | collective-permute-start | bytes 1228808 | tf_op jit(solution)/shard_map/ppermute | solution.py:455
  27.9 17.8 %collective-permute-start.4 = (bf16[384,1024]{1,0:T(8,128)(2,1)S(1)}, bf16[384,1024]{1,0:T(8,128)(2,1)S(1)}, u32[]{:S(2)}, u32[]{:S(2)}) collective-permute-start(bf16[384,1024]{1,0:T(8,128)(2,1)S(1)} %get-tuple-element.43), channel_id=1, source_target_pairs={{1,2},{3,4},{5,6},{7,8},{9,10},{11,12},{13,14},{15,16},{17,18},{19... | collective-permute-start | bytes 2359304 | tf_op jit(solution)/shard_map/ppermute | solution.py:469
  30.0 3.0 %copy-start = (bf16[1024,3,512]{2,0,1:T(8,128)(2,1)S(1)}, bf16[1024,3,512]{2,0,1:T(8,128)(2,1)}, u32[]{:S(2)}) copy-start(bf16[1024,3,512]{2,0,1:T(8,128)(2,1)} %param.21) | copy-start | bytes 9437188
  33.1 6.5 %copy-start.15 = (bf16[896,128]{1,0:T(8,128)(2,1)S(1)}, bf16[896,128]{1,0:T(8,128)(2,1)}, u32[]{:S(2)}) copy-start(bf16[896,128]{1,0:T(8,128)(2,1)} %copy-done.13) | copy-start | bytes 688132
  37.5 8.3 %collective-permute-start.6 = (bf16[384,1024]{1,0:T(8,128)(2,1)S(1)}, bf16[384,1024]{1,0:T(8,128)(2,1)S(1)}, u32[]{:S(2)}, u32[]{:S(2)}) collective-permute-start(bf16[384,1024]{1,0:T(8,128)(2,1)S(1)} %get-tuple-element.49), channel_id=1, source_target_pairs={{0,1},{1,0},{2,3},{3,2},{4,5},{5,4},{6,7},{7,6},{8,9},{9,8},{10,11... | collective-permute-start | bytes 2359304 | tf_op jit(solution)/shard_map/ppermute | solution.py:455
  39.0 6.8 %collective-permute-start.7 = (bf16[1024,384]{1,0:T(8,128)(2,1)S(1)}, bf16[1024,384]{1,0:T(8,128)(2,1)S(1)}, u32[]{:S(2)}, u32[]{:S(2)}) collective-permute-start(bf16[1024,384]{1,0:T(8,128)(2,1)S(1)} %get-tuple-element.50), channel_id=1, source_target_pairs={{0,1},{1,0},{2,3},{3,2},{4,5},{5,4},{6,7},{7,6},{8,9},{9,8},{10,11... | collective-permute-start | bytes 2359304 | tf_op jit(solution)/shard_map/ppermute | solution.py:455
  39.1 6.6 %collective-permute-start.8 = (bf16[256,512]{1,0:T(8,128)(2,1)S(1)}, bf16[256,512]{1,0:T(8,128)(2,1)S(1)}, u32[]{:S(2)}, u32[]{:S(2)}) collective-permute-start(bf16[256,512]{1,0:T(8,128)(2,1)S(1)} %get-tuple-element.57.fold_own), channel_id=1, source_target_pairs={{0,1},{1,0},{2,3},{3,2},{4,5},{5,4},{6,7},{7,6},{8,9},{9,8},{10,11... | collective-permute-start | bytes 786440 | tf_op jit(solution)/shard_map/ppermute | solution.py:455
  54.1 1.4 %collective-permute-start.9 = (bf16[100,512]{1,0:T(8,128)(2,1)S(1)}, bf16[100,512]{1,0:T(8,128)(2,1)S(1)}, u32[]{:S(2)}, u32[]{:S(2)}) collective-permute-start(bf16[100,512]{1,0:T(8,128)(2,1)S(1)} %attend.1), channel_id=1, source_target_pairs={{0,1},{1,0},{2,3},{3,2},{4,5},{5,4},{6,7},{7,6},{8,9},{9,8},{10,11... | collective-permute-start | bytes 307208 | tf_op jit(solution)/shard_map/ppermute | solution.py:455
  55.5 10.4 %collective-permute-start.10 = (bf16[2,100,512]{2,1,0:T(8,128)(2,1)S(1)}, bf16[2,100,512]{2,1,0:T(8,128)(2,1)S(1)}, u32[]{:S(2)}, u32[]{:S(2)}) collective-permute-start(bf16[2,100,512]{2,1,0:T(8,128)(2,1)S(1)} %pad_maximum_fusion.own), channel_id=1, source_target_pairs={{0,2},{2,4},{4,6},{6,8},{8,10},{10,12},{12,14},{14,16},{16,18},{18... | collective-permute-start | bytes 614408 | tf_op jit(solution)/shard_map/ppermute | solution.py:462
  66.0 2.7 %collective-permute-start.11 = (bf16[2,100,512]{2,1,0:T(8,128)(2,1)S(1)}, bf16[2,100,512]{2,1,0:T(8,128)(2,1)S(1)}, u32[]{:S(2)}, u32[]{:S(2)}) collective-permute-start(bf16[2,100,512]{2,1,0:T(8,128)(2,1)S(1)} %collective-permute-done.10.sent), channel_id=1, source_target_pairs={{0,1},{1,0},{2,3},{3,2},{4,5},{5,4},{6,7},{7,6},{8,9},{9,8},{10,11... | collective-permute-start | bytes 614408 | tf_op jit(solution)/shard_map/ppermute | solution.py:455

commit v8 on v7

--- a/solution.py
+++ b/solution.py
@@ -82,18 +82,22 @@
         wide[:C, HALF:] = own[...].astype(F32)
 
 
-def mask_body(offsets, mask):
-    for chunk in range(SPAN // TILE):
-        row = lax.broadcasted_iota(jnp.int32, (TILE, LANES), 0) + (chunk * TILE - WIN)
-        away = row - lax.broadcasted_iota(jnp.int32, (TILE, LANES), 1)
-        hit = away == offsets[0]
-        for k in range(1, K_OFF):
-            hit = hit | (away == offsets[k])
-        mask[chunk * TILE : (chunk + 1) * TILE, :] = jnp.where(hit, 0.0, MASKED).astype(BF16)
+def mask_body(offsets, mask, token, strip, mask_wide):
+    lane = lax.broadcasted_iota(jnp.int32, strip.shape, 1)
+    away = lax.broadcasted_iota(jnp.int32, strip.shape, 0) + (SPAN - WIN - 8) - lane
+    hit = away == offsets[0]
+    for k in range(1, K_OFF):
+        hit = hit | (away == offsets[k])
+    strip[...] = jnp.where(hit, 0.0, MASKED)
+    for begin in range(0, SPAN, 8):
+        shift = SPAN - 8 - begin
+        mask_wide[begin : begin + 8, :] = strip[:, shift : shift + TILE]
+    mask[...] = mask_wide[...].astype(BF16)
+    token[...] = jnp.zeros_like(token)
 
 
 def prepare_body(
-    info, mask, src, dst, weight, gain, win_own, win_peer, dec_own, dec_peer,
+    info, token, src, dst, weight, gain, win_own, win_peer, dec_own, dec_peer,
     sources, targets, weights, gains, w_in, w_decode,
     w_wide,
 ):
@@ -495,13 +499,17 @@
     qkv_own = w_qkv.transpose(1, 0, 2)
     qkv_peer = swapped(qkv_own)
     edges = jax.ShapeDtypeStruct(enc_src.shape, jnp.int32)
-    mask = call(
-        mask_body, (offsets,), 1, jax.ShapeDtypeStruct((SPAN, TILE), BF16), [],
+    mask, token = call(
+        mask_body,
+        (offsets,),
+        1,
+        [jax.ShapeDtypeStruct((SPAN, TILE), BF16), jax.ShapeDtypeStruct((8, LANES), F32)],
+        [pltpu.VMEM((8, SPAN + TILE), F32), pltpu.VMEM((SPAN, TILE), F32)],
         5 * 10 ** 9, 4, "mask",
     )
     sources, targets, weights, gain, w_in_all, dec_all = call(
         prepare_body,
-        (info, mask, enc_src, enc_dst, enc_weight, norm_gain.reshape(1, D), w_in, win_peer,
+        (info, token, enc_src, enc_dst, enc_weight, norm_gain.reshape(1, D), w_in, win_peer,
          dec_own, dec_peer),
         1,
         [

time: 70.7 us -> 70.5 us (level)
  Pallas kernels: 44.9 us -> 43.3 us
  starting transfers between devices: 20.3 us -> 21.4 us
    ppermute x9, starting transfers between devices: 5.11 us -> 7.52 us  [swapped(): return lax.ppermute(value, 'mp', [(0, 1), (1, 0)])]
    pallas_call x12, Pallas kernels: 44.9 us -> 43.3 us  [call(): pl.pallas_call(body, out_shape=outs, in_specs=specs, out_specs=jax.tree.m...]
    ppermute x2, starting transfers between devices: 13.1 us -> 11.9 us  [up_and_down(): return lax.ppermute(value, ('band', 'mp'), pairs)]
    unnamed x32 -> x34, local copies, waits for them, and re-layouts: 2.32 us -> 2.67 us
  transfers between devices with their start and end apart: 12 -> 12, of which waited for: 3 -> 3; matrix products, arithmetic and copies ran while one was open for 0% -> 0% of each run, Pallas kernels for 50% -> 47%
where the time goes in v8:
time: 70.5 us; the launch traced here: 70.2 us
  Pallas kernels  43.3 us (61%)
  starting transfers between devices  21.4 us (30%)
  local copies, waits for them, and re-layouts  2.76 us (4%)
  waiting for transfers between devices  1.72 us (2%)
  between operations  1.03 us (1%)
    pallas_call x12, Pallas kernels, call(): pl.pallas_call(body, out_shape=outs, in_specs=specs, out_specs=jax.tree.m...  43.3 us
    ppermute x2, starting transfers between devices, up_and_down(): return lax.ppermute(value, ('band', 'mp'), pairs)  11.9 us
    ppermute x9, starting transfers between devices, swapped(): return lax.ppermute(value, 'mp', [(0, 1), (1, 0)])  7.52 us
    unnamed x34, local copies, waits for them, and re-layouts  2.67 us
    ppermute x1, starting transfers between devices, over_the_edge(): return lax.ppermute(value, ('band', 'mp'), pairs)  1.92 us
    ppermute x9, waiting for transfers between devices, swapped(): return lax.ppermute(value, 'mp', [(0, 1), (1, 0)])  1.72 us
  transfers between devices with their start and end apart: 12, of which 3 were waited for; matrix products, arithmetic and copies ran while one was open for 0% of the time, Pallas kernels for 47%

profile of v8, /device:TPU:97, one launch (start us, length us, event | category | flops | bytes accessed | tf_op | source)
XLA Modules:
  0.0 70.2 jit_solution(13696141809686524617)
XLA Ops:
  0.0 0.7 collective-permute-start.5
  0.7 0.0 collective-permute-start
  0.7 0.5 collective-permute-start.1
  1.2 0.0 copy-start.7
  1.2 0.0 copy-start.11
  1.2 6.8 %collective-permute-start.2 = (bf16[100,2048]{1,0:T(8,128)(2,1)}, bf16[100,2048]{1,0:T(8,128)(2,1)}, u32[]{:S(2)}, u32[]{:S(2)}) collective-permute-start(bf16[100,2048]{1,0:T(8,128)(2,1)} %bitcast.18), channel_id=1, source_target_pairs={{0,2},{2,4},{4,6},{6,8},{8,10},{10,12},{12,14},{14,16},{16,18},{18... | collective-permute-start | bytes 1228808 | tf_op jit(solution)/shard_map/ppermute | solution.py:466
  8.0 0.0 copy-start.12
  8.0 0.6 copy-done.12
  8.7 0.8 %mask.1 = (bf16[896,128]{1,0:T(8,128)(2,1)S(1)}, f32[8,128]{1,0:T(8,128)S(1)}) custom-call(s32[32]{0:T(128)S(1)} %copy-done.12), custom_call_target="tpu_custom_call" | custom-call | flops 5000000000 | bytes 2000000 | tf_op jit(solution)/shard_map/mask/pallas_call | solution.py:44
  9.5 0.7 copy-done.13
  10.2 0.6 copy-done.15
  11.5 0.1 stack.48.info
  11.6 0.0 collective-permute-done.win_peer
  11.6 0.0 collective-permute-done.1.dec_peer
  11.6 0.0 copy-start.16
  11.6 0.7 copy-done.16
  12.3 1.1 %prepare.1 = (s32[64,128]{1,0:T(8,128)S(1)}, s32[64,128]{1,0:T(8,128)S(1)}, f32[64,128]{1,0:T(8,128)S(1)}, f32[1,1024]{1,0:T(1,128)S(1)}, bf16[128,1024]{1,0:T(8,128)(2,1)S(1)}, /*index=5*/bf16[128,1024]{1,0:T(8,128)(2,1)S(1)}) custom-call(s32[8]{0:T(128)S(1)} %stack.48.info, f32[8,128]{1,0:T(8,128)S(1)} %copy-done.16, s32[64,128]{1,0:T(8,128)S(1)} %copy-done.5, ...), custom_call_target="tpu_custom_call" | custom-call | flops 5000000000 | bytes 2000000 | tf_op jit(solution)/shard_map/prepare/pallas_call | solution.py:44
  13.5 0.0 copy-start.1
  13.5 0.0 copy-start.2
  13.5 3.7 %early.1.spread_in = bf16[3072,1024]{1,0:T(8,128)(2,1)S(1)} custom-call(s32[8]{0:T(128)S(1)} %stack.48.info, bf16[128,1024]{1,0:T(8,128)(2,1)S(1)} %get-tuple-element.42.w_in, s32[24,128]{1,0:T(8,128)S(1)} %copy-done.8, s32[24,128]{1,0:T(8,128)S(1)} %copy-done.9, bf16[24,128]{1,0:T(8,128)(2,1)S(1)} %copy-done.10), custom_call_target="tpu_custom_call" | custom-call | flops 5000000000 | bytes 2000000 | tf_op jit(solution)/shard_map/early/pallas_call | solution.py:44
  17.2 0.0 collective-permute-done.2.sent
  17.2 0.1 collective-permute-start.3
  17.3 1.5 %unpack.1 = (f32[6144,128]{1,0:T(8,128)S(1)}, bf16[256,512]{1,0:T(8,128)(2,1)S(1)}) custom-call(s32[8]{0:T(128)S(1)} %stack.48.info, bf16[100,2048]{1,0:T(8,128)(2,1)S(1)} %bitcast.19, bf16[100,2048]{1,0:T(8,128)(2,1)} %collective-permute-done.2.sent, bf16[512,1024]{1,0:T(8,128)(2,1)S(1)} %copy-done.1, bf16[128,1024]{1,0:T(8,128)(2,1)S(1)} %get-tuple-element.40.w_decode), custom_call_target="tpu_custom_call" | custom-call | flops 2000000000 | bytes 2000000 | tf_op jit(solution)/shard_map/unpack/pallas_call | solution.py:44
  18.8 0.4 collective-permute-done.3.swapped_rows
  19.2 7.5 %encode.1 = (f32[6144,128]{1,0:T(8,128)S(1)}, bf16[512,1024]{1,0:T(8,128)(2,1)S(1)}, bf16[512,1024]{1,0:T(8,128)(2,1)S(1)}, bf16[384,1024]{1,0:T(8,128)(2,1)S(1)}) custom-call(s32[8]{0:T(128)S(1)} %stack.48.info, s32[64,128]{1,0:T(8,128)S(1)} %get-tuple-element.37.src, f32[6144,128]{1,0:T(8,128)S(1)} %get-tuple-element.41.grid_rows, ...), custom_call_target="tpu_custom_call", output_to_operand_aliasing={{0}: (2, {})} | custom-call | flops 7000000000 | bytes 2000000 | tf_op jit(solution)/shard_map/encode/pallas_call | solution.py:44
  26.7 1.9 %collective-permute-start.4 = (bf16[384,1024]{1,0:T(8,128)(2,1)S(1)}, bf16[384,1024]{1,0:T(8,128)(2,1)S(1)}, u32[]{:S(2)}, u32[]{:S(2)}) collective-permute-start(bf16[384,1024]{1,0:T(8,128)(2,1)S(1)} %get-tuple-element.46), channel_id=1, source_target_pairs={{1,2},{3,4},{5,6},{7,8},{9,10},{11,12},{13,14},{15,16},{17,18},{19... | collective-permute-start | bytes 2359304 | tf_op jit(solution)/shard_map/ppermute | solution.py:473
  28.6 0.0 copy-start
  28.6 3.0 %last.1 = (bf16[512,1024]{1,0:T(8,128)(2,1)S(1)}, bf16[512,1024]{1,0:T(8,128)(2,1)S(1)}) custom-call(s32[8]{0:T(128)S(1)} %stack.48.info, s32[64,128]{1,0:T(8,128)S(1)} %get-tuple-element.37.src, f32[6144,128]{1,0:T(8,128)S(1)} %get-tuple-element.47.rows, ...), custom_call_target="tpu_custom_call", output_to_operand_aliasing={{0}: (7, {}), {1}: (8, {})} | custom-call | flops 3000000000 | bytes 2000000 | tf_op jit(solution)/shard_map/last/pallas_call | solution.py:44
  31.6 0.0 collective-permute-done.5.w_peer
  31.7 4.4 %project.1 = (bf16[512,1024]{1,0:T(8,128)(2,1)S(1)}, bf16[512,1024]{1,0:T(8,128)(2,1)S(1)}, bf16[1024,512]{1,0:T(8,128)(2,1)S(1)}, bf16[384,1024]{1,0:T(8,128)(2...) custom-call(s32[8]{0:T(128)S(1)} %stack.48.info, bf16[512,1024]{1,0:T(8,128)(2,1)S(1)} %get-tuple-element.50.normed, ...), custom_call_target="tpu_custom_call" | custom-call | flops 6000000000 | bytes 2000000 | tf_op jit(solution)/shard_map/project/pallas_call | solution.py:44
  36.1 2.7 %collective-permute-start.6 = (bf16[384,1024]{1,0:T(8,128)(2,1)S(1)}, bf16[384,1024]{1,0:T(8,128)(2,1)S(1)}, u32[]{:S(2)}, u32[]{:S(2)}) collective-permute-start(bf16[384,1024]{1,0:T(8,128)(2,1)S(1)} %get-tuple-element.52), channel_id=1, source_target_pairs={{0,1},{1,0},{2,3},{3,2},{4,5},{5,4},{6,7},{7,6},{8,9},{9,8},{10,11... | collective-permute-start | bytes 2359304 | tf_op jit(solution)/shard_map/ppermute | solution.py:459
  38.8 0.1 collective-permute-start.7
  38.9 0.4 collective-permute-start.8
  39.4 6.2 %own.1 = (f32[1024,512]{1,0:T(8,128)S(1)}, f32[8,8,1024]{2,1,0:T(8,128)S(1)}) custom-call(bf16[512,1024]{1,0:T(8,128)(2,1)S(1)} %get-tuple-element.54.queries, bf16[512,1024]{1,0:T(8,128)(2,1)S(1)} %get-tuple-element.55.keys, bf16[1024,512]{1,0:T(8,128)(2,1)S(1)} %get-tuple-element.56.values_t, bf16[896,128]{1,0:T(8,128)(2,1)S(1)} %copy-done.14), custom_call_target="tpu_custom_call" | custom-call | flops 8000000000 | bytes 2000000 | tf_op jit(solution)/shard_map/own/pallas_call | solution.py:44
  45.6 0.0 collective-permute-done.8.fold_peer
  45.6 0.0 collective-permute-done.4.halo
  45.6 0.0 collective-permute-done.6.peer_keys
  45.6 0.0 collective-permute-done.7.peer_values
  45.6 8.3 %attend.1 = bf16[100,512]{1,0:T(8,128)(2,1)S(1)} custom-call(s32[8]{0:T(128)S(1)} %stack.48.info, bf16[384,1024]{1,0:T(8,128)(2,1)S(1)} %collective-permute-done.4.halo, bf16[384,1024]{1,0:T(8,128)(2,1)S(1)} %collective-permute-done.6.peer_keys, bf16[1024,384]{1,0:T(8,128)(2,1)S(1)} %collective-permute-done.7.peer_values, ...), custom_call_target="tpu_custom_call" | custom-call | flops 10000000000 | bytes 2000000 | tf_op jit(solution)/shard_map/attend/pallas_call | solution.py:44
  53.9 0.2 collective-permute-start.9
  54.1 1.2 %collective-permute-done.9 = bf16[100,512]{1,0:T(8,128)(2,1)S(1)} collective-permute-done((bf16[100,512]{1,0:T(8,128)(2,1)S(1)}, bf16[100,512]{1,0:T(8,128)(2,1)S(1)}, u32[]{:S(2)}, u32[]{:S(2)}) %collective-permute-start.9) | collective-permute-done | bytes 102432 | tf_op jit(solution)/shard_map/ppermute | solution.py:459
  55.3 5.1 %collective-permute-start.10 = (bf16[2,100,512]{2,1,0:T(8,128)(2,1)S(1)}, bf16[2,100,512]{2,1,0:T(8,128)(2,1)S(1)}, u32[]{:S(2)}, u32[]{:S(2)}) collective-permute-start(bf16[2,100,512]{2,1,0:T(8,128)(2,1)S(1)} %pad_maximum_fusion.own), channel_id=1, source_target_pairs={{0,2},{2,4},{4,6},{6,8},{8,10},{10,12},{12,14},{14,16},{16,18},{18... | collective-permute-start | bytes 614408 | tf_op jit(solution)/shard_map/ppermute | solution.py:466
  60.4 4.1 %spread.1 = (bf16[3072,1024]{1,0:T(8,128)(2,1)S(1)}, f32[100,1024]{1,0:T(8,128)S(1)}) custom-call(s32[8]{0:T(128)S(1)} %stack.48.info, bf16[3072,1024]{1,0:T(8,128)(2,1)S(1)} %early.1.spread_in, bf16[2,100,512]{2,1,0:T(8,128)(2,1)S(1)} %pad_maximum_fusion.own, s32[24,128]{1,0:T(8,128)S(1)} %copy-done.8, ...), custom_call_target="tpu_custom_call", output_to_operand_aliasing={{0}: (1, {})} | custom-call | flops 8000000000 | bytes 2000000 | tf_op jit(solution)/shard_map/spread/pallas_call | solution.py:44
  64.6 0.0 collective-permute-done.10.sent
  64.6 2.8 %collective-permute-start.11 = (bf16[2,100,512]{2,1,0:T(8,128)(2,1)S(1)}, bf16[2,100,512]{2,1,0:T(8,128)(2,1)S(1)}, u32[]{:S(2)}, u32[]{:S(2)}) collective-permute-start(bf16[2,100,512]{2,1,0:T(8,128)(2,1)S(1)} %collective-permute-done.10.sent), channel_id=1, source_target_pairs={{0,1},{1,0},{2,3},{3,2},{4,5},{5,4},{6,7},{7,6},{8,9},{9,8},{10,11... | collective-permute-start | bytes 614408 | tf_op jit(solution)/shard_map/ppermute | solution.py:459
  67.4 1.0 %sent.1.total = f32[100,1024]{1,0:T(8,128)S(1)} custom-call(s32[8]{0:T(128)S(1)} %stack.48.info, bf16[2,100,512]{2,1,0:T(8,128)(2,1)S(1)} %collective-permute-done.10.sent, bf16[3072,1024]{1,0:T(8,128)(2,1)S(1)} %get-tuple-element.65.spread, f32[100,1024]{1,0:T(8,128)S(1)} %get-tuple-element.66.base), custom_call_target="tpu_custom_call" | custom-call | flops 1000000000 | bytes 2000000 | tf_op jit(solution)/shard_map/sent/pallas_call | solution.py:44
  68.4 0.1 collective-permute-done.11.swapped_rows
  68.5 1.7 %decode.1 = bf16[100,1024]{1,0:T(8,128)(2,1)} custom-call(s32[8]{0:T(128)S(1)} %stack.48.info, bf16[2,100,512]{2,1,0:T(8,128)(2,1)S(1)} %collective-permute-done.11.swapped_rows, bf16[3072,1024]{1,0:T(8,128)(2,1)S(1)} %get-tuple-element.65.spread, f32[100,1024]{1,0:T(8,128)S(1)} %sent.1.total), custom_call_target="tpu_custom_call" | custom-call | flops 1000000000 | bytes 2000000 | tf_op jit(solution)/shard_map/decode/pallas_call | solution.py:44
  (24 shorter events, 0.1 us)
Async XLA Ops:
  0.0 31.6 %collective-permute-start.5 = (bf16[3,1024,512]{2,1,0:T(8,128)(2,1)}, bf16[3,1024,512]{2,1,0:T(8,128)(2,1)S(1)}, u32[]{:S(2)}, u32[]{:S(2)}) collective-permute-start(bf16[3,1024,512]{2,1,0:T(8,128)(2,1)} %bitcast.15), channel_id=1, source_target_pairs={{0,1},{1,0},{2,3},{3,2},{4,5},{5,4},{6,7},{7,6},{8,9},{9,8},{10,11... | collective-permute-start | bytes 9437192 | tf_op jit(solution)/shard_map/ppermute | solution.py:459
  0.7 10.9 %collective-permute-start = (bf16[100,512]{1,0:T(8,128)(2,1)}, bf16[100,512]{1,0:T(8,128)(2,1)S(1)}, u32[]{:S(2)}, u32[]{:S(2)}) collective-permute-start(bf16[100,512]{1,0:T(8,128)(2,1)} %win_own.1), channel_id=1, source_target_pairs={{0,1},{1,0},{2,3},{3,2},{4,5},{5,4},{6,7},{7,6},{8,9},{9,8},{10,11... | collective-permute-start | bytes 307208 | tf_op jit(solution)/shard_map/ppermute | solution.py:459
  0.7 10.9 %collective-permute-start.1 = (bf16[100,512]{1,0:T(8,128)(2,1)}, bf16[100,512]{1,0:T(8,128)(2,1)}, u32[]{:S(2)}, u32[]{:S(2)}) collective-permute-start(bf16[100,512]{1,0:T(8,128)(2,1)} %bitcast.21), channel_id=1, source_target_pairs={{0,1},{1,0},{2,3},{3,2},{4,5},{5,4},{6,7},{7,6},{8,9},{9,8},{10,11... | collective-permute-start | bytes 307208 | tf_op jit(solution)/shard_map/ppermute | solution.py:459
  1.2 10.4 %copy-start.3 = (bf16[100,512]{1,0:T(8,128)(2,1)S(1)}, bf16[100,512]{1,0:T(8,128)(2,1)}, u32[]{:S(2)}) copy-start(bf16[100,512]{1,0:T(8,128)(2,1)} %win_own.1) | copy-start | bytes 307204
  1.2 10.4 %copy-start.4 = (bf16[512,100]{0,1:T(8,128)(2,1)S(1)}, bf16[512,100]{0,1:T(8,128)(2,1)}, u32[]{:S(2)}) copy-start(bf16[512,100]{0,1:T(8,128)(2,1)} %param.24) | copy-start | bytes 307204
  1.2 10.4 %copy-start.5 = (s32[64,128]{1,0:T(8,128)S(1)}, s32[64,128]{1,0:T(8,128)}, u32[]{:S(2)}) copy-start(s32[64,128]{1,0:T(8,128)} %src.3) | copy-start | bytes 98308
  1.2 10.4 %copy-start.6 = (s32[64,128]{1,0:T(8,128)S(1)}, s32[64,128]{1,0:T(8,128)}, u32[]{:S(2)}) copy-start(s32[64,128]{1,0:T(8,128)} %dst.3) | copy-start | bytes 98308
  1.2 10.4 %copy-start.7 = (bf16[64,128]{1,0:T(8,128)(2,1)S(1)}, bf16[64,128]{1,0:T(8,128)(2,1)}, u32[]{:S(2)}) copy-start(bf16[64,128]{1,0:T(8,128)(2,1)} %weight.3) | copy-start | bytes 49156
  1.2 10.4 %copy-start.11 = (f32[1024]{0:T(1024)S(1)}, f32[1024]{0:T(1024)}, u32[]{:S(2)}) copy-start(f32[1024]{0:T(1024)} %param.20) | copy-start | bytes 12292
  1.2 16.0 %collective-permute-start.2 = (bf16[100,2048]{1,0:T(8,128)(2,1)}, bf16[100,2048]{1,0:T(8,128)(2,1)}, u32[]{:S(2)}, u32[]{:S(2)}) collective-permute-start(bf16[100,2048]{1,0:T(8,128)(2,1)} %bitcast.18), channel_id=1, source_target_pairs={{0,2},{2,4},{4,6},{6,8},{8,10},{10,12},{12,14},{14,16},{16,18},{18... | collective-permute-start | bytes 1228808 | tf_op jit(solution)/shard_map/ppermute | solution.py:466
  8.0 0.7 copy-start.12
  9.5 0.7 %copy-start.13 = (bf16[896,128]{1,0:T(8,128)(2,1)}, bf16[896,128]{1,0:T(8,128)(2,1)S(1)}, u32[]{:S(2)}) copy-start(bf16[896,128]{1,0:T(8,128)(2,1)S(1)} %get-tuple-element.57.mask) | copy-start | bytes 688132
  10.2 0.6 copy-start.15
  11.6 0.7 copy-start.16
  12.3 1.1 %copy-start.8 = (s32[24,128]{1,0:T(8,128)S(1)}, s32[24,128]{1,0:T(8,128)}, u32[]{:S(2)}) copy-start(s32[24,128]{1,0:T(8,128)} %src.5) | copy-start | bytes 36868
  12.3 1.1 %copy-start.9 = (s32[24,128]{1,0:T(8,128)S(1)}, s32[24,128]{1,0:T(8,128)}, u32[]{:S(2)}) copy-start(s32[24,128]{1,0:T(8,128)} %dst.5) | copy-start | bytes 36868
  12.3 1.1 %copy-start.10 = (bf16[24,128]{1,0:T(8,128)(2,1)S(1)}, bf16[24,128]{1,0:T(8,128)(2,1)}, u32[]{:S(2)}) copy-start(bf16[24,128]{1,0:T(8,128)(2,1)} %weight.5) | copy-start | bytes 18436
  13.5 3.8 %copy-start.1 = (bf16[512,1024]{1,0:T(8,128)(2,1)S(1)}, bf16[512,1024]{1,0:T(8,128)(2,1)}, u32[]{:S(2)}) copy-start(bf16[512,1024]{1,0:T(8,128)(2,1)} %w_out.1) | copy-start | bytes 3145732
  13.5 3.8 %copy-start.2 = (bf16[2048,100]{0,1:T(8,128)(2,1)S(1)}, bf16[2048,100]{0,1:T(8,128)(2,1)}, u32[]{:S(2)}) copy-start(bf16[2048,100]{0,1:T(8,128)(2,1)} %param.14) | copy-start | bytes 1228804
  17.2 2.1 %collective-permute-start.3 = (bf16[100,2048]{1,0:T(8,128)(2,1)}, bf16[100,2048]{1,0:T(8,128)(2,1)S(1)}, u32[]{:S(2)}, u32[]{:S(2)}) collective-permute-start(bf16[100,2048]{1,0:T(8,128)(2,1)} %collective-permute-done.2.sent), channel_id=1, source_target_pairs={{0,1},{1,0},{2,3},{3,2},{4,5},{5,4},{6,7},{7,6},{8,9},{9,8},{10,11... | collective-permute-start | bytes 1228808 | tf_op jit(solution)/shard_map/ppermute | solution.py:459
  26.7 18.9 %collective-permute-start.4 = (bf16[384,1024]{1,0:T(8,128)(2,1)S(1)}, bf16[384,1024]{1,0:T(8,128)(2,1)S(1)}, u32[]{:S(2)}, u32[]{:S(2)}) collective-permute-start(bf16[384,1024]{1,0:T(8,128)(2,1)S(1)} %get-tuple-element.46), channel_id=1, source_target_pairs={{1,2},{3,4},{5,6},{7,8},{9,10},{11,12},{13,14},{15,16},{17,18},{19... | collective-permute-start | bytes 2359304 | tf_op jit(solution)/shard_map/ppermute | solution.py:473
  28.6 3.0 %copy-start = (bf16[1024,3,512]{2,0,1:T(8,128)(2,1)S(1)}, bf16[1024,3,512]{2,0,1:T(8,128)(2,1)}, u32[]{:S(2)}) copy-start(bf16[1024,3,512]{2,0,1:T(8,128)(2,1)} %param.21) | copy-start | bytes 9437188
  31.7 7.7 %copy-start.14 = (bf16[896,128]{1,0:T(8,128)(2,1)S(1)}, bf16[896,128]{1,0:T(8,128)(2,1)}, u32[]{:S(2)}) copy-start(bf16[896,128]{1,0:T(8,128)(2,1)} %copy-done.13) | copy-start | bytes 688132
  36.1 9.5 %collective-permute-start.6 = (bf16[384,1024]{1,0:T(8,128)(2,1)S(1)}, bf16[384,1024]{1,0:T(8,128)(2,1)S(1)}, u32[]{:S(2)}, u32[]{:S(2)}) collective-permute-start(bf16[384,1024]{1,0:T(8,128)(2,1)S(1)} %get-tuple-element.52), channel_id=1, source_target_pairs={{0,1},{1,0},{2,3},{3,2},{4,5},{5,4},{6,7},{7,6},{8,9},{9,8},{10,11... | collective-permute-start | bytes 2359304 | tf_op jit(solution)/shard_map/ppermute | solution.py:459
  38.8 6.8 %collective-permute-start.7 = (bf16[1024,384]{1,0:T(8,128)(2,1)S(1)}, bf16[1024,384]{1,0:T(8,128)(2,1)S(1)}, u32[]{:S(2)}, u32[]{:S(2)}) collective-permute-start(bf16[1024,384]{1,0:T(8,128)(2,1)S(1)} %get-tuple-element.53), channel_id=1, source_target_pairs={{0,1},{1,0},{2,3},{3,2},{4,5},{5,4},{6,7},{7,6},{8,9},{9,8},{10,11... | collective-permute-start | bytes 2359304 | tf_op jit(solution)/shard_map/ppermute | solution.py:459
  38.9 6.6 %collective-permute-start.8 = (bf16[256,512]{1,0:T(8,128)(2,1)S(1)}, bf16[256,512]{1,0:T(8,128)(2,1)S(1)}, u32[]{:S(2)}, u32[]{:S(2)}) collective-permute-start(bf16[256,512]{1,0:T(8,128)(2,1)S(1)} %get-tuple-element.61.fold_own), channel_id=1, source_target_pairs={{0,1},{1,0},{2,3},{3,2},{4,5},{5,4},{6,7},{7,6},{8,9},{9,8},{10,11... | collective-permute-start | bytes 786440 | tf_op jit(solution)/shard_map/ppermute | solution.py:459
  53.9 1.4 %collective-permute-start.9 = (bf16[100,512]{1,0:T(8,128)(2,1)S(1)}, bf16[100,512]{1,0:T(8,128)(2,1)S(1)}, u32[]{:S(2)}, u32[]{:S(2)}) collective-permute-start(bf16[100,512]{1,0:T(8,128)(2,1)S(1)} %attend.1), channel_id=1, source_target_pairs={{0,1},{1,0},{2,3},{3,2},{4,5},{5,4},{6,7},{7,6},{8,9},{9,8},{10,11... | collective-permute-start | bytes 307208 | tf_op jit(solution)/shard_map/ppermute | solution.py:459
  55.3 9.3 %collective-permute-start.10 = (bf16[2,100,512]{2,1,0:T(8,128)(2,1)S(1)}, bf16[2,100,512]{2,1,0:T(8,128)(2,1)S(1)}, u32[]{:S(2)}, u32[]{:S(2)}) collective-permute-start(bf16[2,100,512]{2,1,0:T(8,128)(2,1)S(1)} %pad_maximum_fusion.own), channel_id=1, source_target_pairs={{0,2},{2,4},{4,6},{6,8},{8,10},{10,12},{12,14},{14,16},{16,18},{18... | collective-permute-start | bytes 614408 | tf_op jit(solution)/shard_map/ppermute | solution.py:466
  64.6 3.9 %collective-permute-start.11 = (bf16[2,100,512]{2,1,0:T(8,128)(2,1)S(1)}, bf16[2,100,512]{2,1,0:T(8,128)(2,1)S(1)}, u32[]{:S(2)}, u32[]{:S(2)}) collective-permute-start(bf16[2,100,512]{2,1,0:T(8,128)(2,1)S(1)} %collective-permute-done.10.sent), channel_id=1, source_target_pairs={{0,1},{1,0},{2,3},{3,2},{4,5},{5,4},{6,7},{7,6},{8,9},{9,8},{10,11... | collective-permute-start | bytes 614408 | tf_op jit(solution)/shard_map/ppermute | solution.py:459

commit v9 on v8

--- a/solution.py
+++ b/solution.py
@@ -23,7 +23,7 @@
 DEC_ROUNDS = 3
 DEC_TILES = 8
 GROUP = 2
-EARLY = 3
+EARLY = 1
 MASKED = -1e30
 SCALE = 64 ** (-0.5) * math.log2(math.e)
 F32 = jnp.float32

time: 70.5 us -> 70.5 us (level)
    ppermute x9, starting transfers between devices: 7.52 us -> 9.47 us  [swapped(): return lax.ppermute(value, 'mp', [(0, 1), (1, 0)])]
    ppermute x2, starting transfers between devices: 11.9 us -> 10.4 us  [up_and_down(): return lax.ppermute(value, ('band', 'mp'), pairs)]
  transfers between devices with their start and end apart: 12 -> 12, of which waited for: 3 -> 2; matrix products, arithmetic and copies ran while one was open for 0% -> 0% of each run, Pallas kernels for 47% -> 47%
where the time goes in v9:
time: 70.5 us; the launch traced here: 70.2 us
  Pallas kernels  43.2 us (61%)
  starting transfers between devices  21.8 us (31%)
  local copies, waits for them, and re-layouts  2.76 us (4%)
  waiting for transfers between devices  1.39 us (2%)
  between operations  1 us (1%)
    pallas_call x12, Pallas kernels, call(): pl.pallas_call(body, out_shape=outs, in_specs=specs, out_specs=jax.tree.m...  43.2 us
    ppermute x2, starting transfers between devices, up_and_down(): return lax.ppermute(value, ('band', 'mp'), pairs)  10.4 us
    ppermute x9, starting transfers between devices, swapped(): return lax.ppermute(value, 'mp', [(0, 1), (1, 0)])  9.47 us
    unnamed x34, local copies, waits for them, and re-layouts  2.67 us
    ppermute x1, starting transfers between devices, over_the_edge(): return lax.ppermute(value, ('band', 'mp'), pairs)  1.92 us
  transfers between devices with their start and end apart: 12, of which 2 were waited for; matrix products, arithmetic and copies ran while one was open for 0% of the time, Pallas kernels for 47%

profile of v9, /device:TPU:97, one launch (start us, length us, event | category | flops | bytes accessed | tf_op | source)
XLA Modules:
  0.0 70.2 jit_solution(6276896256387453803)
XLA Ops:
  0.0 0.7 collective-permute-start.5
  0.7 0.0 collective-permute-start
  0.7 0.5 collective-permute-start.1
  1.2 0.0 copy-start.7
  1.2 0.0 copy-start.11
  1.2 6.8 %collective-permute-start.2 = (bf16[100,2048]{1,0:T(8,128)(2,1)}, bf16[100,2048]{1,0:T(8,128)(2,1)}, u32[]{:S(2)}, u32[]{:S(2)}) collective-permute-start(bf16[100,2048]{1,0:T(8,128)(2,1)} %bitcast.18), channel_id=1, source_target_pairs={{0,2},{2,4},{4,6},{6,8},{8,10},{10,12},{12,14},{14,16},{16,18},{18... | collective-permute-start | bytes 1228808 | tf_op jit(solution)/shard_map/ppermute | solution.py:466
  8.0 0.0 copy-start.12
  8.0 0.6 copy-done.12
  8.7 0.8 %mask.1 = (bf16[896,128]{1,0:T(8,128)(2,1)S(1)}, f32[8,128]{1,0:T(8,128)S(1)}) custom-call(s32[32]{0:T(128)S(1)} %copy-done.12), custom_call_target="tpu_custom_call" | custom-call | flops 5000000000 | bytes 2000000 | tf_op jit(solution)/shard_map/mask/pallas_call | solution.py:44
  9.5 0.7 copy-done.13
  10.2 0.6 copy-done.15
  11.5 0.1 stack.48.info
  11.6 0.0 collective-permute-done.win_peer
  11.6 0.0 collective-permute-done.1.dec_peer
  11.6 0.0 copy-start.16
  11.6 0.7 copy-done.16
  12.3 1.1 %prepare.1 = (s32[64,128]{1,0:T(8,128)S(1)}, s32[64,128]{1,0:T(8,128)S(1)}, f32[64,128]{1,0:T(8,128)S(1)}, f32[1,1024]{1,0:T(1,128)S(1)}, bf16[128,1024]{1,0:T(8,128)(2,1)S(1)}, /*index=5*/bf16[128,1024]{1,0:T(8,128)(2,1)S(1)}) custom-call(s32[8]{0:T(128)S(1)} %stack.48.info, f32[8,128]{1,0:T(8,128)S(1)} %copy-done.16, s32[64,128]{1,0:T(8,128)S(1)} %copy-done.5, ...), custom_call_target="tpu_custom_call" | custom-call | flops 5000000000 | bytes 2000000 | tf_op jit(solution)/shard_map/prepare/pallas_call | solution.py:44
  13.5 0.0 copy-start.1
  13.5 0.0 copy-start.2
  13.5 1.6 %early.1.spread_in = bf16[3072,1024]{1,0:T(8,128)(2,1)S(1)} custom-call(s32[8]{0:T(128)S(1)} %stack.48.info, bf16[128,1024]{1,0:T(8,128)(2,1)S(1)} %get-tuple-element.42.w_in, s32[24,128]{1,0:T(8,128)S(1)} %copy-done.8, s32[24,128]{1,0:T(8,128)S(1)} %copy-done.9, bf16[24,128]{1,0:T(8,128)(2,1)S(1)} %copy-done.10), custom_call_target="tpu_custom_call" | custom-call | flops 5000000000 | bytes 2000000 | tf_op jit(solution)/shard_map/early/pallas_call | solution.py:44
  15.1 0.0 collective-permute-done.2.sent
  15.1 0.8 %collective-permute-start.3 = (bf16[100,2048]{1,0:T(8,128)(2,1)}, bf16[100,2048]{1,0:T(8,128)(2,1)S(1)}, u32[]{:S(2)}, u32[]{:S(2)}) collective-permute-start(bf16[100,2048]{1,0:T(8,128)(2,1)} %collective-permute-done.2.sent), channel_id=1, source_target_pairs={{0,1},{1,0},{2,3},{3,2},{4,5},{5,4},{6,7},{7,6},{8,9},{9,8},{10,11... | collective-permute-start | bytes 1228808 | tf_op jit(solution)/shard_map/ppermute | solution.py:459
  15.9 1.5 %unpack.1 = (f32[6144,128]{1,0:T(8,128)S(1)}, bf16[256,512]{1,0:T(8,128)(2,1)S(1)}) custom-call(s32[8]{0:T(128)S(1)} %stack.48.info, bf16[100,2048]{1,0:T(8,128)(2,1)S(1)} %bitcast.19, bf16[100,2048]{1,0:T(8,128)(2,1)} %collective-permute-done.2.sent, bf16[512,1024]{1,0:T(8,128)(2,1)S(1)} %copy-done.1, bf16[128,1024]{1,0:T(8,128)(2,1)S(1)} %get-tuple-element.40.w_decode), custom_call_target="tpu_custom_call" | custom-call | flops 2000000000 | bytes 2000000 | tf_op jit(solution)/shard_map/unpack/pallas_call | solution.py:44
  17.5 0.0 collective-permute-done.3.swapped_rows
  17.5 7.5 %encode.1 = (f32[6144,128]{1,0:T(8,128)S(1)}, bf16[512,1024]{1,0:T(8,128)(2,1)S(1)}, bf16[512,1024]{1,0:T(8,128)(2,1)S(1)}, bf16[384,1024]{1,0:T(8,128)(2,1)S(1)}) custom-call(s32[8]{0:T(128)S(1)} %stack.48.info, s32[64,128]{1,0:T(8,128)S(1)} %get-tuple-element.37.src, f32[6144,128]{1,0:T(8,128)S(1)} %get-tuple-element.41.grid_rows, ...), custom_call_target="tpu_custom_call", output_to_operand_aliasing={{0}: (2, {})} | custom-call | flops 7000000000 | bytes 2000000 | tf_op jit(solution)/shard_map/encode/pallas_call | solution.py:44
  25.0 1.9 %collective-permute-start.4 = (bf16[384,1024]{1,0:T(8,128)(2,1)S(1)}, bf16[384,1024]{1,0:T(8,128)(2,1)S(1)}, u32[]{:S(2)}, u32[]{:S(2)}) collective-permute-start(bf16[384,1024]{1,0:T(8,128)(2,1)S(1)} %get-tuple-element.46), channel_id=1, source_target_pairs={{1,2},{3,4},{5,6},{7,8},{9,10},{11,12},{13,14},{15,16},{17,18},{19... | collective-permute-start | bytes 2359304 | tf_op jit(solution)/shard_map/ppermute | solution.py:473
  26.9 0.0 copy-start
  27.0 3.0 %last.1 = (bf16[512,1024]{1,0:T(8,128)(2,1)S(1)}, bf16[512,1024]{1,0:T(8,128)(2,1)S(1)}) custom-call(s32[8]{0:T(128)S(1)} %stack.48.info, s32[64,128]{1,0:T(8,128)S(1)} %get-tuple-element.37.src, f32[6144,128]{1,0:T(8,128)S(1)} %get-tuple-element.47.rows, ...), custom_call_target="tpu_custom_call", output_to_operand_aliasing={{0}: (7, {}), {1}: (8, {})} | custom-call | flops 3000000000 | bytes 2000000 | tf_op jit(solution)/shard_map/last/pallas_call | solution.py:44
  30.0 0.0 collective-permute-done.5.w_peer
  30.0 4.4 %project.1 = (bf16[512,1024]{1,0:T(8,128)(2,1)S(1)}, bf16[512,1024]{1,0:T(8,128)(2,1)S(1)}, bf16[1024,512]{1,0:T(8,128)(2,1)S(1)}, bf16[384,1024]{1,0:T(8,128)(2...) custom-call(s32[8]{0:T(128)S(1)} %stack.48.info, bf16[512,1024]{1,0:T(8,128)(2,1)S(1)} %get-tuple-element.50.normed, ...), custom_call_target="tpu_custom_call" | custom-call | flops 6000000000 | bytes 2000000 | tf_op jit(solution)/shard_map/project/pallas_call | solution.py:44
  34.4 4.4 %collective-permute-start.6 = (bf16[384,1024]{1,0:T(8,128)(2,1)S(1)}, bf16[384,1024]{1,0:T(8,128)(2,1)S(1)}, u32[]{:S(2)}, u32[]{:S(2)}) collective-permute-start(bf16[384,1024]{1,0:T(8,128)(2,1)S(1)} %get-tuple-element.52), channel_id=1, source_target_pairs={{0,1},{1,0},{2,3},{3,2},{4,5},{5,4},{6,7},{7,6},{8,9},{9,8},{10,11... | collective-permute-start | bytes 2359304 | tf_op jit(solution)/shard_map/ppermute | solution.py:459
  38.9 0.1 collective-permute-start.7
  38.9 0.4 collective-permute-start.8
  39.4 6.2 %own.1 = (f32[1024,512]{1,0:T(8,128)S(1)}, f32[8,8,1024]{2,1,0:T(8,128)S(1)}) custom-call(bf16[512,1024]{1,0:T(8,128)(2,1)S(1)} %get-tuple-element.54.queries, bf16[512,1024]{1,0:T(8,128)(2,1)S(1)} %get-tuple-element.55.keys, bf16[1024,512]{1,0:T(8,128)(2,1)S(1)} %get-tuple-element.56.values_t, bf16[896,128]{1,0:T(8,128)(2,1)S(1)} %copy-done.14), custom_call_target="tpu_custom_call" | custom-call | flops 8000000000 | bytes 2000000 | tf_op jit(solution)/shard_map/own/pallas_call | solution.py:44
  45.6 0.0 collective-permute-done.8.fold_peer
  45.6 0.0 collective-permute-done.4.halo
  45.6 0.0 collective-permute-done.6.peer_keys
  45.6 0.0 collective-permute-done.7.peer_values
  45.6 8.3 %attend.1 = bf16[100,512]{1,0:T(8,128)(2,1)S(1)} custom-call(s32[8]{0:T(128)S(1)} %stack.48.info, bf16[384,1024]{1,0:T(8,128)(2,1)S(1)} %collective-permute-done.4.halo, bf16[384,1024]{1,0:T(8,128)(2,1)S(1)} %collective-permute-done.6.peer_keys, bf16[1024,384]{1,0:T(8,128)(2,1)S(1)} %collective-permute-done.7.peer_values, ...), custom_call_target="tpu_custom_call" | custom-call | flops 10000000000 | bytes 2000000 | tf_op jit(solution)/shard_map/attend/pallas_call | solution.py:44
  53.9 0.2 collective-permute-start.9
  54.1 1.2 %collective-permute-done.9 = bf16[100,512]{1,0:T(8,128)(2,1)S(1)} collective-permute-done((bf16[100,512]{1,0:T(8,128)(2,1)S(1)}, bf16[100,512]{1,0:T(8,128)(2,1)S(1)}, u32[]{:S(2)}, u32[]{:S(2)}) %collective-permute-start.9) | collective-permute-done | bytes 102432 | tf_op jit(solution)/shard_map/ppermute | solution.py:459
  55.3 3.6 %collective-permute-start.10 = (bf16[2,100,512]{2,1,0:T(8,128)(2,1)S(1)}, bf16[2,100,512]{2,1,0:T(8,128)(2,1)S(1)}, u32[]{:S(2)}, u32[]{:S(2)}) collective-permute-start(bf16[2,100,512]{2,1,0:T(8,128)(2,1)S(1)} %pad_maximum_fusion.own), channel_id=1, source_target_pairs={{0,2},{2,4},{4,6},{6,8},{8,10},{10,12},{12,14},{14,16},{16,18},{18... | collective-permute-start | bytes 614408 | tf_op jit(solution)/shard_map/ppermute | solution.py:466
  59.0 6.1 %spread.1 = (bf16[3072,1024]{1,0:T(8,128)(2,1)S(1)}, f32[100,1024]{1,0:T(8,128)S(1)}) custom-call(s32[8]{0:T(128)S(1)} %stack.48.info, bf16[3072,1024]{1,0:T(8,128)(2,1)S(1)} %early.1.spread_in, bf16[2,100,512]{2,1,0:T(8,128)(2,1)S(1)} %pad_maximum_fusion.own, s32[24,128]{1,0:T(8,128)S(1)} %copy-done.8, ...), custom_call_target="tpu_custom_call", output_to_operand_aliasing={{0}: (1, {})} | custom-call | flops 8000000000 | bytes 2000000 | tf_op jit(solution)/shard_map/spread/pallas_call | solution.py:44
  65.1 0.0 collective-permute-done.10.sent
  65.1 2.4 %collective-permute-start.11 = (bf16[2,100,512]{2,1,0:T(8,128)(2,1)S(1)}, bf16[2,100,512]{2,1,0:T(8,128)(2,1)S(1)}, u32[]{:S(2)}, u32[]{:S(2)}) collective-permute-start(bf16[2,100,512]{2,1,0:T(8,128)(2,1)S(1)} %collective-permute-done.10.sent), channel_id=1, source_target_pairs={{0,1},{1,0},{2,3},{3,2},{4,5},{5,4},{6,7},{7,6},{8,9},{9,8},{10,11... | collective-permute-start | bytes 614408 | tf_op jit(solution)/shard_map/ppermute | solution.py:459
  67.4 1.0 %sent.1.total = f32[100,1024]{1,0:T(8,128)S(1)} custom-call(s32[8]{0:T(128)S(1)} %stack.48.info, bf16[2,100,512]{2,1,0:T(8,128)(2,1)S(1)} %collective-permute-done.10.sent, bf16[3072,1024]{1,0:T(8,128)(2,1)S(1)} %get-tuple-element.65.spread, f32[100,1024]{1,0:T(8,128)S(1)} %get-tuple-element.66.base), custom_call_target="tpu_custom_call" | custom-call | flops 1000000000 | bytes 2000000 | tf_op jit(solution)/shard_map/sent/pallas_call | solution.py:44
  68.5 0.1 collective-permute-done.11.swapped_rows
  68.5 1.7 %decode.1 = bf16[100,1024]{1,0:T(8,128)(2,1)} custom-call(s32[8]{0:T(128)S(1)} %stack.48.info, bf16[2,100,512]{2,1,0:T(8,128)(2,1)S(1)} %collective-permute-done.11.swapped_rows, bf16[3072,1024]{1,0:T(8,128)(2,1)S(1)} %get-tuple-element.65.spread, f32[100,1024]{1,0:T(8,128)S(1)} %sent.1.total), custom_call_target="tpu_custom_call" | custom-call | flops 1000000000 | bytes 2000000 | tf_op jit(solution)/shard_map/decode/pallas_call | solution.py:44
  (24 shorter events, 0.1 us)
Async XLA Ops:
  0.0 30.0 %collective-permute-start.5 = (bf16[3,1024,512]{2,1,0:T(8,128)(2,1)}, bf16[3,1024,512]{2,1,0:T(8,128)(2,1)S(1)}, u32[]{:S(2)}, u32[]{:S(2)}) collective-permute-start(bf16[3,1024,512]{2,1,0:T(8,128)(2,1)} %bitcast.15), channel_id=1, source_target_pairs={{0,1},{1,0},{2,3},{3,2},{4,5},{5,4},{6,7},{7,6},{8,9},{9,8},{10,11... | collective-permute-start | bytes 9437192 | tf_op jit(solution)/shard_map/ppermute | solution.py:459
  0.7 10.9 %collective-permute-start = (bf16[100,512]{1,0:T(8,128)(2,1)}, bf16[100,512]{1,0:T(8,128)(2,1)S(1)}, u32[]{:S(2)}, u32[]{:S(2)}) collective-permute-start(bf16[100,512]{1,0:T(8,128)(2,1)} %win_own.1), channel_id=1, source_target_pairs={{0,1},{1,0},{2,3},{3,2},{4,5},{5,4},{6,7},{7,6},{8,9},{9,8},{10,11... | collective-permute-start | bytes 307208 | tf_op jit(solution)/shard_map/ppermute | solution.py:459
  0.7 10.9 %collective-permute-start.1 = (bf16[100,512]{1,0:T(8,128)(2,1)}, bf16[100,512]{1,0:T(8,128)(2,1)}, u32[]{:S(2)}, u32[]{:S(2)}) collective-permute-start(bf16[100,512]{1,0:T(8,128)(2,1)} %bitcast.21), channel_id=1, source_target_pairs={{0,1},{1,0},{2,3},{3,2},{4,5},{5,4},{6,7},{7,6},{8,9},{9,8},{10,11... | collective-permute-start | bytes 307208 | tf_op jit(solution)/shard_map/ppermute | solution.py:459
  1.2 10.4 %copy-start.3 = (bf16[100,512]{1,0:T(8,128)(2,1)S(1)}, bf16[100,512]{1,0:T(8,128)(2,1)}, u32[]{:S(2)}) copy-start(bf16[100,512]{1,0:T(8,128)(2,1)} %win_own.1) | copy-start | bytes 307204
  1.2 10.4 %copy-start.4 = (bf16[512,100]{0,1:T(8,128)(2,1)S(1)}, bf16[512,100]{0,1:T(8,128)(2,1)}, u32[]{:S(2)}) copy-start(bf16[512,100]{0,1:T(8,128)(2,1)} %param.24) | copy-start | bytes 307204
  1.2 10.4 %copy-start.5 = (s32[64,128]{1,0:T(8,128)S(1)}, s32[64,128]{1,0:T(8,128)}, u32[]{:S(2)}) copy-start(s32[64,128]{1,0:T(8,128)} %src.3) | copy-start | bytes 98308
  1.2 10.4 %copy-start.6 = (s32[64,128]{1,0:T(8,128)S(1)}, s32[64,128]{1,0:T(8,128)}, u32[]{:S(2)}) copy-start(s32[64,128]{1,0:T(8,128)} %dst.3) | copy-start | bytes 98308
  1.2 10.4 %copy-start.7 = (bf16[64,128]{1,0:T(8,128)(2,1)S(1)}, bf16[64,128]{1,0:T(8,128)(2,1)}, u32[]{:S(2)}) copy-start(bf16[64,128]{1,0:T(8,128)(2,1)} %weight.3) | copy-start | bytes 49156
  1.2 10.4 %copy-start.11 = (f32[1024]{0:T(1024)S(1)}, f32[1024]{0:T(1024)}, u32[]{:S(2)}) copy-start(f32[1024]{0:T(1024)} %param.20) | copy-start | bytes 12292
  1.2 13.9 %collective-permute-start.2 = (bf16[100,2048]{1,0:T(8,128)(2,1)}, bf16[100,2048]{1,0:T(8,128)(2,1)}, u32[]{:S(2)}, u32[]{:S(2)}) collective-permute-start(bf16[100,2048]{1,0:T(8,128)(2,1)} %bitcast.18), channel_id=1, source_target_pairs={{0,2},{2,4},{4,6},{6,8},{8,10},{10,12},{12,14},{14,16},{16,18},{18... | collective-permute-start | bytes 1228808 | tf_op jit(solution)/shard_map/ppermute | solution.py:466
  8.0 0.7 copy-start.12
  9.5 0.7 %copy-start.13 = (bf16[896,128]{1,0:T(8,128)(2,1)}, bf16[896,128]{1,0:T(8,128)(2,1)S(1)}, u32[]{:S(2)}) copy-start(bf16[896,128]{1,0:T(8,128)(2,1)S(1)} %get-tuple-element.57.mask) | copy-start | bytes 688132
  10.2 0.6 copy-start.15
  11.6 0.7 copy-start.16
  12.3 1.1 %copy-start.8 = (s32[24,128]{1,0:T(8,128)S(1)}, s32[24,128]{1,0:T(8,128)}, u32[]{:S(2)}) copy-start(s32[24,128]{1,0:T(8,128)} %src.5) | copy-start | bytes 36868
  12.3 1.1 %copy-start.9 = (s32[24,128]{1,0:T(8,128)S(1)}, s32[24,128]{1,0:T(8,128)}, u32[]{:S(2)}) copy-start(s32[24,128]{1,0:T(8,128)} %dst.5) | copy-start | bytes 36868
  12.3 1.1 %copy-start.10 = (bf16[24,128]{1,0:T(8,128)(2,1)S(1)}, bf16[24,128]{1,0:T(8,128)(2,1)}, u32[]{:S(2)}) copy-start(bf16[24,128]{1,0:T(8,128)(2,1)} %weight.5) | copy-start | bytes 18436
  13.5 2.5 %copy-start.1 = (bf16[512,1024]{1,0:T(8,128)(2,1)S(1)}, bf16[512,1024]{1,0:T(8,128)(2,1)}, u32[]{:S(2)}) copy-start(bf16[512,1024]{1,0:T(8,128)(2,1)} %w_out.1) | copy-start | bytes 3145732
  13.5 2.4 %copy-start.2 = (bf16[2048,100]{0,1:T(8,128)(2,1)S(1)}, bf16[2048,100]{0,1:T(8,128)(2,1)}, u32[]{:S(2)}) copy-start(bf16[2048,100]{0,1:T(8,128)(2,1)} %param.14) | copy-start | bytes 1228804
  15.1 2.4 %collective-permute-start.3 = (bf16[100,2048]{1,0:T(8,128)(2,1)}, bf16[100,2048]{1,0:T(8,128)(2,1)S(1)}, u32[]{:S(2)}, u32[]{:S(2)}) collective-permute-start(bf16[100,2048]{1,0:T(8,128)(2,1)} %collective-permute-done.2.sent), channel_id=1, source_target_pairs={{0,1},{1,0},{2,3},{3,2},{4,5},{5,4},{6,7},{7,6},{8,9},{9,8},{10,11... | collective-permute-start | bytes 1228808 | tf_op jit(solution)/shard_map/ppermute | solution.py:459
  25.0 20.6 %collective-permute-start.4 = (bf16[384,1024]{1,0:T(8,128)(2,1)S(1)}, bf16[384,1024]{1,0:T(8,128)(2,1)S(1)}, u32[]{:S(2)}, u32[]{:S(2)}) collective-permute-start(bf16[384,1024]{1,0:T(8,128)(2,1)S(1)} %get-tuple-element.46), channel_id=1, source_target_pairs={{1,2},{3,4},{5,6},{7,8},{9,10},{11,12},{13,14},{15,16},{17,18},{19... | collective-permute-start | bytes 2359304 | tf_op jit(solution)/shard_map/ppermute | solution.py:473
  26.9 3.0 %copy-start = (bf16[1024,3,512]{2,0,1:T(8,128)(2,1)S(1)}, bf16[1024,3,512]{2,0,1:T(8,128)(2,1)}, u32[]{:S(2)}) copy-start(bf16[1024,3,512]{2,0,1:T(8,128)(2,1)} %param.21) | copy-start | bytes 9437188
  30.0 9.4 %copy-start.14 = (bf16[896,128]{1,0:T(8,128)(2,1)S(1)}, bf16[896,128]{1,0:T(8,128)(2,1)}, u32[]{:S(2)}) copy-start(bf16[896,128]{1,0:T(8,128)(2,1)} %copy-done.13) | copy-start | bytes 688132
  34.4 11.2 %collective-permute-start.6 = (bf16[384,1024]{1,0:T(8,128)(2,1)S(1)}, bf16[384,1024]{1,0:T(8,128)(2,1)S(1)}, u32[]{:S(2)}, u32[]{:S(2)}) collective-permute-start(bf16[384,1024]{1,0:T(8,128)(2,1)S(1)} %get-tuple-element.52), channel_id=1, source_target_pairs={{0,1},{1,0},{2,3},{3,2},{4,5},{5,4},{6,7},{7,6},{8,9},{9,8},{10,11... | collective-permute-start | bytes 2359304 | tf_op jit(solution)/shard_map/ppermute | solution.py:459
  38.9 6.8 %collective-permute-start.7 = (bf16[1024,384]{1,0:T(8,128)(2,1)S(1)}, bf16[1024,384]{1,0:T(8,128)(2,1)S(1)}, u32[]{:S(2)}, u32[]{:S(2)}) collective-permute-start(bf16[1024,384]{1,0:T(8,128)(2,1)S(1)} %get-tuple-element.53), channel_id=1, source_target_pairs={{0,1},{1,0},{2,3},{3,2},{4,5},{5,4},{6,7},{7,6},{8,9},{9,8},{10,11... | collective-permute-start | bytes 2359304 | tf_op jit(solution)/shard_map/ppermute | solution.py:459
  38.9 6.6 %collective-permute-start.8 = (bf16[256,512]{1,0:T(8,128)(2,1)S(1)}, bf16[256,512]{1,0:T(8,128)(2,1)S(1)}, u32[]{:S(2)}, u32[]{:S(2)}) collective-permute-start(bf16[256,512]{1,0:T(8,128)(2,1)S(1)} %get-tuple-element.61.fold_own), channel_id=1, source_target_pairs={{0,1},{1,0},{2,3},{3,2},{4,5},{5,4},{6,7},{7,6},{8,9},{9,8},{10,11... | collective-permute-start | bytes 786440 | tf_op jit(solution)/shard_map/ppermute | solution.py:459
  53.9 1.4 %collective-permute-start.9 = (bf16[100,512]{1,0:T(8,128)(2,1)S(1)}, bf16[100,512]{1,0:T(8,128)(2,1)S(1)}, u32[]{:S(2)}, u32[]{:S(2)}) collective-permute-start(bf16[100,512]{1,0:T(8,128)(2,1)S(1)} %attend.1), channel_id=1, source_target_pairs={{0,1},{1,0},{2,3},{3,2},{4,5},{5,4},{6,7},{7,6},{8,9},{9,8},{10,11... | collective-permute-start | bytes 307208 | tf_op jit(solution)/shard_map/ppermute | solution.py:459
  55.3 9.7 %collective-permute-start.10 = (bf16[2,100,512]{2,1,0:T(8,128)(2,1)S(1)}, bf16[2,100,512]{2,1,0:T(8,128)(2,1)S(1)}, u32[]{:S(2)}, u32[]{:S(2)}) collective-permute-start(bf16[2,100,512]{2,1,0:T(8,128)(2,1)S(1)} %pad_maximum_fusion.own), channel_id=1, source_target_pairs={{0,2},{2,4},{4,6},{6,8},{8,10},{10,12},{12,14},{14,16},{16,18},{18... | collective-permute-start | bytes 614408 | tf_op jit(solution)/shard_map/ppermute | solution.py:466
  65.1 3.5 %collective-permute-start.11 = (bf16[2,100,512]{2,1,0:T(8,128)(2,1)S(1)}, bf16[2,100,512]{2,1,0:T(8,128)(2,1)S(1)}, u32[]{:S(2)}, u32[]{:S(2)}) collective-permute-start(bf16[2,100,512]{2,1,0:T(8,128)(2,1)S(1)} %collective-permute-done.10.sent), channel_id=1, source_target_pairs={{0,1},{1,0},{2,3},{3,2},{4,5},{5,4},{6,7},{7,6},{8,9},{9,8},{10,11... | collective-permute-start | bytes 614408 | tf_op jit(solution)/shard_map/ppermute | solution.py:459

commit v10 on v9

--- a/solution.py
+++ b/solution.py
@@ -23,7 +23,7 @@
 DEC_ROUNDS = 3
 DEC_TILES = 8
 GROUP = 2
-EARLY = 1
+EARLY = 2
 MASKED = -1e30
 SCALE = 64 ** (-0.5) * math.log2(math.e)
 F32 = jnp.float32
@@ -82,7 +82,7 @@
         wide[:C, HALF:] = own[...].astype(F32)
 
 
-def mask_body(offsets, mask, token, strip, mask_wide):
+def make_mask(offsets, mask, strip, mask_wide):
     lane = lax.broadcasted_iota(jnp.int32, strip.shape, 1)
     away = lax.broadcasted_iota(jnp.int32, strip.shape, 0) + (SPAN - WIN - 8) - lane
     hit = away == offsets[0]
@@ -93,11 +93,10 @@
         shift = SPAN - 8 - begin
         mask_wide[begin : begin + 8, :] = strip[:, shift : shift + TILE]
     mask[...] = mask_wide[...].astype(BF16)
-    token[...] = jnp.zeros_like(token)
 
 
 def prepare_body(
-    info, token, src, dst, weight, gain, win_own, win_peer, dec_own, dec_peer,
+    info, src, dst, weight, gain, win_own, win_peer, dec_own, dec_peer,
     sources, targets, weights, gains, w_in, w_decode,
     w_wide,
 ):
@@ -195,21 +194,10 @@
     wide[...] = jnp.zeros_like(wide)
     to_rows(swapped_rows, wide, rows, (1 - core) * 2 * G_BAND)
     encode_tiles(
-        core, range(TILES - 1), src, w_in, targets, weights, gain, rows, mesh_zero, normed,
+        core, range(TILES), src, w_in, targets, weights, gain, rows, mesh_zero, normed,
         first, second, total,
     )
     to_band[...] = normed[pl.ds(pl.multiple_of(core * TILE, TILE), WIN), :]
-
-
-def last_body(
-    info, src, rows, w_in, targets, weights, gain, zero_in, normed_in,
-    mesh_zero, normed,
-    first, second, total,
-):
-    encode_tiles(
-        info[0], range(TILES - 1, TILES), src, w_in, targets, weights, gain, rows, mesh_zero,
-        normed, first, second, total,
-    )
 
 
 def identity_pair():
@@ -307,7 +295,10 @@
             values_sent[other, :] = values_t[place, :WIN]
 
 
-def own_body(queries, keys, values_t, mask, sums, stats, first, second):
+def own_body(
+    offsets, queries, keys, values_t, sums, stats, mask, first, second, strip, mask_wide
+):
+    make_mask(offsets, mask, strip, mask_wide)
     eyes, lane = identity_pair()
 
     def score(pair, block, scores):
@@ -425,7 +416,7 @@
     lax.fori_loop(places[0], places[-1] + 1, half, 0)
 
 
-def early_body(info, w_in, src, dst, weight, spread, sources, tables, weights):
+def early_body(info, src, dst, weight, spread, sources, tables, weights):
     spread_halves(info, src, dst, weight, spread, sources, tables, weights, range(EARLY))
 
 
@@ -499,17 +490,20 @@
     qkv_own = w_qkv.transpose(1, 0, 2)
     qkv_peer = swapped(qkv_own)
     edges = jax.ShapeDtypeStruct(enc_src.shape, jnp.int32)
-    mask, token = call(
-        mask_body,
-        (offsets,),
-        1,
-        [jax.ShapeDtypeStruct((SPAN, TILE), BF16), jax.ShapeDtypeStruct((8, LANES), F32)],
-        [pltpu.VMEM((8, SPAN + TILE), F32), pltpu.VMEM((SPAN, TILE), F32)],
-        5 * 10 ** 9, 4, "mask",
-    )
+    spread_out = jax.ShapeDtypeStruct((6 * ROWS, GQ), BF16)
+    spread_scratch = [
+        pltpu.VMEM(dec_src.shape, jnp.int32),
+        pltpu.VMEM((GQ, DEC_ROUNDS * TILE), BF16),
+        pltpu.VMEM(dec_weight.shape, F32),
+    ]
+    spread = call(
+        early_body, (info, dec_src, dec_dst, dec_weight), 1, spread_out,
+        spread_scratch, 5 * 10 ** 9, 10, "early",
+    )
+    spread, info = lax.optimization_barrier((spread, info))
     sources, targets, weights, gain, w_in_all, dec_all = call(
         prepare_body,
-        (info, token, enc_src, enc_dst, enc_weight, norm_gain.reshape(1, D), w_in, win_peer,
+        (info, enc_src, enc_dst, enc_weight, norm_gain.reshape(1, D), w_in, win_peer,
          dec_own, dec_peer),
         1,
         [
@@ -523,16 +517,6 @@
         [pltpu.VMEM((LANES, D), F32)],
         5 * 10 ** 9, 6, "prepare",
     )
-    spread_out = jax.ShapeDtypeStruct((6 * ROWS, GQ), BF16)
-    spread_scratch = [
-        pltpu.VMEM(dec_src.shape, jnp.int32),
-        pltpu.VMEM((GQ, DEC_ROUNDS * TILE), BF16),
-        pltpu.VMEM(dec_weight.shape, F32),
-    ]
-    spread = call(
-        early_body, (info, w_in_all, dec_src, dec_dst, dec_weight), 1, spread_out,
-        spread_scratch, 5 * 10 ** 9, 10, "early",
-    )
     grid_sent, w_in_all, spread = lax.optimization_barrier((grid_sent, w_in_all, spread))
     grid_swapped = swapped(grid_sent)
     grid_rows, fold_own = call(
@@ -549,7 +533,7 @@
     fold_peer = swapped(fold_own)
     band_rows = jax.ShapeDtypeStruct((ROWS, D), BF16)
     step_buffers = [pltpu.VMEM((STEP, LANES), F32)] * 2 + [pltpu.VMEM((ROWS, D), F32)]
-    grid_rows, mesh_zero, normed, to_band = call(
+    _, mesh_zero, normed, to_band = call(
         encode_body,
         (info, sources, grid_rows, grid_swapped, w_in_all, targets, weights, gain),
         2,
@@ -563,14 +547,6 @@
         7 * 10 ** 9, 14, "encode", {2: 0},
     )
     halo_band = over_the_edge(to_band)
-    mesh_zero, normed = call(
-        last_body,
-        (info, sources, grid_rows, w_in_all, targets, weights, gain, mesh_zero, normed),
-        2,
-        [band_rows, band_rows],
-        step_buffers,
-        3 * 10 ** 9, 14, "last", {7: 0, 8: 1},
-    )
     queries, keys, values_t, keys_sent, values_sent, straight = call(
         project_body,
         (info, normed, qkv_own, qkv_peer, mesh_zero, dec_all),
@@ -587,15 +563,17 @@
         6 * 10 ** 9, 10, "project",
     )
     peer_keys, peer_values = swapped(keys_sent), swapped(values_sent)
-    sums, stats = call(
+    sums, stats, mask = call(
         own_body,
-        (queries, keys, values_t, mask),
-        0,
+        (offsets, queries, keys, values_t),
+        1,
         [
             jax.ShapeDtypeStruct((D, ROWS), F32),
             jax.ShapeDtypeStruct((D // LANES, 8, 2 * ROWS), F32),
+            jax.ShapeDtypeStruct((SPAN, TILE), BF16),
         ],
-        [pltpu.VMEM((ROWS, 2 * GROUP * TILE), F32)] * 2,
+        [pltpu.VMEM((ROWS, 2 * GROUP * TILE), F32)] * 2
+        + [pltpu.VMEM((8, SPAN + TILE), F32), pltpu.VMEM((SPAN, TILE), F32)],
         8 * 10 ** 9, 12, "own",
     )
     projected = call(

time: 70.5 us -> 70.2 us (level)
  starting transfers between devices: 21.8 us -> 23.3 us
  Pallas kernels: 43.2 us -> 41.9 us
    pallas_call x12 -> x10, Pallas kernels: 43.2 us -> 41.9 us  [call(): pl.pallas_call(body, out_shape=outs, in_specs=specs, out_specs=jax.tree.m...]
    ppermute x2, starting transfers between devices: 10.4 us -> 11.7 us  [up_and_down(): return lax.ppermute(value, ('band', 'mp'), pairs)]
    unnamed x34 -> x32, local copies, waits for them, and re-layouts: 2.67 us -> 2.18 us
  transfers between devices with their start and end apart: 12 -> 12, of which waited for: 2 -> 2; matrix products, arithmetic and copies ran while one was open for 0% -> 0% of each run, Pallas kernels for 47% -> 45%
where the time goes in v10:
time: 70.2 us; the launch traced here: 69.9 us
  Pallas kernels  41.9 us (60%)
  starting transfers between devices  23.3 us (33%)
  local copies, waits for them, and re-layouts  2.26 us (3%)
  waiting for transfers between devices  1.38 us (2%)
  between operations  0.99 us (1%)
    pallas_call x10, Pallas kernels, call(): pl.pallas_call(body, out_shape=outs, in_specs=specs, out_specs=jax.tree.m...  41.9 us
    ppermute x2, starting transfers between devices, up_and_down(): return lax.ppermute(value, ('band', 'mp'), pairs)  11.7 us
    ppermute x9, starting transfers between devices, swapped(): return lax.ppermute(value, 'mp', [(0, 1), (1, 0)])  9.69 us
    unnamed x32, local copies, waits for them, and re-layouts  2.18 us
    ppermute x1, starting transfers between devices, over_the_edge(): return lax.ppermute(value, ('band', 'mp'), pairs)  1.92 us
  transfers between devices with their start and end apart: 12, of which 2 were waited for; matrix products, arithmetic and copies ran while one was open for 0% of the time, Pallas kernels for 45%

profile of v10, /device:TPU:97, one launch (start us, length us, event | category | flops | bytes accessed | tf_op | source)
XLA Modules:
  0.0 69.9 jit_solution(15659034780845415637)
XLA Ops:
  0.0 0.7 collective-permute-start.5
  0.7 0.0 collective-permute-start
  0.7 0.5 collective-permute-start.1
  1.2 6.7 %collective-permute-start.2 = (bf16[100,2048]{1,0:T(8,128)(2,1)}, bf16[100,2048]{1,0:T(8,128)(2,1)}, u32[]{:S(2)}, u32[]{:S(2)}) collective-permute-start(bf16[100,2048]{1,0:T(8,128)(2,1)} %bitcast.18), channel_id=1, source_target_pairs={{0,2},{2,4},{4,6},{6,8},{8,10},{10,12},{12,14},{14,16},{16,18},{18... | collective-permute-start | bytes 1228808 | tf_op jit(solution)/shard_map/ppermute | solution.py:457
  8.5 0.1 stack.48.info
  8.6 0.7 %copy-done.8 = s32[24,128]{1,0:T(8,128)S(1)} copy-done((s32[24,128]{1,0:T(8,128)S(1)}, s32[24,128]{1,0:T(8,128)}, u32[]{:S(2)}) %copy-start.8) | copy-done | bytes 12312
  9.3 0.7 %copy-done.10 = s32[24,128]{1,0:T(8,128)S(1)} copy-done((s32[24,128]{1,0:T(8,128)S(1)}, s32[24,128]{1,0:T(8,128)}, u32[]{:S(2)}) %copy-start.10) | copy-done | bytes 12312
  10.0 0.7 copy-done.12
  10.7 0.0 copy-start.7
  10.7 0.0 copy-start.14
  10.8 2.7 %early.1.spread_in = bf16[3072,1024]{1,0:T(8,128)(2,1)S(1)} custom-call(s32[8]{0:T(128)S(1)} %stack.48.info, s32[24,128]{1,0:T(8,128)S(1)} %copy-done.8, s32[24,128]{1,0:T(8,128)S(1)} %copy-done.10, bf16[24,128]{1,0:T(8,128)(2,1)S(1)} %copy-done.12), custom_call_target="tpu_custom_call" | custom-call | flops 5000000000 | bytes 2000000 | tf_op jit(solution)/shard_map/early/pallas_call | solution.py:44
  13.4 0.0 collective-permute-done.win_peer
  13.5 0.0 collective-permute-done.1.dec_peer
  13.5 0.0 copy-start.1
  13.5 0.0 copy-start.2
  13.5 0.7 %prepare.1 = (s32[64,128]{1,0:T(8,128)S(1)}, s32[64,128]{1,0:T(8,128)S(1)}, f32[64,128]{1,0:T(8,128)S(1)}, f32[1,1024]{1,0:T(1,128)S(1)}, bf16[128,1024]{1,0:T(8,128)(2,1)S(1)}, /*index=5*/bf16[128,1024]{1,0:T(8,128)(2,1)S(1)}) custom-call(s32[8]{0:T(128)S(1)} %stack.48.info, s32[64,128]{1,0:T(8,128)S(1)} %copy-done.5, s32[64,128]{1,0:T(8,128)S(1)} %copy-done.6, ...), custom_call_target="tpu_custom_call" | custom-call | flops 5000000000 | bytes 2000000 | tf_op jit(solution)/shard_map/prepare/pallas_call | solution.py:44
  14.3 0.0 collective-permute-done.2.sent
  14.3 1.5 %collective-permute-start.3 = (bf16[100,2048]{1,0:T(8,128)(2,1)}, bf16[100,2048]{1,0:T(8,128)(2,1)S(1)}, u32[]{:S(2)}, u32[]{:S(2)}) collective-permute-start(bf16[100,2048]{1,0:T(8,128)(2,1)} %collective-permute-done.2.sent), channel_id=1, source_target_pairs={{0,1},{1,0},{2,3},{3,2},{4,5},{5,4},{6,7},{7,6},{8,9},{9,8},{10,11... | collective-permute-start | bytes 1228808 | tf_op jit(solution)/shard_map/ppermute | solution.py:450
  15.7 1.5 %unpack.1 = (f32[6144,128]{1,0:T(8,128)S(1)}, bf16[256,512]{1,0:T(8,128)(2,1)S(1)}) custom-call(s32[8]{0:T(128)S(1)} %stack.48.info, bf16[100,2048]{1,0:T(8,128)(2,1)S(1)} %bitcast.19, bf16[100,2048]{1,0:T(8,128)(2,1)} %collective-permute-done.2.sent, bf16[512,1024]{1,0:T(8,128)(2,1)S(1)} %copy-done.1, bf16[128,1024]{1,0:T(8,128)(2,1)S(1)} %get-tuple-element.39.w_decode), custom_call_target="tpu_custom_call" | custom-call | flops 2000000000 | bytes 2000000 | tf_op jit(solution)/shard_map/unpack/pallas_call | solution.py:44
  17.3 0.0 collective-permute-done.3.swapped_rows
  17.3 9.3 %encode.1 = (f32[6144,128]{1,0:T(8,128)S(1)}, bf16[512,1024]{1,0:T(8,128)(2,1)S(1)}, bf16[512,1024]{1,0:T(8,128)(2,1)S(1)}, bf16[384,1024]{1,0:T(8,128)(2,1)S(1)}) custom-call(s32[8]{0:T(128)S(1)} %stack.48.info, s32[64,128]{1,0:T(8,128)S(1)} %get-tuple-element.35.src, f32[6144,128]{1,0:T(8,128)S(1)} %get-tuple-element.40.grid_rows, ...), custom_call_target="tpu_custom_call", output_to_operand_aliasing={{0}: (2, {})} | custom-call | flops 7000000000 | bytes 2000000 | tf_op jit(solution)/shard_map/encode/pallas_call | solution.py:44
  26.6 1.9 %collective-permute-start.4 = (bf16[384,1024]{1,0:T(8,128)(2,1)S(1)}, bf16[384,1024]{1,0:T(8,128)(2,1)S(1)}, u32[]{:S(2)}, u32[]{:S(2)}) collective-permute-start(bf16[384,1024]{1,0:T(8,128)(2,1)S(1)} %get-tuple-element.45), channel_id=1, source_target_pairs={{1,2},{3,4},{5,6},{7,8},{9,10},{11,12},{13,14},{15,16},{17,18},{19... | collective-permute-start | bytes 2359304 | tf_op jit(solution)/shard_map/ppermute | solution.py:464
  28.6 0.0 collective-permute-done.5.w_peer
  28.6 0.0 copy-start.15
  28.6 4.4 %project.1 = (bf16[512,1024]{1,0:T(8,128)(2,1)S(1)}, bf16[512,1024]{1,0:T(8,128)(2,1)S(1)}, bf16[1024,512]{1,0:T(8,128)(2,1)S(1)}, bf16[384,1024]{1,0:T(8,128)(2...) custom-call(s32[8]{0:T(128)S(1)} %stack.48.info, bf16[512,1024]{1,0:T(8,128)(2,1)S(1)} %get-tuple-element.46.normed, ...), custom_call_target="tpu_custom_call" | custom-call | flops 6000000000 | bytes 2000000 | tf_op jit(solution)/shard_map/project/pallas_call | solution.py:44
  33.0 4.5 %collective-permute-start.6 = (bf16[384,1024]{1,0:T(8,128)(2,1)S(1)}, bf16[384,1024]{1,0:T(8,128)(2,1)S(1)}, u32[]{:S(2)}, u32[]{:S(2)}) collective-permute-start(bf16[384,1024]{1,0:T(8,128)(2,1)S(1)} %get-tuple-element.48), channel_id=1, source_target_pairs={{0,1},{1,0},{2,3},{3,2},{4,5},{5,4},{6,7},{7,6},{8,9},{9,8},{10,11... | collective-permute-start | bytes 2359304 | tf_op jit(solution)/shard_map/ppermute | solution.py:450
  37.5 0.1 collective-permute-start.7
  37.6 0.4 collective-permute-start.8
  38.0 7.0 %own.1 = (f32[1024,512]{1,0:T(8,128)S(1)}, f32[8,8,1024]{2,1,0:T(8,128)S(1)}, bf16[896,128]{1,0:T(8,128)(2,1)S(1)}) custom-call(s32[32]{0:T(128)S(1)} %copy-done.15, bf16[512,1024]{1,0:T(8,128)(2,1)S(1)} %get-tuple-element.50.queries, bf16[512,1024]{1,0:T(8,128)(2,1)S(1)} %get-tuple-element.51.keys, bf16[1024,512]{1,0:T(8,128)(2,1)S(1)} %get-tuple-element.52.values_t), custom_call_target="tpu_custom_call" | custom-call | flops 8000000000 | bytes 2000000 | tf_op jit(solution)/shard_map/own/pallas_call | solution.py:44
  45.0 0.0 collective-permute-done.8.fold_peer
  45.0 0.0 collective-permute-done.4.halo
  45.0 0.0 collective-permute-done.6.peer_keys
  45.0 0.0 collective-permute-done.7.peer_values
  45.0 0.0 copy-start.9
  45.0 0.0 copy-start.11
  45.0 0.0 copy-start.13
  45.1 8.5 %attend.1 = bf16[100,512]{1,0:T(8,128)(2,1)S(1)} custom-call(s32[8]{0:T(128)S(1)} %stack.48.info, bf16[384,1024]{1,0:T(8,128)(2,1)S(1)} %collective-permute-done.4.halo, bf16[384,1024]{1,0:T(8,128)(2,1)S(1)} %collective-permute-done.6.peer_keys, bf16[1024,384]{1,0:T(8,128)(2,1)S(1)} %collective-permute-done.7.peer_values, ...), custom_call_target="tpu_custom_call" | custom-call | flops 10000000000 | bytes 2000000 | tf_op jit(solution)/shard_map/attend/pallas_call | solution.py:44
  53.5 0.2 collective-permute-start.9
  53.7 1.2 %collective-permute-done.9 = bf16[100,512]{1,0:T(8,128)(2,1)S(1)} collective-permute-done((bf16[100,512]{1,0:T(8,128)(2,1)S(1)}, bf16[100,512]{1,0:T(8,128)(2,1)S(1)}, u32[]{:S(2)}, u32[]{:S(2)}) %collective-permute-start.9) | collective-permute-done | bytes 102432 | tf_op jit(solution)/shard_map/ppermute | solution.py:450
  55.0 5.0 %collective-permute-start.10 = (bf16[2,100,512]{2,1,0:T(8,128)(2,1)S(1)}, bf16[2,100,512]{2,1,0:T(8,128)(2,1)S(1)}, u32[]{:S(2)}, u32[]{:S(2)}) collective-permute-start(bf16[2,100,512]{2,1,0:T(8,128)(2,1)S(1)} %pad_maximum_fusion.own), channel_id=1, source_target_pairs={{0,2},{2,4},{4,6},{6,8},{8,10},{10,12},{12,14},{14,16},{16,18},{18... | collective-permute-start | bytes 614408 | tf_op jit(solution)/shard_map/ppermute | solution.py:457
  60.0 0.0 copy-done.9
  60.0 0.0 copy-done.11
  60.1 5.1 %spread.1 = (bf16[3072,1024]{1,0:T(8,128)(2,1)S(1)}, f32[100,1024]{1,0:T(8,128)S(1)}) custom-call(s32[8]{0:T(128)S(1)} %stack.48.info, bf16[3072,1024]{1,0:T(8,128)(2,1)S(1)} %early.1.spread_in, bf16[2,100,512]{2,1,0:T(8,128)(2,1)S(1)} %pad_maximum_fusion.own, s32[24,128]{1,0:T(8,128)S(1)} %copy-done.9, ...), custom_call_target="tpu_custom_call", output_to_operand_aliasing={{0}: (1, {})} | custom-call | flops 8000000000 | bytes 2000000 | tf_op jit(solution)/shard_map/spread/pallas_call | solution.py:44
  65.2 0.0 collective-permute-done.10.sent
  65.2 1.9 %collective-permute-start.11 = (bf16[2,100,512]{2,1,0:T(8,128)(2,1)S(1)}, bf16[2,100,512]{2,1,0:T(8,128)(2,1)S(1)}, u32[]{:S(2)}, u32[]{:S(2)}) collective-permute-start(bf16[2,100,512]{2,1,0:T(8,128)(2,1)S(1)} %collective-permute-done.10.sent), channel_id=1, source_target_pairs={{0,1},{1,0},{2,3},{3,2},{4,5},{5,4},{6,7},{7,6},{8,9},{9,8},{10,11... | collective-permute-start | bytes 614408 | tf_op jit(solution)/shard_map/ppermute | solution.py:450
  67.1 1.0 %sent.1.total = f32[100,1024]{1,0:T(8,128)S(1)} custom-call(s32[8]{0:T(128)S(1)} %stack.48.info, bf16[2,100,512]{2,1,0:T(8,128)(2,1)S(1)} %collective-permute-done.10.sent, bf16[3072,1024]{1,0:T(8,128)(2,1)S(1)} %get-tuple-element.61.spread, f32[100,1024]{1,0:T(8,128)S(1)} %get-tuple-element.62.base), custom_call_target="tpu_custom_call" | custom-call | flops 1000000000 | bytes 2000000 | tf_op jit(solution)/shard_map/sent/pallas_call | solution.py:44
  68.1 0.1 collective-permute-done.11.swapped_rows
  68.2 1.7 %decode.1 = bf16[100,1024]{1,0:T(8,128)(2,1)} custom-call(s32[8]{0:T(128)S(1)} %stack.48.info, bf16[2,100,512]{2,1,0:T(8,128)(2,1)S(1)} %collective-permute-done.11.swapped_rows, bf16[3072,1024]{1,0:T(8,128)(2,1)S(1)} %get-tuple-element.61.spread, f32[100,1024]{1,0:T(8,128)S(1)} %sent.1.total), custom_call_target="tpu_custom_call" | custom-call | flops 1000000000 | bytes 2000000 | tf_op jit(solution)/shard_map/decode/pallas_call | solution.py:44
  (20 shorter events, 0.1 us)
Async XLA Ops:
  0.0 28.6 %collective-permute-start.5 = (bf16[3,1024,512]{2,1,0:T(8,128)(2,1)}, bf16[3,1024,512]{2,1,0:T(8,128)(2,1)S(1)}, u32[]{:S(2)}, u32[]{:S(2)}) collective-permute-start(bf16[3,1024,512]{2,1,0:T(8,128)(2,1)} %bitcast.15), channel_id=1, source_target_pairs={{0,1},{1,0},{2,3},{3,2},{4,5},{5,4},{6,7},{7,6},{8,9},{9,8},{10,11... | collective-permute-start | bytes 9437192 | tf_op jit(solution)/shard_map/ppermute | solution.py:450
  0.7 12.8 %collective-permute-start = (bf16[100,512]{1,0:T(8,128)(2,1)}, bf16[100,512]{1,0:T(8,128)(2,1)S(1)}, u32[]{:S(2)}, u32[]{:S(2)}) collective-permute-start(bf16[100,512]{1,0:T(8,128)(2,1)} %win_own.1), channel_id=1, source_target_pairs={{0,1},{1,0},{2,3},{3,2},{4,5},{5,4},{6,7},{7,6},{8,9},{9,8},{10,11... | collective-permute-start | bytes 307208 | tf_op jit(solution)/shard_map/ppermute | solution.py:450
  0.7 12.8 %collective-permute-start.1 = (bf16[100,512]{1,0:T(8,128)(2,1)}, bf16[100,512]{1,0:T(8,128)(2,1)S(1)}, u32[]{:S(2)}, u32[]{:S(2)}) collective-permute-start(bf16[100,512]{1,0:T(8,128)(2,1)} %bitcast.21), channel_id=1, source_target_pairs={{0,1},{1,0},{2,3},{3,2},{4,5},{5,4},{6,7},{7,6},{8,9},{9,8},{10,11... | collective-permute-start | bytes 307208 | tf_op jit(solution)/shard_map/ppermute | solution.py:450
  1.2 13.1 %collective-permute-start.2 = (bf16[100,2048]{1,0:T(8,128)(2,1)}, bf16[100,2048]{1,0:T(8,128)(2,1)}, u32[]{:S(2)}, u32[]{:S(2)}) collective-permute-start(bf16[100,2048]{1,0:T(8,128)(2,1)} %bitcast.18), channel_id=1, source_target_pairs={{0,2},{2,4},{4,6},{6,8},{8,10},{10,12},{12,14},{14,16},{16,18},{18... | collective-permute-start | bytes 1228808 | tf_op jit(solution)/shard_map/ppermute | solution.py:457
  8.6 0.7 %copy-start.8 = (s32[24,128]{1,0:T(8,128)S(1)}, s32[24,128]{1,0:T(8,128)}, u32[]{:S(2)}) copy-start(s32[24,128]{1,0:T(8,128)} %src.5) | copy-start | bytes 36868
  9.3 0.7 %copy-start.10 = (s32[24,128]{1,0:T(8,128)S(1)}, s32[24,128]{1,0:T(8,128)}, u32[]{:S(2)}) copy-start(s32[24,128]{1,0:T(8,128)} %dst.5) | copy-start | bytes 36868
  10.0 0.7 copy-start.12
  10.7 2.7 %copy-start.3 = (bf16[100,512]{1,0:T(8,128)(2,1)S(1)}, bf16[100,512]{1,0:T(8,128)(2,1)}, u32[]{:S(2)}) copy-start(bf16[100,512]{1,0:T(8,128)(2,1)} %win_own.1) | copy-start | bytes 307204
  10.7 2.8 %copy-start.4 = (bf16[512,100]{0,1:T(8,128)(2,1)S(1)}, bf16[512,100]{0,1:T(8,128)(2,1)}, u32[]{:S(2)}) copy-start(bf16[512,100]{0,1:T(8,128)(2,1)} %param.24) | copy-start | bytes 307204
  10.7 2.8 %copy-start.5 = (s32[64,128]{1,0:T(8,128)S(1)}, s32[64,128]{1,0:T(8,128)}, u32[]{:S(2)}) copy-start(s32[64,128]{1,0:T(8,128)} %src.4) | copy-start | bytes 98308
  10.7 2.8 %copy-start.6 = (s32[64,128]{1,0:T(8,128)S(1)}, s32[64,128]{1,0:T(8,128)}, u32[]{:S(2)}) copy-start(s32[64,128]{1,0:T(8,128)} %dst.4) | copy-start | bytes 98308
  10.7 2.8 %copy-start.7 = (bf16[64,128]{1,0:T(8,128)(2,1)S(1)}, bf16[64,128]{1,0:T(8,128)(2,1)}, u32[]{:S(2)}) copy-start(bf16[64,128]{1,0:T(8,128)(2,1)} %weight.4) | copy-start | bytes 49156
  10.7 2.8 %copy-start.14 = (f32[1024]{0:T(1024)S(1)}, f32[1024]{0:T(1024)}, u32[]{:S(2)}) copy-start(f32[1024]{0:T(1024)} %param.20) | copy-start | bytes 12292
  13.5 2.2 %copy-start.1 = (bf16[512,1024]{1,0:T(8,128)(2,1)S(1)}, bf16[512,1024]{1,0:T(8,128)(2,1)}, u32[]{:S(2)}) copy-start(bf16[512,1024]{1,0:T(8,128)(2,1)} %w_out.1) | copy-start | bytes 3145732
  13.5 2.2 %copy-start.2 = (bf16[2048,100]{0,1:T(8,128)(2,1)S(1)}, bf16[2048,100]{0,1:T(8,128)(2,1)}, u32[]{:S(2)}) copy-start(bf16[2048,100]{0,1:T(8,128)(2,1)} %param.14) | copy-start | bytes 1228804
  14.3 3.1 %collective-permute-start.3 = (bf16[100,2048]{1,0:T(8,128)(2,1)}, bf16[100,2048]{1,0:T(8,128)(2,1)S(1)}, u32[]{:S(2)}, u32[]{:S(2)}) collective-permute-start(bf16[100,2048]{1,0:T(8,128)(2,1)} %collective-permute-done.2.sent), channel_id=1, source_target_pairs={{0,1},{1,0},{2,3},{3,2},{4,5},{5,4},{6,7},{7,6},{8,9},{9,8},{10,11... | collective-permute-start | bytes 1228808 | tf_op jit(solution)/shard_map/ppermute | solution.py:450
  17.3 11.2 %copy-start = (bf16[1024,3,512]{2,0,1:T(8,128)(2,1)S(1)}, bf16[1024,3,512]{2,0,1:T(8,128)(2,1)}, u32[]{:S(2)}) copy-start(bf16[1024,3,512]{2,0,1:T(8,128)(2,1)} %param.21) | copy-start | bytes 9437188
  26.6 18.4 %collective-permute-start.4 = (bf16[384,1024]{1,0:T(8,128)(2,1)S(1)}, bf16[384,1024]{1,0:T(8,128)(2,1)S(1)}, u32[]{:S(2)}, u32[]{:S(2)}) collective-permute-start(bf16[384,1024]{1,0:T(8,128)(2,1)S(1)} %get-tuple-element.45), channel_id=1, source_target_pairs={{1,2},{3,4},{5,6},{7,8},{9,10},{11,12},{13,14},{15,16},{17,18},{19... | collective-permute-start | bytes 2359304 | tf_op jit(solution)/shard_map/ppermute | solution.py:464
  28.6 9.4 %copy-start.15 = (s32[32]{0:T(128)S(1)}, s32[32]{0:T(128)}, u32[]{:S(2)}) copy-start(s32[32]{0:T(128)} %offsets.1) | copy-start | bytes 388
  33.0 12.0 %collective-permute-start.6 = (bf16[384,1024]{1,0:T(8,128)(2,1)S(1)}, bf16[384,1024]{1,0:T(8,128)(2,1)S(1)}, u32[]{:S(2)}, u32[]{:S(2)}) collective-permute-start(bf16[384,1024]{1,0:T(8,128)(2,1)S(1)} %get-tuple-element.48), channel_id=1, source_target_pairs={{0,1},{1,0},{2,3},{3,2},{4,5},{5,4},{6,7},{7,6},{8,9},{9,8},{10,11... | collective-permute-start | bytes 2359304 | tf_op jit(solution)/shard_map/ppermute | solution.py:450
  37.5 7.5 %collective-permute-start.7 = (bf16[1024,384]{1,0:T(8,128)(2,1)S(1)}, bf16[1024,384]{1,0:T(8,128)(2,1)S(1)}, u32[]{:S(2)}, u32[]{:S(2)}) collective-permute-start(bf16[1024,384]{1,0:T(8,128)(2,1)S(1)} %get-tuple-element.49), channel_id=1, source_target_pairs={{0,1},{1,0},{2,3},{3,2},{4,5},{5,4},{6,7},{7,6},{8,9},{9,8},{10,11... | collective-permute-start | bytes 2359304 | tf_op jit(solution)/shard_map/ppermute | solution.py:450
  37.6 7.4 %collective-permute-start.8 = (bf16[256,512]{1,0:T(8,128)(2,1)S(1)}, bf16[256,512]{1,0:T(8,128)(2,1)S(1)}, u32[]{:S(2)}, u32[]{:S(2)}) collective-permute-start(bf16[256,512]{1,0:T(8,128)(2,1)S(1)} %get-tuple-element.57.fold_own), channel_id=1, source_target_pairs={{0,1},{1,0},{2,3},{3,2},{4,5},{5,4},{6,7},{7,6},{8,9},{9,8},{10,11... | collective-permute-start | bytes 786440 | tf_op jit(solution)/shard_map/ppermute | solution.py:450
  45.0 15.0 %copy-start.9 = (s32[24,128]{1,0:T(8,128)S(1)}, s32[24,128]{1,0:T(8,128)}, u32[]{:S(2)}) copy-start(s32[24,128]{1,0:T(8,128)} %src.5) | copy-start | bytes 36868
  45.0 15.0 %copy-start.11 = (s32[24,128]{1,0:T(8,128)S(1)}, s32[24,128]{1,0:T(8,128)}, u32[]{:S(2)}) copy-start(s32[24,128]{1,0:T(8,128)} %dst.5) | copy-start | bytes 36868
  45.0 15.0 %copy-start.13 = (bf16[24,128]{1,0:T(8,128)(2,1)S(1)}, bf16[24,128]{1,0:T(8,128)(2,1)}, u32[]{:S(2)}) copy-start(bf16[24,128]{1,0:T(8,128)(2,1)} %weight.5) | copy-start | bytes 18436
  53.5 1.4 %collective-permute-start.9 = (bf16[100,512]{1,0:T(8,128)(2,1)S(1)}, bf16[100,512]{1,0:T(8,128)(2,1)S(1)}, u32[]{:S(2)}, u32[]{:S(2)}) collective-permute-start(bf16[100,512]{1,0:T(8,128)(2,1)S(1)} %attend.1), channel_id=1, source_target_pairs={{0,1},{1,0},{2,3},{3,2},{4,5},{5,4},{6,7},{7,6},{8,9},{9,8},{10,11... | collective-permute-start | bytes 307208 | tf_op jit(solution)/shard_map/ppermute | solution.py:450
  55.0 10.2 %collective-permute-start.10 = (bf16[2,100,512]{2,1,0:T(8,128)(2,1)S(1)}, bf16[2,100,512]{2,1,0:T(8,128)(2,1)S(1)}, u32[]{:S(2)}, u32[]{:S(2)}) collective-permute-start(bf16[2,100,512]{2,1,0:T(8,128)(2,1)S(1)} %pad_maximum_fusion.own), channel_id=1, source_target_pairs={{0,2},{2,4},{4,6},{6,8},{8,10},{10,12},{12,14},{14,16},{16,18},{18... | collective-permute-start | bytes 614408 | tf_op jit(solution)/shard_map/ppermute | solution.py:457
  65.2 3.0 %collective-permute-start.11 = (bf16[2,100,512]{2,1,0:T(8,128)(2,1)S(1)}, bf16[2,100,512]{2,1,0:T(8,128)(2,1)S(1)}, u32[]{:S(2)}, u32[]{:S(2)}) collective-permute-start(bf16[2,100,512]{2,1,0:T(8,128)(2,1)S(1)} %collective-permute-done.10.sent), channel_id=1, source_target_pairs={{0,1},{1,0},{2,3},{3,2},{4,5},{5,4},{6,7},{7,6},{8,9},{9,8},{10,11... | collective-permute-start | bytes 614408 | tf_op jit(solution)/shard_map/ppermute | solution.py:450

commit v11 on v10

--- a/solution.py
+++ b/solution.py
@@ -95,29 +95,15 @@
     mask[...] = mask_wide[...].astype(BF16)
 
 
-def prepare_body(
-    info, src, dst, weight, gain, win_own, win_peer, dec_own, dec_peer,
-    sources, targets, weights, gains, w_in, w_decode,
-    w_wide,
-):
-    core, live, mesh_base = info[0], info[1], info[3]
-    w_wide[...] = jnp.zeros_like(w_wide)
-    by_core(core, w_wide, win_own, win_peer)
-    w_in[...] = (w_wide[...] * 0.5).astype(BF16)
-    by_core(core, w_wide, dec_own, dec_peer)
-    w_decode[...] = w_wide[...].astype(BF16)
+def prepare_body(info, src, dst, weight, gain, sources, targets, weights, gains):
     slots = lax.broadcasted_iota(jnp.int32, weights.shape, 0)
-    weights[...] = jnp.where(slots < live, weight[...].astype(F32), 0.0)
-    targets[...] = dst[...] - mesh_base
+    weights[...] = jnp.where(slots < info[1], weight[...].astype(F32), 0.0)
+    targets[...] = dst[...] - info[3]
     sources[...] = src[...] - info[2]
     gains[...] = gain[...]
 
 
-def unpack_body(info, grid, sent, w_out, w_decode, rows, fold, wide):
-    folded = matmul_t(w_decode[...], w_out[...])
-    upper = folded.astype(BF16)
-    fold[:LANES, :] = upper
-    fold[LANES:, :] = (folded - upper.astype(F32)).astype(BF16)
+def unpack_body(info, grid, sent, rows, wide):
     wide[...] = jnp.zeros_like(wide)
     to_rows(grid, wide, rows, G_BAND)
     to_rows(sent, wide, rows, info[0] * 2 * G_BAND)
@@ -186,11 +172,14 @@
 
 
 def encode_body(
-    info, src, grid_rows, swapped_rows, w_in, targets, weights, gain,
+    info, src, grid_rows, swapped_rows, win_own, win_peer, targets, weights, gain,
     rows, mesh_zero, normed, to_band,
-    wide, first, second, total,
+    wide, w_wide, w_in, first, second, total,
 ):
     core = info[0]
+    w_wide[...] = jnp.zeros_like(w_wide)
+    by_core(core, w_wide, win_own, win_peer)
+    w_in[...] = (w_wide[...] * 0.5).astype(BF16)
     wide[...] = jnp.zeros_like(wide)
     to_rows(swapped_rows, wide, rows, (1 - core) * 2 * G_BAND)
     encode_tiles(
@@ -267,9 +256,17 @@
 
 
 def project_body(
-    info, normed, w_own, w_peer, mesh_zero, w_decode,
-    queries, keys, values_t, keys_sent, values_sent, straight,
+    info, normed, w_own, w_peer, mesh_zero, dec_own, dec_peer, w_out,
+    queries, keys, values_t, keys_sent, values_sent, straight, fold,
+    w_wide, w_decode,
 ):
+    w_wide[...] = jnp.zeros_like(w_wide)
+    by_core(info[0], w_wide, dec_own, dec_peer)
+    w_decode[...] = w_wide[...].astype(BF16)
+    folded = matmul_t(w_decode[...], w_out[...])
+    upper = folded.astype(BF16)
+    fold[:LANES, :] = upper
+    fold[LANES:, :] = (folded - upper.astype(F32)).astype(BF16)
     rows = normed[...]
     straight[...] = matmul_t(w_decode[...], mesh_zero[...])
     for half, weight in enumerate((w_own, w_peer)):
@@ -381,9 +378,12 @@
     projected[...] = (straight[...] + both[:LANES, :] + both[LANES:, :])[:C, :].astype(BF16)
 
 
-def half_term(part, spread, place):
-    rows = pl.ds(pl.multiple_of(place * ROWS, ROWS), ROWS)
-    return matmul(part, spread[rows, :])
+def pair_term(core, pair, spread, place):
+    rows = pl.ds(pl.multiple_of(place * ROWS, 2 * ROWS), 2 * ROWS)
+    low = jnp.where(core == 0, pair[0].astype(F32), pair[1].astype(F32))
+    high = jnp.where(core == 0, pair[1].astype(F32), pair[0].astype(F32))
+    halves = jnp.concatenate([low, high], axis=1).astype(BF16)
+    return matmul(halves, spread[rows, :])
 
 
 def spread_halves(info, src, dst, weight, spread, sources, tables, weights, places):
@@ -426,24 +426,17 @@
     core = info[0]
     spread_halves(info, src, dst, weight, spread, sources, tables, weights, range(EARLY, 6))
     fields = grid[:, pl.ds(pl.multiple_of(core * GQ, GQ), GQ)].astype(F32)
-    terms = half_term(own[0], spread, 2 + core) + half_term(own[1], spread, 3 - core)
-    base[...] = fields + terms
+    base[...] = fields + pair_term(core, own, spread, 2)
 
 
 def sent_body(info, sent, spread, base, total):
     core = info[0]
-    total[...] = (
-        base[...]
-        + half_term(sent[0], spread, 5 * core)
-        + half_term(sent[1], spread, 3 * core + 1)
-    )
+    total[...] = base[...] + pair_term(core, sent, spread, 4 * core)
 
 
 def decode_body(info, swapped_rows, spread, total, out):
     other = 1 - info[0]
-    terms = half_term(swapped_rows[0], spread, 5 * other)
-    terms = terms + half_term(swapped_rows[1], spread, 3 * other + 1)
-    out[...] = (total[...] + terms).astype(BF16)
+    out[...] = (total[...] + pair_term(other, swapped_rows, spread, 4 * other)).astype(BF16)
 
 
 def swapped(value):
@@ -484,11 +477,8 @@
         (band - 1) * 2 * ROWS,
         device * GQ,
     ]).astype(jnp.int32)
-    win_peer = swapped(w_in)
     dec_own = w_decode.T
-    dec_peer = swapped(dec_own)
     qkv_own = w_qkv.transpose(1, 0, 2)
-    qkv_peer = swapped(qkv_own)
     edges = jax.ShapeDtypeStruct(enc_src.shape, jnp.int32)
     spread_out = jax.ShapeDtypeStruct((6 * ROWS, GQ), BF16)
     spread_scratch = [
@@ -501,41 +491,38 @@
         spread_scratch, 5 * 10 ** 9, 10, "early",
     )
     spread, info = lax.optimization_barrier((spread, info))
-    sources, targets, weights, gain, w_in_all, dec_all = call(
+    sources, targets, weights, gain = call(
         prepare_body,
-        (info, enc_src, enc_dst, enc_weight, norm_gain.reshape(1, D), w_in, win_peer,
-         dec_own, dec_peer),
+        (info, enc_src, enc_dst, enc_weight, norm_gain.reshape(1, D)),
         1,
         [
             edges,
             edges,
             jax.ShapeDtypeStruct(enc_weight.shape, F32),
             jax.ShapeDtypeStruct((1, D), F32),
-            jax.ShapeDtypeStruct((LANES, D), BF16),
-            jax.ShapeDtypeStruct((LANES, D), BF16),
         ],
-        [pltpu.VMEM((LANES, D), F32)],
-        5 * 10 ** 9, 6, "prepare",
-    )
-    grid_sent, w_in_all, spread = lax.optimization_barrier((grid_sent, w_in_all, spread))
-    grid_swapped = swapped(grid_sent)
-    grid_rows, fold_own = call(
+        [],
+        5 * 10 ** 9, 4, "prepare",
+    )
+    grid_sent, gain, spread, w_in = lax.optimization_barrier((grid_sent, gain, spread, w_in))
+    grid_swapped, win_peer = swapped(grid_sent), swapped(w_in)
+    grid_rows = call(
         unpack_body,
-        (info, grid, grid_sent, w_out_attn, dec_all),
+        (info, grid, grid_sent),
         1,
-        [
-            jax.ShapeDtypeStruct((3 * G_BAND, LANES), F32),
-            jax.ShapeDtypeStruct((2 * LANES, HALF), BF16),
-        ],
+        jax.ShapeDtypeStruct((3 * G_BAND, LANES), F32),
         [pltpu.VMEM((LANES, G_BAND), F32)],
         2 * 10 ** 9, 6, "unpack",
     )
-    fold_peer = swapped(fold_own)
+    grid_swapped, grid_rows, win_peer, dec_own, qkv_own = lax.optimization_barrier(
+        (grid_swapped, grid_rows, win_peer, dec_own, qkv_own)
+    )
+    dec_peer, qkv_peer = swapped(dec_own), swapped(qkv_own)
     band_rows = jax.ShapeDtypeStruct((ROWS, D), BF16)
     step_buffers = [pltpu.VMEM((STEP, LANES), F32)] * 2 + [pltpu.VMEM((ROWS, D), F32)]
     _, mesh_zero, normed, to_band = call(
         encode_body,
-        (info, sources, grid_rows, grid_swapped, w_in_all, targets, weights, gain),
+        (info, sources, grid_rows, grid_swapped, w_in, win_peer, targets, weights, gain),
         2,
         [
             jax.ShapeDtypeStruct((3 * G_BAND, LANES), F32),
@@ -543,13 +530,17 @@
             band_rows,
             jax.ShapeDtypeStruct((WIN, D), BF16),
         ],
-        [pltpu.VMEM((LANES, G_BAND), F32)] + step_buffers,
+        [
+            pltpu.VMEM((LANES, G_BAND), F32),
+            pltpu.VMEM((LANES, D), F32),
+            pltpu.VMEM((LANES, D), BF16),
+        ] + step_buffers,
         7 * 10 ** 9, 14, "encode", {2: 0},
     )
     halo_band = over_the_edge(to_band)
-    queries, keys, values_t, keys_sent, values_sent, straight = call(
+    queries, keys, values_t, keys_sent, values_sent, straight, fold_own = call(
         project_body,
-        (info, normed, qkv_own, qkv_peer, mesh_zero, dec_all),
+        (info, normed, qkv_own, qkv_peer, mesh_zero, dec_own, dec_peer, w_out_attn),
         1,
         [
             jax.ShapeDtypeStruct((ROWS, D), BF16),
@@ -558,11 +549,13 @@
             jax.ShapeDtypeStruct((WIN, D), BF16),
             jax.ShapeDtypeStruct((D, WIN), BF16),
             jax.ShapeDtypeStruct((LANES, ROWS), F32),
+            jax.ShapeDtypeStruct((2 * LANES, HALF), BF16),
         ],
-        [],
+        [pltpu.VMEM((LANES, D), F32), pltpu.VMEM((LANES, D), BF16)],
         6 * 10 ** 9, 10, "project",
     )
     peer_keys, peer_values = swapped(keys_sent), swapped(values_sent)
+    fold_peer = swapped(fold_own)
     sums, stats, mask = call(
         own_body,
         (offsets, queries, keys, values_t),

time: 70.2 us -> 69.9 us (level)
  transfers between devices with their start and end apart: 12 -> 12, of which waited for: 2 -> 3; matrix products, arithmetic and copies ran while one was open for 0% -> 0% of each run, Pallas kernels for 45% -> 45%
where the time goes in v11:
time: 69.9 us; the launch traced here: 69.5 us
  Pallas kernels  41.6 us (60%)
  starting transfers between devices  22.9 us (33%)
  local copies, waits for them, and re-layouts  2.26 us (3%)
  waiting for transfers between devices  1.88 us (3%)
  between operations  0.96 us (1%)
    pallas_call x10, Pallas kernels, call(): pl.pallas_call(body, out_shape=outs, in_specs=specs, out_specs=jax.tree.m...  41.6 us
    ppermute x2, starting transfers between devices, up_and_down(): return lax.ppermute(value, ('band', 'mp'), pairs)  11.3 us
    ppermute x9, starting transfers between devices, swapped(): return lax.ppermute(value, 'mp', [(0, 1), (1, 0)])  9.65 us
    unnamed x32, local copies, waits for them, and re-layouts  2.18 us
    ppermute x1, starting transfers between devices, over_the_edge(): return lax.ppermute(value, ('band', 'mp'), pairs)  1.92 us
    ppermute x9, waiting for transfers between devices, swapped(): return lax.ppermute(value, 'mp', [(0, 1), (1, 0)])  1.87 us
  transfers between devices with their start and end apart: 12, of which 3 were waited for; matrix products, arithmetic and copies ran while one was open for 0% of the time, Pallas kernels for 45%

profile of v11, /device:TPU:97, one launch (start us, length us, event | category | flops | bytes accessed | tf_op | source)
XLA Modules:
  0.0 69.5 jit_solution(17064731444148319423)
XLA Ops:
  0.0 6.7 %collective-permute-start = (bf16[100,2048]{1,0:T(8,128)(2,1)}, bf16[100,2048]{1,0:T(8,128)(2,1)S(1)}, u32[]{:S(2)}, u32[]{:S(2)}) collective-permute-start(bf16[100,2048]{1,0:T(8,128)(2,1)} %bitcast.18), channel_id=1, source_target_pairs={{0,2},{2,4},{4,6},{6,8},{8,10},{10,12},{12,14},{14,16},{16,18},{18... | collective-permute-start | bytes 1228808 | tf_op jit(solution)/shard_map/ppermute | solution.py:450
  7.3 0.1 stack.48.info
  7.4 0.7 %copy-done.8 = s32[24,128]{1,0:T(8,128)S(1)} copy-done((s32[24,128]{1,0:T(8,128)S(1)}, s32[24,128]{1,0:T(8,128)}, u32[]{:S(2)}) %copy-start.8) | copy-done | bytes 12312
  8.1 0.7 %copy-done.10 = s32[24,128]{1,0:T(8,128)S(1)} copy-done((s32[24,128]{1,0:T(8,128)S(1)}, s32[24,128]{1,0:T(8,128)}, u32[]{:S(2)}) %copy-start.10) | copy-done | bytes 12312
  8.8 0.7 copy-done.12
  9.5 2.7 %early.1.spread_in = bf16[3072,1024]{1,0:T(8,128)(2,1)S(1)} custom-call(s32[8]{0:T(128)S(1)} %stack.48.info, s32[24,128]{1,0:T(8,128)S(1)} %copy-done.8, s32[24,128]{1,0:T(8,128)S(1)} %copy-done.10, bf16[24,128]{1,0:T(8,128)(2,1)S(1)} %copy-done.12), custom_call_target="tpu_custom_call" | custom-call | flops 5000000000 | bytes 2000000 | tf_op jit(solution)/shard_map/early/pallas_call | solution.py:44
  12.2 0.0 copy-done.5
  12.2 0.0 copy-done.6
  12.3 0.0 copy-start.3
  12.3 0.0 copy-start.2
  12.3 0.6 prepare.1
  12.9 0.0 collective-permute-done.sent
  12.9 0.0 copy-start
  12.9 0.0 copy-start.4
  12.9 2.2 %collective-permute-start.1 = (bf16[100,2048]{1,0:T(8,128)(2,1)S(1)}, bf16[100,2048]{1,0:T(8,128)(2,1)S(1)}, u32[]{:S(2)}, u32[]{:S(2)}) collective-permute-start(bf16[100,2048]{1,0:T(8,128)(2,1)S(1)} %collective-permute-done.sent), channel_id=1, source_target_pairs={{0,1},{1,0},{2,3},{3,2},{4,5},{5,4},{6,7},{7,6},{8,9},{9,8},{10,11... | collective-permute-start | bytes 1228808 | tf_op jit(solution)/shard_map/ppermute | solution.py:443
  15.1 0.1 collective-permute-start.2
  15.2 0.9 %unpack.1.grid_rows = f32[6144,128]{1,0:T(8,128)S(1)} custom-call(s32[8]{0:T(128)S(1)} %stack.48.info, bf16[100,2048]{1,0:T(8,128)(2,1)S(1)} %bitcast.19, bf16[100,2048]{1,0:T(8,128)(2,1)S(1)} %collective-permute-done.sent), custom_call_target="tpu_custom_call" | custom-call | flops 2000000000 | bytes 2000000 | tf_op jit(solution)/shard_map/unpack/pallas_call | solution.py:44
  16.1 0.6 collective-permute-done.2.win_peer
  16.7 0.0 collective-permute-done.1.swapped_rows
  16.7 0.4 collective-permute-start.4
  17.1 0.1 collective-permute-start.5
  17.2 9.3 %encode.1 = (f32[6144,128]{1,0:T(8,128)S(1)}, bf16[512,1024]{1,0:T(8,128)(2,1)S(1)}, bf16[512,1024]{1,0:T(8,128)(2,1)S(1)}, bf16[384,1024]{1,0:T(8,128)(2,1)S(1)}) custom-call(s32[8]{0:T(128)S(1)} %stack.48.info, s32[64,128]{1,0:T(8,128)S(1)} %get-tuple-element.38.src, f32[6144,128]{1,0:T(8,128)S(1)} %unpack.1.grid_rows, ...), custom_call_target="tpu_custom_call", output_to_operand_aliasing={{0}: (2, {})} | custom-call | flops 7000000000 | bytes 2000000 | tf_op jit(solution)/shard_map/encode/pallas_call | solution.py:44
  26.5 1.9 %collective-permute-start.3 = (bf16[384,1024]{1,0:T(8,128)(2,1)S(1)}, bf16[384,1024]{1,0:T(8,128)(2,1)S(1)}, u32[]{:S(2)}, u32[]{:S(2)}) collective-permute-start(bf16[384,1024]{1,0:T(8,128)(2,1)S(1)} %get-tuple-element.49), channel_id=1, source_target_pairs={{1,2},{3,4},{5,6},{7,8},{9,10},{11,12},{13,14},{15,16},{17,18},{19... | collective-permute-start | bytes 2359304 | tf_op jit(solution)/shard_map/ppermute | solution.py:457
  28.4 0.0 collective-permute-done.5.dec_peer
  28.4 0.0 collective-permute-done.4.w_peer
  28.4 0.0 copy-start.15
  28.4 4.9 %project.1 = (bf16[512,1024]{1,0:T(8,128)(2,1)S(1)}, bf16[512,1024]{1,0:T(8,128)(2,1)S(1)}, bf16[1024,512]{1,0:T(8,128)(2,1)S(1)}, bf16[384,1024]{1,0:T(8,128)(2...) custom-call(s32[8]{0:T(128)S(1)} %stack.48.info, ...), custom_call_target="tpu_custom_call" | custom-call | flops 6000000000 | bytes 2000000 | tf_op jit(solution)/shard_map/project/pallas_call | solution.py:44
  33.3 3.8 %collective-permute-start.6 = (bf16[384,1024]{1,0:T(8,128)(2,1)S(1)}, bf16[384,1024]{1,0:T(8,128)(2,1)S(1)}, u32[]{:S(2)}, u32[]{:S(2)}) collective-permute-start(bf16[384,1024]{1,0:T(8,128)(2,1)S(1)} %get-tuple-element.54), channel_id=1, source_target_pairs={{0,1},{1,0},{2,3},{3,2},{4,5},{5,4},{6,7},{7,6},{8,9},{9,8},{10,11... | collective-permute-start | bytes 2359304 | tf_op jit(solution)/shard_map/ppermute | solution.py:443
  37.1 0.1 collective-permute-start.7
  37.2 0.4 collective-permute-start.8
  37.7 7.0 %own.1 = (f32[1024,512]{1,0:T(8,128)S(1)}, f32[8,8,1024]{2,1,0:T(8,128)S(1)}, bf16[896,128]{1,0:T(8,128)(2,1)S(1)}) custom-call(s32[32]{0:T(128)S(1)} %copy-done.15, bf16[512,1024]{1,0:T(8,128)(2,1)S(1)} %get-tuple-element.56.queries, bf16[512,1024]{1,0:T(8,128)(2,1)S(1)} %get-tuple-element.57.keys, bf16[1024,512]{1,0:T(8,128)(2,1)S(1)} %get-tuple-element.58.values_t), custom_call_target="tpu_custom_call" | custom-call | flops 8000000000 | bytes 2000000 | tf_op jit(solution)/shard_map/own/pallas_call | solution.py:44
  44.6 0.0 collective-permute-done.3.halo
  44.6 0.0 collective-permute-done.8.fold_peer
  44.7 0.0 collective-permute-done.6.peer_keys
  44.7 0.0 collective-permute-done.7.peer_values
  44.7 0.0 copy-start.9
  44.7 0.0 copy-start.11
  44.7 0.0 copy-start.13
  44.7 8.5 %attend.1 = bf16[100,512]{1,0:T(8,128)(2,1)S(1)} custom-call(s32[8]{0:T(128)S(1)} %stack.48.info, bf16[384,1024]{1,0:T(8,128)(2,1)S(1)} %collective-permute-done.3.halo, bf16[384,1024]{1,0:T(8,128)(2,1)S(1)} %collective-permute-done.6.peer_keys, bf16[1024,384]{1,0:T(8,128)(2,1)S(1)} %collective-permute-done.7.peer_values, ...), custom_call_target="tpu_custom_call" | custom-call | flops 10000000000 | bytes 2000000 | tf_op jit(solution)/shard_map/attend/pallas_call | solution.py:44
  53.2 0.2 collective-permute-start.9
  53.4 1.2 %collective-permute-done.9 = bf16[100,512]{1,0:T(8,128)(2,1)S(1)} collective-permute-done((bf16[100,512]{1,0:T(8,128)(2,1)S(1)}, bf16[100,512]{1,0:T(8,128)(2,1)S(1)}, u32[]{:S(2)}, u32[]{:S(2)}) %collective-permute-start.9) | collective-permute-done | bytes 102432 | tf_op jit(solution)/shard_map/ppermute | solution.py:443
  54.6 4.6 %collective-permute-start.10 = (bf16[2,100,512]{2,1,0:T(8,128)(2,1)S(1)}, bf16[2,100,512]{2,1,0:T(8,128)(2,1)S(1)}, u32[]{:S(2)}, u32[]{:S(2)}) collective-permute-start(bf16[2,100,512]{2,1,0:T(8,128)(2,1)S(1)} %pad_maximum_fusion.own), channel_id=1, source_target_pairs={{0,2},{2,4},{4,6},{6,8},{8,10},{10,12},{12,14},{14,16},{16,18},{18... | collective-permute-start | bytes 614408 | tf_op jit(solution)/shard_map/ppermute | solution.py:450
  59.3 5.1 %spread.1 = (bf16[3072,1024]{1,0:T(8,128)(2,1)S(1)}, f32[100,1024]{1,0:T(8,128)S(1)}) custom-call(s32[8]{0:T(128)S(1)} %stack.48.info, bf16[3072,1024]{1,0:T(8,128)(2,1)S(1)} %early.1.spread_in, bf16[2,100,512]{2,1,0:T(8,128)(2,1)S(1)} %pad_maximum_fusion.own, s32[24,128]{1,0:T(8,128)S(1)} %copy-done.9, ...), custom_call_target="tpu_custom_call", output_to_operand_aliasing={{0}: (1, {})} | custom-call | flops 8000000000 | bytes 2000000 | tf_op jit(solution)/shard_map/spread/pallas_call | solution.py:44
  64.4 0.0 collective-permute-done.10.sent
  64.4 2.3 %collective-permute-start.11 = (bf16[2,100,512]{2,1,0:T(8,128)(2,1)S(1)}, bf16[2,100,512]{2,1,0:T(8,128)(2,1)S(1)}, u32[]{:S(2)}, u32[]{:S(2)}) collective-permute-start(bf16[2,100,512]{2,1,0:T(8,128)(2,1)S(1)} %collective-permute-done.10.sent), channel_id=1, source_target_pairs={{0,1},{1,0},{2,3},{3,2},{4,5},{5,4},{6,7},{7,6},{8,9},{9,8},{10,11... | collective-permute-start | bytes 614408 | tf_op jit(solution)/shard_map/ppermute | solution.py:443
  66.7 1.0 %sent.1.total = f32[100,1024]{1,0:T(8,128)S(1)} custom-call(s32[8]{0:T(128)S(1)} %stack.48.info, bf16[2,100,512]{2,1,0:T(8,128)(2,1)S(1)} %collective-permute-done.10.sent, bf16[3072,1024]{1,0:T(8,128)(2,1)S(1)} %get-tuple-element.67.spread, f32[100,1024]{1,0:T(8,128)S(1)} %get-tuple-element.68.base), custom_call_target="tpu_custom_call" | custom-call | flops 1000000000 | bytes 2000000 | tf_op jit(solution)/shard_map/sent/pallas_call | solution.py:44
  67.8 0.1 collective-permute-done.11.swapped_rows
  67.8 1.7 %decode.1 = bf16[100,1024]{1,0:T(8,128)(2,1)} custom-call(s32[8]{0:T(128)S(1)} %stack.48.info, bf16[2,100,512]{2,1,0:T(8,128)(2,1)S(1)} %collective-permute-done.11.swapped_rows, bf16[3072,1024]{1,0:T(8,128)(2,1)S(1)} %get-tuple-element.67.spread, f32[100,1024]{1,0:T(8,128)S(1)} %sent.1.total), custom_call_target="tpu_custom_call" | custom-call | flops 1000000000 | bytes 2000000 | tf_op jit(solution)/shard_map/decode/pallas_call | solution.py:44
  (20 shorter events, 0.1 us)
Async XLA Ops:
  0.0 12.9 %collective-permute-start = (bf16[100,2048]{1,0:T(8,128)(2,1)}, bf16[100,2048]{1,0:T(8,128)(2,1)S(1)}, u32[]{:S(2)}, u32[]{:S(2)}) collective-permute-start(bf16[100,2048]{1,0:T(8,128)(2,1)} %bitcast.18), channel_id=1, source_target_pairs={{0,2},{2,4},{4,6},{6,8},{8,10},{10,12},{12,14},{14,16},{16,18},{18... | collective-permute-start | bytes 1228808 | tf_op jit(solution)/shard_map/ppermute | solution.py:450
  7.4 0.7 %copy-start.8 = (s32[24,128]{1,0:T(8,128)S(1)}, s32[24,128]{1,0:T(8,128)}, u32[]{:S(2)}) copy-start(s32[24,128]{1,0:T(8,128)} %src.5) | copy-start | bytes 36868
  8.1 0.7 %copy-start.10 = (s32[24,128]{1,0:T(8,128)S(1)}, s32[24,128]{1,0:T(8,128)}, u32[]{:S(2)}) copy-start(s32[24,128]{1,0:T(8,128)} %dst.5) | copy-start | bytes 36868
  8.8 0.7 copy-start.12
  9.5 2.7 %copy-start.5 = (s32[64,128]{1,0:T(8,128)S(1)}, s32[64,128]{1,0:T(8,128)}, u32[]{:S(2)}) copy-start(s32[64,128]{1,0:T(8,128)} %src.4) | copy-start | bytes 98308
  9.5 2.7 %copy-start.6 = (s32[64,128]{1,0:T(8,128)S(1)}, s32[64,128]{1,0:T(8,128)}, u32[]{:S(2)}) copy-start(s32[64,128]{1,0:T(8,128)} %dst.4) | copy-start | bytes 98308
  9.5 2.7 %copy-start.7 = (bf16[64,128]{1,0:T(8,128)(2,1)S(1)}, bf16[64,128]{1,0:T(8,128)(2,1)}, u32[]{:S(2)}) copy-start(bf16[64,128]{1,0:T(8,128)(2,1)} %weight.4) | copy-start | bytes 49156
  9.5 2.7 %copy-start.14 = (f32[1024]{0:T(1024)S(1)}, f32[1024]{0:T(1024)}, u32[]{:S(2)}) copy-start(f32[1024]{0:T(1024)} %param.20) | copy-start | bytes 12292
  12.3 2.9 %copy-start.3 = (bf16[100,512]{1,0:T(8,128)(2,1)S(1)}, bf16[100,512]{1,0:T(8,128)(2,1)}, u32[]{:S(2)}) copy-start(bf16[100,512]{1,0:T(8,128)(2,1)} %win_own) | copy-start | bytes 307204
  12.3 2.9 %copy-start.2 = (bf16[2048,100]{0,1:T(8,128)(2,1)S(1)}, bf16[2048,100]{0,1:T(8,128)(2,1)}, u32[]{:S(2)}) copy-start(bf16[2048,100]{0,1:T(8,128)(2,1)} %param.14) | copy-start | bytes 1228804
  12.9 3.8 %copy-start = (bf16[1024,3,512]{2,0,1:T(8,128)(2,1)S(1)}, bf16[1024,3,512]{2,0,1:T(8,128)(2,1)}, u32[]{:S(2)}) copy-start(bf16[1024,3,512]{2,0,1:T(8,128)(2,1)} %param.21) | copy-start | bytes 9437188
  12.9 4.2 %copy-start.4 = (bf16[512,100]{0,1:T(8,128)(2,1)S(1)}, bf16[512,100]{0,1:T(8,128)(2,1)}, u32[]{:S(2)}) copy-start(bf16[512,100]{0,1:T(8,128)(2,1)} %param.24) | copy-start | bytes 307204
  12.9 3.8 %collective-permute-start.1 = (bf16[100,2048]{1,0:T(8,128)(2,1)S(1)}, bf16[100,2048]{1,0:T(8,128)(2,1)S(1)}, u32[]{:S(2)}, u32[]{:S(2)}) collective-permute-start(bf16[100,2048]{1,0:T(8,128)(2,1)S(1)} %collective-permute-done.sent), channel_id=1, source_target_pairs={{0,1},{1,0},{2,3},{3,2},{4,5},{5,4},{6,7},{7,6},{8,9},{9,8},{10,11... | collective-permute-start | bytes 1228808 | tf_op jit(solution)/shard_map/ppermute | solution.py:443
  15.1 1.5 %collective-permute-start.2 = (bf16[100,512]{1,0:T(8,128)(2,1)S(1)}, bf16[100,512]{1,0:T(8,128)(2,1)S(1)}, u32[]{:S(2)}, u32[]{:S(2)}) collective-permute-start(bf16[100,512]{1,0:T(8,128)(2,1)S(1)} %copy-done.3), channel_id=1, source_target_pairs={{0,1},{1,0},{2,3},{3,2},{4,5},{5,4},{6,7},{7,6},{8,9},{9,8},{10,11... | collective-permute-start | bytes 307208 | tf_op jit(solution)/shard_map/ppermute | solution.py:443
  16.7 11.7 %collective-permute-start.4 = (bf16[3,1024,512]{2,1,0:T(8,128)(2,1)S(1)}, bf16[3,1024,512]{2,1,0:T(8,128)(2,1)S(1)}, u32[]{:S(2)}, u32[]{:S(2)}) collective-permute-start(bf16[3,1024,512]{2,1,0:T(8,128)(2,1)S(1)} %bitcast.15), channel_id=1, source_target_pairs={{0,1},{1,0},{2,3},{3,2},{4,5},{5,4},{6,7},{7,6},{8,9},{9,8},{10,11... | collective-permute-start | bytes 9437192 | tf_op jit(solution)/shard_map/ppermute | solution.py:443
  17.1 11.4 %collective-permute-start.5 = (bf16[100,512]{1,0:T(8,128)(2,1)S(1)}, bf16[100,512]{1,0:T(8,128)(2,1)S(1)}, u32[]{:S(2)}, u32[]{:S(2)}) collective-permute-start(bf16[100,512]{1,0:T(8,128)(2,1)S(1)} %bitcast.21), channel_id=1, source_target_pairs={{0,1},{1,0},{2,3},{3,2},{4,5},{5,4},{6,7},{7,6},{8,9},{9,8},{10,11... | collective-permute-start | bytes 307208 | tf_op jit(solution)/shard_map/ppermute | solution.py:443
  17.2 11.2 %copy-start.1 = (bf16[512,1024]{1,0:T(8,128)(2,1)S(1)}, bf16[512,1024]{1,0:T(8,128)(2,1)}, u32[]{:S(2)}) copy-start(bf16[512,1024]{1,0:T(8,128)(2,1)} %w_out.1) | copy-start | bytes 3145732
  26.5 18.2 %collective-permute-start.3 = (bf16[384,1024]{1,0:T(8,128)(2,1)S(1)}, bf16[384,1024]{1,0:T(8,128)(2,1)S(1)}, u32[]{:S(2)}, u32[]{:S(2)}) collective-permute-start(bf16[384,1024]{1,0:T(8,128)(2,1)S(1)} %get-tuple-element.49), channel_id=1, source_target_pairs={{1,2},{3,4},{5,6},{7,8},{9,10},{11,12},{13,14},{15,16},{17,18},{19... | collective-permute-start | bytes 2359304 | tf_op jit(solution)/shard_map/ppermute | solution.py:457
  28.4 9.2 %copy-start.15 = (s32[32]{0:T(128)S(1)}, s32[32]{0:T(128)}, u32[]{:S(2)}) copy-start(s32[32]{0:T(128)} %offsets.1) | copy-start | bytes 388
  33.3 11.3 %collective-permute-start.6 = (bf16[384,1024]{1,0:T(8,128)(2,1)S(1)}, bf16[384,1024]{1,0:T(8,128)(2,1)S(1)}, u32[]{:S(2)}, u32[]{:S(2)}) collective-permute-start(bf16[384,1024]{1,0:T(8,128)(2,1)S(1)} %get-tuple-element.54), channel_id=1, source_target_pairs={{0,1},{1,0},{2,3},{3,2},{4,5},{5,4},{6,7},{7,6},{8,9},{9,8},{10,11... | collective-permute-start | bytes 2359304 | tf_op jit(solution)/shard_map/ppermute | solution.py:443
  37.1 7.5 %collective-permute-start.7 = (bf16[1024,384]{1,0:T(8,128)(2,1)S(1)}, bf16[1024,384]{1,0:T(8,128)(2,1)S(1)}, u32[]{:S(2)}, u32[]{:S(2)}) collective-permute-start(bf16[1024,384]{1,0:T(8,128)(2,1)S(1)} %get-tuple-element.55), channel_id=1, source_target_pairs={{0,1},{1,0},{2,3},{3,2},{4,5},{5,4},{6,7},{7,6},{8,9},{9,8},{10,11... | collective-permute-start | bytes 2359304 | tf_op jit(solution)/shard_map/ppermute | solution.py:443
  37.2 7.4 %collective-permute-start.8 = (bf16[256,512]{1,0:T(8,128)(2,1)S(1)}, bf16[256,512]{1,0:T(8,128)(2,1)S(1)}, u32[]{:S(2)}, u32[]{:S(2)}) collective-permute-start(bf16[256,512]{1,0:T(8,128)(2,1)S(1)} %get-tuple-element.63.fold_own), channel_id=1, source_target_pairs={{0,1},{1,0},{2,3},{3,2},{4,5},{5,4},{6,7},{7,6},{8,9},{9,8},{10,11... | collective-permute-start | bytes 786440 | tf_op jit(solution)/shard_map/ppermute | solution.py:443
  44.7 14.6 %copy-start.9 = (s32[24,128]{1,0:T(8,128)S(1)}, s32[24,128]{1,0:T(8,128)}, u32[]{:S(2)}) copy-start(s32[24,128]{1,0:T(8,128)} %src.5) | copy-start | bytes 36868
  44.7 14.6 %copy-start.11 = (s32[24,128]{1,0:T(8,128)S(1)}, s32[24,128]{1,0:T(8,128)}, u32[]{:S(2)}) copy-start(s32[24,128]{1,0:T(8,128)} %dst.5) | copy-start | bytes 36868
  44.7 14.6 %copy-start.13 = (bf16[24,128]{1,0:T(8,128)(2,1)S(1)}, bf16[24,128]{1,0:T(8,128)(2,1)}, u32[]{:S(2)}) copy-start(bf16[24,128]{1,0:T(8,128)(2,1)} %weight.5) | copy-start | bytes 18436
  53.2 1.4 %collective-permute-start.9 = (bf16[100,512]{1,0:T(8,128)(2,1)S(1)}, bf16[100,512]{1,0:T(8,128)(2,1)S(1)}, u32[]{:S(2)}, u32[]{:S(2)}) collective-permute-start(bf16[100,512]{1,0:T(8,128)(2,1)S(1)} %attend.1), channel_id=1, source_target_pairs={{0,1},{1,0},{2,3},{3,2},{4,5},{5,4},{6,7},{7,6},{8,9},{9,8},{10,11... | collective-permute-start | bytes 307208 | tf_op jit(solution)/shard_map/ppermute | solution.py:443
  54.6 9.8 %collective-permute-start.10 = (bf16[2,100,512]{2,1,0:T(8,128)(2,1)S(1)}, bf16[2,100,512]{2,1,0:T(8,128)(2,1)S(1)}, u32[]{:S(2)}, u32[]{:S(2)}) collective-permute-start(bf16[2,100,512]{2,1,0:T(8,128)(2,1)S(1)} %pad_maximum_fusion.own), channel_id=1, source_target_pairs={{0,2},{2,4},{4,6},{6,8},{8,10},{10,12},{12,14},{14,16},{16,18},{18... | collective-permute-start | bytes 614408 | tf_op jit(solution)/shard_map/ppermute | solution.py:450
  64.4 3.4 %collective-permute-start.11 = (bf16[2,100,512]{2,1,0:T(8,128)(2,1)S(1)}, bf16[2,100,512]{2,1,0:T(8,128)(2,1)S(1)}, u32[]{:S(2)}, u32[]{:S(2)}) collective-permute-start(bf16[2,100,512]{2,1,0:T(8,128)(2,1)S(1)} %collective-permute-done.10.sent), channel_id=1, source_target_pairs={{0,1},{1,0},{2,3},{3,2},{4,5},{5,4},{6,7},{7,6},{8,9},{9,8},{10,11... | collective-permute-start | bytes 614408 | tf_op jit(solution)/shard_map/ppermute | solution.py:443

commit v12 on v11

--- a/solution.py
+++ b/solution.py
@@ -104,7 +104,7 @@
 
 
 def unpack_body(info, grid, sent, rows, wide):
-    wide[...] = jnp.zeros_like(wide)
+    wide[96:, :] = jnp.zeros((LANES - 96, G_BAND), F32)
     to_rows(grid, wide, rows, G_BAND)
     to_rows(sent, wide, rows, info[0] * 2 * G_BAND)
 
@@ -180,7 +180,7 @@
     w_wide[...] = jnp.zeros_like(w_wide)
     by_core(core, w_wide, win_own, win_peer)
     w_in[...] = (w_wide[...] * 0.5).astype(BF16)
-    wide[...] = jnp.zeros_like(wide)
+    wide[96:, :] = jnp.zeros((LANES - 96, G_BAND), F32)
     to_rows(swapped_rows, wide, rows, (1 - core) * 2 * G_BAND)
     encode_tiles(
         core, range(TILES), src, w_in, targets, weights, gain, rows, mesh_zero, normed,
@@ -504,8 +504,12 @@
         [],
         5 * 10 ** 9, 4, "prepare",
     )
-    grid_sent, gain, spread, w_in = lax.optimization_barrier((grid_sent, gain, spread, w_in))
-    grid_swapped, win_peer = swapped(grid_sent), swapped(w_in)
+    gain, w_in, dec_own = lax.optimization_barrier((gain, w_in, dec_own))
+    win_peer, dec_peer = swapped(w_in), swapped(dec_own)
+    grid_sent, gain, spread, win_peer, dec_peer = lax.optimization_barrier(
+        (grid_sent, gain, spread, win_peer, dec_peer)
+    )
+    grid_swapped = swapped(grid_sent)
     grid_rows = call(
         unpack_body,
         (info, grid, grid_sent),
@@ -514,10 +518,10 @@
         [pltpu.VMEM((LANES, G_BAND), F32)],
         2 * 10 ** 9, 6, "unpack",
     )
-    grid_swapped, grid_rows, win_peer, dec_own, qkv_own = lax.optimization_barrier(
-        (grid_swapped, grid_rows, win_peer, dec_own, qkv_own)
-    )
-    dec_peer, qkv_peer = swapped(dec_own), swapped(qkv_own)
+    grid_swapped, grid_rows, qkv_own = lax.optimization_barrier(
+        (grid_swapped, grid_rows, qkv_own)
+    )
+    qkv_peer = swapped(qkv_own)
     band_rows = jax.ShapeDtypeStruct((ROWS, D), BF16)
     step_buffers = [pltpu.VMEM((STEP, LANES), F32)] * 2 + [pltpu.VMEM((ROWS, D), F32)]
     _, mesh_zero, normed, to_band = call(

time: 69.9 us -> 69.3 us (level)
  starting transfers between devices: 22.9 us -> 21 us
  waiting for transfers between devices: 1.88 us -> 2.76 us
    ppermute x9, starting transfers between devices: 9.65 us -> 7.81 us  [swapped(): return lax.ppermute(value, 'mp', [(0, 1), (1, 0)])]
    ppermute x9, waiting for transfers between devices: 1.87 us -> 2.76 us  [swapped(): return lax.ppermute(value, 'mp', [(0, 1), (1, 0)])]
  transfers between devices with their start and end apart: 12 -> 12, of which waited for: 3 -> 5; matrix products, arithmetic and copies ran while one was open for 0% -> 0% of each run, Pallas kernels for 45% -> 46%
where the time goes in v12:
time: 69.3 us; the launch traced here: 68.9 us
  Pallas kernels  41.6 us (60%)
  starting transfers between devices  21 us (30%)
  waiting for transfers between devices  2.76 us (4%)
  local copies, waits for them, and re-layouts  2.6 us (4%)
  between operations  0.94 us (1%)
    pallas_call x10, Pallas kernels, call(): pl.pallas_call(body, out_shape=outs, in_specs=specs, out_specs=jax.tree.m...  41.6 us
    ppermute x2, starting transfers between devices, up_and_down(): return lax.ppermute(value, ('band', 'mp'), pairs)  11.3 us
    ppermute x9, starting transfers between devices, swapped(): return lax.ppermute(value, 'mp', [(0, 1), (1, 0)])  7.81 us
    ppermute x9, waiting for transfers between devices, swapped(): return lax.ppermute(value, 'mp', [(0, 1), (1, 0)])  2.76 us
    unnamed x32, local copies, waits for them, and re-layouts  2.52 us
    ppermute x1, starting transfers between devices, over_the_edge(): return lax.ppermute(value, ('band', 'mp'), pairs)  1.92 us
  transfers between devices with their start and end apart: 12, of which 5 were waited for; matrix products, arithmetic and copies ran while one was open for 0% of the time, Pallas kernels for 46%

profile of v12, /device:TPU:97, one launch (start us, length us, event | category | flops | bytes accessed | tf_op | source)
XLA Modules:
  0.0 68.9 jit_solution(11442368058668517619)
XLA Ops:
  0.0 6.7 %collective-permute-start = (bf16[100,2048]{1,0:T(8,128)(2,1)}, bf16[100,2048]{1,0:T(8,128)(2,1)S(1)}, u32[]{:S(2)}, u32[]{:S(2)}) collective-permute-start(bf16[100,2048]{1,0:T(8,128)(2,1)} %bitcast.18), channel_id=1, source_target_pairs={{0,2},{2,4},{4,6},{6,8},{8,10},{10,12},{12,14},{14,16},{16,18},{18... | collective-permute-start | bytes 1228808 | tf_op jit(solution)/shard_map/ppermute | solution.py:450
  7.3 0.1 stack.48.info
  7.4 0.7 %copy-done.8 = s32[24,128]{1,0:T(8,128)S(1)} copy-done((s32[24,128]{1,0:T(8,128)S(1)}, s32[24,128]{1,0:T(8,128)}, u32[]{:S(2)}) %copy-start.8) | copy-done | bytes 12312
  8.1 0.7 %copy-done.10 = s32[24,128]{1,0:T(8,128)S(1)} copy-done((s32[24,128]{1,0:T(8,128)S(1)}, s32[24,128]{1,0:T(8,128)}, u32[]{:S(2)}) %copy-start.10) | copy-done | bytes 12312
  8.8 0.7 %copy-done.12 = bf16[24,128]{1,0:T(8,128)(2,1)S(1)} copy-done((bf16[24,128]{1,0:T(8,128)(2,1)S(1)}, bf16[24,128]{1,0:T(8,128)(2,1)}, u32[]{:S(2)}) %copy-start.12) | copy-done | bytes 6168
  9.5 2.7 %early.1.spread_in = bf16[3072,1024]{1,0:T(8,128)(2,1)S(1)} custom-call(s32[8]{0:T(128)S(1)} %stack.48.info, s32[24,128]{1,0:T(8,128)S(1)} %copy-done.8, s32[24,128]{1,0:T(8,128)S(1)} %copy-done.10, bf16[24,128]{1,0:T(8,128)(2,1)S(1)} %copy-done.12), custom_call_target="tpu_custom_call" | custom-call | flops 5000000000 | bytes 2000000 | tf_op jit(solution)/shard_map/early/pallas_call | solution.py:44
  12.3 0.0 copy-start.3
  12.3 0.0 copy-start.4
  12.3 0.0 copy-start.2
  12.3 0.6 prepare.1
  12.9 0.3 copy-done.3
  13.2 0.0 collective-permute-start.1
  13.2 0.0 copy-done.4
  13.2 0.5 collective-permute-start.2
  13.7 0.8 %collective-permute-done.1.win_peer = bf16[100,512]{1,0:T(8,128)(2,1)S(1)} collective-permute-done((bf16[100,512]{1,0:T(8,128)(2,1)S(1)}, bf16[100,512]{1,0:T(8,128)(2,1)S(1)}, u32[]{:S(2)}, u32[]{:S(2)}) %collective-permute-start.1) | collective-permute-done | bytes 102432 | tf_op jit(solution)/shard_map/ppermute | solution.py:443
  14.5 0.2 collective-permute-done.2.dec_peer
  14.6 0.0 collective-permute-done.sent
  14.6 0.5 collective-permute-start.3
  15.1 0.9 %unpack.1.grid_rows = f32[6144,128]{1,0:T(8,128)S(1)} custom-call(s32[8]{0:T(128)S(1)} %stack.48.info, bf16[100,2048]{1,0:T(8,128)(2,1)S(1)} %bitcast.19, bf16[100,2048]{1,0:T(8,128)(2,1)S(1)} %collective-permute-done.sent), custom_call_target="tpu_custom_call" | custom-call | flops 2000000000 | bytes 2000000 | tf_op jit(solution)/shard_map/unpack/pallas_call | solution.py:44
  16.0 0.5 collective-permute-done.3.swapped_rows
  16.5 0.4 collective-permute-start.5
  16.9 9.3 %encode.1 = (f32[6144,128]{1,0:T(8,128)S(1)}, bf16[512,1024]{1,0:T(8,128)(2,1)S(1)}, bf16[512,1024]{1,0:T(8,128)(2,1)S(1)}, bf16[384,1024]{1,0:T(8,128)(2,1)S(1)}) custom-call(s32[8]{0:T(128)S(1)} %stack.48.info, s32[64,128]{1,0:T(8,128)S(1)} %get-tuple-element.40.src, f32[6144,128]{1,0:T(8,128)S(1)} %unpack.1.grid_rows, ...), custom_call_target="tpu_custom_call", output_to_operand_aliasing={{0}: (2, {})} | custom-call | flops 7000000000 | bytes 2000000 | tf_op jit(solution)/shard_map/encode/pallas_call | solution.py:44
  26.2 1.9 %collective-permute-start.4 = (bf16[384,1024]{1,0:T(8,128)(2,1)S(1)}, bf16[384,1024]{1,0:T(8,128)(2,1)S(1)}, u32[]{:S(2)}, u32[]{:S(2)}) collective-permute-start(bf16[384,1024]{1,0:T(8,128)(2,1)S(1)} %get-tuple-element.53), channel_id=1, source_target_pairs={{1,2},{3,4},{5,6},{7,8},{9,10},{11,12},{13,14},{15,16},{17,18},{19... | collective-permute-start | bytes 2359304 | tf_op jit(solution)/shard_map/ppermute | solution.py:457
  28.1 0.0 collective-permute-done.5.w_peer
  28.1 0.0 copy-start.15
  28.2 4.9 %project.1 = (bf16[512,1024]{1,0:T(8,128)(2,1)S(1)}, bf16[512,1024]{1,0:T(8,128)(2,1)S(1)}, bf16[1024,512]{1,0:T(8,128)(2,1)S(1)}, bf16[384,1024]{1,0:T(8,128)(2...) custom-call(s32[8]{0:T(128)S(1)} %stack.48.info, ...), custom_call_target="tpu_custom_call" | custom-call | flops 6000000000 | bytes 2000000 | tf_op jit(solution)/shard_map/project/pallas_call | solution.py:44
  33.0 3.5 %collective-permute-start.6 = (bf16[384,1024]{1,0:T(8,128)(2,1)S(1)}, bf16[384,1024]{1,0:T(8,128)(2,1)S(1)}, u32[]{:S(2)}, u32[]{:S(2)}) collective-permute-start(bf16[384,1024]{1,0:T(8,128)(2,1)S(1)} %get-tuple-element.58), channel_id=1, source_target_pairs={{0,1},{1,0},{2,3},{3,2},{4,5},{5,4},{6,7},{7,6},{8,9},{9,8},{10,11... | collective-permute-start | bytes 2359304 | tf_op jit(solution)/shard_map/ppermute | solution.py:443
  36.5 0.1 collective-permute-start.7
  36.6 0.4 collective-permute-start.8
  37.1 0.0 copy-done.15
  37.1 7.0 %own.1 = (f32[1024,512]{1,0:T(8,128)S(1)}, f32[8,8,1024]{2,1,0:T(8,128)S(1)}, bf16[896,128]{1,0:T(8,128)(2,1)S(1)}) custom-call(s32[32]{0:T(128)S(1)} %copy-done.15, bf16[512,1024]{1,0:T(8,128)(2,1)S(1)} %get-tuple-element.60.queries, bf16[512,1024]{1,0:T(8,128)(2,1)S(1)} %get-tuple-element.61.keys, bf16[1024,512]{1,0:T(8,128)(2,1)S(1)} %get-tuple-element.62.values_t), custom_call_target="tpu_custom_call" | custom-call | flops 8000000000 | bytes 2000000 | tf_op jit(solution)/shard_map/own/pallas_call | solution.py:44
  44.0 0.0 collective-permute-done.4.halo
  44.0 0.0 collective-permute-done.8.fold_peer
  44.0 0.0 collective-permute-done.6.peer_keys
  44.1 0.0 collective-permute-done.7.peer_values
  44.1 0.0 copy-start.9
  44.1 0.0 copy-start.11
  44.1 0.0 copy-start.13
  44.1 8.5 %attend.1 = bf16[100,512]{1,0:T(8,128)(2,1)S(1)} custom-call(s32[8]{0:T(128)S(1)} %stack.48.info, bf16[384,1024]{1,0:T(8,128)(2,1)S(1)} %collective-permute-done.4.halo, bf16[384,1024]{1,0:T(8,128)(2,1)S(1)} %collective-permute-done.6.peer_keys, bf16[1024,384]{1,0:T(8,128)(2,1)S(1)} %collective-permute-done.7.peer_values, ...), custom_call_target="tpu_custom_call" | custom-call | flops 10000000000 | bytes 2000000 | tf_op jit(solution)/shard_map/attend/pallas_call | solution.py:44
  52.6 0.2 collective-permute-start.9
  52.8 1.2 %collective-permute-done.9 = bf16[100,512]{1,0:T(8,128)(2,1)S(1)} collective-permute-done((bf16[100,512]{1,0:T(8,128)(2,1)S(1)}, bf16[100,512]{1,0:T(8,128)(2,1)S(1)}, u32[]{:S(2)}, u32[]{:S(2)}) %collective-permute-start.9) | collective-permute-done | bytes 102432 | tf_op jit(solution)/shard_map/ppermute | solution.py:443
  54.0 4.6 %collective-permute-start.10 = (bf16[2,100,512]{2,1,0:T(8,128)(2,1)S(1)}, bf16[2,100,512]{2,1,0:T(8,128)(2,1)S(1)}, u32[]{:S(2)}, u32[]{:S(2)}) collective-permute-start(bf16[2,100,512]{2,1,0:T(8,128)(2,1)S(1)} %pad_maximum_fusion.own), channel_id=1, source_target_pairs={{0,2},{2,4},{4,6},{6,8},{8,10},{10,12},{12,14},{14,16},{16,18},{18... | collective-permute-start | bytes 614408 | tf_op jit(solution)/shard_map/ppermute | solution.py:450
  58.7 5.1 %spread.1 = (bf16[3072,1024]{1,0:T(8,128)(2,1)S(1)}, f32[100,1024]{1,0:T(8,128)S(1)}) custom-call(s32[8]{0:T(128)S(1)} %stack.48.info, bf16[3072,1024]{1,0:T(8,128)(2,1)S(1)} %early.1.spread_in, bf16[2,100,512]{2,1,0:T(8,128)(2,1)S(1)} %pad_maximum_fusion.own, s32[24,128]{1,0:T(8,128)S(1)} %copy-done.9, ...), custom_call_target="tpu_custom_call", output_to_operand_aliasing={{0}: (1, {})} | custom-call | flops 8000000000 | bytes 2000000 | tf_op jit(solution)/shard_map/spread/pallas_call | solution.py:44
  63.8 0.0 collective-permute-done.10.sent
  63.9 2.3 %collective-permute-start.11 = (bf16[2,100,512]{2,1,0:T(8,128)(2,1)S(1)}, bf16[2,100,512]{2,1,0:T(8,128)(2,1)S(1)}, u32[]{:S(2)}, u32[]{:S(2)}) collective-permute-start(bf16[2,100,512]{2,1,0:T(8,128)(2,1)S(1)} %collective-permute-done.10.sent), channel_id=1, source_target_pairs={{0,1},{1,0},{2,3},{3,2},{4,5},{5,4},{6,7},{7,6},{8,9},{9,8},{10,11... | collective-permute-start | bytes 614408 | tf_op jit(solution)/shard_map/ppermute | solution.py:443
  66.1 1.0 %sent.1.total = f32[100,1024]{1,0:T(8,128)S(1)} custom-call(s32[8]{0:T(128)S(1)} %stack.48.info, bf16[2,100,512]{2,1,0:T(8,128)(2,1)S(1)} %collective-permute-done.10.sent, bf16[3072,1024]{1,0:T(8,128)(2,1)S(1)} %get-tuple-element.71.spread, f32[100,1024]{1,0:T(8,128)S(1)} %get-tuple-element.72.base), custom_call_target="tpu_custom_call" | custom-call | flops 1000000000 | bytes 2000000 | tf_op jit(solution)/shard_map/sent/pallas_call | solution.py:44
  67.2 0.1 collective-permute-done.11.swapped_rows
  67.2 1.7 %decode.1 = bf16[100,1024]{1,0:T(8,128)(2,1)} custom-call(s32[8]{0:T(128)S(1)} %stack.48.info, bf16[2,100,512]{2,1,0:T(8,128)(2,1)S(1)} %collective-permute-done.11.swapped_rows, bf16[3072,1024]{1,0:T(8,128)(2,1)S(1)} %get-tuple-element.71.spread, f32[100,1024]{1,0:T(8,128)S(1)} %sent.1.total), custom_call_target="tpu_custom_call" | custom-call | flops 1000000000 | bytes 2000000 | tf_op jit(solution)/shard_map/decode/pallas_call | solution.py:44
  (20 shorter events, 0.1 us)
Async XLA Ops:
  0.0 14.6 %collective-permute-start = (bf16[100,2048]{1,0:T(8,128)(2,1)}, bf16[100,2048]{1,0:T(8,128)(2,1)S(1)}, u32[]{:S(2)}, u32[]{:S(2)}) collective-permute-start(bf16[100,2048]{1,0:T(8,128)(2,1)} %bitcast.18), channel_id=1, source_target_pairs={{0,2},{2,4},{4,6},{6,8},{8,10},{10,12},{12,14},{14,16},{16,18},{18... | collective-permute-start | bytes 1228808 | tf_op jit(solution)/shard_map/ppermute | solution.py:450
  7.4 0.7 %copy-start.8 = (s32[24,128]{1,0:T(8,128)S(1)}, s32[24,128]{1,0:T(8,128)}, u32[]{:S(2)}) copy-start(s32[24,128]{1,0:T(8,128)} %src.5) | copy-start | bytes 36868
  8.1 0.7 %copy-start.10 = (s32[24,128]{1,0:T(8,128)S(1)}, s32[24,128]{1,0:T(8,128)}, u32[]{:S(2)}) copy-start(s32[24,128]{1,0:T(8,128)} %dst.5) | copy-start | bytes 36868
  8.8 0.7 %copy-start.12 = (bf16[24,128]{1,0:T(8,128)(2,1)S(1)}, bf16[24,128]{1,0:T(8,128)(2,1)}, u32[]{:S(2)}) copy-start(bf16[24,128]{1,0:T(8,128)(2,1)} %weight.5) | copy-start | bytes 18436
  9.5 2.7 %copy-start.5 = (s32[64,128]{1,0:T(8,128)S(1)}, s32[64,128]{1,0:T(8,128)}, u32[]{:S(2)}) copy-start(s32[64,128]{1,0:T(8,128)} %src.4) | copy-start | bytes 98308
  9.5 2.7 %copy-start.6 = (s32[64,128]{1,0:T(8,128)S(1)}, s32[64,128]{1,0:T(8,128)}, u32[]{:S(2)}) copy-start(s32[64,128]{1,0:T(8,128)} %dst.4) | copy-start | bytes 98308
  9.5 2.7 %copy-start.7 = (bf16[64,128]{1,0:T(8,128)(2,1)S(1)}, bf16[64,128]{1,0:T(8,128)(2,1)}, u32[]{:S(2)}) copy-start(bf16[64,128]{1,0:T(8,128)(2,1)} %weight.4) | copy-start | bytes 49156
  9.5 2.7 %copy-start.14 = (f32[1024]{0:T(1024)S(1)}, f32[1024]{0:T(1024)}, u32[]{:S(2)}) copy-start(f32[1024]{0:T(1024)} %param.20) | copy-start | bytes 12292
  12.3 0.9 %copy-start.3 = (bf16[100,512]{1,0:T(8,128)(2,1)S(1)}, bf16[100,512]{1,0:T(8,128)(2,1)}, u32[]{:S(2)}) copy-start(bf16[100,512]{1,0:T(8,128)(2,1)} %win_own) | copy-start | bytes 307204
  12.3 0.9 %copy-start.4 = (bf16[512,100]{0,1:T(8,128)(2,1)S(1)}, bf16[512,100]{0,1:T(8,128)(2,1)}, u32[]{:S(2)}) copy-start(bf16[512,100]{0,1:T(8,128)(2,1)} %param.24) | copy-start | bytes 307204
  12.3 2.8 %copy-start.2 = (bf16[2048,100]{0,1:T(8,128)(2,1)S(1)}, bf16[2048,100]{0,1:T(8,128)(2,1)}, u32[]{:S(2)}) copy-start(bf16[2048,100]{0,1:T(8,128)(2,1)} %param.14) | copy-start | bytes 1228804
  13.2 3.4 %copy-start = (bf16[1024,3,512]{2,0,1:T(8,128)(2,1)S(1)}, bf16[1024,3,512]{2,0,1:T(8,128)(2,1)}, u32[]{:S(2)}) copy-start(bf16[1024,3,512]{2,0,1:T(8,128)(2,1)} %param.21) | copy-start | bytes 9437188
  13.2 1.3 %collective-permute-start.1 = (bf16[100,512]{1,0:T(8,128)(2,1)S(1)}, bf16[100,512]{1,0:T(8,128)(2,1)S(1)}, u32[]{:S(2)}, u32[]{:S(2)}) collective-permute-start(bf16[100,512]{1,0:T(8,128)(2,1)S(1)} %copy-done.3), channel_id=1, source_target_pairs={{0,1},{1,0},{2,3},{3,2},{4,5},{5,4},{6,7},{7,6},{8,9},{9,8},{10,11... | collective-permute-start | bytes 307208 | tf_op jit(solution)/shard_map/ppermute | solution.py:443
  13.2 1.4 %collective-permute-start.2 = (bf16[100,512]{1,0:T(8,128)(2,1)S(1)}, bf16[100,512]{1,0:T(8,128)(2,1)S(1)}, u32[]{:S(2)}, u32[]{:S(2)}) collective-permute-start(bf16[100,512]{1,0:T(8,128)(2,1)S(1)} %bitcast.21), channel_id=1, source_target_pairs={{0,1},{1,0},{2,3},{3,2},{4,5},{5,4},{6,7},{7,6},{8,9},{9,8},{10,11... | collective-permute-start | bytes 307208 | tf_op jit(solution)/shard_map/ppermute | solution.py:443
  14.6 1.9 %collective-permute-start.3 = (bf16[100,2048]{1,0:T(8,128)(2,1)S(1)}, bf16[100,2048]{1,0:T(8,128)(2,1)S(1)}, u32[]{:S(2)}, u32[]{:S(2)}) collective-permute-start(bf16[100,2048]{1,0:T(8,128)(2,1)S(1)} %collective-permute-done.sent), channel_id=1, source_target_pairs={{0,1},{1,0},{2,3},{3,2},{4,5},{5,4},{6,7},{7,6},{8,9},{9,8},{10,11... | collective-permute-start | bytes 1228808 | tf_op jit(solution)/shard_map/ppermute | solution.py:443
  16.5 11.6 %collective-permute-start.5 = (bf16[3,1024,512]{2,1,0:T(8,128)(2,1)S(1)}, bf16[3,1024,512]{2,1,0:T(8,128)(2,1)S(1)}, u32[]{:S(2)}, u32[]{:S(2)}) collective-permute-start(bf16[3,1024,512]{2,1,0:T(8,128)(2,1)S(1)} %bitcast.15), channel_id=1, source_target_pairs={{0,1},{1,0},{2,3},{3,2},{4,5},{5,4},{6,7},{7,6},{8,9},{9,8},{10,11... | collective-permute-start | bytes 9437192 | tf_op jit(solution)/shard_map/ppermute | solution.py:443
  16.9 11.2 %copy-start.1 = (bf16[512,1024]{1,0:T(8,128)(2,1)S(1)}, bf16[512,1024]{1,0:T(8,128)(2,1)}, u32[]{:S(2)}) copy-start(bf16[512,1024]{1,0:T(8,128)(2,1)} %w_out.1) | copy-start | bytes 3145732
  26.2 17.8 %collective-permute-start.4 = (bf16[384,1024]{1,0:T(8,128)(2,1)S(1)}, bf16[384,1024]{1,0:T(8,128)(2,1)S(1)}, u32[]{:S(2)}, u32[]{:S(2)}) collective-permute-start(bf16[384,1024]{1,0:T(8,128)(2,1)S(1)} %get-tuple-element.53), channel_id=1, source_target_pairs={{1,2},{3,4},{5,6},{7,8},{9,10},{11,12},{13,14},{15,16},{17,18},{19... | collective-permute-start | bytes 2359304 | tf_op jit(solution)/shard_map/ppermute | solution.py:457
  28.1 8.9 %copy-start.15 = (s32[32]{0:T(128)S(1)}, s32[32]{0:T(128)}, u32[]{:S(2)}) copy-start(s32[32]{0:T(128)} %offsets.1) | copy-start | bytes 388
  33.0 11.0 %collective-permute-start.6 = (bf16[384,1024]{1,0:T(8,128)(2,1)S(1)}, bf16[384,1024]{1,0:T(8,128)(2,1)S(1)}, u32[]{:S(2)}, u32[]{:S(2)}) collective-permute-start(bf16[384,1024]{1,0:T(8,128)(2,1)S(1)} %get-tuple-element.58), channel_id=1, source_target_pairs={{0,1},{1,0},{2,3},{3,2},{4,5},{5,4},{6,7},{7,6},{8,9},{9,8},{10,11... | collective-permute-start | bytes 2359304 | tf_op jit(solution)/shard_map/ppermute | solution.py:443
  36.5 7.5 %collective-permute-start.7 = (bf16[1024,384]{1,0:T(8,128)(2,1)S(1)}, bf16[1024,384]{1,0:T(8,128)(2,1)S(1)}, u32[]{:S(2)}, u32[]{:S(2)}) collective-permute-start(bf16[1024,384]{1,0:T(8,128)(2,1)S(1)} %get-tuple-element.59), channel_id=1, source_target_pairs={{0,1},{1,0},{2,3},{3,2},{4,5},{5,4},{6,7},{7,6},{8,9},{9,8},{10,11... | collective-permute-start | bytes 2359304 | tf_op jit(solution)/shard_map/ppermute | solution.py:443
  36.6 7.4 %collective-permute-start.8 = (bf16[256,512]{1,0:T(8,128)(2,1)S(1)}, bf16[256,512]{1,0:T(8,128)(2,1)S(1)}, u32[]{:S(2)}, u32[]{:S(2)}) collective-permute-start(bf16[256,512]{1,0:T(8,128)(2,1)S(1)} %get-tuple-element.67.fold_own), channel_id=1, source_target_pairs={{0,1},{1,0},{2,3},{3,2},{4,5},{5,4},{6,7},{7,6},{8,9},{9,8},{10,11... | collective-permute-start | bytes 786440 | tf_op jit(solution)/shard_map/ppermute | solution.py:443
  44.1 14.6 %copy-start.9 = (s32[24,128]{1,0:T(8,128)S(1)}, s32[24,128]{1,0:T(8,128)}, u32[]{:S(2)}) copy-start(s32[24,128]{1,0:T(8,128)} %src.5) | copy-start | bytes 36868
  44.1 14.6 %copy-start.11 = (s32[24,128]{1,0:T(8,128)S(1)}, s32[24,128]{1,0:T(8,128)}, u32[]{:S(2)}) copy-start(s32[24,128]{1,0:T(8,128)} %dst.5) | copy-start | bytes 36868
  44.1 14.6 %copy-start.13 = (bf16[24,128]{1,0:T(8,128)(2,1)S(1)}, bf16[24,128]{1,0:T(8,128)(2,1)}, u32[]{:S(2)}) copy-start(bf16[24,128]{1,0:T(8,128)(2,1)} %weight.5) | copy-start | bytes 18436
  52.6 1.4 %collective-permute-start.9 = (bf16[100,512]{1,0:T(8,128)(2,1)S(1)}, bf16[100,512]{1,0:T(8,128)(2,1)S(1)}, u32[]{:S(2)}, u32[]{:S(2)}) collective-permute-start(bf16[100,512]{1,0:T(8,128)(2,1)S(1)} %attend.1), channel_id=1, source_target_pairs={{0,1},{1,0},{2,3},{3,2},{4,5},{5,4},{6,7},{7,6},{8,9},{9,8},{10,11... | collective-permute-start | bytes 307208 | tf_op jit(solution)/shard_map/ppermute | solution.py:443
  54.0 9.8 %collective-permute-start.10 = (bf16[2,100,512]{2,1,0:T(8,128)(2,1)S(1)}, bf16[2,100,512]{2,1,0:T(8,128)(2,1)S(1)}, u32[]{:S(2)}, u32[]{:S(2)}) collective-permute-start(bf16[2,100,512]{2,1,0:T(8,128)(2,1)S(1)} %pad_maximum_fusion.own), channel_id=1, source_target_pairs={{0,2},{2,4},{4,6},{6,8},{8,10},{10,12},{12,14},{14,16},{16,18},{18... | collective-permute-start | bytes 614408 | tf_op jit(solution)/shard_map/ppermute | solution.py:450
  63.9 3.4 %collective-permute-start.11 = (bf16[2,100,512]{2,1,0:T(8,128)(2,1)S(1)}, bf16[2,100,512]{2,1,0:T(8,128)(2,1)S(1)}, u32[]{:S(2)}, u32[]{:S(2)}) collective-permute-start(bf16[2,100,512]{2,1,0:T(8,128)(2,1)S(1)} %collective-permute-done.10.sent), channel_id=1, source_target_pairs={{0,1},{1,0},{2,3},{3,2},{4,5},{5,4},{6,7},{7,6},{8,9},{9,8},{10,11... | collective-permute-start | bytes 614408 | tf_op jit(solution)/shard_map/ppermute | solution.py:443

commit v13 on v12

--- a/solution.py
+++ b/solution.py
@@ -23,6 +23,7 @@
 DEC_ROUNDS = 3
 DEC_TILES = 8
 GROUP = 2
+HALO_GROUP = 4
 EARLY = 2
 MASKED = -1e30
 SCALE = 64 ** (-0.5) * math.log2(math.e)
@@ -229,27 +230,27 @@
     return both, result[TILE : TILE + 1, :]
 
 
-def pipeline(score, finish, first, second):
+def pipeline(score, finish, first, second, size):
     buffers = (first, second)
-    groups = D // LANES // GROUP
+    groups = D // LANES // size
 
     def part_of(buffer, member):
         return buffer.at[:, member * 2 * TILE : (member + 1) * 2 * TILE]
 
-    for member in range(GROUP):
+    for member in range(size):
         score(member, 0, part_of(first, member))
 
     def head_group(group, carry):
         for block in range(TILES):
             here, ahead = buffers[block % 2], buffers[(block + 1) % 2]
-            for member in range(GROUP):
+            for member in range(size):
                 if block + 1 < TILES:
-                    pair = group * GROUP + member
+                    pair = group * size + member
                 else:
-                    pair = jnp.minimum(group + 1, groups - 1) * GROUP + member
+                    pair = jnp.minimum(group + 1, groups - 1) * size + member
                 score(pair, (block + 1) % TILES, part_of(ahead, member))
-            for member in range(GROUP):
-                finish(group * GROUP + member, block, part_of(here, member))
+            for member in range(size):
+                finish(group * size + member, block, part_of(here, member))
         return carry
 
     lax.fori_loop(0, groups, head_group, 0)
@@ -313,7 +314,7 @@
         stats[pair, 0:1, columns] = top
         stats[pair, 1:2, columns] = total
 
-    pipeline(score, finish, first, second)
+    pipeline(score, finish, first, second, GROUP)
 
 
 def attend_body(
@@ -373,7 +374,7 @@
         ], axis=0)
         attended[lanes_of(pair), rows_of(block)] = result.astype(BF16)
 
-    pipeline(score, finish, first, second)
+    pipeline(score, finish, first, second, HALO_GROUP)
     both = matmul(fold_own[...], attended[:HALF, :]) + matmul(fold_peer[...], attended[HALF:, :])
     projected[...] = (straight[...] + both[:LANES, :] + both[LANES:, :])[:C, :].astype(BF16)
 
@@ -584,8 +585,8 @@
             pltpu.VMEM((D, 2 * WIN), BF16),
             pltpu.VMEM((TILES, WIN, TILE), BF16),
             pltpu.VMEM((D, ROWS), BF16),
-            pltpu.VMEM((WIN, 2 * GROUP * TILE), F32),
-            pltpu.VMEM((WIN, 2 * GROUP * TILE), F32),
+            pltpu.VMEM((WIN, 2 * HALO_GROUP * TILE), F32),
+            pltpu.VMEM((WIN, 2 * HALO_GROUP * TILE), F32),
         ],
         10 ** 10, 16, "attend",
     )

time: 69.3 us -> 68.9 us (level)
  no operation moved by 1% of the time
where the time goes in v13:
time: 68.9 us; the launch traced here: 68.6 us
  Pallas kernels  41.2 us (60%)
  starting transfers between devices  21.1 us (31%)
  waiting for transfers between devices  2.77 us (4%)
  local copies, waits for them, and re-layouts  2.6 us (4%)
  between operations  0.94 us (1%)
    pallas_call x10, Pallas kernels, call(): pl.pallas_call(body, out_shape=outs, in_specs=specs, out_specs=jax.tree.m...  41.2 us
    ppermute x2, starting transfers between devices, up_and_down(): return lax.ppermute(value, ('band', 'mp'), pairs)  11.3 us
    ppermute x9, starting transfers between devices, swapped(): return lax.ppermute(value, 'mp', [(0, 1), (1, 0)])  7.83 us
    ppermute x9, waiting for transfers between devices, swapped(): return lax.ppermute(value, 'mp', [(0, 1), (1, 0)])  2.76 us
    unnamed x32, local copies, waits for them, and re-layouts  2.52 us
    ppermute x1, starting transfers between devices, over_the_edge(): return lax.ppermute(value, ('band', 'mp'), pairs)  1.92 us
  transfers between devices with their start and end apart: 12, of which 5 were waited for; matrix products, arithmetic and copies ran while one was open for 0% of the time, Pallas kernels for 46%

profile of v13, /device:TPU:97, one launch (start us, length us, event | category | flops | bytes accessed | tf_op | source)
XLA Modules:
  0.0 68.6 jit_solution(2478123550094313033)
XLA Ops:
  0.0 6.7 %collective-permute-start = (bf16[100,2048]{1,0:T(8,128)(2,1)}, bf16[100,2048]{1,0:T(8,128)(2,1)S(1)}, u32[]{:S(2)}, u32[]{:S(2)}) collective-permute-start(bf16[100,2048]{1,0:T(8,128)(2,1)} %bitcast.18), channel_id=1, source_target_pairs={{0,2},{2,4},{4,6},{6,8},{8,10},{10,12},{12,14},{14,16},{16,18},{18... | collective-permute-start | bytes 1228808 | tf_op jit(solution)/shard_map/ppermute | solution.py:451
  7.3 0.1 stack.48.info
  7.4 0.7 %copy-done.8 = s32[24,128]{1,0:T(8,128)S(1)} copy-done((s32[24,128]{1,0:T(8,128)S(1)}, s32[24,128]{1,0:T(8,128)}, u32[]{:S(2)}) %copy-start.8) | copy-done | bytes 12312
  8.1 0.7 %copy-done.10 = s32[24,128]{1,0:T(8,128)S(1)} copy-done((s32[24,128]{1,0:T(8,128)S(1)}, s32[24,128]{1,0:T(8,128)}, u32[]{:S(2)}) %copy-start.10) | copy-done | bytes 12312
  8.8 0.7 %copy-done.12 = bf16[24,128]{1,0:T(8,128)(2,1)S(1)} copy-done((bf16[24,128]{1,0:T(8,128)(2,1)S(1)}, bf16[24,128]{1,0:T(8,128)(2,1)}, u32[]{:S(2)}) %copy-start.12) | copy-done | bytes 6168
  9.5 2.7 %early.1.spread_in = bf16[3072,1024]{1,0:T(8,128)(2,1)S(1)} custom-call(s32[8]{0:T(128)S(1)} %stack.48.info, s32[24,128]{1,0:T(8,128)S(1)} %copy-done.8, s32[24,128]{1,0:T(8,128)S(1)} %copy-done.10, bf16[24,128]{1,0:T(8,128)(2,1)S(1)} %copy-done.12), custom_call_target="tpu_custom_call" | custom-call | flops 5000000000 | bytes 2000000 | tf_op jit(solution)/shard_map/early/pallas_call | solution.py:45
  12.3 0.0 copy-start.3
  12.3 0.0 copy-start.4
  12.3 0.0 copy-start.2
  12.3 0.6 prepare.1
  12.9 0.3 copy-done.3
  13.2 0.0 collective-permute-start.1
  13.2 0.0 copy-done.4
  13.2 0.5 collective-permute-start.2
  13.7 0.8 %collective-permute-done.1.win_peer = bf16[100,512]{1,0:T(8,128)(2,1)S(1)} collective-permute-done((bf16[100,512]{1,0:T(8,128)(2,1)S(1)}, bf16[100,512]{1,0:T(8,128)(2,1)S(1)}, u32[]{:S(2)}, u32[]{:S(2)}) %collective-permute-start.1) | collective-permute-done | bytes 102432 | tf_op jit(solution)/shard_map/ppermute | solution.py:444
  14.5 0.2 collective-permute-done.2.dec_peer
  14.6 0.0 collective-permute-done.sent
  14.6 0.5 collective-permute-start.3
  15.1 0.9 %unpack.1.grid_rows = f32[6144,128]{1,0:T(8,128)S(1)} custom-call(s32[8]{0:T(128)S(1)} %stack.48.info, bf16[100,2048]{1,0:T(8,128)(2,1)S(1)} %bitcast.19, bf16[100,2048]{1,0:T(8,128)(2,1)S(1)} %collective-permute-done.sent), custom_call_target="tpu_custom_call" | custom-call | flops 2000000000 | bytes 2000000 | tf_op jit(solution)/shard_map/unpack/pallas_call | solution.py:45
  16.0 0.5 collective-permute-done.3.swapped_rows
  16.5 0.4 collective-permute-start.5
  16.9 9.3 %encode.1 = (f32[6144,128]{1,0:T(8,128)S(1)}, bf16[512,1024]{1,0:T(8,128)(2,1)S(1)}, bf16[512,1024]{1,0:T(8,128)(2,1)S(1)}, bf16[384,1024]{1,0:T(8,128)(2,1)S(1)}) custom-call(s32[8]{0:T(128)S(1)} %stack.48.info, s32[64,128]{1,0:T(8,128)S(1)} %get-tuple-element.40.src, f32[6144,128]{1,0:T(8,128)S(1)} %unpack.1.grid_rows, ...), custom_call_target="tpu_custom_call", output_to_operand_aliasing={{0}: (2, {})} | custom-call | flops 7000000000 | bytes 2000000 | tf_op jit(solution)/shard_map/encode/pallas_call | solution.py:45
  26.2 1.9 %collective-permute-start.4 = (bf16[384,1024]{1,0:T(8,128)(2,1)S(1)}, bf16[384,1024]{1,0:T(8,128)(2,1)S(1)}, u32[]{:S(2)}, u32[]{:S(2)}) collective-permute-start(bf16[384,1024]{1,0:T(8,128)(2,1)S(1)} %get-tuple-element.53), channel_id=1, source_target_pairs={{1,2},{3,4},{5,6},{7,8},{9,10},{11,12},{13,14},{15,16},{17,18},{19... | collective-permute-start | bytes 2359304 | tf_op jit(solution)/shard_map/ppermute | solution.py:458
  28.1 0.0 collective-permute-done.5.w_peer
  28.1 0.0 copy-done.1
  28.1 0.0 copy-start.15
  28.1 4.9 %project.1 = (bf16[512,1024]{1,0:T(8,128)(2,1)S(1)}, bf16[512,1024]{1,0:T(8,128)(2,1)S(1)}, bf16[1024,512]{1,0:T(8,128)(2,1)S(1)}, bf16[384,1024]{1,0:T(8,128)(2...) custom-call(s32[8]{0:T(128)S(1)} %stack.48.info, ...), custom_call_target="tpu_custom_call" | custom-call | flops 6000000000 | bytes 2000000 | tf_op jit(solution)/shard_map/project/pallas_call | solution.py:45
  33.0 3.5 %collective-permute-start.6 = (bf16[384,1024]{1,0:T(8,128)(2,1)S(1)}, bf16[384,1024]{1,0:T(8,128)(2,1)S(1)}, u32[]{:S(2)}, u32[]{:S(2)}) collective-permute-start(bf16[384,1024]{1,0:T(8,128)(2,1)S(1)} %get-tuple-element.58), channel_id=1, source_target_pairs={{0,1},{1,0},{2,3},{3,2},{4,5},{5,4},{6,7},{7,6},{8,9},{9,8},{10,11... | collective-permute-start | bytes 2359304 | tf_op jit(solution)/shard_map/ppermute | solution.py:444
  36.6 0.1 collective-permute-start.7
  36.6 0.4 collective-permute-start.8
  37.1 7.0 %own.1 = (f32[1024,512]{1,0:T(8,128)S(1)}, f32[8,8,1024]{2,1,0:T(8,128)S(1)}, bf16[896,128]{1,0:T(8,128)(2,1)S(1)}) custom-call(s32[32]{0:T(128)S(1)} %copy-done.15, bf16[512,1024]{1,0:T(8,128)(2,1)S(1)} %get-tuple-element.60.queries, bf16[512,1024]{1,0:T(8,128)(2,1)S(1)} %get-tuple-element.61.keys, bf16[1024,512]{1,0:T(8,128)(2,1)S(1)} %get-tuple-element.62.values_t), custom_call_target="tpu_custom_call" | custom-call | flops 8000000000 | bytes 2000000 | tf_op jit(solution)/shard_map/own/pallas_call | solution.py:45
  44.0 0.0 collective-permute-done.4.halo
  44.0 0.0 collective-permute-done.8.fold_peer
  44.1 0.0 collective-permute-done.6.peer_keys
  44.1 0.0 collective-permute-done.7.peer_values
  44.1 0.0 copy-start.9
  44.1 0.0 copy-start.11
  44.1 0.0 copy-start.13
  44.1 8.1 %attend.1 = bf16[100,512]{1,0:T(8,128)(2,1)S(1)} custom-call(s32[8]{0:T(128)S(1)} %stack.48.info, bf16[384,1024]{1,0:T(8,128)(2,1)S(1)} %collective-permute-done.4.halo, bf16[384,1024]{1,0:T(8,128)(2,1)S(1)} %collective-permute-done.6.peer_keys, bf16[1024,384]{1,0:T(8,128)(2,1)S(1)} %collective-permute-done.7.peer_values, ...), custom_call_target="tpu_custom_call" | custom-call | flops 10000000000 | bytes 2000000 | tf_op jit(solution)/shard_map/attend/pallas_call | solution.py:45
  52.2 0.2 collective-permute-start.9
  52.4 1.2 %collective-permute-done.9 = bf16[100,512]{1,0:T(8,128)(2,1)S(1)} collective-permute-done((bf16[100,512]{1,0:T(8,128)(2,1)S(1)}, bf16[100,512]{1,0:T(8,128)(2,1)S(1)}, u32[]{:S(2)}, u32[]{:S(2)}) %collective-permute-start.9) | collective-permute-done | bytes 102432 | tf_op jit(solution)/shard_map/ppermute | solution.py:444
  53.6 4.6 %collective-permute-start.10 = (bf16[2,100,512]{2,1,0:T(8,128)(2,1)S(1)}, bf16[2,100,512]{2,1,0:T(8,128)(2,1)S(1)}, u32[]{:S(2)}, u32[]{:S(2)}) collective-permute-start(bf16[2,100,512]{2,1,0:T(8,128)(2,1)S(1)} %pad_maximum_fusion.own), channel_id=1, source_target_pairs={{0,2},{2,4},{4,6},{6,8},{8,10},{10,12},{12,14},{14,16},{16,18},{18... | collective-permute-start | bytes 614408 | tf_op jit(solution)/shard_map/ppermute | solution.py:451
  58.3 5.1 %spread.1 = (bf16[3072,1024]{1,0:T(8,128)(2,1)S(1)}, f32[100,1024]{1,0:T(8,128)S(1)}) custom-call(s32[8]{0:T(128)S(1)} %stack.48.info, bf16[3072,1024]{1,0:T(8,128)(2,1)S(1)} %early.1.spread_in, bf16[2,100,512]{2,1,0:T(8,128)(2,1)S(1)} %pad_maximum_fusion.own, s32[24,128]{1,0:T(8,128)S(1)} %copy-done.9, ...), custom_call_target="tpu_custom_call", output_to_operand_aliasing={{0}: (1, {})} | custom-call | flops 8000000000 | bytes 2000000 | tf_op jit(solution)/shard_map/spread/pallas_call | solution.py:45
  63.5 0.0 collective-permute-done.10.sent
  63.5 2.3 %collective-permute-start.11 = (bf16[2,100,512]{2,1,0:T(8,128)(2,1)S(1)}, bf16[2,100,512]{2,1,0:T(8,128)(2,1)S(1)}, u32[]{:S(2)}, u32[]{:S(2)}) collective-permute-start(bf16[2,100,512]{2,1,0:T(8,128)(2,1)S(1)} %collective-permute-done.10.sent), channel_id=1, source_target_pairs={{0,1},{1,0},{2,3},{3,2},{4,5},{5,4},{6,7},{7,6},{8,9},{9,8},{10,11... | collective-permute-start | bytes 614408 | tf_op jit(solution)/shard_map/ppermute | solution.py:444
  65.8 1.0 %sent.1.total = f32[100,1024]{1,0:T(8,128)S(1)} custom-call(s32[8]{0:T(128)S(1)} %stack.48.info, bf16[2,100,512]{2,1,0:T(8,128)(2,1)S(1)} %collective-permute-done.10.sent, bf16[3072,1024]{1,0:T(8,128)(2,1)S(1)} %get-tuple-element.71.spread, f32[100,1024]{1,0:T(8,128)S(1)} %get-tuple-element.72.base), custom_call_target="tpu_custom_call" | custom-call | flops 1000000000 | bytes 2000000 | tf_op jit(solution)/shard_map/sent/pallas_call | solution.py:45
  66.8 0.1 collective-permute-done.11.swapped_rows
  66.8 1.7 %decode.1 = bf16[100,1024]{1,0:T(8,128)(2,1)} custom-call(s32[8]{0:T(128)S(1)} %stack.48.info, bf16[2,100,512]{2,1,0:T(8,128)(2,1)S(1)} %collective-permute-done.11.swapped_rows, bf16[3072,1024]{1,0:T(8,128)(2,1)S(1)} %get-tuple-element.71.spread, f32[100,1024]{1,0:T(8,128)S(1)} %sent.1.total), custom_call_target="tpu_custom_call" | custom-call | flops 1000000000 | bytes 2000000 | tf_op jit(solution)/shard_map/decode/pallas_call | solution.py:45
  (20 shorter events, 0.1 us)
Async XLA Ops:
  0.0 14.6 %collective-permute-start = (bf16[100,2048]{1,0:T(8,128)(2,1)}, bf16[100,2048]{1,0:T(8,128)(2,1)S(1)}, u32[]{:S(2)}, u32[]{:S(2)}) collective-permute-start(bf16[100,2048]{1,0:T(8,128)(2,1)} %bitcast.18), channel_id=1, source_target_pairs={{0,2},{2,4},{4,6},{6,8},{8,10},{10,12},{12,14},{14,16},{16,18},{18... | collective-permute-start | bytes 1228808 | tf_op jit(solution)/shard_map/ppermute | solution.py:451
  7.4 0.7 %copy-start.8 = (s32[24,128]{1,0:T(8,128)S(1)}, s32[24,128]{1,0:T(8,128)}, u32[]{:S(2)}) copy-start(s32[24,128]{1,0:T(8,128)} %src.5) | copy-start | bytes 36868
  8.1 0.7 %copy-start.10 = (s32[24,128]{1,0:T(8,128)S(1)}, s32[24,128]{1,0:T(8,128)}, u32[]{:S(2)}) copy-start(s32[24,128]{1,0:T(8,128)} %dst.5) | copy-start | bytes 36868
  8.8 0.7 %copy-start.12 = (bf16[24,128]{1,0:T(8,128)(2,1)S(1)}, bf16[24,128]{1,0:T(8,128)(2,1)}, u32[]{:S(2)}) copy-start(bf16[24,128]{1,0:T(8,128)(2,1)} %weight.5) | copy-start | bytes 18436
  9.5 2.7 %copy-start.5 = (s32[64,128]{1,0:T(8,128)S(1)}, s32[64,128]{1,0:T(8,128)}, u32[]{:S(2)}) copy-start(s32[64,128]{1,0:T(8,128)} %src.4) | copy-start | bytes 98308
  9.5 2.7 %copy-start.6 = (s32[64,128]{1,0:T(8,128)S(1)}, s32[64,128]{1,0:T(8,128)}, u32[]{:S(2)}) copy-start(s32[64,128]{1,0:T(8,128)} %dst.4) | copy-start | bytes 98308
  9.5 2.7 %copy-start.7 = (bf16[64,128]{1,0:T(8,128)(2,1)S(1)}, bf16[64,128]{1,0:T(8,128)(2,1)}, u32[]{:S(2)}) copy-start(bf16[64,128]{1,0:T(8,128)(2,1)} %weight.4) | copy-start | bytes 49156
  9.5 2.7 %copy-start.14 = (f32[1024]{0:T(1024)S(1)}, f32[1024]{0:T(1024)}, u32[]{:S(2)}) copy-start(f32[1024]{0:T(1024)} %param.20) | copy-start | bytes 12292
  12.3 0.9 %copy-start.3 = (bf16[100,512]{1,0:T(8,128)(2,1)S(1)}, bf16[100,512]{1,0:T(8,128)(2,1)}, u32[]{:S(2)}) copy-start(bf16[100,512]{1,0:T(8,128)(2,1)} %win_own) | copy-start | bytes 307204
  12.3 0.9 %copy-start.4 = (bf16[512,100]{0,1:T(8,128)(2,1)S(1)}, bf16[512,100]{0,1:T(8,128)(2,1)}, u32[]{:S(2)}) copy-start(bf16[512,100]{0,1:T(8,128)(2,1)} %param.24) | copy-start | bytes 307204
  12.3 2.8 %copy-start.2 = (bf16[2048,100]{0,1:T(8,128)(2,1)S(1)}, bf16[2048,100]{0,1:T(8,128)(2,1)}, u32[]{:S(2)}) copy-start(bf16[2048,100]{0,1:T(8,128)(2,1)} %param.14) | copy-start | bytes 1228804
  13.2 3.4 %copy-start = (bf16[1024,3,512]{2,0,1:T(8,128)(2,1)S(1)}, bf16[1024,3,512]{2,0,1:T(8,128)(2,1)}, u32[]{:S(2)}) copy-start(bf16[1024,3,512]{2,0,1:T(8,128)(2,1)} %param.21) | copy-start | bytes 9437188
  13.2 1.3 %collective-permute-start.1 = (bf16[100,512]{1,0:T(8,128)(2,1)S(1)}, bf16[100,512]{1,0:T(8,128)(2,1)S(1)}, u32[]{:S(2)}, u32[]{:S(2)}) collective-permute-start(bf16[100,512]{1,0:T(8,128)(2,1)S(1)} %copy-done.3), channel_id=1, source_target_pairs={{0,1},{1,0},{2,3},{3,2},{4,5},{5,4},{6,7},{7,6},{8,9},{9,8},{10,11... | collective-permute-start | bytes 307208 | tf_op jit(solution)/shard_map/ppermute | solution.py:444
  13.2 1.4 %collective-permute-start.2 = (bf16[100,512]{1,0:T(8,128)(2,1)S(1)}, bf16[100,512]{1,0:T(8,128)(2,1)S(1)}, u32[]{:S(2)}, u32[]{:S(2)}) collective-permute-start(bf16[100,512]{1,0:T(8,128)(2,1)S(1)} %bitcast.21), channel_id=1, source_target_pairs={{0,1},{1,0},{2,3},{3,2},{4,5},{5,4},{6,7},{7,6},{8,9},{9,8},{10,11... | collective-permute-start | bytes 307208 | tf_op jit(solution)/shard_map/ppermute | solution.py:444
  14.6 1.9 %collective-permute-start.3 = (bf16[100,2048]{1,0:T(8,128)(2,1)S(1)}, bf16[100,2048]{1,0:T(8,128)(2,1)S(1)}, u32[]{:S(2)}, u32[]{:S(2)}) collective-permute-start(bf16[100,2048]{1,0:T(8,128)(2,1)S(1)} %collective-permute-done.sent), channel_id=1, source_target_pairs={{0,1},{1,0},{2,3},{3,2},{4,5},{5,4},{6,7},{7,6},{8,9},{9,8},{10,11... | collective-permute-start | bytes 1228808 | tf_op jit(solution)/shard_map/ppermute | solution.py:444
  16.5 11.6 %collective-permute-start.5 = (bf16[3,1024,512]{2,1,0:T(8,128)(2,1)S(1)}, bf16[3,1024,512]{2,1,0:T(8,128)(2,1)S(1)}, u32[]{:S(2)}, u32[]{:S(2)}) collective-permute-start(bf16[3,1024,512]{2,1,0:T(8,128)(2,1)S(1)} %bitcast.15), channel_id=1, source_target_pairs={{0,1},{1,0},{2,3},{3,2},{4,5},{5,4},{6,7},{7,6},{8,9},{9,8},{10,11... | collective-permute-start | bytes 9437192 | tf_op jit(solution)/shard_map/ppermute | solution.py:444
  16.9 11.2 %copy-start.1 = (bf16[512,1024]{1,0:T(8,128)(2,1)S(1)}, bf16[512,1024]{1,0:T(8,128)(2,1)}, u32[]{:S(2)}) copy-start(bf16[512,1024]{1,0:T(8,128)(2,1)} %w_out.1) | copy-start | bytes 3145732
  26.2 17.9 %collective-permute-start.4 = (bf16[384,1024]{1,0:T(8,128)(2,1)S(1)}, bf16[384,1024]{1,0:T(8,128)(2,1)S(1)}, u32[]{:S(2)}, u32[]{:S(2)}) collective-permute-start(bf16[384,1024]{1,0:T(8,128)(2,1)S(1)} %get-tuple-element.53), channel_id=1, source_target_pairs={{1,2},{3,4},{5,6},{7,8},{9,10},{11,12},{13,14},{15,16},{17,18},{19... | collective-permute-start | bytes 2359304 | tf_op jit(solution)/shard_map/ppermute | solution.py:458
  28.1 8.9 %copy-start.15 = (s32[32]{0:T(128)S(1)}, s32[32]{0:T(128)}, u32[]{:S(2)}) copy-start(s32[32]{0:T(128)} %offsets.1) | copy-start | bytes 388
  33.0 11.1 %collective-permute-start.6 = (bf16[384,1024]{1,0:T(8,128)(2,1)S(1)}, bf16[384,1024]{1,0:T(8,128)(2,1)S(1)}, u32[]{:S(2)}, u32[]{:S(2)}) collective-permute-start(bf16[384,1024]{1,0:T(8,128)(2,1)S(1)} %get-tuple-element.58), channel_id=1, source_target_pairs={{0,1},{1,0},{2,3},{3,2},{4,5},{5,4},{6,7},{7,6},{8,9},{9,8},{10,11... | collective-permute-start | bytes 2359304 | tf_op jit(solution)/shard_map/ppermute | solution.py:444
  36.6 7.5 %collective-permute-start.7 = (bf16[1024,384]{1,0:T(8,128)(2,1)S(1)}, bf16[1024,384]{1,0:T(8,128)(2,1)S(1)}, u32[]{:S(2)}, u32[]{:S(2)}) collective-permute-start(bf16[1024,384]{1,0:T(8,128)(2,1)S(1)} %get-tuple-element.59), channel_id=1, source_target_pairs={{0,1},{1,0},{2,3},{3,2},{4,5},{5,4},{6,7},{7,6},{8,9},{9,8},{10,11... | collective-permute-start | bytes 2359304 | tf_op jit(solution)/shard_map/ppermute | solution.py:444
  36.6 7.4 %collective-permute-start.8 = (bf16[256,512]{1,0:T(8,128)(2,1)S(1)}, bf16[256,512]{1,0:T(8,128)(2,1)S(1)}, u32[]{:S(2)}, u32[]{:S(2)}) collective-permute-start(bf16[256,512]{1,0:T(8,128)(2,1)S(1)} %get-tuple-element.67.fold_own), channel_id=1, source_target_pairs={{0,1},{1,0},{2,3},{3,2},{4,5},{5,4},{6,7},{7,6},{8,9},{9,8},{10,11... | collective-permute-start | bytes 786440 | tf_op jit(solution)/shard_map/ppermute | solution.py:444
  44.1 14.2 %copy-start.9 = (s32[24,128]{1,0:T(8,128)S(1)}, s32[24,128]{1,0:T(8,128)}, u32[]{:S(2)}) copy-start(s32[24,128]{1,0:T(8,128)} %src.5) | copy-start | bytes 36868
  44.1 14.2 %copy-start.11 = (s32[24,128]{1,0:T(8,128)S(1)}, s32[24,128]{1,0:T(8,128)}, u32[]{:S(2)}) copy-start(s32[24,128]{1,0:T(8,128)} %dst.5) | copy-start | bytes 36868
  44.1 14.2 %copy-start.13 = (bf16[24,128]{1,0:T(8,128)(2,1)S(1)}, bf16[24,128]{1,0:T(8,128)(2,1)}, u32[]{:S(2)}) copy-start(bf16[24,128]{1,0:T(8,128)(2,1)} %weight.5) | copy-start | bytes 18436
  52.2 1.4 %collective-permute-start.9 = (bf16[100,512]{1,0:T(8,128)(2,1)S(1)}, bf16[100,512]{1,0:T(8,128)(2,1)S(1)}, u32[]{:S(2)}, u32[]{:S(2)}) collective-permute-start(bf16[100,512]{1,0:T(8,128)(2,1)S(1)} %attend.1), channel_id=1, source_target_pairs={{0,1},{1,0},{2,3},{3,2},{4,5},{5,4},{6,7},{7,6},{8,9},{9,8},{10,11... | collective-permute-start | bytes 307208 | tf_op jit(solution)/shard_map/ppermute | solution.py:444
  53.6 9.8 %collective-permute-start.10 = (bf16[2,100,512]{2,1,0:T(8,128)(2,1)S(1)}, bf16[2,100,512]{2,1,0:T(8,128)(2,1)S(1)}, u32[]{:S(2)}, u32[]{:S(2)}) collective-permute-start(bf16[2,100,512]{2,1,0:T(8,128)(2,1)S(1)} %pad_maximum_fusion.own), channel_id=1, source_target_pairs={{0,2},{2,4},{4,6},{6,8},{8,10},{10,12},{12,14},{14,16},{16,18},{18... | collective-permute-start | bytes 614408 | tf_op jit(solution)/shard_map/ppermute | solution.py:451
  63.5 3.4 %collective-permute-start.11 = (bf16[2,100,512]{2,1,0:T(8,128)(2,1)S(1)}, bf16[2,100,512]{2,1,0:T(8,128)(2,1)S(1)}, u32[]{:S(2)}, u32[]{:S(2)}) collective-permute-start(bf16[2,100,512]{2,1,0:T(8,128)(2,1)S(1)} %collective-permute-done.10.sent), channel_id=1, source_target_pairs={{0,1},{1,0},{2,3},{3,2},{4,5},{5,4},{6,7},{7,6},{8,9},{9,8},{10,11... | collective-permute-start | bytes 614408 | tf_op jit(solution)/shard_map/ppermute | solution.py:444

commit v14 on v13

--- a/solution.py
+++ b/solution.py
@@ -23,7 +23,7 @@
 DEC_ROUNDS = 3
 DEC_TILES = 8
 GROUP = 2
-HALO_GROUP = 4
+HALO_GROUP = 8
 EARLY = 2
 MASKED = -1e30
 SCALE = 64 ** (-0.5) * math.log2(math.e)
@@ -248,7 +248,8 @@
                     pair = group * size + member
                 else:
                     pair = jnp.minimum(group + 1, groups - 1) * size + member
-                score(pair, (block + 1) % TILES, part_of(ahead, member))
+                if block + 1 < TILES or groups > 1:
+                    score(pair, (block + 1) % TILES, part_of(ahead, member))
             for member in range(size):
                 finish(group * size + member, block, part_of(here, member))
         return carry

time: 68.9 us -> 68 us (0.987)
  Pallas kernels: 41.2 us -> 40.3 us
    pallas_call x10, Pallas kernels: 41.2 us -> 40.3 us  [call(): pl.pallas_call(body, out_shape=outs, in_specs=specs, out_specs=jax.tree.m...]
where the time goes in v14:
time: 68 us; the launch traced here: 67.7 us
  Pallas kernels  40.3 us (59%)
  starting transfers between devices  21.1 us (31%)
  waiting for transfers between devices  2.76 us (4%)
  local copies, waits for them, and re-layouts  2.6 us (4%)
  between operations  0.94 us (1%)
    pallas_call x10, Pallas kernels, call(): pl.pallas_call(body, out_shape=outs, in_specs=specs, out_specs=jax.tree.m...  40.3 us
    ppermute x2, starting transfers between devices, up_and_down(): return lax.ppermute(value, ('band', 'mp'), pairs)  11.3 us
    ppermute x9, starting transfers between devices, swapped(): return lax.ppermute(value, 'mp', [(0, 1), (1, 0)])  7.83 us
    ppermute x9, waiting for transfers between devices, swapped(): return lax.ppermute(value, 'mp', [(0, 1), (1, 0)])  2.76 us
    unnamed x32, local copies, waits for them, and re-layouts  2.52 us
    ppermute x1, starting transfers between devices, over_the_edge(): return lax.ppermute(value, ('band', 'mp'), pairs)  1.92 us
  transfers between devices with their start and end apart: 12, of which 5 were waited for; matrix products, arithmetic and copies ran while one was open for 0% of the time, Pallas kernels for 46%

profile of v14, /device:TPU:97, one launch (start us, length us, event | category | flops | bytes accessed | tf_op | source)
XLA Modules:
  0.0 67.7 jit_solution(17268877258970271514)
XLA Ops:
  0.0 6.7 %collective-permute-start = (bf16[100,2048]{1,0:T(8,128)(2,1)}, bf16[100,2048]{1,0:T(8,128)(2,1)S(1)}, u32[]{:S(2)}, u32[]{:S(2)}) collective-permute-start(bf16[100,2048]{1,0:T(8,128)(2,1)} %bitcast.18), channel_id=1, source_target_pairs={{0,2},{2,4},{4,6},{6,8},{8,10},{10,12},{12,14},{14,16},{16,18},{18... | collective-permute-start | bytes 1228808 | tf_op jit(solution)/shard_map/ppermute | solution.py:452
  7.3 0.1 stack.48.info
  7.4 0.7 %copy-done.8 = s32[24,128]{1,0:T(8,128)S(1)} copy-done((s32[24,128]{1,0:T(8,128)S(1)}, s32[24,128]{1,0:T(8,128)}, u32[]{:S(2)}) %copy-start.8) | copy-done | bytes 12312
  8.1 0.7 %copy-done.10 = s32[24,128]{1,0:T(8,128)S(1)} copy-done((s32[24,128]{1,0:T(8,128)S(1)}, s32[24,128]{1,0:T(8,128)}, u32[]{:S(2)}) %copy-start.10) | copy-done | bytes 12312
  8.8 0.7 %copy-done.12 = bf16[24,128]{1,0:T(8,128)(2,1)S(1)} copy-done((bf16[24,128]{1,0:T(8,128)(2,1)S(1)}, bf16[24,128]{1,0:T(8,128)(2,1)}, u32[]{:S(2)}) %copy-start.12) | copy-done | bytes 6168
  9.5 2.7 %early.1.spread_in = bf16[3072,1024]{1,0:T(8,128)(2,1)S(1)} custom-call(s32[8]{0:T(128)S(1)} %stack.48.info, s32[24,128]{1,0:T(8,128)S(1)} %copy-done.8, s32[24,128]{1,0:T(8,128)S(1)} %copy-done.10, bf16[24,128]{1,0:T(8,128)(2,1)S(1)} %copy-done.12), custom_call_target="tpu_custom_call" | custom-call | flops 5000000000 | bytes 2000000 | tf_op jit(solution)/shard_map/early/pallas_call | solution.py:45
  12.3 0.0 copy-start.3
  12.3 0.0 copy-start.4
  12.3 0.0 copy-start.2
  12.3 0.6 prepare.1
  12.9 0.3 copy-done.3
  13.2 0.0 collective-permute-start.1
  13.2 0.0 copy-done.4
  13.2 0.5 collective-permute-start.2
  13.7 0.8 %collective-permute-done.1.win_peer = bf16[100,512]{1,0:T(8,128)(2,1)S(1)} collective-permute-done((bf16[100,512]{1,0:T(8,128)(2,1)S(1)}, bf16[100,512]{1,0:T(8,128)(2,1)S(1)}, u32[]{:S(2)}, u32[]{:S(2)}) %collective-permute-start.1) | collective-permute-done | bytes 102432 | tf_op jit(solution)/shard_map/ppermute | solution.py:445
  14.5 0.2 collective-permute-done.2.dec_peer
  14.6 0.0 collective-permute-done.sent
  14.6 0.5 collective-permute-start.3
  15.1 0.0 copy-done.2
  15.1 0.9 %unpack.1.grid_rows = f32[6144,128]{1,0:T(8,128)S(1)} custom-call(s32[8]{0:T(128)S(1)} %stack.48.info, bf16[100,2048]{1,0:T(8,128)(2,1)S(1)} %bitcast.19, bf16[100,2048]{1,0:T(8,128)(2,1)S(1)} %collective-permute-done.sent), custom_call_target="tpu_custom_call" | custom-call | flops 2000000000 | bytes 2000000 | tf_op jit(solution)/shard_map/unpack/pallas_call | solution.py:45
  16.0 0.5 collective-permute-done.3.swapped_rows
  16.5 0.4 collective-permute-start.5
  16.9 9.3 %encode.1 = (f32[6144,128]{1,0:T(8,128)S(1)}, bf16[512,1024]{1,0:T(8,128)(2,1)S(1)}, bf16[512,1024]{1,0:T(8,128)(2,1)S(1)}, bf16[384,1024]{1,0:T(8,128)(2,1)S(1)}) custom-call(s32[8]{0:T(128)S(1)} %stack.48.info, s32[64,128]{1,0:T(8,128)S(1)} %get-tuple-element.40.src, f32[6144,128]{1,0:T(8,128)S(1)} %unpack.1.grid_rows, ...), custom_call_target="tpu_custom_call", output_to_operand_aliasing={{0}: (2, {})} | custom-call | flops 7000000000 | bytes 2000000 | tf_op jit(solution)/shard_map/encode/pallas_call | solution.py:45
  26.2 1.9 %collective-permute-start.4 = (bf16[384,1024]{1,0:T(8,128)(2,1)S(1)}, bf16[384,1024]{1,0:T(8,128)(2,1)S(1)}, u32[]{:S(2)}, u32[]{:S(2)}) collective-permute-start(bf16[384,1024]{1,0:T(8,128)(2,1)S(1)} %get-tuple-element.53), channel_id=1, source_target_pairs={{1,2},{3,4},{5,6},{7,8},{9,10},{11,12},{13,14},{15,16},{17,18},{19... | collective-permute-start | bytes 2359304 | tf_op jit(solution)/shard_map/ppermute | solution.py:459
  28.1 0.0 collective-permute-done.5.w_peer
  28.1 0.0 copy-start.15
  28.1 4.9 %project.1 = (bf16[512,1024]{1,0:T(8,128)(2,1)S(1)}, bf16[512,1024]{1,0:T(8,128)(2,1)S(1)}, bf16[1024,512]{1,0:T(8,128)(2,1)S(1)}, bf16[384,1024]{1,0:T(8,128)(2...) custom-call(s32[8]{0:T(128)S(1)} %stack.48.info, ...), custom_call_target="tpu_custom_call" | custom-call | flops 6000000000 | bytes 2000000 | tf_op jit(solution)/shard_map/project/pallas_call | solution.py:45
  33.0 3.5 %collective-permute-start.6 = (bf16[384,1024]{1,0:T(8,128)(2,1)S(1)}, bf16[384,1024]{1,0:T(8,128)(2,1)S(1)}, u32[]{:S(2)}, u32[]{:S(2)}) collective-permute-start(bf16[384,1024]{1,0:T(8,128)(2,1)S(1)} %get-tuple-element.58), channel_id=1, source_target_pairs={{0,1},{1,0},{2,3},{3,2},{4,5},{5,4},{6,7},{7,6},{8,9},{9,8},{10,11... | collective-permute-start | bytes 2359304 | tf_op jit(solution)/shard_map/ppermute | solution.py:445
  36.6 0.1 collective-permute-start.7
  36.6 0.4 collective-permute-start.8
  37.1 7.0 %own.1 = (f32[1024,512]{1,0:T(8,128)S(1)}, f32[8,8,1024]{2,1,0:T(8,128)S(1)}, bf16[896,128]{1,0:T(8,128)(2,1)S(1)}) custom-call(s32[32]{0:T(128)S(1)} %copy-done.15, bf16[512,1024]{1,0:T(8,128)(2,1)S(1)} %get-tuple-element.60.queries, bf16[512,1024]{1,0:T(8,128)(2,1)S(1)} %get-tuple-element.61.keys, bf16[1024,512]{1,0:T(8,128)(2,1)S(1)} %get-tuple-element.62.values_t), custom_call_target="tpu_custom_call" | custom-call | flops 8000000000 | bytes 2000000 | tf_op jit(solution)/shard_map/own/pallas_call | solution.py:45
  44.0 0.0 collective-permute-done.4.halo
  44.0 0.0 collective-permute-done.8.fold_peer
  44.1 0.0 collective-permute-done.6.peer_keys
  44.1 0.0 collective-permute-done.7.peer_values
  44.1 0.0 copy-start.9
  44.1 0.0 copy-start.11
  44.1 0.0 copy-start.13
  44.1 7.2 %attend.1 = bf16[100,512]{1,0:T(8,128)(2,1)S(1)} custom-call(s32[8]{0:T(128)S(1)} %stack.48.info, bf16[384,1024]{1,0:T(8,128)(2,1)S(1)} %collective-permute-done.4.halo, bf16[384,1024]{1,0:T(8,128)(2,1)S(1)} %collective-permute-done.6.peer_keys, bf16[1024,384]{1,0:T(8,128)(2,1)S(1)} %collective-permute-done.7.peer_values, ...), custom_call_target="tpu_custom_call" | custom-call | flops 10000000000 | bytes 2000000 | tf_op jit(solution)/shard_map/attend/pallas_call | solution.py:45
  51.3 0.2 collective-permute-start.9
  51.5 1.2 %collective-permute-done.9 = bf16[100,512]{1,0:T(8,128)(2,1)S(1)} collective-permute-done((bf16[100,512]{1,0:T(8,128)(2,1)S(1)}, bf16[100,512]{1,0:T(8,128)(2,1)S(1)}, u32[]{:S(2)}, u32[]{:S(2)}) %collective-permute-start.9) | collective-permute-done | bytes 102432 | tf_op jit(solution)/shard_map/ppermute | solution.py:445
  52.8 4.6 %collective-permute-start.10 = (bf16[2,100,512]{2,1,0:T(8,128)(2,1)S(1)}, bf16[2,100,512]{2,1,0:T(8,128)(2,1)S(1)}, u32[]{:S(2)}, u32[]{:S(2)}) collective-permute-start(bf16[2,100,512]{2,1,0:T(8,128)(2,1)S(1)} %pad_maximum_fusion.own), channel_id=1, source_target_pairs={{0,2},{2,4},{4,6},{6,8},{8,10},{10,12},{12,14},{14,16},{16,18},{18... | collective-permute-start | bytes 614408 | tf_op jit(solution)/shard_map/ppermute | solution.py:452
  57.4 5.1 %spread.1 = (bf16[3072,1024]{1,0:T(8,128)(2,1)S(1)}, f32[100,1024]{1,0:T(8,128)S(1)}) custom-call(s32[8]{0:T(128)S(1)} %stack.48.info, bf16[3072,1024]{1,0:T(8,128)(2,1)S(1)} %early.1.spread_in, bf16[2,100,512]{2,1,0:T(8,128)(2,1)S(1)} %pad_maximum_fusion.own, s32[24,128]{1,0:T(8,128)S(1)} %copy-done.9, ...), custom_call_target="tpu_custom_call", output_to_operand_aliasing={{0}: (1, {})} | custom-call | flops 8000000000 | bytes 2000000 | tf_op jit(solution)/shard_map/spread/pallas_call | solution.py:45
  62.6 0.0 collective-permute-done.10.sent
  62.6 2.3 %collective-permute-start.11 = (bf16[2,100,512]{2,1,0:T(8,128)(2,1)S(1)}, bf16[2,100,512]{2,1,0:T(8,128)(2,1)S(1)}, u32[]{:S(2)}, u32[]{:S(2)}) collective-permute-start(bf16[2,100,512]{2,1,0:T(8,128)(2,1)S(1)} %collective-permute-done.10.sent), channel_id=1, source_target_pairs={{0,1},{1,0},{2,3},{3,2},{4,5},{5,4},{6,7},{7,6},{8,9},{9,8},{10,11... | collective-permute-start | bytes 614408 | tf_op jit(solution)/shard_map/ppermute | solution.py:445
  64.9 1.0 %sent.1.total = f32[100,1024]{1,0:T(8,128)S(1)} custom-call(s32[8]{0:T(128)S(1)} %stack.48.info, bf16[2,100,512]{2,1,0:T(8,128)(2,1)S(1)} %collective-permute-done.10.sent, bf16[3072,1024]{1,0:T(8,128)(2,1)S(1)} %get-tuple-element.71.spread, f32[100,1024]{1,0:T(8,128)S(1)} %get-tuple-element.72.base), custom_call_target="tpu_custom_call" | custom-call | flops 1000000000 | bytes 2000000 | tf_op jit(solution)/shard_map/sent/pallas_call | solution.py:45
  65.9 0.1 collective-permute-done.11.swapped_rows
  66.0 1.7 %decode.1 = bf16[100,1024]{1,0:T(8,128)(2,1)} custom-call(s32[8]{0:T(128)S(1)} %stack.48.info, bf16[2,100,512]{2,1,0:T(8,128)(2,1)S(1)} %collective-permute-done.11.swapped_rows, bf16[3072,1024]{1,0:T(8,128)(2,1)S(1)} %get-tuple-element.71.spread, f32[100,1024]{1,0:T(8,128)S(1)} %sent.1.total), custom_call_target="tpu_custom_call" | custom-call | flops 1000000000 | bytes 2000000 | tf_op jit(solution)/shard_map/decode/pallas_call | solution.py:45
  (20 shorter events, 0.1 us)
Async XLA Ops:
  0.0 14.6 %collective-permute-start = (bf16[100,2048]{1,0:T(8,128)(2,1)}, bf16[100,2048]{1,0:T(8,128)(2,1)S(1)}, u32[]{:S(2)}, u32[]{:S(2)}) collective-permute-start(bf16[100,2048]{1,0:T(8,128)(2,1)} %bitcast.18), channel_id=1, source_target_pairs={{0,2},{2,4},{4,6},{6,8},{8,10},{10,12},{12,14},{14,16},{16,18},{18... | collective-permute-start | bytes 1228808 | tf_op jit(solution)/shard_map/ppermute | solution.py:452
  7.4 0.7 %copy-start.8 = (s32[24,128]{1,0:T(8,128)S(1)}, s32[24,128]{1,0:T(8,128)}, u32[]{:S(2)}) copy-start(s32[24,128]{1,0:T(8,128)} %src.5) | copy-start | bytes 36868
  8.1 0.7 %copy-start.10 = (s32[24,128]{1,0:T(8,128)S(1)}, s32[24,128]{1,0:T(8,128)}, u32[]{:S(2)}) copy-start(s32[24,128]{1,0:T(8,128)} %dst.5) | copy-start | bytes 36868
  8.8 0.7 %copy-start.12 = (bf16[24,128]{1,0:T(8,128)(2,1)S(1)}, bf16[24,128]{1,0:T(8,128)(2,1)}, u32[]{:S(2)}) copy-start(bf16[24,128]{1,0:T(8,128)(2,1)} %weight.5) | copy-start | bytes 18436
  9.5 2.7 %copy-start.5 = (s32[64,128]{1,0:T(8,128)S(1)}, s32[64,128]{1,0:T(8,128)}, u32[]{:S(2)}) copy-start(s32[64,128]{1,0:T(8,128)} %src.4) | copy-start | bytes 98308
  9.5 2.7 %copy-start.6 = (s32[64,128]{1,0:T(8,128)S(1)}, s32[64,128]{1,0:T(8,128)}, u32[]{:S(2)}) copy-start(s32[64,128]{1,0:T(8,128)} %dst.4) | copy-start | bytes 98308
  9.5 2.7 %copy-start.7 = (bf16[64,128]{1,0:T(8,128)(2,1)S(1)}, bf16[64,128]{1,0:T(8,128)(2,1)}, u32[]{:S(2)}) copy-start(bf16[64,128]{1,0:T(8,128)(2,1)} %weight.4) | copy-start | bytes 49156
  9.5 2.7 %copy-start.14 = (f32[1024]{0:T(1024)S(1)}, f32[1024]{0:T(1024)}, u32[]{:S(2)}) copy-start(f32[1024]{0:T(1024)} %param.20) | copy-start | bytes 12292
  12.3 0.9 %copy-start.3 = (bf16[100,512]{1,0:T(8,128)(2,1)S(1)}, bf16[100,512]{1,0:T(8,128)(2,1)}, u32[]{:S(2)}) copy-start(bf16[100,512]{1,0:T(8,128)(2,1)} %win_own) | copy-start | bytes 307204
  12.3 0.9 %copy-start.4 = (bf16[512,100]{0,1:T(8,128)(2,1)S(1)}, bf16[512,100]{0,1:T(8,128)(2,1)}, u32[]{:S(2)}) copy-start(bf16[512,100]{0,1:T(8,128)(2,1)} %param.24) | copy-start | bytes 307204
  12.3 2.8 %copy-start.2 = (bf16[2048,100]{0,1:T(8,128)(2,1)S(1)}, bf16[2048,100]{0,1:T(8,128)(2,1)}, u32[]{:S(2)}) copy-start(bf16[2048,100]{0,1:T(8,128)(2,1)} %param.14) | copy-start | bytes 1228804
  13.2 3.4 %copy-start = (bf16[1024,3,512]{2,0,1:T(8,128)(2,1)S(1)}, bf16[1024,3,512]{2,0,1:T(8,128)(2,1)}, u32[]{:S(2)}) copy-start(bf16[1024,3,512]{2,0,1:T(8,128)(2,1)} %param.21) | copy-start | bytes 9437188
  13.2 1.3 %collective-permute-start.1 = (bf16[100,512]{1,0:T(8,128)(2,1)S(1)}, bf16[100,512]{1,0:T(8,128)(2,1)S(1)}, u32[]{:S(2)}, u32[]{:S(2)}) collective-permute-start(bf16[100,512]{1,0:T(8,128)(2,1)S(1)} %copy-done.3), channel_id=1, source_target_pairs={{0,1},{1,0},{2,3},{3,2},{4,5},{5,4},{6,7},{7,6},{8,9},{9,8},{10,11... | collective-permute-start | bytes 307208 | tf_op jit(solution)/shard_map/ppermute | solution.py:445
  13.2 1.4 %collective-permute-start.2 = (bf16[100,512]{1,0:T(8,128)(2,1)S(1)}, bf16[100,512]{1,0:T(8,128)(2,1)S(1)}, u32[]{:S(2)}, u32[]{:S(2)}) collective-permute-start(bf16[100,512]{1,0:T(8,128)(2,1)S(1)} %bitcast.21), channel_id=1, source_target_pairs={{0,1},{1,0},{2,3},{3,2},{4,5},{5,4},{6,7},{7,6},{8,9},{9,8},{10,11... | collective-permute-start | bytes 307208 | tf_op jit(solution)/shard_map/ppermute | solution.py:445
  14.6 1.9 %collective-permute-start.3 = (bf16[100,2048]{1,0:T(8,128)(2,1)S(1)}, bf16[100,2048]{1,0:T(8,128)(2,1)S(1)}, u32[]{:S(2)}, u32[]{:S(2)}) collective-permute-start(bf16[100,2048]{1,0:T(8,128)(2,1)S(1)} %collective-permute-done.sent), channel_id=1, source_target_pairs={{0,1},{1,0},{2,3},{3,2},{4,5},{5,4},{6,7},{7,6},{8,9},{9,8},{10,11... | collective-permute-start | bytes 1228808 | tf_op jit(solution)/shard_map/ppermute | solution.py:445
  16.5 11.6 %collective-permute-start.5 = (bf16[3,1024,512]{2,1,0:T(8,128)(2,1)S(1)}, bf16[3,1024,512]{2,1,0:T(8,128)(2,1)S(1)}, u32[]{:S(2)}, u32[]{:S(2)}) collective-permute-start(bf16[3,1024,512]{2,1,0:T(8,128)(2,1)S(1)} %bitcast.15), channel_id=1, source_target_pairs={{0,1},{1,0},{2,3},{3,2},{4,5},{5,4},{6,7},{7,6},{8,9},{9,8},{10,11... | collective-permute-start | bytes 9437192 | tf_op jit(solution)/shard_map/ppermute | solution.py:445
  16.9 11.2 %copy-start.1 = (bf16[512,1024]{1,0:T(8,128)(2,1)S(1)}, bf16[512,1024]{1,0:T(8,128)(2,1)}, u32[]{:S(2)}) copy-start(bf16[512,1024]{1,0:T(8,128)(2,1)} %w_out.1) | copy-start | bytes 3145732
  26.2 17.9 %collective-permute-start.4 = (bf16[384,1024]{1,0:T(8,128)(2,1)S(1)}, bf16[384,1024]{1,0:T(8,128)(2,1)S(1)}, u32[]{:S(2)}, u32[]{:S(2)}) collective-permute-start(bf16[384,1024]{1,0:T(8,128)(2,1)S(1)} %get-tuple-element.53), channel_id=1, source_target_pairs={{1,2},{3,4},{5,6},{7,8},{9,10},{11,12},{13,14},{15,16},{17,18},{19... | collective-permute-start | bytes 2359304 | tf_op jit(solution)/shard_map/ppermute | solution.py:459
  28.1 8.9 %copy-start.15 = (s32[32]{0:T(128)S(1)}, s32[32]{0:T(128)}, u32[]{:S(2)}) copy-start(s32[32]{0:T(128)} %offsets.1) | copy-start | bytes 388
  33.0 11.1 %collective-permute-start.6 = (bf16[384,1024]{1,0:T(8,128)(2,1)S(1)}, bf16[384,1024]{1,0:T(8,128)(2,1)S(1)}, u32[]{:S(2)}, u32[]{:S(2)}) collective-permute-start(bf16[384,1024]{1,0:T(8,128)(2,1)S(1)} %get-tuple-element.58), channel_id=1, source_target_pairs={{0,1},{1,0},{2,3},{3,2},{4,5},{5,4},{6,7},{7,6},{8,9},{9,8},{10,11... | collective-permute-start | bytes 2359304 | tf_op jit(solution)/shard_map/ppermute | solution.py:445
  36.6 7.5 %collective-permute-start.7 = (bf16[1024,384]{1,0:T(8,128)(2,1)S(1)}, bf16[1024,384]{1,0:T(8,128)(2,1)S(1)}, u32[]{:S(2)}, u32[]{:S(2)}) collective-permute-start(bf16[1024,384]{1,0:T(8,128)(2,1)S(1)} %get-tuple-element.59), channel_id=1, source_target_pairs={{0,1},{1,0},{2,3},{3,2},{4,5},{5,4},{6,7},{7,6},{8,9},{9,8},{10,11... | collective-permute-start | bytes 2359304 | tf_op jit(solution)/shard_map/ppermute | solution.py:445
  36.6 7.4 %collective-permute-start.8 = (bf16[256,512]{1,0:T(8,128)(2,1)S(1)}, bf16[256,512]{1,0:T(8,128)(2,1)S(1)}, u32[]{:S(2)}, u32[]{:S(2)}) collective-permute-start(bf16[256,512]{1,0:T(8,128)(2,1)S(1)} %get-tuple-element.67.fold_own), channel_id=1, source_target_pairs={{0,1},{1,0},{2,3},{3,2},{4,5},{5,4},{6,7},{7,6},{8,9},{9,8},{10,11... | collective-permute-start | bytes 786440 | tf_op jit(solution)/shard_map/ppermute | solution.py:445
  44.1 13.3 %copy-start.9 = (s32[24,128]{1,0:T(8,128)S(1)}, s32[24,128]{1,0:T(8,128)}, u32[]{:S(2)}) copy-start(s32[24,128]{1,0:T(8,128)} %src.5) | copy-start | bytes 36868
  44.1 13.3 %copy-start.11 = (s32[24,128]{1,0:T(8,128)S(1)}, s32[24,128]{1,0:T(8,128)}, u32[]{:S(2)}) copy-start(s32[24,128]{1,0:T(8,128)} %dst.5) | copy-start | bytes 36868
  44.1 13.3 %copy-start.13 = (bf16[24,128]{1,0:T(8,128)(2,1)S(1)}, bf16[24,128]{1,0:T(8,128)(2,1)}, u32[]{:S(2)}) copy-start(bf16[24,128]{1,0:T(8,128)(2,1)} %weight.5) | copy-start | bytes 18436
  51.3 1.4 %collective-permute-start.9 = (bf16[100,512]{1,0:T(8,128)(2,1)S(1)}, bf16[100,512]{1,0:T(8,128)(2,1)S(1)}, u32[]{:S(2)}, u32[]{:S(2)}) collective-permute-start(bf16[100,512]{1,0:T(8,128)(2,1)S(1)} %attend.1), channel_id=1, source_target_pairs={{0,1},{1,0},{2,3},{3,2},{4,5},{5,4},{6,7},{7,6},{8,9},{9,8},{10,11... | collective-permute-start | bytes 307208 | tf_op jit(solution)/shard_map/ppermute | solution.py:445
  52.8 9.8 %collective-permute-start.10 = (bf16[2,100,512]{2,1,0:T(8,128)(2,1)S(1)}, bf16[2,100,512]{2,1,0:T(8,128)(2,1)S(1)}, u32[]{:S(2)}, u32[]{:S(2)}) collective-permute-start(bf16[2,100,512]{2,1,0:T(8,128)(2,1)S(1)} %pad_maximum_fusion.own), channel_id=1, source_target_pairs={{0,2},{2,4},{4,6},{6,8},{8,10},{10,12},{12,14},{14,16},{16,18},{18... | collective-permute-start | bytes 614408 | tf_op jit(solution)/shard_map/ppermute | solution.py:452
  62.6 3.4 %collective-permute-start.11 = (bf16[2,100,512]{2,1,0:T(8,128)(2,1)S(1)}, bf16[2,100,512]{2,1,0:T(8,128)(2,1)S(1)}, u32[]{:S(2)}, u32[]{:S(2)}) collective-permute-start(bf16[2,100,512]{2,1,0:T(8,128)(2,1)S(1)} %collective-permute-done.10.sent), channel_id=1, source_target_pairs={{0,1},{1,0},{2,3},{3,2},{4,5},{5,4},{6,7},{7,6},{8,9},{9,8},{10,11... | collective-permute-start | bytes 614408 | tf_op jit(solution)/shard_map/ppermute | solution.py:445
